TPU v7x, 32 devices: a whole 2x2x4 slice. The times are simulated.
32 devices in a mesh: chan: 8 (over y, x, core), tile: 4 (over z).
Axes of the slice: x: 2, y: 2, z: 4, core: 2. Of those that a mesh axis runs over, the one named last changes fastest.
Arguments:
- generator: bfloat16 [32, 1024, 1024], P('chan', 'tile'), as said below
- hamiltonian: bfloat16 [32, 1024, 1024], P('chan', 'tile')
- chan_sizes: int32 [32], P('chan'), may hold values from 512 to 1024
- pair_occupation: int32 [2, 32, 1024], P(None, 'chan'), may hold values 0 or 1
- recoupled_occupation: int32 [2, 32, 1024], P(None, ('chan', 'tile')), may hold values 0 or 1
- recouple_map: int32 [32, 1024], P(('chan', 'tile')), may hold values from 0 to 1023, each once within a row
- recouple_weights: float32 [32, 1024, 1024], P(('chan', 'tile')), may hold values from -2 to 2
Outputs:
- commutator: bfloat16 [32, 1024, 1024], P('chan', 'tile')
Inputs may be any that keep to these rules, and one draw needn't show every extreme that they name: generator[c] is antisymmetric and hamiltonian[c] is symmetric in every channel.
All inputs are finite; a program needn't handle non-finite values. No bound on the sum of `pair_occupation` or of `recoupled_occupation` on one device may be relied on, other than what follows from the above.
Results may differ from a plain program's by a relative error of at most 0.0045.
Values may be sent and summed in bfloat16 or wider, within the bound.
No kernel may reach another device: no remote copies, remote signals or barrier semaphores. Data moves between devices by JAX's collectives and lax.ppermute only.
A program may use at most 128 MiB of HBM per device.

v0:
```python
import jax
import jax.numpy as jnp
from jax import lax
from jax.sharding import PartitionSpec as P


def per_device(
    generator,
    hamiltonian,
    chan_sizes,
    pair_occupation,
    recoupled_occupation,
    recouple_map,
    recouple_weights,
):
    chan_count, tile_rows, states = generator.shape
    tile_place = lax.axis_index("tile")
    columns = lax.broadcasted_iota(jnp.int32, (chan_count, states), 1)
    live_columns = columns < chan_sizes[:, None]
    row_index = tile_place * tile_rows + lax.broadcasted_iota(jnp.int32, (chan_count, tile_rows), 1)
    live_rows = row_index < chan_sizes[:, None]
    live_mask = live_rows[:, :, None] & live_columns[:, None, :]
    zero = jnp.zeros((), jnp.bfloat16)
    eta_live = jnp.where(live_mask, generator, zero)
    gamma_live = jnp.where(live_mask, hamiltonian, zero)
    weight = (
        (1 - pair_occupation[0] - pair_occupation[1]) * live_columns.astype(jnp.int32)
    ).astype(jnp.bfloat16)
    eta_weighted = eta_live * weight[:, None, :]
    first = jnp.einsum(
        "crk,ckj->crj",
        eta_weighted,
        lax.all_gather(gamma_live, "tile", axis=1, tiled=True),
        preferred_element_type=jnp.float32,
    )
    mirrored = lax.all_to_all(first, "tile", split_axis=2, concat_axis=1, tiled=True)
    ladder = first + jnp.swapaxes(mirrored, 1, 2)
    block_rows = chan_count * tile_rows
    ph_count, ph_states = recouple_map.shape
    flat_eta = eta_live.reshape(block_rows, states)
    flat_gamma = gamma_live.reshape(block_rows, states)
    recv_eta, recv_gamma = (
        lax.all_to_all(flat_eta, "chan", split_axis=0, concat_axis=0, tiled=True),
        lax.all_to_all(flat_gamma, "chan", split_axis=0, concat_axis=0, tiled=True),
    )
    recv_eta = recv_eta.reshape(block_rows, ph_count, ph_states)
    recv_gamma = recv_gamma.reshape(block_rows, ph_count, ph_states)
    weights_turned = jnp.transpose(recouple_weights, (1, 0, 2))
    index_map = recouple_map[None, :, :]
    eta_bar = (
        jnp.take_along_axis(recv_eta, index_map, axis=2).astype(jnp.float32) * weights_turned
    ).astype(jnp.bfloat16)
    gamma_bar = (
        jnp.take_along_axis(recv_gamma, index_map, axis=2).astype(jnp.float32) * weights_turned
    ).astype(jnp.bfloat16)
    signs = (recoupled_occupation[0] - recoupled_occupation[1]).astype(jnp.bfloat16)
    crossed = jnp.einsum(
        "iqk,kqj->iqj", eta_bar * signs[None, :, :], gamma_bar, preferred_element_type=jnp.float32
    )
    crossed = crossed - jnp.einsum(
        "iqk,kqj->iqj", gamma_bar * signs[None, :, :], eta_bar, preferred_element_type=jnp.float32
    )
    inverse = jnp.argsort(recouple_map, axis=1)
    back_bar = jnp.take_along_axis(crossed * weights_turned, inverse[None, :, :], axis=2).astype(
        jnp.bfloat16
    )
    back = lax.all_to_all(
        back_bar.reshape(block_rows, states), "chan", split_axis=0, concat_axis=0, tiled=True
    )
    total = ladder + back.reshape(chan_count, tile_rows, states).astype(jnp.float32)
    return jnp.where(live_mask, total, jnp.zeros((), jnp.float32)).astype(jnp.bfloat16)


def solution(mesh):
    return jax.shard_map(
        per_device,
        mesh=mesh,
        in_specs=(
            P("chan", "tile", None),
            P("chan", "tile", None),
            P("chan"),
            P(None, "chan", None),
            P(None, ("chan", "tile"), None),
            P(("chan", "tile"), None),
            P(("chan", "tile"), None, None),
        ),
        out_specs=P("chan", "tile", None),
        check_vma=False,
    )
```

profile of v0, /device:TPU:0, one launch (start us, length us, event | category | flops | bytes accessed | tf_op | source)
XLA Modules:
  0.0 323.6 jit_solution(17872049762530281484)
XLA Ops:
  7.4 0.7 iota_compare_fusion
  8.1 0.7 broadcast_compare_fusion
  8.8 5.3 %and_select_fusion.2 = (bf16[4,256,1024]{2,1,0:T(8,128)(2,1)}, bf16[4,256,1024]{2,1,0:T(8,128)(2,1)}) fusion(bf16[4,256,1024]{2,1,0:T(8,128)(2,1)} %param.9, pred[4,1024]{1,0:T(4,128)(4,1)S(1)} %iota_compare_fusion, pred[4,256]{1,0:T(4,128)(4,1)S(1)} %broadcast_compare_fusion, bf16[4,256,1024]{2,1,0:T(8,128)(2,1)} %param.10), kind=kLoop, calls=%fused_computation.5 | loop fusion | flops 3145728 | bytes 8393728 | tf_op jit(solution)/shard_map/jit(_where)/select_n | solution.py:24
  14.2 1.6 copy-done.1
  15.7 31.7 %all_to_all.42 = bf16[8,128,1024]{2,1,0:T(8,128)(2,1)} all-to-all(bf16[8,128,1024]{2,1,0:T(8,128)(2,1)S(1)} %bitcast.106), channel_id=1, replica_groups=mesh['chan'=8,'tile'=4] {'chan'}, dimensions={0} | all-to-all | bytes 4194304 | tf_op jit(solution)/shard_map/all_to_all | solution.py:44
  47.4 3.7 %all-to-all-start.2 = ((bf16[8,128,1024]{2,1,0:T(8,128)(2,1)}), bf16[8,128,1024]{2,1,0:T(8,128)(2,1)S(1)}, u32[]{:S(2)}, u32[]{:S(2)}) async-start(bf16[8,128,1024]{2,1,0:T(8,128)(2,1)} %bitcast.14), calls=%async_computation.2 | async-start | bytes 4194304 | tf_op jit(solution)/shard_map/all_to_all | solution.py:43
  51.2 115.4 %all-gather.2.cloned.1.call-done = bf16[4,1024,1024]{2,1,0:T(8,128)(2,1)} async-done(((bf16[4,256,1024]{2,1,0:T(8,128)(2,1)}), bf16[4,1024,1024]{2,1,0:T(8,128)(2,1)}) %all-gather.2.cloned.1.call-update) | async-done | bytes 8388624 | tf_op jit(solution)/shard_map/all_gather | solution.py:33
  166.7 8.3 %fusion.12 = f32[4,256,1024]{2,1,0:T(8,128)} fusion(bf16[4,1024,1024]{2,1,0:T(8,128)(2,1)} %all-gather.2.cloned.1.call-done, bf16[4,256,1024]{2,1,0:T(8,128)(2,1)} %get-tuple-element.10, bf16[4,1024]{1,0:T(4,128)(2,1)S(1)} %fusion.25), kind=kOutput, calls=%fused_computation.27 | convolution fusion | flops 2148532224 | bytes 14688256 | tf_op jit(solution)/shard_map/crk,ckj->crj/dot_general | solution.py:30
  175.0 5.3 %copy.18 = f32[4,256,1024]{1,0,2:T(4,128)} copy(f32[4,256,1024]{2,1,0:T(8,128)} %fusion.12) | data formatting | bytes 8388608 | tf_op jit(solution)/shard_map/crk,ckj->crj/dot_general | solution.py:30
  180.3 1.3 copy-done.5
  181.6 4.8 %all-to-all-start = ((f32[4,256,1024]{1,0,2:T(4,128)}), f32[4,256,1024]{1,0,2:T(4,128)}, u32[]{:S(2)}, u32[]{:S(2)}) async-start(f32[4,256,1024]{1,0,2:T(4,128)} %copy.18), calls=%async_computation | async-start | bytes 8388608 | tf_op jit(solution)/shard_map/all_to_all | solution.py:36
  186.4 0.2 sort.19.cloned.1.call-start
  186.7 0.6 iota.25
  187.4 5.5 %copy.21 = f32[1,1024,1024]{1,2,0:T(8,128)} copy(f32[1,1024,1024]{2,1,0:T(8,128)} %param.15) | data formatting | bytes 8388608 | tf_op args[6]
  192.9 1.1 sort.19.cloned.1.call-done
  194.0 0.7 compare_and_fusion
  194.7 0.7 compare_select_fusion.1
  195.4 2.6 copy.24
  198.0 2.9 copy.25
  200.8 7.9 %gather_fusion.1 = bf16[1024,1024]{1,0:T(8,128)(2,1)} fusion(bf16[1024,1024]{0,1:T(8,128)(2,1)} %bitcast.105, s32[1024]{0:T(1024)S(1)} %broadcast_clamp_fusion.1), kind=kCustom, calls=%fused_computation.clone | custom fusion | bytes 4198400 | tf_op jit(solution)/shard_map/jit(take_along_axis)/gather | solution.py:54
  208.8 5.3 %gather_fusion.2 = bf16[1024,1024]{1,0:T(8,128)(2,1)} fusion(bf16[1024,1024]{0,1:T(8,128)(2,1)S(1)} %bitcast.104, s32[1024]{0:T(1024)S(1)} %broadcast_clamp_fusion.1), kind=kCustom, calls=%fused_computation.1.clone | custom fusion | bytes 4198400 | tf_op jit(solution)/shard_map/jit(take_along_axis)/gather | solution.py:51
  214.1 7.3 %fusion.4 = f32[1024,1024]{1,0:T(8,128)S(1)} fusion(bf16[1024]{0:T(1024)(128)(2,1)S(1)} %convert_reduce_fusion, f32[1,1024,1024]{1,2,0:T(8,128)} %copy.21, bf16[1024,1024]{1,0:T(8,128)(2,1)} %gather_fusion.2, pred[1024]{0:T(1024)(128)(4,1)S(1)} %get-tuple-element.8, bf16[1024,1024]{1,0:T(8,128)(2,1)} %gather_fusion.1), kind=kOutput, calls=%fused_computation.19 | convolution fusion | flops 2156920832 | bytes 12585984 | tf_op jit(solution)/shard_map/iqk,kqj->iqj/dot_general | solution.py:60
  221.4 2.8 fusion.1
  224.3 5.3 %gather_fusion = bf16[1024,1024]{1,0:T(8,128)(2,1)} fusion(bf16[1024,1024]{0,1:T(8,128)(2,1)S(1)} %fusion.1, s32[1024]{0:T(1024)S(1)} %broadcast_clamp_fusion), kind=kCustom, calls=%fused_computation.2 | custom fusion | bytes 4198400 | tf_op jit(solution)/shard_map/jit(take_along_axis)/gather | solution.py:64
  229.6 2.9 copy.26
  232.5 1.9 select_convert_fusion
  234.4 45.8 %all-to-all-done = f32[4,256,1024]{1,0,2:T(4,128)} async-done(((f32[4,256,1024]{1,0,2:T(4,128)}), f32[4,256,1024]{1,0,2:T(4,128)}, u32[]{:S(2)}, u32[]{:S(2)}) %all-to-all-start) | async-done | bytes 4194336 | tf_op jit(solution)/shard_map/all_to_all | solution.py:36
  280.1 3.8 %all-to-all-start.3 = ((bf16[8,128,1024]{2,1,0:T(8,128)(2,1)}), bf16[8,128,1024]{2,1,0:T(8,128)(2,1)S(1)}, u32[]{:S(2)}, u32[]{:S(2)}) async-start(bf16[8,128,1024]{2,1,0:T(8,128)(2,1)} %select_convert_fusion), calls=%async_computation.3 | async-start | bytes 4194304 | tf_op jit(solution)/shard_map/all_to_all | solution.py:67
  284.0 6.8 %copy.28 = f32[4,256,4,256]{1,2,3,0:T(4,128)} copy(f32[4,256,4,256]{1,0,3,2:T(4,128)} %bitcast.1) | data formatting | bytes 8388608 | tf_op jit(solution)/shard_map/all_to_all | solution.py:36
  290.8 5.8 %all_to_all.32 = f32[4,1024,256]{1,2,0:T(8,128)} reshape(f32[4,4,256,256]{2,1,3,0:T(4,128)} %bitcast.107) | data formatting | bytes 8388608 | tf_op jit(solution)/shard_map/all_to_all | solution.py:36
  296.6 13.8 %all-to-all-done.3 = bf16[8,128,1024]{2,1,0:T(8,128)(2,1)S(1)} async-done(((bf16[8,128,1024]{2,1,0:T(8,128)(2,1)}), bf16[8,128,1024]{2,1,0:T(8,128)(2,1)S(1)}, u32[]{:S(2)}, u32[]{:S(2)}) %all-to-all-start.3) | async-done | bytes 2097184 | tf_op jit(solution)/shard_map/all_to_all | solution.py:67
  310.4 5.7 %fusion = bf16[4,256,1024]{2,1,0:T(8,128)(2,1)} fusion(f32[4,256,1024]{2,1,0:T(8,128)} %fusion.12, f32[4,1024,256]{1,2,0:T(8,128)} %all_to_all.32, pred[4,1024]{1,0:T(4,128)(4,1)S(1)} %iota_compare_fusion, pred[4,256]{1,0:T(4,128)(4,1)S(1)} %broadcast_compare_fusion, bf16[4,256,1024]{2,1,0:T(8,128)(2,1)S(1)} %bitcast.112), kind=kLoop, calls=%fused_computation.6 | loop fusion | flops 6291456 | bytes 12588032 | tf_op jit(solution)/shard_map/convert_element_type | solution.py:71
  (28 shorter events, 0.2 us)
Async XLA Ops:
  7.4 159.3 %all-gather.2.cloned.1.call-start = ((), (), s32[]{:S(2)}) async-start(), calls=%async_computation.4 | async-start | bytes 10485760 | tf_op jit(solution)/shard_map/all_gather | solution.py:33
  14.1 1.6 copy-start.1
  47.4 3.8 %copy-start.6 = (s32[2,4,1024]{2,1,0:T(4,128)S(1)}, s32[2,4,1024]{2,1,0:T(4,128)}, u32[]{:S(2)}) copy-start(s32[2,4,1024]{2,1,0:T(4,128)} %param.12) | copy-start | bytes 98308
  47.4 3.8 %copy-start.9 = (s32[4]{0:T(128)S(1)}, s32[4]{0:T(128)}, u32[]{:S(2)}) copy-start(s32[4]{0:T(128)} %param.11) | copy-start | bytes 52
  47.4 132.9 %all-to-all-start.2 = ((bf16[8,128,1024]{2,1,0:T(8,128)(2,1)}), bf16[8,128,1024]{2,1,0:T(8,128)(2,1)S(1)}, u32[]{:S(2)}, u32[]{:S(2)}) async-start(bf16[8,128,1024]{2,1,0:T(8,128)(2,1)} %bitcast.14), calls=%async_computation.2 | async-start | bytes 4194304 | tf_op jit(solution)/shard_map/all_to_all | solution.py:43
  180.2 7.0 %copy-start.7 = (s32[1,1024]{1,0:T(1,128)S(1)}, s32[1,1024]{1,0:T(1,128)}, u32[]{:S(2)}) copy-start(s32[1,1024]{1,0:T(1,128)} %param.14) | copy-start | bytes 12292
  180.2 7.1 %copy-start.8 = (s32[2,1,1024]{2,1,0:T(1,128)S(1)}, s32[2,1,1024]{2,1,0:T(1,128)}, u32[]{:S(2)}) copy-start(s32[2,1,1024]{2,1,0:T(1,128)} %param.13) | copy-start | bytes 24580
  180.3 1.3 copy-start.5
  181.6 98.5 %all-to-all-start = ((f32[4,256,1024]{1,0,2:T(4,128)}), f32[4,256,1024]{1,0,2:T(4,128)}, u32[]{:S(2)}, u32[]{:S(2)}) async-start(f32[4,256,1024]{1,0,2:T(4,128)} %copy.18), calls=%async_computation | async-start | bytes 8388608 | tf_op jit(solution)/shard_map/all_to_all | solution.py:36
  186.4 7.6 %sort.19.cloned.1.call-start = ((), (), s32[]{:S(2)}) async-start(), calls=%async_computation.5 | async-start | bytes 24608 | tf_op jit(solution)/shard_map/jit(argsort)/sort | solution.py:63
  187.4 8.0 %copy-start.4 = (bf16[8,128,1024]{2,1,0:T(8,128)(2,1)S(1)}, bf16[8,128,1024]{2,1,0:T(8,128)(2,1)}, u32[]{:S(2)}) copy-start(bf16[8,128,1024]{2,1,0:T(8,128)(2,1)} %all_to_all.42) | copy-start | bytes 6291460
  214.1 7.3 %copy-start = (f32[1,1024,1024]{1,2,0:T(8,128)S(1)}, f32[1,1024,1024]{1,2,0:T(8,128)}, u32[]{:S(2)}) copy-start(f32[1,1024,1024]{1,2,0:T(8,128)} %copy.21) | copy-start | bytes 12582916
  214.1 7.3 %copy-start.2 = (bf16[1024,1024]{1,0:T(8,128)(2,1)S(1)}, bf16[1024,1024]{1,0:T(8,128)(2,1)}, u32[]{:S(2)}) copy-start(bf16[1024,1024]{1,0:T(8,128)(2,1)} %gather_fusion.1) | copy-start | bytes 6291460
  214.1 7.3 %copy-start.3 = (bf16[1024,1024]{1,0:T(8,128)(2,1)S(1)}, bf16[1024,1024]{1,0:T(8,128)(2,1)}, u32[]{:S(2)}) copy-start(bf16[1024,1024]{1,0:T(8,128)(2,1)} %gather_fusion.2) | copy-start | bytes 6291460
  280.1 30.3 %all-to-all-start.3 = ((bf16[8,128,1024]{2,1,0:T(8,128)(2,1)}), bf16[8,128,1024]{2,1,0:T(8,128)(2,1)S(1)}, u32[]{:S(2)}, u32[]{:S(2)}) async-start(bf16[8,128,1024]{2,1,0:T(8,128)(2,1)} %select_convert_fusion), calls=%async_computation.3 | async-start | bytes 4194304 | tf_op jit(solution)/shard_map/all_to_all | solution.py:67
Sparse Core Ops, SparseCore 0:
  14.3 152.3 all-gather.1
Sparse Core Ops, SparseCore 1:
  189.4 4.4 sort.21.cloned.1.call-done
  (1 shorter events, 0.0 us)
where the time goes:
time: 325 us; the launch traced here: 324 us
  waiting for transfers between devices  175 us (54%)
  local copies, waits for them, and re-layouts  55.2 us (17%)
  blocking collectives  31.7 us (10%)
  matrix products  18.4 us (6%)
  other arithmetic  15.9 us (5%)
  between operations  15 us (5%)
  starting transfers between devices  12.4 us (4%)
    all_gather x1, waiting for transfers between devices, per_device(): lax.all_gather(gamma_live, 'tile', axis=1, tiled=True)  115 us
    all_to_all x1, waiting for transfers between devices, per_device(): lax.all_to_all(first, 'tile', split_axis=2, concat_axis=1, tiled=True)  45.8 us
    all_to_all x1, blocking collectives, per_device(): lax.all_to_all(flat_gamma, 'chan', split_axis=0, concat_axis=0, tiled=True)  31.7 us
    all_to_all x1, waiting for transfers between devices, per_device(): lax.all_to_all(back_bar.reshape(block_rows, states), 'chan', split_axis=0...  13.8 us
    all_to_all x2, local copies, waits for them, and re-layouts, per_device(): lax.all_to_all(first, 'tile', split_axis=2, concat_axis=1, tiled=True)  12.6 us
    unnamed x22, local copies, waits for them, and re-layouts  8.43 us
    dot_general x1, matrix products, per_device(): jnp.einsum('crk,ckj->crj', eta_weighted, lax.all_gather(gamma_live, 'tile...  8.32 us
    gather x2, local copies, waits for them, and re-layouts, per_device(): jnp.take_along_axis(crossed * weights_turned, inverse[None, :, :], axis=2)  8.19 us
  transfers between devices with their start and end apart: 4, of which 3 were waited for; matrix products, arithmetic and copies ran while one was open for 21% of the time, Pallas kernels for 0%

commit v1 on v0

v1 whole, which is shorter than its diff:
```python
import functools

import jax
import jax.numpy as jnp
from jax import lax
from jax.experimental import pallas as pl
from jax.experimental.pallas import tpu as pltpu
from jax.sharding import PartitionSpec as P

BF16 = jnp.bfloat16
F32 = jnp.float32
ANY = pl.BlockSpec(memory_space=pl.ANY)
VMEM = pl.BlockSpec(memory_space=pltpu.VMEM)
SMEM = pl.BlockSpec(memory_space=pltpu.SMEM)


def params(mib):
    return pltpu.CompilerParams(vmem_limit_bytes=mib << 20)


def xor_permute(block, axis, size, step):
    return lax.ppermute(block, axis, [(i, i ^ step) for i in range(size)])


def aligned(start, size):
    return pl.ds(pl.multiple_of(start, size), size)


def row_tiles(states):
    rows = min(256, states)
    return [(start, rows) for start in range(0, states, rows)]


def prepare_kernel(ph_count, states, map_ref, occ_ref, weights_ref, turned_ref, select_ref):
    for q in range(ph_count):
        map_row = map_ref[q : q + 1, :]
        signs = (occ_ref[0, q : q + 1, :] - occ_ref[1, q : q + 1, :]).astype(F32)
        for start, rows in row_tiles(states):
            here = lax.broadcasted_iota(jnp.int32, (rows, states), 0) + start == map_row
            hot = jnp.where(here, 1.0, 0.0).astype(F32)
            select_ref[q, start : start + rows, :] = (hot * signs).astype(BF16)
            hot = hot.astype(BF16)
            for top, height in row_tiles(states):
                rest = weights_ref[q, top : top + height, :]
                total = jnp.zeros((height, rows), F32)
                for _ in range(3):
                    part = rest.astype(BF16)
                    rest = rest - part.astype(F32)
                    total = total + lax.dot_general(
                        part, hot, (((1,), (1,)), ((), ())), preferred_element_type=F32
                    )
                turned_ref[q, top : top + height, start : start + rows] = total


def prepare(recouple_map, recoupled_occupation, recouple_weights):
    ph_count, states = recouple_map.shape
    return pl.pallas_call(
        functools.partial(prepare_kernel, ph_count, states),
        out_shape=(
            jax.ShapeDtypeStruct(recouple_weights.shape, F32),
            jax.ShapeDtypeStruct(recouple_weights.shape, BF16),
        ),
        in_specs=[VMEM] * 3,
        out_specs=(VMEM, VMEM),
        compiler_params=params(40),
        name="prepare",
    )(recouple_map, recoupled_occupation, recouple_weights)


def block_starts(me, blocks, rows):
    return [(me ^ d) * rows for d in range(blocks)]


def left_kernel(ph_count, states, blocks, me_ref, turned_ref, select_ref, *rest):
    recv_refs, (bar_ref, left_ref, recv, sems) = rest[:blocks], rest[blocks:]
    rows = recv_refs[0].shape[0]
    copies = []
    for d, start in enumerate(block_starts(me_ref[0], blocks, rows)):
        copy = pltpu.make_async_copy(recv_refs[d], recv.at[aligned(start, rows), :], sems.at[d])
        copy.start()
        copies.append(copy)
    for copy in copies:
        copy.wait()
    for q in range(ph_count):
        for top, height in row_tiles(states):
            span = slice(top, top + height)
            values = recv[span, q * states : (q + 1) * states].astype(F32) * turned_ref[q, span, :]
            values = values.astype(BF16)
            bar_ref[q, span, :] = values
            left_ref[q, span, :] = jnp.dot(
                values, select_ref[q], preferred_element_type=F32
            ).astype(BF16)


def left_operand(me, turned, select, received):
    ph_count, states, _ = turned.shape
    blocks = len(received)
    return pl.pallas_call(
        functools.partial(left_kernel, ph_count, states, blocks),
        out_shape=(
            jax.ShapeDtypeStruct(turned.shape, BF16),
            jax.ShapeDtypeStruct(turned.shape, BF16),
        ),
        in_specs=[SMEM, VMEM, VMEM] + [ANY] * blocks,
        out_specs=(VMEM, VMEM),
        scratch_shapes=[
            pltpu.VMEM((states, ph_count * states), BF16),
            pltpu.SemaphoreType.DMA((blocks,)),
        ],
        compiler_params=params(40),
        name="left_operand",
    )(me, turned, select, *received)


def crossed_kernel(
    ph_count, states, blocks, me_ref, turned_ref, select_ref, eta_bar_ref, eta_left_ref, *rest
):
    recv_refs, out_refs = rest[:blocks], rest[blocks : 2 * blocks]
    recv, bar, left, back, sems = rest[2 * blocks :]
    rows = recv_refs[0].shape[0]
    starts = block_starts(me_ref[0], blocks, rows)
    copies = []
    for d, start in enumerate(starts):
        copy = pltpu.make_async_copy(recv_refs[d], recv.at[aligned(start, rows), :], sems.at[d])
        copy.start()
        copies.append(copy)
    for copy in copies:
        copy.wait()
    for q in range(ph_count):
        columns = slice(q * states, (q + 1) * states)
        for top, height in row_tiles(states):
            span = slice(top, top + height)
            values = recv[span, columns].astype(F32) * turned_ref[q, span, :]
            values = values.astype(BF16)
            bar[span, :] = values
            left[span, :] = jnp.dot(values, select_ref[q], preferred_element_type=F32).astype(BF16)
        for top, height in row_tiles(states):
            span = slice(top, top + height)
            crossed = jnp.dot(eta_left_ref[q, span, :], bar[...], preferred_element_type=F32)
            crossed = crossed - jnp.dot(
                left[span, :], eta_bar_ref[q], preferred_element_type=F32
            )
            back[span, columns] = (crossed * turned_ref[q, span, :]).astype(BF16)
    copies = []
    for d, start in enumerate(starts):
        copy = pltpu.make_async_copy(back.at[aligned(start, rows), :], out_refs[d], sems.at[d])
        copy.start()
        copies.append(copy)
    for copy in copies:
        copy.wait()


def crossed_blocks(me, turned, select, eta_bar, eta_left, received):
    ph_count, states, _ = turned.shape
    blocks = len(received)
    return pl.pallas_call(
        functools.partial(crossed_kernel, ph_count, states, blocks),
        out_shape=[jax.ShapeDtypeStruct(block.shape, BF16) for block in received],
        in_specs=[SMEM, VMEM, VMEM, VMEM, VMEM] + [ANY] * blocks,
        out_specs=[ANY] * blocks,
        scratch_shapes=[
            pltpu.VMEM((states, ph_count * states), BF16),
            pltpu.VMEM((states, states), BF16),
            pltpu.VMEM((states, states), BF16),
            pltpu.VMEM((states, ph_count * states), BF16),
            pltpu.SemaphoreType.DMA((blocks,)),
        ],
        compiler_params=params(48),
        name="crossed",
    )(me, turned, select, eta_bar, eta_left, *received)


def pack_kernel(tiles, rows, place_ref, eta_ref, gamma_ref, *rest):
    out_refs, sems = rest[:-1], rest[-1]
    place = place_ref[0]
    copies = []
    for step in range(1, tiles):
        owner = place ^ step
        for n, source in enumerate((eta_ref, gamma_ref)):
            for m, other in enumerate(range(step, tiles)):
                column = owner ^ other
                copies.append(
                    pltpu.make_async_copy(
                        source.at[owner, :, aligned(column * rows, rows)],
                        out_refs[step - 1].at[n, m],
                        sems.at[len(copies)],
                    )
                )
    for copy in copies:
        copy.start()
    for copy in copies:
        copy.wait()


def pack(place, eta, gamma):
    tiles, rows, _ = eta.shape
    return pl.pallas_call(
        functools.partial(pack_kernel, tiles, rows),
        out_shape=[
            jax.ShapeDtypeStruct((2, tiles - step, rows, rows), BF16) for step in range(1, tiles)
        ],
        in_specs=[SMEM, ANY, ANY],
        out_specs=[ANY] * (tiles - 1),
        scratch_shapes=[pltpu.SemaphoreType.DMA((tiles * (tiles - 1),))],
        name="pack",
    )(place, eta, gamma)


def ladder_kernel(tiles, rows, place_ref, sizes_ref, occ_ref, eta_ref, gamma_ref, *rest):
    packed_refs = rest[: tiles - 1]
    out_refs = rest[tiles - 1 : 2 * tiles - 1]
    eta, gamma, weight, sems = rest[2 * tiles - 1 :]
    place = place_ref[0]
    size = sizes_ref[place]
    states = tiles * rows
    copies = []
    for source, full in ((eta_ref, eta), (gamma_ref, gamma)):
        for k in range(tiles):
            copies.append(
                pltpu.make_async_copy(
                    source.at[place, :, aligned((place ^ k) * rows, rows)],
                    full.at[0:rows, k * rows : (k + 1) * rows],
                    sems.at[len(copies)],
                )
            )
    for copy in copies:
        copy.start()
    occupied = occ_ref[0] + occ_ref[1]
    own = lax.broadcasted_iota(jnp.int32, occupied.shape, 0) == place
    free = jnp.sum(jnp.where(own, 1 - occupied, 0), axis=0, keepdims=True)
    free = jnp.where(lax.broadcasted_iota(jnp.int32, free.shape, 1) < size, free, 0)
    weight[...] = free.astype(F32)
    for k in range(1, tiles):
        for n, full in enumerate((eta, gamma)):
            for m, other in enumerate(range(k, tiles)):
                full[k * rows : (k + 1) * rows, other * rows : (other + 1) * rows] = packed_refs[
                    k - 1
                ][n, m]
    for copy in copies:
        copy.wait()
    for k in range(tiles):
        for other in range(k + 1, tiles):
            here, there = slice(k * rows, (k + 1) * rows), slice(other * rows, (other + 1) * rows)
            eta[there, here] = -eta[here, there].T
            gamma[there, here] = gamma[here, there].T
    scale = jnp.concatenate(
        [weight[:, aligned((place ^ k) * rows, rows)] for k in range(tiles)], axis=1
    ).astype(BF16)
    for k in range(tiles):
        here = slice(k * rows, (k + 1) * rows)
        total = jnp.dot(eta[here, :] * scale, gamma[...], preferred_element_type=F32)
        total = total - jnp.dot(gamma[here, :] * scale, eta[...], preferred_element_type=F32)
        total = total.astype(BF16)
        for other in range(tiles):
            out_refs[k][:, aligned((place ^ other) * rows, rows)] = total[
                :, other * rows : (other + 1) * rows
            ]


def ladder_blocks(place, sizes, pair_occupation, eta, gamma, packed):
    tiles, rows, states = eta.shape
    return pl.pallas_call(
        functools.partial(ladder_kernel, tiles, rows),
        out_shape=[jax.ShapeDtypeStruct((rows, states), BF16) for _ in range(tiles)],
        in_specs=[SMEM, SMEM, VMEM, ANY, ANY] + [VMEM] * (tiles - 1),
        out_specs=[VMEM] * tiles,
        scratch_shapes=[
            pltpu.VMEM((states, states), BF16),
            pltpu.VMEM((states, states), BF16),
            pltpu.VMEM((1, states), F32),
            pltpu.SemaphoreType.DMA((2 * tiles,)),
        ],
        compiler_params=params(32),
        name="ladder",
    )(place, sizes, pair_occupation, eta, gamma, *packed)


def finish_kernel(
    chan_count, tile_rows, blocks, ladders, me_ref, place_ref, sizes_ref, *rest
):
    back_refs, ladder_refs = rest[:blocks], rest[blocks : blocks + ladders]
    out_ref, back, ladder, sems = rest[blocks + ladders :]
    place = place_ref[0]
    rows = back_refs[0].shape[0]
    height = ladder_refs[0].shape[0]
    copies = []
    for k in range(ladders):
        copies.append(
            pltpu.make_async_copy(
                ladder_refs[k],
                ladder.at[aligned((place ^ k if ladders > 1 else 0) * height, height), :],
                sems.at[len(copies)],
            )
        )
    for d, start in enumerate(block_starts(me_ref[0], blocks, rows)):
        copies.append(
            pltpu.make_async_copy(
                back_refs[d], back.at[aligned(start, rows), :], sems.at[len(copies)]
            )
        )
    for copy in copies:
        copy.start()
    for copy in copies:
        copy.wait()
    states = out_ref.shape[2]
    for c in range(chan_count):
        size = sizes_ref[c]
        span = slice(c * tile_rows, (c + 1) * tile_rows)
        total = ladder[span, :].astype(F32) + back[span, :].astype(F32)
        row = place * tile_rows + lax.broadcasted_iota(jnp.int32, (tile_rows, states), 0)
        column = lax.broadcasted_iota(jnp.int32, (tile_rows, states), 1)
        live = jnp.maximum(row, column) < size
        out_ref[c] = jnp.where(live, total, 0.0).astype(BF16)


def finish(me, place, sizes, shape, back, ladder):
    chan_count, tile_rows, states = shape
    flat = (chan_count * tile_rows, states)
    return pl.pallas_call(
        functools.partial(finish_kernel, chan_count, tile_rows, len(back), len(ladder)),
        out_shape=jax.ShapeDtypeStruct(shape, BF16),
        in_specs=[SMEM] * 3 + [ANY] * (len(back) + len(ladder)),
        out_specs=VMEM,
        scratch_shapes=[
            pltpu.VMEM(flat, BF16),
            pltpu.VMEM(flat, ladder[0].dtype),
            pltpu.SemaphoreType.DMA((len(back) + len(ladder),)),
        ],
        compiler_params=params(32),
        name="finish",
    )(me, place, sizes, *back, *ladder)


def ladder_gathered(live_columns, pair_occupation, eta_live, gamma_live):
    weight = (1 - pair_occupation[0] - pair_occupation[1]) * live_columns.astype(jnp.int32)
    first = jnp.einsum(
        "crk,ckj->crj",
        eta_live * weight.astype(BF16)[:, None, :],
        lax.all_gather(gamma_live, "tile", axis=1, tiled=True),
        preferred_element_type=F32,
    )
    mirrored = lax.all_to_all(first, "tile", split_axis=2, concat_axis=1, tiled=True)
    total = first + jnp.swapaxes(mirrored, 1, 2)
    return [total.reshape(-1, total.shape[2])]


def per_device(
    chans,
    tiles,
    generator,
    hamiltonian,
    chan_sizes,
    pair_occupation,
    recoupled_occupation,
    recouple_map,
    recouple_weights,
):
    chan_count, tile_rows, states = generator.shape
    block_rows = chan_count * tile_rows
    chan_place = lax.axis_index("chan")
    tile_place = lax.axis_index("tile")
    me = jnp.reshape(chan_place, (1,))
    place = jnp.reshape(tile_place, (1,))
    owned = tiles == chan_count
    stepped = chans <= 8 and chans & (chans - 1) == 0

    columns = lax.broadcasted_iota(jnp.int32, (chan_count, states), 1)
    live_columns = columns < chan_sizes[:, None]
    row_index = tile_place * tile_rows + lax.broadcasted_iota(jnp.int32, (chan_count, tile_rows), 1)
    live_rows = row_index < chan_sizes[:, None]
    live_mask = live_rows[:, :, None] & live_columns[:, None, :]
    zero = jnp.zeros((), BF16)
    eta_live = jnp.where(live_mask, generator, zero)
    gamma_live = jnp.where(live_mask, hamiltonian, zero)

    def cut(values):
        flat = values.reshape(block_rows, states)
        if not stepped:
            return [flat]
        rows = block_rows // chans
        return [
            lax.dynamic_slice_in_dim(flat, (chan_place ^ d) * rows, rows, 0) for d in range(chans)
        ]

    def exchange(blocks):
        if not stepped:
            return [lax.all_to_all(blocks[0], "chan", split_axis=0, concat_axis=0, tiled=True)]
        return [blocks[0]] + [
            xor_permute(block, "chan", chans, d) for d, block in enumerate(blocks) if d
        ]

    recv_eta = exchange(cut(eta_live))
    if owned:
        packed = pack(place, generator, hamiltonian)
        packed = [xor_permute(p, "tile", tiles, k + 1) for k, p in enumerate(packed)]
    recv_gamma = exchange(cut(gamma_live))
    turned, select = prepare(recouple_map, recoupled_occupation, recouple_weights)
    eta_bar, eta_left = left_operand(me, turned, select, recv_eta)
    if owned:
        ladder = ladder_blocks(place, chan_sizes, pair_occupation, generator, hamiltonian, packed)
        ladder = [ladder[0]] + [
            xor_permute(block, "tile", tiles, k) for k, block in enumerate(ladder) if k
        ]
    else:
        ladder = ladder_gathered(live_columns, pair_occupation, eta_live, gamma_live)
    back = exchange(crossed_blocks(me, turned, select, eta_bar, eta_left, recv_gamma))
    return finish(me, place, chan_sizes, generator.shape, back, ladder)


def solution(mesh):
    return jax.shard_map(
        functools.partial(per_device, mesh.shape["chan"], mesh.shape["tile"]),
        mesh=mesh,
        in_specs=(
            P("chan", "tile", None),
            P("chan", "tile", None),
            P("chan"),
            P(None, "chan", None),
            P(None, ("chan", "tile"), None),
            P(("chan", "tile"), None),
            P(("chan", "tile"), None, None),
        ),
        out_specs=P("chan", "tile", None),
        check_vma=False,
    )
```

time: 325 us -> 195 us (0.60)
  the two profiles are of different devices: /device:TPU:0 before, /device:TPU:18 now
where the time goes in v1:
time: 195 us
  Pallas kernels  79.9 us (41%)
  waiting for transfers between devices  63.4 us (33%)
  starting transfers between devices  24 us (12%)
  local copies, waits for them, and re-layouts  22.6 us (12%)
  other arithmetic  4.7 us (2%)
    ppermute x27, waiting for transfers between devices, xor_permute(): return lax.ppermute(block, axis, [(i, i ^ step) for i in range(size)])  63.4 us
    pallas_call x1, Pallas kernels, pack(): pl.pallas_call(functools.partial(pack_kernel, tiles, rows), out_shape=[ja...  48.9 us
    ppermute x27, starting transfers between devices, xor_permute(): return lax.ppermute(block, axis, [(i, i ^ step) for i in range(size)])  24 us
    unnamed x78, local copies, waits for them, and re-layouts  20.5 us
    pallas_call x1, Pallas kernels, crossed_blocks(): pl.pallas_call(functools.partial(crossed_kernel, ph_count, states, blocks...  11.3 us
    pallas_call x1, Pallas kernels, prepare(): pl.pallas_call(functools.partial(prepare_kernel, ph_count, states), out_s...  7.42 us
    pallas_call x1, Pallas kernels, ladder_blocks(): pl.pallas_call(functools.partial(ladder_kernel, tiles, rows), out_shape=[...  6.35 us
  transfers between devices with their start and end apart: 27, of which 10 were waited for; matrix products, arithmetic and copies ran while one was open for 1% of the time, Pallas kernels for 39%

profile of v1, /device:TPU:18, one launch (start us, length us, event | category | flops | bytes accessed | tf_op | source)
XLA Modules:
  0.0 195.0 jit_solution(4394536140463893979)
XLA Ops:
  1.5 3.2 %and_select_fusion = (bf16[4,256,1024]{2,1,0:T(8,128)(2,1)S(1)}, bf16[4,256,1024]{2,1,0:T(8,128)(2,1)S(1)}) fusion(bf16[4,256,1024]{2,1,0:T(8,128)(2,1)} %gamma_ref.3, pred[4,1024]{1,0:T(4,128)(4,1)S(1)} %iota_compare_fusion, pred[4,256]{1,0:T(4,128)(4,1)S(1)} %broadcast_compare_fusion, bf16[4,256,1024]{2,1,0:T(8,128)(2,1)} %eta_ref.3), kind=kLoop, calls=%fused_computation | loop fusion | flops 3145728 | bytes 8393728 | tf_op jit(solution)/shard_map/jit(_where)/select_n | solution.py:374
  6.3 1.3 collective-permute-start.2
  7.6 1.5 collective-permute-start.3
  10.0 1.5 collective-permute-start.5
  11.5 3.4 %collective-permute-done.1.rest_2_ = bf16[128,1024]{1,0:T(8,128)(2,1)S(1)} collective-permute-done((bf16[128,1024]{1,0:T(8,128)(2,1)S(1)}, bf16[128,1024]{1,0:T(8,128)(2,1)S(1)}, u32[]{:S(2)}, u32[]{:S(2)}) %collective-permute-start.1) | collective-permute-done | bytes 262176 | tf_op jit(solution)/shard_map/ppermute | solution.py:22
  17.0 2.7 %collective-permute-done.2.rest_3_ = bf16[128,1024]{1,0:T(8,128)(2,1)S(1)} collective-permute-done((bf16[128,1024]{1,0:T(8,128)(2,1)S(1)}, bf16[128,1024]{1,0:T(8,128)(2,1)S(1)}, u32[]{:S(2)}, u32[]{:S(2)}) %collective-permute-start.2) | collective-permute-done | bytes 262176 | tf_op jit(solution)/shard_map/ppermute | solution.py:22
  20.4 1.5 collective-permute-start.10
  21.9 48.9 %pack.1 = (bf16[2,3,256,256]{3,2,1,0:T(8,128)(2,1)}, bf16[2,2,256,256]{3,2,1,0:T(8,128)(2,1)}, bf16[2,1,256,256]{3,2,1,0:T(8,128)(2,1)}) custom-call(s32[1]{0:T(128)} %bitcast.1.place_ref, bf16[4,256,1024]{2,1,0:T(8,128)(2,1)} %eta_ref.3, bf16[4,256,1024]{2,1,0:T(8,128)(2,1)} %gamma_ref.3), custom_call_target="tpu_custom_call" | custom-call | tf_op jit(solution)/shard_map/pack/pallas_call | solution.py:197
  72.9 1.5 collective-permute-start.12
  76.5 1.6 collective-permute-start.21
  79.4 11.4 %collective-permute-done.11.rest_5_ = bf16[128,1024]{1,0:T(8,128)(2,1)S(1)} collective-permute-done((bf16[128,1024]{1,0:T(8,128)(2,1)}, bf16[128,1024]{1,0:T(8,128)(2,1)S(1)}, u32[]{:S(2)}, u32[]{:S(2)}) %collective-permute-start.11) | collective-permute-done | bytes 262176 | tf_op jit(solution)/shard_map/ppermute | solution.py:22
  93.8 1.4 collective-permute-start.9
  95.9 2.7 %collective-permute-start.23 = (bf16[2,1,256,256]{3,2,1,0:T(8,128)(2,1)}, bf16[2,1,256,256]{3,2,1,0:T(8,128)(2,1)}, u32[]{:S(2)}, u32[]{:S(2)}) collective-permute-start(bf16[2,1,256,256]{3,2,1,0:T(8,128)(2,1)} %get-tuple-element.38), channel_id=1, source_target_pairs={{0,3},{1,2},{2,1},{3,0},{4,7},{5,6},{6,5},{7,4},{8,11},{9,10},{10,... | collective-permute-start | bytes 786440 | tf_op jit(solution)/shard_map/ppermute | solution.py:22
  98.6 2.2 %copy-done.4 = f32[1,1024,1024]{2,1,0:T(8,128)S(1)} copy-done((f32[1,1024,1024]{2,1,0:T(8,128)S(1)}, f32[1,1024,1024]{2,1,0:T(8,128)}, u32[]{:S(2)}) %copy-start.4) | copy-done | bytes 4194328
  100.8 7.4 %prepare.1 = (f32[1,1024,1024]{2,1,0:T(8,128)S(1)}, bf16[1,1024,1024]{2,1,0:T(8,128)(2,1)S(1)}) custom-call(s32[1,1024]{1,0:T(1,128)S(1)} %copy-done.38, s32[2,1,1024]{2,1,0:T(1,128)S(1)} %copy-done.36, f32[1,1024,1024]{2,1,0:T(8,128)S(1)} %copy-done.4), custom_call_target="tpu_custom_call" | custom-call | tf_op jit(solution)/shard_map/prepare/pallas_call | solution.py:57
  108.3 2.8 %left_operand.1 = (bf16[1,1024,1024]{2,1,0:T(8,128)(2,1)S(1)}, bf16[1,1024,1024]{2,1,0:T(8,128)(2,1)S(1)}) custom-call(s32[1]{0:T(128)} %bitcast.me_ref, f32[1,1024,1024]{2,1,0:T(8,128)S(1)} %get-tuple-element.24.turned_ref, bf16[1,1024,1024]{2,1,0:T(8,128)(2,1)S(1)} %get-tuple-element.25.select_ref, bf16[128,1024]{1,0:T(8,128)(2,1)S(1)} %get-tuple-element.58.rest_0_, ...), custom_call_target="tpu_custom_call" | custom-call | tf_op jit(solution)/shard_map/left_operand/pallas_call | solution.py:98
  111.2 1.3 copy-done.5
  112.5 1.4 copy-done.6
  121.0 11.3 %crossed.1 = (bf16[128,1024]{1,0:T(8,128)(2,1)S(1)}, bf16[128,1024]{1,0:T(8,128)(2,1)S(1)}, bf16[128,1024]{1,0:T(8,128)(2,1)S(1)}, bf16[128,1024]{1,0:T(8,128)(2...) custom-call(s32[1]{0:T(128)} %bitcast.me_ref, ...), custom_call_target="tpu_custom_call" | custom-call | tf_op jit(solution)/shard_map/crossed/pallas_call | solution.py:156
  133.0 1.3 collective-permute-start.16
  134.8 1.2 collective-permute-start.18
  136.0 6.3 %ladder.1 = (bf16[256,1024]{1,0:T(8,128)(2,1)S(1)}, bf16[256,1024]{1,0:T(8,128)(2,1)S(1)}, bf16[256,1024]{1,0:T(8,128)(2,1)S(1)}, bf16[256,1024]{1,0:T(8,128)(2,1)S(1)}) custom-call(s32[1]{0:T(128)} %bitcast.1.place_ref, s32[4]{0:T(128)S(1)} %copy-done.37, s32[2,4,1024]{2,1,0:T(4,128)S(1)} %copy-done.35, bf16[4,256,1024]{2,1,0:T(8,128)(2,1)S(1)} %copy-done.1, ...), custom_call_target="tpu_custom_call" | custom-call | tf_op jit(solution)/shard_map/ladder/pallas_call | solution.py:262
  142.4 1.4 collective-permute-start.24
  144.0 2.3 %collective-permute-done.16.rest_3_ = bf16[128,1024]{1,0:T(8,128)(2,1)S(1)} collective-permute-done((bf16[128,1024]{1,0:T(8,128)(2,1)S(1)}, bf16[128,1024]{1,0:T(8,128)(2,1)S(1)}, u32[]{:S(2)}, u32[]{:S(2)}) %collective-permute-start.16) | collective-permute-done | bytes 262176 | tf_op jit(solution)/shard_map/ppermute | solution.py:22
  146.8 1.1 collective-permute-done.18.rest_5_
  147.9 1.2 collective-permute-start.20
  149.1 7.2 %collective-permute-done.19.rest_6_ = bf16[128,1024]{1,0:T(8,128)(2,1)S(1)} collective-permute-done((bf16[128,1024]{1,0:T(8,128)(2,1)S(1)}, bf16[128,1024]{1,0:T(8,128)(2,1)S(1)}, u32[]{:S(2)}, u32[]{:S(2)}) %collective-permute-start.19) | collective-permute-done | bytes 262176 | tf_op jit(solution)/shard_map/ppermute | solution.py:22
  156.3 5.0 %collective-permute-done.20.rest_7_ = bf16[128,1024]{1,0:T(8,128)(2,1)S(1)} collective-permute-done((bf16[128,1024]{1,0:T(8,128)(2,1)S(1)}, bf16[128,1024]{1,0:T(8,128)(2,1)S(1)}, u32[]{:S(2)}, u32[]{:S(2)}) %collective-permute-start.20) | collective-permute-done | bytes 262176 | tf_op jit(solution)/shard_map/ppermute | solution.py:22
  161.3 3.8 %collective-permute-done.24.rest_9_ = bf16[256,1024]{1,0:T(8,128)(2,1)S(1)} collective-permute-done((bf16[256,1024]{1,0:T(8,128)(2,1)S(1)}, bf16[256,1024]{1,0:T(8,128)(2,1)S(1)}, u32[]{:S(2)}, u32[]{:S(2)}) %collective-permute-start.24) | collective-permute-done | bytes 524320 | tf_op jit(solution)/shard_map/ppermute | solution.py:22
  165.1 13.5 %collective-permute-done.25.rest_10_ = bf16[256,1024]{1,0:T(8,128)(2,1)S(1)} collective-permute-done((bf16[256,1024]{1,0:T(8,128)(2,1)S(1)}, bf16[256,1024]{1,0:T(8,128)(2,1)S(1)}, u32[]{:S(2)}, u32[]{:S(2)}) %collective-permute-start.25) | collective-permute-done | bytes 524320 | tf_op jit(solution)/shard_map/ppermute | solution.py:22
  178.6 13.0 %collective-permute-done.26.rest_11_ = bf16[256,1024]{1,0:T(8,128)(2,1)S(1)} collective-permute-done((bf16[256,1024]{1,0:T(8,128)(2,1)S(1)}, bf16[256,1024]{1,0:T(8,128)(2,1)S(1)}, u32[]{:S(2)}, u32[]{:S(2)}) %collective-permute-start.26) | collective-permute-done | bytes 524320 | tf_op jit(solution)/shard_map/ppermute | solution.py:22
  191.6 3.2 %finish.1 = bf16[4,256,1024]{2,1,0:T(8,128)(2,1)} custom-call(s32[1]{0:T(128)} %bitcast.me_ref, s32[1]{0:T(128)} %bitcast.1.place_ref, s32[4]{0:T(128)S(1)} %copy-done.37, bf16[128,1024]{1,0:T(8,128)(2,1)S(1)} %get-tuple-element.28.rest_0_, bf16[128,1024]{1,0:T(8,128)(2,1)S(1)} %collective-permute-done.14.rest_1_, ...), custom_call_target="tpu_custom_call" | custom-call | tf_op jit(solution)/shard_map/finish/pallas_call | solution.py:319
  (112 shorter events, 25.0 us)
Async XLA Ops:
  5.7 3.5 %collective-permute-start = (bf16[128,1024]{1,0:T(8,128)(2,1)S(1)}, bf16[128,1024]{1,0:T(8,128)(2,1)S(1)}, u32[]{:S(2)}, u32[]{:S(2)}) collective-permute-start(bf16[128,1024]{1,0:T(8,128)(2,1)S(1)} %get-tuple-element.57), channel_id=1, source_target_pairs={{0,4},{4,0},{8,12},{12,8},{16,20},{20,16},{24,28},{28,24},{1,5},{5... | collective-permute-start | bytes 786440 | tf_op jit(solution)/shard_map/ppermute | solution.py:22
  5.7 9.1 %collective-permute-start.1 = (bf16[128,1024]{1,0:T(8,128)(2,1)S(1)}, bf16[128,1024]{1,0:T(8,128)(2,1)S(1)}, u32[]{:S(2)}, u32[]{:S(2)}) collective-permute-start(bf16[128,1024]{1,0:T(8,128)(2,1)S(1)} %get-tuple-element.56), channel_id=1, source_target_pairs={{0,8},{4,12},{8,0},{12,4},{16,24},{20,28},{24,16},{28,20},{1,9},{5... | collective-permute-start | bytes 786440 | tf_op jit(solution)/shard_map/ppermute | solution.py:22
  6.3 13.4 %collective-permute-start.2 = (bf16[128,1024]{1,0:T(8,128)(2,1)S(1)}, bf16[128,1024]{1,0:T(8,128)(2,1)S(1)}, u32[]{:S(2)}, u32[]{:S(2)}) collective-permute-start(bf16[128,1024]{1,0:T(8,128)(2,1)S(1)} %get-tuple-element.55), channel_id=1, source_target_pairs={{0,12},{4,8},{8,4},{12,0},{16,28},{20,24},{24,20},{28,16},{1,13},{... | collective-permute-start | bytes 786440 | tf_op jit(solution)/shard_map/ppermute | solution.py:22
  7.6 63.2 %collective-permute-start.3 = (bf16[128,1024]{1,0:T(8,128)(2,1)}, bf16[128,1024]{1,0:T(8,128)(2,1)S(1)}, u32[]{:S(2)}, u32[]{:S(2)}) collective-permute-start(bf16[128,1024]{1,0:T(8,128)(2,1)} %get-tuple-element.54), channel_id=1, source_target_pairs={{0,16},{4,20},{8,24},{12,28},{16,0},{20,4},{24,8},{28,12},{1,17},{... | collective-permute-start | bytes 786440 | tf_op jit(solution)/shard_map/ppermute | solution.py:22
  9.1 63.1 %collective-permute-start.4 = (bf16[128,1024]{1,0:T(8,128)(2,1)}, bf16[128,1024]{1,0:T(8,128)(2,1)S(1)}, u32[]{:S(2)}, u32[]{:S(2)}) collective-permute-start(bf16[128,1024]{1,0:T(8,128)(2,1)} %get-tuple-element.53), channel_id=1, source_target_pairs={{0,20},{4,16},{8,28},{12,24},{16,4},{20,0},{24,12},{28,8},{1,21},{... | collective-permute-start | bytes 786440 | tf_op jit(solution)/shard_map/ppermute | solution.py:22
  10.0 64.4 %collective-permute-start.5 = (bf16[128,1024]{1,0:T(8,128)(2,1)S(1)}, bf16[128,1024]{1,0:T(8,128)(2,1)S(1)}, u32[]{:S(2)}, u32[]{:S(2)}) collective-permute-start(bf16[128,1024]{1,0:T(8,128)(2,1)S(1)} %get-tuple-element.52), channel_id=1, source_target_pairs={{0,24},{4,28},{8,16},{12,20},{16,8},{20,12},{24,0},{28,4},{1,25},{... | collective-permute-start | bytes 786440 | tf_op jit(solution)/shard_map/ppermute | solution.py:22
  15.6 60.2 %collective-permute-start.6 = (bf16[128,1024]{1,0:T(8,128)(2,1)S(1)}, bf16[128,1024]{1,0:T(8,128)(2,1)S(1)}, u32[]{:S(2)}, u32[]{:S(2)}) collective-permute-start(bf16[128,1024]{1,0:T(8,128)(2,1)S(1)} %get-tuple-element.51), channel_id=1, source_target_pairs={{0,28},{4,24},{8,20},{12,16},{16,12},{20,8},{24,4},{28,0},{1,29},{... | collective-permute-start | bytes 786440 | tf_op jit(solution)/shard_map/ppermute | solution.py:22
  20.4 57.7 %collective-permute-start.10 = (bf16[128,1024]{1,0:T(8,128)(2,1)}, bf16[128,1024]{1,0:T(8,128)(2,1)S(1)}, u32[]{:S(2)}, u32[]{:S(2)}) collective-permute-start(bf16[128,1024]{1,0:T(8,128)(2,1)} %get-tuple-element.46), channel_id=1, source_target_pairs={{0,16},{4,20},{8,24},{12,28},{16,0},{20,4},{24,8},{28,12},{1,17},{... | collective-permute-start | bytes 786440 | tf_op jit(solution)/shard_map/ppermute | solution.py:22
  21.9 76.7 %copy-start.36 = (s32[2,1,1024]{2,1,0:T(1,128)S(1)}, s32[2,1,1024]{2,1,0:T(1,128)}, u32[]{:S(2)}) copy-start(s32[2,1,1024]{2,1,0:T(1,128)} %occ_ref.2) | copy-start | bytes 24580
  21.9 76.7 %copy-start.38 = (s32[1,1024]{1,0:T(1,128)S(1)}, s32[1,1024]{1,0:T(1,128)}, u32[]{:S(2)}) copy-start(s32[1,1024]{1,0:T(1,128)} %map_ref.1) | copy-start | bytes 12292
  71.5 19.3 %collective-permute-start.11 = (bf16[128,1024]{1,0:T(8,128)(2,1)}, bf16[128,1024]{1,0:T(8,128)(2,1)S(1)}, u32[]{:S(2)}, u32[]{:S(2)}) collective-permute-start(bf16[128,1024]{1,0:T(8,128)(2,1)} %get-tuple-element.45), channel_id=1, source_target_pairs={{0,20},{4,16},{8,28},{12,24},{16,4},{20,0},{24,12},{28,8},{1,21},{... | collective-permute-start | bytes 786440 | tf_op jit(solution)/shard_map/ppermute | solution.py:22
  72.9 19.1 %collective-permute-start.12 = (bf16[128,1024]{1,0:T(8,128)(2,1)}, bf16[128,1024]{1,0:T(8,128)(2,1)S(1)}, u32[]{:S(2)}, u32[]{:S(2)}) collective-permute-start(bf16[128,1024]{1,0:T(8,128)(2,1)} %get-tuple-element.44), channel_id=1, source_target_pairs={{0,24},{4,28},{8,16},{12,20},{16,8},{20,12},{24,0},{28,4},{1,25},{... | collective-permute-start | bytes 786440 | tf_op jit(solution)/shard_map/ppermute | solution.py:22
  75.1 17.9 %collective-permute-start.13 = (bf16[128,1024]{1,0:T(8,128)(2,1)S(1)}, bf16[128,1024]{1,0:T(8,128)(2,1)S(1)}, u32[]{:S(2)}, u32[]{:S(2)}) collective-permute-start(bf16[128,1024]{1,0:T(8,128)(2,1)S(1)} %get-tuple-element.43), channel_id=1, source_target_pairs={{0,28},{4,24},{8,20},{12,16},{16,12},{20,8},{24,4},{28,0},{1,29},{... | collective-permute-start | bytes 786440 | tf_op jit(solution)/shard_map/ppermute | solution.py:22
  76.5 58.3 %collective-permute-start.21 = (bf16[2,3,256,256]{3,2,1,0:T(8,128)(2,1)}, bf16[2,3,256,256]{3,2,1,0:T(8,128)(2,1)S(1)}, u32[]{:S(2)}, u32[]{:S(2)}) collective-permute-start(bf16[2,3,256,256]{3,2,1,0:T(8,128)(2,1)} %get-tuple-element.36), channel_id=1, source_target_pairs={{0,1},{1,0},{2,3},{3,2},{4,5},{5,4},{6,7},{7,6},{8,9},{9,8},{10,11... | collective-permute-start | bytes 2359304 | tf_op jit(solution)/shard_map/ppermute | solution.py:22
  78.8 16.4 %collective-permute-start.7 = (bf16[128,1024]{1,0:T(8,128)(2,1)S(1)}, bf16[128,1024]{1,0:T(8,128)(2,1)S(1)}, u32[]{:S(2)}, u32[]{:S(2)}) collective-permute-start(bf16[128,1024]{1,0:T(8,128)(2,1)S(1)} %get-tuple-element.49), channel_id=1, source_target_pairs={{0,4},{4,0},{8,12},{12,8},{16,20},{20,16},{24,28},{28,24},{1,5},{5... | collective-permute-start | bytes 786440 | tf_op jit(solution)/shard_map/ppermute | solution.py:22
  91.5 22.4 %collective-permute-start.8 = (bf16[128,1024]{1,0:T(8,128)(2,1)S(1)}, bf16[128,1024]{1,0:T(8,128)(2,1)S(1)}, u32[]{:S(2)}, u32[]{:S(2)}) collective-permute-start(bf16[128,1024]{1,0:T(8,128)(2,1)S(1)} %get-tuple-element.48), channel_id=1, source_target_pairs={{0,8},{4,12},{8,0},{12,4},{16,24},{20,28},{24,16},{28,20},{1,9},{5... | collective-permute-start | bytes 786440 | tf_op jit(solution)/shard_map/ppermute | solution.py:22
  92.7 41.6 %collective-permute-start.22 = (bf16[2,2,256,256]{3,2,1,0:T(8,128)(2,1)}, bf16[2,2,256,256]{3,2,1,0:T(8,128)(2,1)S(1)}, u32[]{:S(2)}, u32[]{:S(2)}) collective-permute-start(bf16[2,2,256,256]{3,2,1,0:T(8,128)(2,1)} %get-tuple-element.37), channel_id=1, source_target_pairs={{0,2},{1,3},{2,0},{3,1},{4,6},{5,7},{6,4},{7,5},{8,10},{9,11},{10,... | collective-permute-start | bytes 1572872 | tf_op jit(solution)/shard_map/ppermute | solution.py:22
  93.8 20.8 %collective-permute-start.9 = (bf16[128,1024]{1,0:T(8,128)(2,1)S(1)}, bf16[128,1024]{1,0:T(8,128)(2,1)S(1)}, u32[]{:S(2)}, u32[]{:S(2)}) collective-permute-start(bf16[128,1024]{1,0:T(8,128)(2,1)S(1)} %get-tuple-element.47), channel_id=1, source_target_pairs={{0,12},{4,8},{8,4},{12,0},{16,28},{20,24},{24,20},{28,16},{1,13},{... | collective-permute-start | bytes 786440 | tf_op jit(solution)/shard_map/ppermute | solution.py:22
  95.9 37.1 %collective-permute-start.23 = (bf16[2,1,256,256]{3,2,1,0:T(8,128)(2,1)}, bf16[2,1,256,256]{3,2,1,0:T(8,128)(2,1)}, u32[]{:S(2)}, u32[]{:S(2)}) collective-permute-start(bf16[2,1,256,256]{3,2,1,0:T(8,128)(2,1)} %get-tuple-element.38), channel_id=1, source_target_pairs={{0,3},{1,2},{2,1},{3,0},{4,7},{5,6},{6,5},{7,4},{8,11},{9,10},{10,... | collective-permute-start | bytes 786440 | tf_op jit(solution)/shard_map/ppermute | solution.py:22
  121.0 15.0 %copy-start.1 = (bf16[4,256,1024]{2,1,0:T(8,128)(2,1)S(1)}, bf16[4,256,1024]{2,1,0:T(8,128)(2,1)}, u32[]{:S(2)}) copy-start(bf16[4,256,1024]{2,1,0:T(8,128)(2,1)} %eta_ref.3) | copy-start | bytes 6291460
  121.0 15.0 %copy-start.35 = (s32[2,4,1024]{2,1,0:T(4,128)S(1)}, s32[2,4,1024]{2,1,0:T(4,128)}, u32[]{:S(2)}) copy-start(s32[2,4,1024]{2,1,0:T(4,128)} %occ_ref.3) | copy-start | bytes 98308
  121.0 15.0 %copy-start.37 = (s32[4]{0:T(128)S(1)}, s32[4]{0:T(128)}, u32[]{:S(2)}) copy-start(s32[4]{0:T(128)} %sizes_ref.3) | copy-start | bytes 52
  132.3 10.0 %collective-permute-start.14 = (bf16[128,1024]{1,0:T(8,128)(2,1)S(1)}, bf16[128,1024]{1,0:T(8,128)(2,1)S(1)}, u32[]{:S(2)}, u32[]{:S(2)}) collective-permute-start(bf16[128,1024]{1,0:T(8,128)(2,1)S(1)} %get-tuple-element.29), channel_id=1, source_target_pairs={{0,4},{4,0},{8,12},{12,8},{16,20},{20,16},{24,28},{28,24},{1,5},{5... | collective-permute-start | bytes 786440 | tf_op jit(solution)/shard_map/ppermute | solution.py:22
  132.4 11.4 %collective-permute-start.15 = (bf16[128,1024]{1,0:T(8,128)(2,1)S(1)}, bf16[128,1024]{1,0:T(8,128)(2,1)S(1)}, u32[]{:S(2)}, u32[]{:S(2)}) collective-permute-start(bf16[128,1024]{1,0:T(8,128)(2,1)S(1)} %get-tuple-element.30), channel_id=1, source_target_pairs={{0,8},{4,12},{8,0},{12,4},{16,24},{20,28},{24,16},{28,20},{1,9},{5... | collective-permute-start | bytes 786440 | tf_op jit(solution)/shard_map/ppermute | solution.py:22
  133.0 13.3 %collective-permute-start.16 = (bf16[128,1024]{1,0:T(8,128)(2,1)S(1)}, bf16[128,1024]{1,0:T(8,128)(2,1)S(1)}, u32[]{:S(2)}, u32[]{:S(2)}) collective-permute-start(bf16[128,1024]{1,0:T(8,128)(2,1)S(1)} %get-tuple-element.31), channel_id=1, source_target_pairs={{0,12},{4,8},{8,4},{12,0},{16,28},{20,24},{24,20},{28,16},{1,13},{... | collective-permute-start | bytes 786440 | tf_op jit(solution)/shard_map/ppermute | solution.py:22
  134.3 12.0 %collective-permute-start.17 = (bf16[128,1024]{1,0:T(8,128)(2,1)S(1)}, bf16[128,1024]{1,0:T(8,128)(2,1)S(1)}, u32[]{:S(2)}, u32[]{:S(2)}) collective-permute-start(bf16[128,1024]{1,0:T(8,128)(2,1)S(1)} %get-tuple-element.32), channel_id=1, source_target_pairs={{0,16},{4,20},{8,24},{12,28},{16,0},{20,4},{24,8},{28,12},{1,17},{... | collective-permute-start | bytes 786440 | tf_op jit(solution)/shard_map/ppermute | solution.py:22
  134.8 13.1 %collective-permute-start.18 = (bf16[128,1024]{1,0:T(8,128)(2,1)S(1)}, bf16[128,1024]{1,0:T(8,128)(2,1)S(1)}, u32[]{:S(2)}, u32[]{:S(2)}) collective-permute-start(bf16[128,1024]{1,0:T(8,128)(2,1)S(1)} %get-tuple-element.33), channel_id=1, source_target_pairs={{0,20},{4,16},{8,28},{12,24},{16,4},{20,0},{24,12},{28,8},{1,21},{... | collective-permute-start | bytes 786440 | tf_op jit(solution)/shard_map/ppermute | solution.py:22
  142.4 22.7 %collective-permute-start.24 = (bf16[256,1024]{1,0:T(8,128)(2,1)S(1)}, bf16[256,1024]{1,0:T(8,128)(2,1)S(1)}, u32[]{:S(2)}, u32[]{:S(2)}) collective-permute-start(bf16[256,1024]{1,0:T(8,128)(2,1)S(1)} %get-tuple-element.40), channel_id=1, source_target_pairs={{0,1},{1,0},{2,3},{3,2},{4,5},{5,4},{6,7},{7,6},{8,9},{9,8},{10,11... | collective-permute-start | bytes 1572872 | tf_op jit(solution)/shard_map/ppermute | solution.py:22
  143.8 34.9 %collective-permute-start.25 = (bf16[256,1024]{1,0:T(8,128)(2,1)S(1)}, bf16[256,1024]{1,0:T(8,128)(2,1)S(1)}, u32[]{:S(2)}, u32[]{:S(2)}) collective-permute-start(bf16[256,1024]{1,0:T(8,128)(2,1)S(1)} %get-tuple-element.41), channel_id=1, source_target_pairs={{0,2},{1,3},{2,0},{3,1},{4,6},{5,7},{6,4},{7,5},{8,10},{9,11},{10,... | collective-permute-start | bytes 1572872 | tf_op jit(solution)/shard_map/ppermute | solution.py:22
  146.3 45.3 %collective-permute-start.26 = (bf16[256,1024]{1,0:T(8,128)(2,1)S(1)}, bf16[256,1024]{1,0:T(8,128)(2,1)S(1)}, u32[]{:S(2)}, u32[]{:S(2)}) collective-permute-start(bf16[256,1024]{1,0:T(8,128)(2,1)S(1)} %get-tuple-element.42), channel_id=1, source_target_pairs={{0,3},{1,2},{2,1},{3,0},{4,7},{5,6},{6,5},{7,4},{8,11},{9,10},{10,... | collective-permute-start | bytes 1572872 | tf_op jit(solution)/shard_map/ppermute | solution.py:22
  146.3 10.0 %collective-permute-start.19 = (bf16[128,1024]{1,0:T(8,128)(2,1)S(1)}, bf16[128,1024]{1,0:T(8,128)(2,1)S(1)}, u32[]{:S(2)}, u32[]{:S(2)}) collective-permute-start(bf16[128,1024]{1,0:T(8,128)(2,1)S(1)} %get-tuple-element.34), channel_id=1, source_target_pairs={{0,24},{4,28},{8,16},{12,20},{16,8},{20,12},{24,0},{28,4},{1,25},{... | collective-permute-start | bytes 786440 | tf_op jit(solution)/shard_map/ppermute | solution.py:22
  147.9 13.4 %collective-permute-start.20 = (bf16[128,1024]{1,0:T(8,128)(2,1)S(1)}, bf16[128,1024]{1,0:T(8,128)(2,1)S(1)}, u32[]{:S(2)}, u32[]{:S(2)}) collective-permute-start(bf16[128,1024]{1,0:T(8,128)(2,1)S(1)} %get-tuple-element.35), channel_id=1, source_target_pairs={{0,28},{4,24},{8,20},{12,16},{16,12},{20,8},{24,4},{28,0},{1,29},{... | collective-permute-start | bytes 786440 | tf_op jit(solution)/shard_map/ppermute | solution.py:22
  (34 other events, 100.8 us)

commit v2 on v0

v2 whole, which is shorter than its diff:
```python
import functools

import jax
import jax.numpy as jnp
from jax import lax
from jax.experimental import pallas as pl
from jax.experimental.pallas import tpu as pltpu
from jax.sharding import PartitionSpec as P

BF16 = jnp.bfloat16
F32 = jnp.float32
ANY = pl.BlockSpec(memory_space=pl.ANY)
VMEM = pl.BlockSpec(memory_space=pltpu.VMEM)
SMEM = pl.BlockSpec(memory_space=pltpu.SMEM)


def params(mib):
    return pltpu.CompilerParams(vmem_limit_bytes=mib << 20)


def xor_permute(block, axis, size, step):
    return lax.ppermute(block, axis, [(i, i ^ step) for i in range(size)])


def aligned(start, size):
    return pl.ds(pl.multiple_of(start, size), size)


def row_tiles(states):
    rows = min(256, states)
    return [(start, rows) for start in range(0, states, rows)]


def block_order(blocks):
    half = list(range(0, blocks, 2))
    return half, [d for d in range(blocks) if d not in half]


def prepare_kernel(
    ph_count, states, order, me_ref, map_ref, occ_ref, weights_ref, turned_ref, select_ref
):
    rows = states // len(order)
    for q in range(ph_count):
        map_row = map_ref[q : q + 1, :]
        spans = [aligned((me_ref[0] ^ d) * rows, rows) for d in order]
        kept_map = jnp.concatenate([map_ref[q : q + 1, s] for s in spans], axis=1)
        signs = jnp.concatenate(
            [occ_ref[0, q : q + 1, s] - occ_ref[1, q : q + 1, s] for s in spans], axis=1
        ).astype(F32)
        for start, height in row_tiles(states):
            index = lax.broadcasted_iota(jnp.int32, (height, states), 0) + start
            select_ref[q, start : start + height, :] = jnp.where(
                index == kept_map, signs, 0.0
            ).astype(BF16)
            hot = jnp.where(index == map_row, 1.0, 0.0).astype(BF16)
            for top, tall in row_tiles(states):
                rest = weights_ref[q, top : top + tall, :]
                total = jnp.zeros((tall, height), F32)
                for _ in range(3):
                    part = rest.astype(BF16)
                    rest = rest - part.astype(F32)
                    total = total + lax.dot_general(
                        part, hot, (((1,), (1,)), ((), ())), preferred_element_type=F32
                    )
                turned_ref[q, top : top + tall, start : start + height] = total


def prepare(me, order, recouple_map, recoupled_occupation, recouple_weights):
    ph_count, states = recouple_map.shape
    return pl.pallas_call(
        functools.partial(prepare_kernel, ph_count, states, order),
        out_shape=(
            jax.ShapeDtypeStruct(recouple_weights.shape, F32),
            jax.ShapeDtypeStruct(recouple_weights.shape, BF16),
        ),
        in_specs=[SMEM] + [VMEM] * 3,
        out_specs=(VMEM, VMEM),
        compiler_params=params(12),
        name="prepare",
    )(me, recouple_map, recoupled_occupation, recouple_weights)


def weigh_blocks(states, order, me, turned_ref, select_ref, recv_refs, bar_ref, left_ref):
    for recv_ref, (slot, d) in zip(recv_refs, enumerate(order)):
        rows = recv_ref.shape[1]
        span = aligned((me ^ d) * rows, rows)
        for q in range(turned_ref.shape[0]):
            weights = turned_ref[q, span, :]
            for n in range(2):
                values = recv_ref[n, :, q * states : (q + 1) * states].astype(F32) * weights
                bar_ref[n, q, slot * rows : (slot + 1) * rows, :] = values.astype(BF16)
    for q in range(turned_ref.shape[0]):
        for n in range(2):
            for top, height in row_tiles(bar_ref.shape[2]):
                span = slice(top, top + height)
                left_ref[n, q, span, :] = jnp.dot(
                    bar_ref[n, q, span, :], select_ref[q], preferred_element_type=F32
                ).astype(BF16)


def weigh_kernel(states, order, me_ref, turned_ref, select_ref, *rest):
    weigh_blocks(states, order, me_ref[0], turned_ref, select_ref, rest[:-2], *rest[-2:])


def weigh(me, order, turned, select, received):
    ph_count, states, _ = turned.shape
    rows = received[0].shape[1]
    shape = jax.ShapeDtypeStruct((2, ph_count, rows * len(order), states), BF16)
    return pl.pallas_call(
        functools.partial(weigh_kernel, states, order),
        out_shape=(shape, shape),
        in_specs=[SMEM] + [VMEM] * (2 + len(order)),
        out_specs=(VMEM, VMEM),
        compiler_params=params(8),
        name="weigh",
    )(me, turned, select, *received)


def crossed_kernel(
    states, first, second, me_ref, turned_ref, select_ref, bar_ref, left_ref, *rest
):
    blocks = len(first) + len(second)
    recv_refs, out_refs = rest[: len(second)], rest[len(second) : len(second) + blocks]
    scratch = rest[len(second) + blocks :]
    me = me_ref[0]
    halves = [(first, bar_ref, left_ref)]
    if second:
        weigh_blocks(states, second, me, turned_ref, select_ref, recv_refs, *scratch)
        halves.append((second, *scratch))
    for q in range(turned_ref.shape[0]):
        columns = slice(q * states, (q + 1) * states)
        for order, _, left in halves:
            for top, height in row_tiles(left.shape[2]):
                crossed = jnp.zeros((height, states), F32)
                start = 0
                for _, bar, _ in halves:
                    inner = slice(start, start + bar.shape[2])
                    start = inner.stop
                    crossed += jnp.dot(
                        left[0, q, top : top + height, inner],
                        bar[1, q],
                        preferred_element_type=F32,
                    )
                    crossed -= jnp.dot(
                        left[1, q, top : top + height, inner],
                        bar[0, q],
                        preferred_element_type=F32,
                    )
                rows = out_refs[0].shape[0]
                step = min(rows, height)
                for base in range(0, height, step):
                    d = order[(top + base) // rows]
                    inside = (top + base) % rows
                    weights = turned_ref[q, aligned((me ^ d) * rows + inside, step), :]
                    out_refs[d][inside : inside + step, columns] = (
                        crossed[base : base + step] * weights
                    ).astype(BF16)


def crossed_blocks(me, order, turned, select, bar, left, received, flat):
    ph_count, states, _ = turned.shape
    first, second = order
    blocks = len(first) + len(second)
    scratch = []
    if second:
        scratch = [pltpu.VMEM((2, ph_count, states - bar.shape[2], states), BF16)] * 2
    return pl.pallas_call(
        functools.partial(crossed_kernel, states, first, second),
        out_shape=[jax.ShapeDtypeStruct((flat[0] // blocks, flat[1]), BF16)] * blocks,
        in_specs=[SMEM] + [VMEM] * (4 + len(second)),
        out_specs=[VMEM] * blocks,
        scratch_shapes=scratch,
        compiler_params=params(16),
        name="crossed",
    )(me, turned, select, bar, left, *received)


def pack_kernel(
    shape, blocks, tiles, me_ref, place_ref, sizes_ref, eta_ref, gamma_ref, *rest
):
    chan_count, tile_rows, states = shape
    block_refs, owner_refs = rest[:blocks], rest[blocks:-3]
    eta, gamma, sems = rest[-3:]
    me, place = me_ref[0], place_ref[0]
    copies = [
        pltpu.make_async_copy(source, full, sems.at[n])
        for n, (source, full) in enumerate(((eta_ref, eta), (gamma_ref, gamma)))
    ]
    for copy in copies:
        copy.start()
    rows = chan_count * tile_rows // blocks
    row = lax.broadcasted_iota(jnp.int32, (rows, states), 0)
    column = lax.broadcasted_iota(jnp.int32, (rows, states), 1)
    for copy in copies:
        copy.wait()
    for d, out_ref in enumerate(block_refs):
        start = (me ^ d) * rows
        chan = start // tile_rows
        inside = start - chan * tile_rows
        live = jnp.maximum(row + (place * tile_rows + inside), column) < sizes_ref[chan]
        for n, full in enumerate((eta, gamma)):
            values = full[chan, aligned(inside, rows), :]
            out_ref[n] = jnp.where(live, values, jnp.zeros_like(values))
    for step, out_ref in enumerate(owner_refs, 1):
        owner = place ^ step
        for n, full in enumerate((eta, gamma)):
            for m, other in enumerate(range(step, tiles)):
                out_ref[n, m] = full[owner, :, aligned((owner ^ other) * tile_rows, tile_rows)]


def pack(me, place, sizes, eta, gamma, blocks, tiles):
    chan_count, rows, states = eta.shape
    shapes = [(2, chan_count * rows // blocks, states)] * blocks
    shapes += [(2, tiles - step, rows, rows) for step in range(1, tiles)]
    out = pl.pallas_call(
        functools.partial(pack_kernel, eta.shape, blocks, tiles),
        out_shape=[jax.ShapeDtypeStruct(shape, BF16) for shape in shapes],
        in_specs=[SMEM] * 3 + [ANY] * 2,
        out_specs=[VMEM] * len(shapes),
        scratch_shapes=[
            pltpu.VMEM(eta.shape, BF16),
            pltpu.VMEM(eta.shape, BF16),
            pltpu.SemaphoreType.DMA((2,)),
        ],
        compiler_params=params(12),
        name="pack",
    )(me, place, sizes, eta, gamma)
    return out[:blocks], out[blocks:]


def ladder_kernel(tiles, rows, place_ref, sizes_ref, occ_ref, eta_ref, gamma_ref, *rest):
    packed_refs = rest[: tiles - 1]
    out_refs = rest[tiles - 1 : 2 * tiles - 1]
    eta, gamma, weight, sems = rest[2 * tiles - 1 :]
    place = place_ref[0]
    size = sizes_ref[place]
    states = tiles * rows
    copies = []
    for source, full in ((eta_ref, eta), (gamma_ref, gamma)):
        for k in range(tiles):
            copies.append(
                pltpu.make_async_copy(
                    source.at[place, :, aligned((place ^ k) * rows, rows)],
                    full.at[0:rows, k * rows : (k + 1) * rows],
                    sems.at[len(copies)],
                )
            )
    for copy in copies:
        copy.start()
    occupied = occ_ref[0] + occ_ref[1]
    own = lax.broadcasted_iota(jnp.int32, occupied.shape, 0) == place
    free = jnp.sum(jnp.where(own, 1 - occupied, 0), axis=0, keepdims=True)
    free = jnp.where(lax.broadcasted_iota(jnp.int32, free.shape, 1) < size, free, 0)
    weight[...] = free.astype(F32)
    for k in range(1, tiles):
        for n, full in enumerate((eta, gamma)):
            for m, other in enumerate(range(k, tiles)):
                full[k * rows : (k + 1) * rows, other * rows : (other + 1) * rows] = packed_refs[
                    k - 1
                ][n, m]
    for copy in copies:
        copy.wait()
    for k in range(tiles):
        for other in range(k + 1, tiles):
            here, there = slice(k * rows, (k + 1) * rows), slice(other * rows, (other + 1) * rows)
            eta[there, here] = -eta[here, there].T
            gamma[there, here] = gamma[here, there].T
    scale = jnp.concatenate(
        [weight[:, aligned((place ^ k) * rows, rows)] for k in range(tiles)], axis=1
    ).astype(BF16)
    for k in range(tiles):
        here = slice(k * rows, (k + 1) * rows)
        total = jnp.dot(eta[here, :] * scale, gamma[...], preferred_element_type=F32)
        total = total - jnp.dot(gamma[here, :] * scale, eta[...], preferred_element_type=F32)
        total = total.astype(BF16)
        for other in range(tiles):
            out_refs[k][:, aligned((place ^ other) * rows, rows)] = total[
                :, other * rows : (other + 1) * rows
            ]


def ladder_blocks(place, sizes, pair_occupation, eta, gamma, packed):
    tiles, rows, states = eta.shape
    return pl.pallas_call(
        functools.partial(ladder_kernel, tiles, rows),
        out_shape=[jax.ShapeDtypeStruct((rows, states), BF16) for _ in range(tiles)],
        in_specs=[SMEM, SMEM, VMEM, ANY, ANY] + [VMEM] * (tiles - 1),
        out_specs=[VMEM] * tiles,
        scratch_shapes=[
            pltpu.VMEM((states, states), BF16),
            pltpu.VMEM((states, states), BF16),
            pltpu.VMEM((1, states), F32),
            pltpu.SemaphoreType.DMA((2 * tiles,)),
        ],
        compiler_params=params(14),
        name="ladder",
    )(place, sizes, pair_occupation, eta, gamma, *packed)


def finish_kernel(blocks, ladders, me_ref, place_ref, sizes_ref, *rest):
    back_refs, ladder_refs = rest[:blocks], rest[blocks : blocks + ladders]
    out_ref, back = rest[blocks + ladders :]
    chan_count, tile_rows, states = out_ref.shape
    place = place_ref[0]
    rows = back_refs[0].shape[0]
    for d, back_ref in enumerate(back_refs):
        back[aligned((me_ref[0] ^ d) * rows, rows), :] = back_ref[...]
    row = lax.broadcasted_iota(jnp.int32, (tile_rows, states), 0) + place * tile_rows
    highest = jnp.maximum(row, lax.broadcasted_iota(jnp.int32, (tile_rows, states), 1))
    for k in range(chan_count):
        c, ladder = (place ^ k, ladder_refs[k][...]) if ladders > 1 else (k, ladder_refs[0][k])
        total = ladder.astype(F32) + back[aligned(c * tile_rows, tile_rows), :].astype(F32)
        out_ref[c] = jnp.where(highest < sizes_ref[c], total, 0.0).astype(BF16)


def finish(me, place, sizes, shape, back, ladder):
    chan_count, tile_rows, states = shape
    return pl.pallas_call(
        functools.partial(finish_kernel, len(back), len(ladder)),
        out_shape=jax.ShapeDtypeStruct(shape, BF16),
        in_specs=[SMEM] * 3 + [VMEM] * (len(back) + len(ladder)),
        out_specs=VMEM,
        scratch_shapes=[pltpu.VMEM((chan_count * tile_rows, states), BF16)],
        compiler_params=params(12),
        name="finish",
    )(me, place, sizes, *back, *ladder)


def ladder_gathered(sizes, pair_occupation, eta, gamma):
    _, rows, states = eta.shape
    columns = lax.broadcasted_iota(jnp.int32, (eta.shape[0], states), 1)
    weight = (1 - pair_occupation[0] - pair_occupation[1]) * (columns < sizes[:, None])
    first = jnp.einsum(
        "crk,ckj->crj",
        eta * weight.astype(BF16)[:, None, :],
        lax.all_gather(gamma, "tile", axis=1, tiled=True),
        preferred_element_type=F32,
    )
    mirrored = lax.all_to_all(first, "tile", split_axis=2, concat_axis=1, tiled=True)
    return first + jnp.swapaxes(mirrored, 1, 2)


def per_device(
    chans,
    tiles,
    generator,
    hamiltonian,
    chan_sizes,
    pair_occupation,
    recoupled_occupation,
    recouple_map,
    recouple_weights,
):
    chan_count, tile_rows, states = generator.shape
    flat = (chan_count * tile_rows, states)
    me = jnp.reshape(lax.axis_index("chan"), (1,))
    place = jnp.reshape(lax.axis_index("tile"), (1,))
    owned = tiles == chan_count
    stepped = chans <= 8 and chans & (chans - 1) == 0 and tile_rows % (flat[0] // chans) == 0
    blocks = chans if stepped else chan_count
    order = block_order(chans) if stepped else ([0], [])

    def exchange(sent):
        return [sent[0]] + [
            xor_permute(block, "chan", chans, d) for d, block in enumerate(sent) if d
        ]

    def exchange_whole(values):
        return [lax.all_to_all(values, "chan", values.ndim - 2, values.ndim - 2, tiled=True)]

    packed, owned_blocks = pack(
        me if stepped else jnp.zeros_like(me),
        place,
        chan_sizes,
        generator,
        hamiltonian,
        blocks,
        tiles if owned else 1,
    )
    if stepped:
        received = exchange(packed)
    else:
        received = exchange_whole(jnp.concatenate(packed, axis=1))
        me = jnp.zeros_like(me)
    if owned:
        lacking = [xor_permute(p, "tile", tiles, k) for k, p in enumerate(owned_blocks, 1)]
    turned, select = prepare(
        me, order[0] + order[1], recouple_map, recoupled_occupation, recouple_weights
    )
    bar, left = weigh(me, order[0], turned, select, [received[d] for d in order[0]])
    if owned:
        ladder = ladder_blocks(place, chan_sizes, pair_occupation, generator, hamiltonian, lacking)
        ladder = [ladder[0]] + [
            xor_permute(block, "tile", tiles, k) for k, block in enumerate(ladder) if k
        ]
    else:
        ladder = [ladder_gathered(chan_sizes, pair_occupation, generator, hamiltonian)]
    back = crossed_blocks(
        me, order, turned, select, bar, left, [received[d] for d in order[1]], flat
    )
    back = exchange(back) if stepped else exchange_whole(back[0])
    return finish(me, place, chan_sizes, generator.shape, back, ladder)


def solution(mesh):
    return jax.shard_map(
        functools.partial(per_device, mesh.shape["chan"], mesh.shape["tile"]),
        mesh=mesh,
        in_specs=(
            P("chan", "tile", None),
            P("chan", "tile", None),
            P("chan"),
            P(None, "chan", None),
            P(None, ("chan", "tile"), None),
            P(("chan", "tile"), None),
            P(("chan", "tile"), None, None),
        ),
        out_specs=P("chan", "tile", None),
        check_vma=False,
    )
```

time: 325 us -> 140 us (0.43)
  the two profiles are of different devices: /device:TPU:0 before, /device:TPU:12 now
where the time goes in v2:
time: 140 us
  waiting for transfers between devices  85 us (61%)
  Pallas kernels  28.2 us (20%)
  starting transfers between devices  22.8 us (16%)
  local copies, waits for them, and re-layouts  3.87 us (3%)
    ppermute x20, waiting for transfers between devices, xor_permute(): return lax.ppermute(block, axis, [(i, i ^ step) for i in range(size)])  85 us
    ppermute x20, starting transfers between devices, xor_permute(): return lax.ppermute(block, axis, [(i, i ^ step) for i in range(size)])  22.8 us
    pallas_call x1, Pallas kernels, prepare(): pl.pallas_call(functools.partial(prepare_kernel, ph_count, states, order)...  7.51 us
    pallas_call x1, Pallas kernels, crossed_blocks(): pl.pallas_call(functools.partial(crossed_kernel, states, first, second),...  7.27 us
    pallas_call x1, Pallas kernels, ladder_blocks(): pl.pallas_call(functools.partial(ladder_kernel, tiles, rows), out_shape=[...  5.68 us
    unnamed x20, local copies, waits for them, and re-layouts  3.87 us
    pallas_call x1, Pallas kernels, finish(): pl.pallas_call(functools.partial(finish_kernel, len(back), len(ladder)),...  3.36 us
  transfers between devices with their start and end apart: 20, of which 9 were waited for; matrix products, arithmetic and copies ran while one was open for 0% of the time, Pallas kernels for 16%

profile of v2, /device:TPU:12, one launch (start us, length us, event | category | flops | bytes accessed | tf_op | source)
XLA Modules:
  0.0 140.0 jit_solution(11849133878632027367)
XLA Ops:
  0.0 1.6 %copy-done = bf16[4,256,1024]{2,1,0:T(8,128)(2,1)S(1)} copy-done((bf16[4,256,1024]{2,1,0:T(8,128)(2,1)S(1)}, bf16[4,256,1024]{2,1,0:T(8,128)(2,1)}, u32[]{:S(2)}) %copy-start) | copy-done | bytes 2097176
  1.6 1.6 %copy-done.2 = bf16[4,256,1024]{2,1,0:T(8,128)(2,1)S(1)} copy-done((bf16[4,256,1024]{2,1,0:T(8,128)(2,1)S(1)}, bf16[4,256,1024]{2,1,0:T(8,128)(2,1)}, u32[]{:S(2)}) %copy-start.2) | copy-done | bytes 2097176
  3.2 0.7 copy-done.7
  3.8 1.9 %pack.1 = (bf16[2,128,1024]{2,1,0:T(8,128)(2,1)S(1)}, bf16[2,128,1024]{2,1,0:T(8,128)(2,1)S(1)}, bf16[2,128,1024]{2,1,0:T(8,128)(2,1)S(1)}, bf16[2,128,1024]{2,1...) custom-call(s32[1]{0:T(128)} %bitcast.me_ref, ...), custom_call_target="tpu_custom_call" | custom-call | tf_op jit(solution)/shard_map/pack/pallas_call | solution.py:215
  5.8 1.6 %collective-permute-start = (bf16[2,128,1024]{2,1,0:T(8,128)(2,1)S(1)}, bf16[2,128,1024]{2,1,0:T(8,128)(2,1)S(1)}, u32[]{:S(2)}, u32[]{:S(2)}) collective-permute-start(bf16[2,128,1024]{2,1,0:T(8,128)(2,1)S(1)} %get-tuple-element.35), channel_id=1, source_target_pairs={{0,8},{4,12},{8,0},{12,4},{16,24},{20,28},{24,16},{28,20},{1,9},{5... | collective-permute-start | bytes 1572872 | tf_op jit(solution)/shard_map/ppermute | solution.py:22
  7.8 1.5 %collective-permute-start.2 = (bf16[2,128,1024]{2,1,0:T(8,128)(2,1)S(1)}, bf16[2,128,1024]{2,1,0:T(8,128)(2,1)S(1)}, u32[]{:S(2)}, u32[]{:S(2)}) collective-permute-start(bf16[2,128,1024]{2,1,0:T(8,128)(2,1)S(1)} %get-tuple-element.37), channel_id=1, source_target_pairs={{0,24},{4,28},{8,16},{12,20},{16,8},{20,12},{24,0},{28,4},{1,25},{... | collective-permute-start | bytes 1572872 | tf_op jit(solution)/shard_map/ppermute | solution.py:22
  9.3 1.6 %collective-permute-start.4 = (bf16[2,128,1024]{2,1,0:T(8,128)(2,1)S(1)}, bf16[2,128,1024]{2,1,0:T(8,128)(2,1)S(1)}, u32[]{:S(2)}, u32[]{:S(2)}) collective-permute-start(bf16[2,128,1024]{2,1,0:T(8,128)(2,1)S(1)} %get-tuple-element.41), channel_id=1, source_target_pairs={{0,12},{4,8},{8,4},{12,0},{16,28},{20,24},{24,20},{28,16},{1,13},{... | collective-permute-start | bytes 1572872 | tf_op jit(solution)/shard_map/ppermute | solution.py:22
  10.9 9.7 %collective-permute-done.rest_1_ = bf16[2,128,1024]{2,1,0:T(8,128)(2,1)S(1)} collective-permute-done((bf16[2,128,1024]{2,1,0:T(8,128)(2,1)S(1)}, bf16[2,128,1024]{2,1,0:T(8,128)(2,1)S(1)}, u32[]{:S(2)}, u32[]{:S(2)}) %collective-permute-start) | collective-permute-done | bytes 524320 | tf_op jit(solution)/shard_map/ppermute | solution.py:22
  20.6 12.4 %collective-permute-done.1.rest_2_ = bf16[2,128,1024]{2,1,0:T(8,128)(2,1)S(1)} collective-permute-done((bf16[2,128,1024]{2,1,0:T(8,128)(2,1)S(1)}, bf16[2,128,1024]{2,1,0:T(8,128)(2,1)S(1)}, u32[]{:S(2)}, u32[]{:S(2)}) %collective-permute-start.1) | collective-permute-done | bytes 524320 | tf_op jit(solution)/shard_map/ppermute | solution.py:22
  33.1 0.7 collective-permute-start.14
  33.8 2.4 %collective-permute-start.15 = (bf16[2,2,256,256]{3,2,1,0:T(8,128)(2,1)S(1)}, bf16[2,2,256,256]{3,2,1,0:T(8,128)(2,1)S(1)}, u32[]{:S(2)}, u32[]{:S(2)}) collective-permute-start(bf16[2,2,256,256]{3,2,1,0:T(8,128)(2,1)S(1)} %get-tuple-element.53), channel_id=1, source_target_pairs={{0,2},{1,3},{2,0},{3,1},{4,6},{5,7},{6,4},{7,5},{8,10},{9,11},{10,... | collective-permute-start | bytes 1572872 | tf_op jit(solution)/shard_map/ppermute | solution.py:22
  36.1 6.1 %collective-permute-done.4.rest_1_ = bf16[2,128,1024]{2,1,0:T(8,128)(2,1)S(1)} collective-permute-done((bf16[2,128,1024]{2,1,0:T(8,128)(2,1)S(1)}, bf16[2,128,1024]{2,1,0:T(8,128)(2,1)S(1)}, u32[]{:S(2)}, u32[]{:S(2)}) %collective-permute-start.4) | collective-permute-done | bytes 524320 | tf_op jit(solution)/shard_map/ppermute | solution.py:22
  42.2 1.6 %collective-permute-start.16 = (bf16[2,1,256,256]{3,2,1,0:T(8,128)(2,1)S(1)}, bf16[2,1,256,256]{3,2,1,0:T(8,128)(2,1)S(1)}, u32[]{:S(2)}, u32[]{:S(2)}) collective-permute-start(bf16[2,1,256,256]{3,2,1,0:T(8,128)(2,1)S(1)} %get-tuple-element.54), channel_id=1, source_target_pairs={{0,3},{1,2},{2,1},{3,0},{4,7},{5,6},{6,5},{7,4},{8,11},{9,10},{10,... | collective-permute-start | bytes 786440 | tf_op jit(solution)/shard_map/ppermute | solution.py:22
  43.8 7.5 %prepare.1 = (f32[1,1024,1024]{2,1,0:T(8,128)S(1)}, bf16[1,1024,1024]{2,1,0:T(8,128)(2,1)S(1)}) custom-call(s32[1]{0:T(128)} %bitcast.me_ref, s32[1,1024]{1,0:T(1,128)S(1)} %copy-done.9, s32[2,1,1024]{2,1,0:T(1,128)S(1)} %copy-done.6, f32[1,1024,1024]{2,1,0:T(8,128)S(1)} %copy-done.4), custom_call_target="tpu_custom_call" | custom-call | tf_op jit(solution)/shard_map/prepare/pallas_call | solution.py:70
  51.3 2.4 %weigh.1 = (bf16[2,1,512,1024]{3,2,1,0:T(8,128)(2,1)S(1)}, bf16[2,1,512,1024]{3,2,1,0:T(8,128)(2,1)S(1)}) custom-call(s32[1]{0:T(128)} %bitcast.me_ref, f32[1,1024,1024]{2,1,0:T(8,128)S(1)} %get-tuple-element.32.turned_ref, bf16[1,1024,1024]{2,1,0:T(8,128)(2,1)S(1)} %get-tuple-element.33.select_ref, bf16[2,128,1024]{2,1,0:T(8,128)(2,1)S(1)} %get-tuple-element.34.rest_0_, ...), custom_call_target="tpu_custom_call" | custom-call | tf_op jit(solution)/shard_map/weigh/pallas_call | solution.py:109
  53.8 7.3 %crossed.1 = (bf16[128,1024]{1,0:T(8,128)(2,1)S(1)}, bf16[128,1024]{1,0:T(8,128)(2,1)S(1)}, bf16[128,1024]{1,0:T(8,128)(2,1)S(1)}, bf16[128,1024]{1,0:T(8,128)(2...) custom-call(s32[1]{0:T(128)} %bitcast.me_ref, ...), custom_call_target="tpu_custom_call" | custom-call | tf_op jit(solution)/shard_map/crossed/pallas_call | solution.py:167
  61.1 1.1 collective-permute-start.10
  62.2 1.1 collective-permute-start.11
  63.3 4.8 %collective-permute-done.16.rest_2_ = bf16[2,1,256,256]{3,2,1,0:T(8,128)(2,1)S(1)} collective-permute-done((bf16[2,1,256,256]{3,2,1,0:T(8,128)(2,1)S(1)}, bf16[2,1,256,256]{3,2,1,0:T(8,128)(2,1)S(1)}, u32[]{:S(2)}, u32[]{:S(2)}) %collective-permute-start.16) | collective-permute-done | bytes 262176 | tf_op jit(solution)/shard_map/ppermute | solution.py:22
  68.1 3.7 %collective-permute-start.12 = (bf16[128,1024]{1,0:T(8,128)(2,1)S(1)}, bf16[128,1024]{1,0:T(8,128)(2,1)S(1)}, u32[]{:S(2)}, u32[]{:S(2)}) collective-permute-start(bf16[128,1024]{1,0:T(8,128)(2,1)S(1)} %get-tuple-element.50), channel_id=1, source_target_pairs={{0,24},{4,28},{8,16},{12,20},{16,8},{20,12},{24,0},{28,4},{1,25},{... | collective-permute-start | bytes 786440 | tf_op jit(solution)/shard_map/ppermute | solution.py:22
  71.7 1.1 collective-permute-start.13
  73.0 5.7 %ladder.1 = (bf16[256,1024]{1,0:T(8,128)(2,1)S(1)}, bf16[256,1024]{1,0:T(8,128)(2,1)S(1)}, bf16[256,1024]{1,0:T(8,128)(2,1)S(1)}, bf16[256,1024]{1,0:T(8,128)(2,1)S(1)}) custom-call(s32[1]{0:T(128)} %bitcast.1.place_ref, s32[4]{0:T(128)S(1)} %copy-done.8, s32[2,4,1024]{2,1,0:T(4,128)S(1)} %copy-done.5, bf16[4,256,1024]{2,1,0:T(8,128)(2,1)S(1)} %copy-done.1, ...), custom_call_target="tpu_custom_call" | custom-call | tf_op jit(solution)/shard_map/ladder/pallas_call | solution.py:284
  78.7 0.9 collective-permute-start.17
  79.6 7.3 %collective-permute-done.11.rest_5_ = bf16[128,1024]{1,0:T(8,128)(2,1)S(1)} collective-permute-done((bf16[128,1024]{1,0:T(8,128)(2,1)S(1)}, bf16[128,1024]{1,0:T(8,128)(2,1)S(1)}, u32[]{:S(2)}, u32[]{:S(2)}) %collective-permute-start.11) | collective-permute-done | bytes 262176 | tf_op jit(solution)/shard_map/ppermute | solution.py:22
  86.9 2.4 %collective-permute-start.18 = (bf16[256,1024]{1,0:T(8,128)(2,1)S(1)}, bf16[256,1024]{1,0:T(8,128)(2,1)S(1)}, u32[]{:S(2)}, u32[]{:S(2)}) collective-permute-start(bf16[256,1024]{1,0:T(8,128)(2,1)S(1)} %get-tuple-element.57), channel_id=1, source_target_pairs={{0,2},{1,3},{2,0},{3,1},{4,6},{5,7},{6,4},{7,5},{8,10},{9,11},{10,... | collective-permute-start | bytes 1572872 | tf_op jit(solution)/shard_map/ppermute | solution.py:22
  89.3 1.5 %collective-permute-start.19 = (bf16[256,1024]{1,0:T(8,128)(2,1)S(1)}, bf16[256,1024]{1,0:T(8,128)(2,1)S(1)}, u32[]{:S(2)}, u32[]{:S(2)}) collective-permute-start(bf16[256,1024]{1,0:T(8,128)(2,1)S(1)} %get-tuple-element.58), channel_id=1, source_target_pairs={{0,3},{1,2},{2,1},{3,0},{4,7},{5,6},{6,5},{7,4},{8,11},{9,10},{10,... | collective-permute-start | bytes 1572872 | tf_op jit(solution)/shard_map/ppermute | solution.py:22
  90.8 0.8 collective-permute-start.8
  91.9 8.2 %collective-permute-done.8.rest_2_ = bf16[128,1024]{1,0:T(8,128)(2,1)S(1)} collective-permute-done((bf16[128,1024]{1,0:T(8,128)(2,1)S(1)}, bf16[128,1024]{1,0:T(8,128)(2,1)S(1)}, u32[]{:S(2)}, u32[]{:S(2)}) %collective-permute-start.8) | collective-permute-done | bytes 262176 | tf_op jit(solution)/shard_map/ppermute | solution.py:22
  100.0 3.0 %collective-permute-done.9.rest_3_ = bf16[128,1024]{1,0:T(8,128)(2,1)S(1)} collective-permute-done((bf16[128,1024]{1,0:T(8,128)(2,1)S(1)}, bf16[128,1024]{1,0:T(8,128)(2,1)S(1)}, u32[]{:S(2)}, u32[]{:S(2)}) %collective-permute-start.9) | collective-permute-done | bytes 262176 | tf_op jit(solution)/shard_map/ppermute | solution.py:22
  103.0 21.1 %collective-permute-done.18.rest_10_ = bf16[256,1024]{1,0:T(8,128)(2,1)S(1)} collective-permute-done((bf16[256,1024]{1,0:T(8,128)(2,1)S(1)}, bf16[256,1024]{1,0:T(8,128)(2,1)S(1)}, u32[]{:S(2)}, u32[]{:S(2)}) %collective-permute-start.18) | collective-permute-done | bytes 524320 | tf_op jit(solution)/shard_map/ppermute | solution.py:22
  124.1 12.5 %collective-permute-done.19.rest_11_ = bf16[256,1024]{1,0:T(8,128)(2,1)S(1)} collective-permute-done((bf16[256,1024]{1,0:T(8,128)(2,1)S(1)}, bf16[256,1024]{1,0:T(8,128)(2,1)S(1)}, u32[]{:S(2)}, u32[]{:S(2)}) %collective-permute-start.19) | collective-permute-done | bytes 524320 | tf_op jit(solution)/shard_map/ppermute | solution.py:22
  136.6 3.4 %finish.1 = bf16[4,256,1024]{2,1,0:T(8,128)(2,1)} custom-call(s32[1]{0:T(128)} %bitcast.me_ref, s32[1]{0:T(128)} %bitcast.1.place_ref, s32[4]{0:T(128)S(1)} %copy-done.8, bf16[128,1024]{1,0:T(8,128)(2,1)S(1)} %get-tuple-element.44.rest_0_, bf16[128,1024]{1,0:T(8,128)(2,1)S(1)} %collective-permute-done.7.rest_1_, ...), custom_call_target="tpu_custom_call" | custom-call | tf_op jit(solution)/shard_map/finish/pallas_call | solution.py:318
  (34 shorter events, 1.0 us)
Async XLA Ops:
  0.0 1.6 %copy-start = (bf16[4,256,1024]{2,1,0:T(8,128)(2,1)S(1)}, bf16[4,256,1024]{2,1,0:T(8,128)(2,1)}, u32[]{:S(2)}) copy-start(bf16[4,256,1024]{2,1,0:T(8,128)(2,1)} %eta_ref.3) | copy-start | bytes 6291460
  1.6 1.6 %copy-start.2 = (bf16[4,256,1024]{2,1,0:T(8,128)(2,1)S(1)}, bf16[4,256,1024]{2,1,0:T(8,128)(2,1)}, u32[]{:S(2)}) copy-start(bf16[4,256,1024]{2,1,0:T(8,128)(2,1)} %gamma_ref.3) | copy-start | bytes 6291460
  3.2 0.7 copy-start.7
  3.8 39.9 %copy-start.4 = (f32[1,1024,1024]{2,1,0:T(8,128)S(1)}, f32[1,1024,1024]{2,1,0:T(8,128)}, u32[]{:S(2)}) copy-start(f32[1,1024,1024]{2,1,0:T(8,128)} %weights_ref.1) | copy-start | bytes 12582916
  3.8 39.9 %copy-start.6 = (s32[2,1,1024]{2,1,0:T(1,128)S(1)}, s32[2,1,1024]{2,1,0:T(1,128)}, u32[]{:S(2)}) copy-start(s32[2,1,1024]{2,1,0:T(1,128)} %occ_ref.2) | copy-start | bytes 24580
  3.8 39.9 %copy-start.9 = (s32[1,1024]{1,0:T(1,128)S(1)}, s32[1,1024]{1,0:T(1,128)}, u32[]{:S(2)}) copy-start(s32[1,1024]{1,0:T(1,128)} %map_ref.1) | copy-start | bytes 12292
  5.8 14.9 %collective-permute-start = (bf16[2,128,1024]{2,1,0:T(8,128)(2,1)S(1)}, bf16[2,128,1024]{2,1,0:T(8,128)(2,1)S(1)}, u32[]{:S(2)}, u32[]{:S(2)}) collective-permute-start(bf16[2,128,1024]{2,1,0:T(8,128)(2,1)S(1)} %get-tuple-element.35), channel_id=1, source_target_pairs={{0,8},{4,12},{8,0},{12,4},{16,24},{20,28},{24,16},{28,20},{1,9},{5... | collective-permute-start | bytes 1572872 | tf_op jit(solution)/shard_map/ppermute | solution.py:22
  7.3 25.7 %collective-permute-start.1 = (bf16[2,128,1024]{2,1,0:T(8,128)(2,1)S(1)}, bf16[2,128,1024]{2,1,0:T(8,128)(2,1)S(1)}, u32[]{:S(2)}, u32[]{:S(2)}) collective-permute-start(bf16[2,128,1024]{2,1,0:T(8,128)(2,1)S(1)} %get-tuple-element.36), channel_id=1, source_target_pairs={{0,16},{4,20},{8,24},{12,28},{16,0},{20,4},{24,8},{28,12},{1,17},{... | collective-permute-start | bytes 1572872 | tf_op jit(solution)/shard_map/ppermute | solution.py:22
  7.8 25.2 %collective-permute-start.2 = (bf16[2,128,1024]{2,1,0:T(8,128)(2,1)S(1)}, bf16[2,128,1024]{2,1,0:T(8,128)(2,1)S(1)}, u32[]{:S(2)}, u32[]{:S(2)}) collective-permute-start(bf16[2,128,1024]{2,1,0:T(8,128)(2,1)S(1)} %get-tuple-element.37), channel_id=1, source_target_pairs={{0,24},{4,28},{8,16},{12,20},{16,8},{20,12},{24,0},{28,4},{1,25},{... | collective-permute-start | bytes 1572872 | tf_op jit(solution)/shard_map/ppermute | solution.py:22
  9.3 24.4 %collective-permute-start.3 = (bf16[2,128,1024]{2,1,0:T(8,128)(2,1)S(1)}, bf16[2,128,1024]{2,1,0:T(8,128)(2,1)S(1)}, u32[]{:S(2)}, u32[]{:S(2)}) collective-permute-start(bf16[2,128,1024]{2,1,0:T(8,128)(2,1)S(1)} %get-tuple-element.40), channel_id=1, source_target_pairs={{0,4},{4,0},{8,12},{12,8},{16,20},{20,16},{24,28},{28,24},{1,5},{5... | collective-permute-start | bytes 1572872 | tf_op jit(solution)/shard_map/ppermute | solution.py:22
  9.3 32.8 %collective-permute-start.4 = (bf16[2,128,1024]{2,1,0:T(8,128)(2,1)S(1)}, bf16[2,128,1024]{2,1,0:T(8,128)(2,1)S(1)}, u32[]{:S(2)}, u32[]{:S(2)}) collective-permute-start(bf16[2,128,1024]{2,1,0:T(8,128)(2,1)S(1)} %get-tuple-element.41), channel_id=1, source_target_pairs={{0,12},{4,8},{8,4},{12,0},{16,28},{20,24},{24,20},{28,16},{1,13},{... | collective-permute-start | bytes 1572872 | tf_op jit(solution)/shard_map/ppermute | solution.py:22
  20.6 33.1 %collective-permute-start.5 = (bf16[2,128,1024]{2,1,0:T(8,128)(2,1)S(1)}, bf16[2,128,1024]{2,1,0:T(8,128)(2,1)S(1)}, u32[]{:S(2)}, u32[]{:S(2)}) collective-permute-start(bf16[2,128,1024]{2,1,0:T(8,128)(2,1)S(1)} %get-tuple-element.42), channel_id=1, source_target_pairs={{0,20},{4,16},{8,28},{12,24},{16,4},{20,0},{24,12},{28,8},{1,21},{... | collective-permute-start | bytes 1572872 | tf_op jit(solution)/shard_map/ppermute | solution.py:22
  33.0 20.7 %collective-permute-start.6 = (bf16[2,128,1024]{2,1,0:T(8,128)(2,1)S(1)}, bf16[2,128,1024]{2,1,0:T(8,128)(2,1)S(1)}, u32[]{:S(2)}, u32[]{:S(2)}) collective-permute-start(bf16[2,128,1024]{2,1,0:T(8,128)(2,1)S(1)} %get-tuple-element.43), channel_id=1, source_target_pairs={{0,28},{4,24},{8,20},{12,16},{16,12},{20,8},{24,4},{28,0},{1,29},{... | collective-permute-start | bytes 1572872 | tf_op jit(solution)/shard_map/ppermute | solution.py:22
  33.1 39.8 %collective-permute-start.14 = (bf16[2,3,256,256]{3,2,1,0:T(8,128)(2,1)S(1)}, bf16[2,3,256,256]{3,2,1,0:T(8,128)(2,1)S(1)}, u32[]{:S(2)}, u32[]{:S(2)}) collective-permute-start(bf16[2,3,256,256]{3,2,1,0:T(8,128)(2,1)S(1)} %get-tuple-element.52), channel_id=1, source_target_pairs={{0,1},{1,0},{2,3},{3,2},{4,5},{5,4},{6,7},{7,6},{8,9},{9,8},{10,11... | collective-permute-start | bytes 2359304 | tf_op jit(solution)/shard_map/ppermute | solution.py:22
  33.8 38.0 %collective-permute-start.15 = (bf16[2,2,256,256]{3,2,1,0:T(8,128)(2,1)S(1)}, bf16[2,2,256,256]{3,2,1,0:T(8,128)(2,1)S(1)}, u32[]{:S(2)}, u32[]{:S(2)}) collective-permute-start(bf16[2,2,256,256]{3,2,1,0:T(8,128)(2,1)S(1)} %get-tuple-element.53), channel_id=1, source_target_pairs={{0,2},{1,3},{2,0},{3,1},{4,6},{5,7},{6,4},{7,5},{8,10},{9,11},{10,... | collective-permute-start | bytes 1572872 | tf_op jit(solution)/shard_map/ppermute | solution.py:22
  42.2 25.9 %collective-permute-start.16 = (bf16[2,1,256,256]{3,2,1,0:T(8,128)(2,1)S(1)}, bf16[2,1,256,256]{3,2,1,0:T(8,128)(2,1)S(1)}, u32[]{:S(2)}, u32[]{:S(2)}) collective-permute-start(bf16[2,1,256,256]{3,2,1,0:T(8,128)(2,1)S(1)} %get-tuple-element.54), channel_id=1, source_target_pairs={{0,3},{1,2},{2,1},{3,0},{4,7},{5,6},{6,5},{7,4},{8,11},{9,10},{10,... | collective-permute-start | bytes 786440 | tf_op jit(solution)/shard_map/ppermute | solution.py:22
  53.7 19.3 %copy-start.1 = (bf16[4,256,1024]{2,1,0:T(8,128)(2,1)S(1)}, bf16[4,256,1024]{2,1,0:T(8,128)(2,1)}, u32[]{:S(2)}) copy-start(bf16[4,256,1024]{2,1,0:T(8,128)(2,1)} %eta_ref.3) | copy-start | bytes 6291460
  53.7 19.3 %copy-start.3 = (bf16[4,256,1024]{2,1,0:T(8,128)(2,1)S(1)}, bf16[4,256,1024]{2,1,0:T(8,128)(2,1)}, u32[]{:S(2)}) copy-start(bf16[4,256,1024]{2,1,0:T(8,128)(2,1)} %gamma_ref.3) | copy-start | bytes 6291460
  53.7 19.3 %copy-start.5 = (s32[2,4,1024]{2,1,0:T(4,128)S(1)}, s32[2,4,1024]{2,1,0:T(4,128)}, u32[]{:S(2)}) copy-start(s32[2,4,1024]{2,1,0:T(4,128)} %occ_ref.3) | copy-start | bytes 98308
  53.8 19.3 %copy-start.8 = (s32[4]{0:T(128)S(1)}, s32[4]{0:T(128)}, u32[]{:S(2)}) copy-start(s32[4]{0:T(128)} %sizes_ref.5) | copy-start | bytes 52
  61.1 17.7 %collective-permute-start.10 = (bf16[128,1024]{1,0:T(8,128)(2,1)S(1)}, bf16[128,1024]{1,0:T(8,128)(2,1)S(1)}, u32[]{:S(2)}, u32[]{:S(2)}) collective-permute-start(bf16[128,1024]{1,0:T(8,128)(2,1)S(1)} %get-tuple-element.48), channel_id=1, source_target_pairs={{0,16},{4,20},{8,24},{12,28},{16,0},{20,4},{24,8},{28,12},{1,17},{... | collective-permute-start | bytes 786440 | tf_op jit(solution)/shard_map/ppermute | solution.py:22
  62.2 24.7 %collective-permute-start.11 = (bf16[128,1024]{1,0:T(8,128)(2,1)S(1)}, bf16[128,1024]{1,0:T(8,128)(2,1)S(1)}, u32[]{:S(2)}, u32[]{:S(2)}) collective-permute-start(bf16[128,1024]{1,0:T(8,128)(2,1)S(1)} %get-tuple-element.49), channel_id=1, source_target_pairs={{0,20},{4,16},{8,28},{12,24},{16,4},{20,0},{24,12},{28,8},{1,21},{... | collective-permute-start | bytes 786440 | tf_op jit(solution)/shard_map/ppermute | solution.py:22
  68.1 21.2 %collective-permute-start.12 = (bf16[128,1024]{1,0:T(8,128)(2,1)S(1)}, bf16[128,1024]{1,0:T(8,128)(2,1)S(1)}, u32[]{:S(2)}, u32[]{:S(2)}) collective-permute-start(bf16[128,1024]{1,0:T(8,128)(2,1)S(1)} %get-tuple-element.50), channel_id=1, source_target_pairs={{0,24},{4,28},{8,16},{12,20},{16,8},{20,12},{24,0},{28,4},{1,25},{... | collective-permute-start | bytes 786440 | tf_op jit(solution)/shard_map/ppermute | solution.py:22
  71.7 19.1 %collective-permute-start.13 = (bf16[128,1024]{1,0:T(8,128)(2,1)S(1)}, bf16[128,1024]{1,0:T(8,128)(2,1)S(1)}, u32[]{:S(2)}, u32[]{:S(2)}) collective-permute-start(bf16[128,1024]{1,0:T(8,128)(2,1)S(1)} %get-tuple-element.51), channel_id=1, source_target_pairs={{0,28},{4,24},{8,20},{12,16},{16,12},{20,8},{24,4},{28,0},{1,29},{... | collective-permute-start | bytes 786440 | tf_op jit(solution)/shard_map/ppermute | solution.py:22
  72.9 18.8 %collective-permute-start.7 = (bf16[128,1024]{1,0:T(8,128)(2,1)S(1)}, bf16[128,1024]{1,0:T(8,128)(2,1)S(1)}, u32[]{:S(2)}, u32[]{:S(2)}) collective-permute-start(bf16[128,1024]{1,0:T(8,128)(2,1)S(1)} %get-tuple-element.45), channel_id=1, source_target_pairs={{0,4},{4,0},{8,12},{12,8},{16,20},{20,16},{24,28},{28,24},{1,5},{5... | collective-permute-start | bytes 786440 | tf_op jit(solution)/shard_map/ppermute | solution.py:22
  78.7 24.3 %collective-permute-start.17 = (bf16[256,1024]{1,0:T(8,128)(2,1)S(1)}, bf16[256,1024]{1,0:T(8,128)(2,1)S(1)}, u32[]{:S(2)}, u32[]{:S(2)}) collective-permute-start(bf16[256,1024]{1,0:T(8,128)(2,1)S(1)} %get-tuple-element.56), channel_id=1, source_target_pairs={{0,1},{1,0},{2,3},{3,2},{4,5},{5,4},{6,7},{7,6},{8,9},{9,8},{10,11... | collective-permute-start | bytes 1572872 | tf_op jit(solution)/shard_map/ppermute | solution.py:22
  86.9 37.2 %collective-permute-start.18 = (bf16[256,1024]{1,0:T(8,128)(2,1)S(1)}, bf16[256,1024]{1,0:T(8,128)(2,1)S(1)}, u32[]{:S(2)}, u32[]{:S(2)}) collective-permute-start(bf16[256,1024]{1,0:T(8,128)(2,1)S(1)} %get-tuple-element.57), channel_id=1, source_target_pairs={{0,2},{1,3},{2,0},{3,1},{4,6},{5,7},{6,4},{7,5},{8,10},{9,11},{10,... | collective-permute-start | bytes 1572872 | tf_op jit(solution)/shard_map/ppermute | solution.py:22
  89.3 47.3 %collective-permute-start.19 = (bf16[256,1024]{1,0:T(8,128)(2,1)S(1)}, bf16[256,1024]{1,0:T(8,128)(2,1)S(1)}, u32[]{:S(2)}, u32[]{:S(2)}) collective-permute-start(bf16[256,1024]{1,0:T(8,128)(2,1)S(1)} %get-tuple-element.58), channel_id=1, source_target_pairs={{0,3},{1,2},{2,1},{3,0},{4,7},{5,6},{6,5},{7,4},{8,11},{9,10},{10,... | collective-permute-start | bytes 1572872 | tf_op jit(solution)/shard_map/ppermute | solution.py:22
  90.8 9.2 %collective-permute-start.8 = (bf16[128,1024]{1,0:T(8,128)(2,1)S(1)}, bf16[128,1024]{1,0:T(8,128)(2,1)S(1)}, u32[]{:S(2)}, u32[]{:S(2)}) collective-permute-start(bf16[128,1024]{1,0:T(8,128)(2,1)S(1)} %get-tuple-element.46), channel_id=1, source_target_pairs={{0,8},{4,12},{8,0},{12,4},{16,24},{20,28},{24,16},{28,20},{1,9},{5... | collective-permute-start | bytes 786440 | tf_op jit(solution)/shard_map/ppermute | solution.py:22
  91.6 11.4 %collective-permute-start.9 = (bf16[128,1024]{1,0:T(8,128)(2,1)S(1)}, bf16[128,1024]{1,0:T(8,128)(2,1)S(1)}, u32[]{:S(2)}, u32[]{:S(2)}) collective-permute-start(bf16[128,1024]{1,0:T(8,128)(2,1)S(1)} %get-tuple-element.47), channel_id=1, source_target_pairs={{0,12},{4,8},{8,4},{12,0},{16,28},{20,24},{24,20},{28,16},{1,13},{... | collective-permute-start | bytes 786440 | tf_op jit(solution)/shard_map/ppermute | solution.py:22

commit v3 on v2

v3 whole, which is shorter than its diff:
```python
import functools

import jax
import jax.numpy as jnp
from jax import lax
from jax.experimental import pallas as pl
from jax.experimental.pallas import tpu as pltpu
from jax.sharding import PartitionSpec as P

BF16 = jnp.bfloat16
F32 = jnp.float32
HBM = pl.BlockSpec(memory_space=pltpu.HBM)
VMEM = pl.BlockSpec(memory_space=pltpu.VMEM)
NT = (((1,), (1,)), ((), ()))
SMEM = pl.BlockSpec(memory_space=pltpu.SMEM)


def params(mib):
    return pltpu.CompilerParams(vmem_limit_bytes=mib << 20)


def cost(flops, moved):
    return pl.CostEstimate(flops=int(flops), bytes_accessed=int(moved), transcendentals=0)


def xor_permute(block, axis, size, step):
    return lax.ppermute(block, axis, [(i, i ^ step) for i in range(size)])


def after(message, *arrived):
    return lax.optimization_barrier((message, *arrived))[0]


def aligned(start, size):
    return pl.ds(pl.multiple_of(start, size), size)


def row_tiles(states):
    rows = min(256, states)
    return [(start, rows) for start in range(0, states, rows)]


def block_order(blocks):
    half = list(range(0, blocks, 2))
    return half, [d for d in range(blocks) if d not in half]


def prepare_kernel(
    ph_count, states, order, me_ref, map_ref, occ_ref, weights_ref, turned_ref, select_ref
):
    rows = states // len(order)
    for q in range(ph_count):
        map_row = map_ref[q : q + 1, :]
        spans = [aligned((me_ref[0] ^ d) * rows, rows) for d in order]
        kept_map = jnp.concatenate([map_ref[q : q + 1, s] for s in spans], axis=1)
        signs = jnp.concatenate(
            [occ_ref[0, q : q + 1, s] - occ_ref[1, q : q + 1, s] for s in spans], axis=1
        ).astype(F32)
        for start, height in row_tiles(states):
            index = lax.broadcasted_iota(jnp.int32, (height, states), 0) + start
            select_ref[q, start : start + height, :] = jnp.where(
                index == kept_map, signs, 0.0
            ).astype(BF16)
            hot = jnp.where(index == map_row, 1.0, 0.0).astype(BF16)
            for top, tall in row_tiles(states):
                rest = weights_ref[q, top : top + tall, :]
                total = jnp.zeros((tall, height), F32)
                for _ in range(3):
                    part = rest.astype(BF16)
                    rest = rest - part.astype(F32)
                    total = total + lax.dot_general(
                        part, hot, NT, preferred_element_type=F32
                    )
                turned_ref[q, top : top + tall, start : start + height] = total


def prepare(me, order, recouple_map, recoupled_occupation, recouple_weights):
    ph_count, states = recouple_map.shape
    return pl.pallas_call(
        functools.partial(prepare_kernel, ph_count, states, order),
        out_shape=(
            jax.ShapeDtypeStruct(recouple_weights.shape, F32),
            jax.ShapeDtypeStruct(recouple_weights.shape, BF16),
        ),
        in_specs=[SMEM] + [VMEM] * 3,
        out_specs=(VMEM, VMEM),
        compiler_params=params(12),
        cost_estimate=cost(6 * ph_count * states**3, 14 * ph_count * states**2),
        name="prepare",
    )(me, recouple_map, recoupled_occupation, recouple_weights)


def weigh_blocks(states, order, me, turned_ref, recv_refs, bar_ref):
    for recv_ref, (slot, d) in zip(recv_refs, enumerate(order)):
        rows = recv_ref.shape[1]
        span = aligned((me ^ d) * rows, rows)
        for q in range(turned_ref.shape[0]):
            weights = turned_ref[q, span, :]
            for n in range(2):
                values = recv_ref[n, :, q * states : (q + 1) * states].astype(F32) * weights
                bar_ref[n, q, slot * rows : (slot + 1) * rows, :] = values.astype(BF16)


def turn_blocks(select_ref, bar_ref, left_ref):
    for q in range(select_ref.shape[0]):
        for n in range(2):
            for top, height in row_tiles(bar_ref.shape[2]):
                span = slice(top, top + height)
                left_ref[n, q, span, :] = jnp.dot(
                    bar_ref[n, q, span, :], select_ref[q], preferred_element_type=F32
                ).astype(BF16)


def cross_blocks(states, order, me, turned_ref, left_ref, bar_refs, out_refs):
    rows = out_refs[0].shape[0]
    for q in range(turned_ref.shape[0]):
        columns = slice(q * states, (q + 1) * states)
        for top, height in row_tiles(left_ref.shape[2]):
            span = slice(top, top + height)
            crossed = jnp.zeros((height, states), F32)
            start = 0
            for bar_ref in bar_refs:
                inner = slice(start, start + bar_ref.shape[2])
                start = inner.stop
                for n, sign in ((0, 1), (1, -1)):
                    crossed += sign * jnp.dot(
                        left_ref[n, q, span, inner], bar_ref[1 - n, q], preferred_element_type=F32
                    )
            step = min(rows, height)
            for base in range(0, height, step):
                slot, inside = divmod(top + base, rows)
                weights = turned_ref[q, aligned((me ^ order[slot]) * rows + inside, step), :]
                out_refs[slot][inside : inside + step, columns] = (
                    crossed[base : base + step] * weights
                ).astype(BF16)


def first_kernel(states, order, me_ref, turned_ref, select_ref, *rest):
    recv_refs, (bar_ref, left_ref) = rest[:-2], rest[-2:]
    weigh_blocks(states, order, me_ref[0], turned_ref, recv_refs, bar_ref)
    turn_blocks(select_ref, bar_ref, left_ref)


def first_half(me, order, turned, select, received):
    ph_count, states, _ = turned.shape
    rows = received[0].shape[1]
    shape = jax.ShapeDtypeStruct((2, ph_count, rows * len(order), states), BF16)
    return pl.pallas_call(
        functools.partial(first_kernel, states, order),
        out_shape=(shape, shape),
        in_specs=[SMEM] + [VMEM] * (2 + len(order)),
        out_specs=(VMEM, VMEM),
        compiler_params=params(8),
        cost_estimate=cost(4 * ph_count * shape.shape[2] * states**2, 14 * ph_count * states**2),
        name="first_half",
    )(me, turned, select, *received)


def cross_first_kernel(states, order, me_ref, turned_ref, bar_ref, left_ref, *rest):
    first, second = order
    recv_refs, out_refs = rest[: len(second)], rest[len(second) : len(second) + len(first)]
    bar_refs = [bar_ref]
    if second:
        weigh_blocks(states, second, me_ref[0], turned_ref, recv_refs, rest[-1])
        bar_refs.append(rest[-1])
    cross_blocks(states, first, me_ref[0], turned_ref, left_ref, bar_refs, out_refs)


def cross_first(me, order, turned, bar, left, received, flat):
    ph_count, states, _ = turned.shape
    first, second = order
    blocks = len(first) + len(second)
    out_shape = [jax.ShapeDtypeStruct((flat[0] // blocks, flat[1]), BF16)] * len(first)
    if second:
        out_shape.append(
            jax.ShapeDtypeStruct((2, ph_count, states - bar.shape[2], states), BF16)
        )
    out = pl.pallas_call(
        functools.partial(cross_first_kernel, states, order),
        out_shape=out_shape,
        in_specs=[SMEM] + [VMEM] * (3 + len(second)),
        out_specs=[VMEM] * len(out_shape),
        compiler_params=params(8),
        cost_estimate=cost(2 * ph_count * states**3, 14 * ph_count * states**2),
        name="cross_first",
    )(me, turned, bar, left, *received)
    return out[: len(first)], out[-1]


def cross_second_kernel(
    states, order, me_ref, turned_ref, select_ref, bar_ref, second_bar_ref, *rest
):
    out_refs, left_ref = rest[:-1], rest[-1]
    turn_blocks(select_ref, second_bar_ref, left_ref)
    cross_blocks(
        states, order, me_ref[0], turned_ref, left_ref, [bar_ref, second_bar_ref], out_refs
    )


def cross_second(me, order, turned, select, bar, second_bar, flat, blocks):
    ph_count, states, _ = turned.shape
    return pl.pallas_call(
        functools.partial(cross_second_kernel, states, order),
        out_shape=[jax.ShapeDtypeStruct((flat[0] // blocks, flat[1]), BF16)] * len(order),
        in_specs=[SMEM] + [VMEM] * 4,
        out_specs=[VMEM] * len(order),
        scratch_shapes=[pltpu.VMEM(second_bar.shape, BF16)],
        compiler_params=params(12),
        cost_estimate=cost(4 * ph_count * states**3, 14 * ph_count * states**2),
        name="cross_second",
    )(me, turned, select, bar, second_bar)


def pack_rows_kernel(shape, blocks, partners, me_ref, place_ref, sizes_ref, *rest):
    chan_count, tile_rows, states = shape
    source_refs, out_refs = rest[:2], rest[2 : 2 + len(partners)]
    held, sems = rest[2 + len(partners) :]
    rows = chan_count * tile_rows // blocks
    copies = []
    for slot, d in enumerate(partners):
        start = (me_ref[0] ^ d) * rows
        chan = start // tile_rows
        inside = start - chan * tile_rows
        for n, source_ref in enumerate(source_refs):
            copies.append(
                pltpu.make_async_copy(
                    source_ref.at[chan, aligned(inside, rows), :],
                    held.at[slot, n],
                    sems.at[len(copies)],
                )
            )
    for copy in copies:
        copy.start()
    row = lax.broadcasted_iota(jnp.int32, (rows, states), 0) + place_ref[0] * tile_rows
    column = lax.broadcasted_iota(jnp.int32, (rows, states), 1)
    for slot, d in enumerate(partners):
        start = (me_ref[0] ^ d) * rows
        chan = start // tile_rows
        inside = start - chan * tile_rows
        live = jnp.maximum(row + inside, column) < sizes_ref[chan]
        for n in range(2):
            copies[2 * slot + n].wait()
            values = held[slot, n]
            out_refs[slot][n] = jnp.where(live, values, jnp.zeros_like(values))


def pack_rows(me, place, sizes, eta, gamma, blocks, partners):
    chan_count, tile_rows, states = eta.shape
    shape = (2, chan_count * tile_rows // blocks, states)
    return pl.pallas_call(
        functools.partial(pack_rows_kernel, eta.shape, blocks, partners),
        out_shape=[jax.ShapeDtypeStruct(shape, BF16)] * len(partners),
        in_specs=[SMEM] * 3 + [HBM] * 2,
        out_specs=[VMEM] * len(partners),
        scratch_shapes=[
            pltpu.VMEM((len(partners), *shape), BF16),
            pltpu.SemaphoreType.DMA((2 * len(partners),)),
        ],
        compiler_params=params(8),
        cost_estimate=cost(0, 8 * len(partners) * shape[1] * states),
        name="pack_rows",
    )(me, place, sizes, eta, gamma)


def pack_owners_kernel(tiles, rows, place_ref, eta_ref, gamma_ref, *rest):
    out_refs, sems = rest[:-1], rest[-1]
    copies = []
    for step in range(1, tiles):
        owner = place_ref[0] ^ step
        for n, source_ref in enumerate((eta_ref, gamma_ref)):
            for m, other in enumerate(range(step, tiles)):
                copies.append(
                    pltpu.make_async_copy(
                        source_ref.at[owner, :, aligned((owner ^ other) * rows, rows)],
                        out_refs[step - 1].at[n, m],
                        sems.at[len(copies)],
                    )
                )
    for copy in copies:
        copy.start()
    for copy in copies:
        copy.wait()


def pack_owners(place, eta, gamma):
    tiles, rows, _ = eta.shape
    return pl.pallas_call(
        functools.partial(pack_owners_kernel, tiles, rows),
        out_shape=[
            jax.ShapeDtypeStruct((2, tiles - step, rows, rows), BF16) for step in range(1, tiles)
        ],
        in_specs=[SMEM] + [HBM] * 2,
        out_specs=[VMEM] * (tiles - 1),
        scratch_shapes=[pltpu.SemaphoreType.DMA((tiles * (tiles - 1),))],
        compiler_params=params(8),
        cost_estimate=cost(0, 4 * tiles * (tiles - 1) * rows * rows),
        name="pack_owners",
    )(place, eta, gamma)


def free_weight(occ_ref, chan, size):
    occupied = occ_ref[0] + occ_ref[1]
    own = lax.broadcasted_iota(jnp.int32, occupied.shape, 0) == chan
    free = jnp.sum(jnp.where(own, 1 - occupied, 0), axis=0, keepdims=True)
    live = lax.broadcasted_iota(jnp.int32, free.shape, 1) < size
    return jnp.where(live, free, 0).astype(F32)


def diagonal_kernel(sizes_ref, occ_ref, eta_ref, gamma_ref, out_ref):
    for c in range(eta_ref.shape[0]):
        weight = free_weight(occ_ref, c, sizes_ref[c]).astype(BF16)
        out_ref[c] = lax.dot_general(
            eta_ref[c] * weight, gamma_ref[c], NT, preferred_element_type=F32
        ) + lax.dot_general(gamma_ref[c] * weight, eta_ref[c], NT, preferred_element_type=F32)


def ladder_diagonal(sizes, pair_occupation, eta, gamma):
    chan_count, rows, states = eta.shape
    return pl.pallas_call(
        diagonal_kernel,
        out_shape=jax.ShapeDtypeStruct((chan_count, rows, rows), F32),
        in_specs=[SMEM] + [VMEM] * 3,
        out_specs=VMEM,
        compiler_params=params(8),
        cost_estimate=cost(4 * chan_count * rows * rows * states, 8 * chan_count * rows * states),
        name="ladder_diagonal",
    )(sizes, pair_occupation, eta, gamma)


def ladder_kernel(tiles, rows, place_ref, sizes_ref, occ_ref, eta_ref, gamma_ref, *rest):
    packed_refs = rest[: tiles - 1]
    out_refs = rest[tiles - 1 : 2 * tiles - 1]
    eta, gamma, weight, sems = rest[2 * tiles - 1 :]
    place = place_ref[0]
    copies = []
    for source, full in ((eta_ref, eta), (gamma_ref, gamma)):
        for k in range(tiles):
            copies.append(
                pltpu.make_async_copy(
                    source.at[place, :, aligned((place ^ k) * rows, rows)],
                    full.at[0:rows, k * rows : (k + 1) * rows],
                    sems.at[len(copies)],
                )
            )
    for copy in copies:
        copy.start()
    weight[...] = free_weight(occ_ref, place, sizes_ref[place])
    scale = jnp.concatenate(
        [weight[:, aligned((place ^ k) * rows, rows)] for k in range(tiles)], axis=1
    ).astype(BF16)
    for k in range(1, tiles):
        for n, full in enumerate((eta, gamma)):
            for m, other in enumerate(range(k, tiles)):
                block = packed_refs[k - 1][n, m]
                here, there = slice(k * rows, (k + 1) * rows), slice(other * rows, (other + 1) * rows)
                full[here, there] = block
                if other > k:
                    full[there, here] = block.T if n else -block.T
    for copy in copies:
        copy.wait()
    for other in range(1, tiles):
        here, there = slice(0, rows), slice(other * rows, (other + 1) * rows)
        eta[there, here] = -eta[here, there].T
        gamma[there, here] = gamma[here, there].T
    for k in reversed(range(tiles)):
        here = slice(k * rows, (k + 1) * rows)
        total = jnp.dot(eta[here, :] * scale, gamma[...], preferred_element_type=F32)
        total = total - jnp.dot(gamma[here, :] * scale, eta[...], preferred_element_type=F32)
        for m in range(1, tiles):
            out_refs[k][:, (m - 1) * rows : m * rows] = total[
                :, (k ^ m) * rows : ((k ^ m) + 1) * rows
            ].astype(BF16)


def ladder_blocks(place, sizes, pair_occupation, eta, gamma, packed):
    tiles, rows, states = eta.shape
    return pl.pallas_call(
        functools.partial(ladder_kernel, tiles, rows),
        out_shape=[jax.ShapeDtypeStruct((rows, states - rows), BF16)] * tiles,
        in_specs=[SMEM, SMEM, VMEM, HBM, HBM] + [VMEM] * (tiles - 1),
        out_specs=[VMEM] * tiles,
        scratch_shapes=[
            pltpu.VMEM((states, states), BF16),
            pltpu.VMEM((states, states), BF16),
            pltpu.VMEM((1, states), F32),
            pltpu.SemaphoreType.DMA((2 * tiles,)),
        ],
        compiler_params=params(12),
        cost_estimate=cost(4 * states**3, 8 * states**2),
        name="ladder",
    )(place, sizes, pair_occupation, eta, gamma, *packed)


def finish_kernel(blocks, me_ref, place_ref, sizes_ref, diagonal_ref, *rest):
    back_refs, ladder_refs = rest[:blocks], rest[blocks:-2]
    out_ref, back = rest[-2:]
    chan_count, tile_rows, states = out_ref.shape
    place = place_ref[0]
    rows = back_refs[0].shape[0]
    for d, back_ref in enumerate(back_refs):
        back[aligned((me_ref[0] ^ d) * rows, rows), :] = back_ref[...]
    row = lax.broadcasted_iota(jnp.int32, (tile_rows, tile_rows), 0)
    column = lax.broadcasted_iota(jnp.int32, (tile_rows, tile_rows), 1)
    for k, ladder_ref in enumerate(ladder_refs):
        c = place ^ k
        for m in range(len(ladder_refs)):
            ladder = ladder_ref[:, (m - 1) * tile_rows : m * tile_rows] if m else diagonal_ref[c]
            start = (place ^ m) * tile_rows
            span = aligned(start, tile_rows)
            total = ladder.astype(F32) + back[aligned(c * tile_rows, tile_rows), span].astype(F32)
            live = jnp.maximum(row + place * tile_rows, column + start) < sizes_ref[c]
            out_ref[c, :, span] = jnp.where(live, total, 0.0).astype(BF16)


def finish(me, place, sizes, shape, diagonal, back, ladder):
    chan_count, tile_rows, states = shape
    return pl.pallas_call(
        functools.partial(finish_kernel, len(back)),
        out_shape=jax.ShapeDtypeStruct(shape, BF16),
        in_specs=[SMEM] * 3 + [VMEM] * (1 + len(back) + len(ladder)),
        out_specs=VMEM,
        scratch_shapes=[pltpu.VMEM((chan_count * tile_rows, states), BF16)],
        compiler_params=params(12),
        cost_estimate=cost(0, 6 * chan_count * tile_rows * states),
        name="finish",
    )(me, place, sizes, diagonal, *back, *ladder)


def ladder_gathered(sizes, pair_occupation, eta, gamma):
    _, rows, states = eta.shape
    columns = lax.broadcasted_iota(jnp.int32, (eta.shape[0], states), 1)
    weight = (1 - pair_occupation[0] - pair_occupation[1]) * (columns < sizes[:, None])
    first = jnp.einsum(
        "crk,ckj->crj",
        eta * weight.astype(BF16)[:, None, :],
        lax.all_gather(gamma, "tile", axis=1, tiled=True),
        preferred_element_type=F32,
    )
    mirrored = lax.all_to_all(first, "tile", split_axis=2, concat_axis=1, tiled=True)
    return first + jnp.swapaxes(mirrored, 1, 2)


def per_device(
    chans,
    tiles,
    generator,
    hamiltonian,
    chan_sizes,
    pair_occupation,
    recoupled_occupation,
    recouple_map,
    recouple_weights,
):
    chan_count, tile_rows, states = generator.shape
    flat = (chan_count * tile_rows, states)
    me = jnp.reshape(lax.axis_index("chan"), (1,))
    place = jnp.reshape(lax.axis_index("tile"), (1,))
    paired = chans & (chans - 1) == 0 and tiles & (tiles - 1) == 0
    if not (paired and tiles == chan_count and chans in (tiles, 2 * tiles)):
        return per_device_whole(
            place,
            generator,
            hamiltonian,
            chan_sizes,
            pair_occupation,
            recoupled_occupation,
            recouple_map,
            recouple_weights,
        )

    def to_chan(message, d):
        return xor_permute(message, "chan", chans, d)

    def to_tile(message, k):
        return xor_permute(message, "tile", tiles, k)

    first, second = order = block_order(chans)
    near = [d for d in first if d]
    late = [d for d in range(chans) if d not in near]
    packed = dict(
        zip(near, pack_rows(me, place, chan_sizes, generator, hamiltonian, chans, near))
    )
    received = {d: to_chan(packed[d], d) for d in near}
    lacking = list(pack_owners(place, generator, hamiltonian))
    packed.update(
        zip(late, pack_rows(me, place, chan_sizes, generator, hamiltonian, chans, late))
    )
    turned, select = prepare(
        me, first + second, recouple_map, recoupled_occupation, recouple_weights
    )
    for k in range(1, tiles):
        if k > 2:
            lacking[k - 1] = after(lacking[k - 1], lacking[k - 2], select)
        lacking[k - 1] = to_tile(lacking[k - 1], k)
    received[0] = packed[0]
    for d in near:
        received[d + 1] = to_chan(after(packed[d + 1], received[d], select), d + 1)
    received[1] = to_chan(after(packed[1], lacking[0], select), 1)
    diagonal = ladder_diagonal(chan_sizes, pair_occupation, generator, hamiltonian)

    bar, left = first_half(me, first, turned, select, [received[d] for d in first])
    ladder = ladder_blocks(place, chan_sizes, pair_occupation, generator, hamiltonian, lacking)
    ladder = [to_tile(block, k) if k else block for k, block in enumerate(ladder)]

    back = {}
    sent, second_bar = cross_first(
        me, order, turned, bar, left, [received[d] for d in second], flat
    )
    back[0] = sent[0]
    for d, block in zip(first, sent):
        if d:
            back[d] = to_chan(block, d)
    sent = cross_second(me, second, turned, select, bar, second_bar, flat, chans)
    for d, block in zip(second, sent):
        back[d] = to_chan(block if d == 1 else after(block, back[d - 1]), d)
    back = [back[d] for d in range(chans)]
    return finish(me, place, chan_sizes, generator.shape, diagonal, back, ladder)


def per_device_whole(
    place,
    generator,
    hamiltonian,
    chan_sizes,
    pair_occupation,
    recoupled_occupation,
    recouple_map,
    recouple_weights,
):
    chan_count, tile_rows, states = generator.shape
    flat = (chan_count * tile_rows, states)
    alone = jnp.zeros_like(place)
    row = place * tile_rows + jnp.arange(tile_rows, dtype=jnp.int32)
    highest = jnp.maximum(row[:, None], jnp.arange(states, dtype=jnp.int32)[None, :])
    live = highest[None] < chan_sizes[:, None, None]
    pair = jnp.where(live, jnp.stack([generator, hamiltonian]), jnp.zeros((), BF16))
    received = lax.all_to_all(pair.reshape(2, *flat), "chan", 1, 1, tiled=True)
    order = ([0], [])
    turned, select = prepare(
        alone, order[0], recouple_map, recoupled_occupation, recouple_weights
    )
    bar, left = first_half(alone, order[0], turned, select, [received])
    sent, _ = cross_first(alone, order, turned, bar, left, [], flat)
    back = lax.all_to_all(sent[0], "chan", 0, 0, tiled=True).reshape(generator.shape)
    ladder = ladder_gathered(chan_sizes, pair_occupation, generator, hamiltonian)
    return jnp.where(live, ladder + back.astype(F32), 0.0).astype(BF16)


def solution(mesh):
    return jax.shard_map(
        functools.partial(per_device, mesh.shape["chan"], mesh.shape["tile"]),
        mesh=mesh,
        in_specs=(
            P("chan", "tile", None),
            P("chan", "tile", None),
            P("chan"),
            P(None, "chan", None),
            P(None, ("chan", "tile"), None),
            P(("chan", "tile"), None),
            P(("chan", "tile"), None, None),
        ),
        out_specs=P("chan", "tile", None),
        check_vma=False,
    )
```

time: 140 us -> 111 us (0.79)
  the two profiles are of different devices: /device:TPU:12 before, /device:TPU:0 now
where the time goes in v3:
time: 111 us; the launch traced here: 110 us
  waiting for transfers between devices  49.9 us (45%)
  Pallas kernels  31.4 us (28%)
  starting transfers between devices  23.5 us (21%)
  local copies, waits for them, and re-layouts  5.49 us (5%)
    ppermute x20, waiting for transfers between devices, xor_permute(): return lax.ppermute(block, axis, [(i, i ^ step) for i in range(size)])  49.9 us
    ppermute x20, starting transfers between devices, xor_permute(): return lax.ppermute(block, axis, [(i, i ^ step) for i in range(size)])  23.5 us
    pallas_call x1, Pallas kernels, prepare(): pl.pallas_call(functools.partial(prepare_kernel, ph_count, states, order)...  7.47 us
    unnamed x24, local copies, waits for them, and re-layouts  5.49 us
    pallas_call x1, Pallas kernels, ladder_blocks(): pl.pallas_call(functools.partial(ladder_kernel, tiles, rows), out_shape=[...  4.82 us
    pallas_call x1, Pallas kernels, cross_second(): pl.pallas_call(functools.partial(cross_second_kernel, states, order), out...  4.67 us
    pallas_call x1, Pallas kernels, finish(): pl.pallas_call(functools.partial(finish_kernel, len(back)), out_shape=jax...  3.21 us
    pallas_call x2, Pallas kernels, pack_rows(): pl.pallas_call(functools.partial(pack_rows_kernel, eta.shape, blocks, par...  2.9 us
  transfers between devices with their start and end apart: 20, of which 9 were waited for; matrix products, arithmetic and copies ran while one was open for 0% of the time, Pallas kernels for 24%

profile of v3, /device:TPU:0, one launch (start us, length us, event | category | flops | bytes accessed | tf_op | source)
XLA Modules:
  0.0 110.4 jit_solution(3029731487870626836)
XLA Ops:
  0.0 1.6 %copy-done = bf16[4,256,1024]{2,1,0:T(8,128)(2,1)S(1)} copy-done((bf16[4,256,1024]{2,1,0:T(8,128)(2,1)S(1)}, bf16[4,256,1024]{2,1,0:T(8,128)(2,1)}, u32[]{:S(2)}) %copy-start) | copy-done | bytes 2097176
  1.6 1.6 %copy-done.2 = bf16[4,256,1024]{2,1,0:T(8,128)(2,1)S(1)} copy-done((bf16[4,256,1024]{2,1,0:T(8,128)(2,1)S(1)}, bf16[4,256,1024]{2,1,0:T(8,128)(2,1)}, u32[]{:S(2)}) %copy-start.2) | copy-done | bytes 2097176
  3.2 1.2 %pack_owners.1 = (bf16[2,3,256,256]{3,2,1,0:T(8,128)(2,1)}, bf16[2,2,256,256]{3,2,1,0:T(8,128)(2,1)S(1)}, bf16[2,1,256,256]{3,2,1,0:T(8,128)(2,1)S(1)}) custom-call(s32[1]{0:T(128)} %bitcast.1.place_ref, bf16[4,256,1024]{2,1,0:T(8,128)(2,1)S(1)} %copy-done, bf16[4,256,1024]{2,1,0:T(8,128)(2,1)S(1)} %copy-done.2), custom_call_target="tpu_custom_call" | custom-call | bytes 3145728 | tf_op jit(solution)/shard_map/pack_owners/pallas_call | solution.py:287
  5.1 3.0 %collective-permute-start.3 = (bf16[2,3,256,256]{3,2,1,0:T(8,128)(2,1)}, bf16[2,3,256,256]{3,2,1,0:T(8,128)(2,1)S(1)}, u32[]{:S(2)}, u32[]{:S(2)}) collective-permute-start(bf16[2,3,256,256]{3,2,1,0:T(8,128)(2,1)} %get-tuple-element.50), channel_id=1, source_target_pairs={{0,1},{1,0},{2,3},{3,2},{4,5},{5,4},{6,7},{7,6},{8,9},{9,8},{10,11... | collective-permute-start | bytes 2359304 | tf_op jit(solution)/shard_map/ppermute | solution.py:27
  8.2 1.6 %copy-done.3 = bf16[4,256,1024]{2,1,0:T(8,128)(2,1)S(1)} copy-done((bf16[4,256,1024]{2,1,0:T(8,128)(2,1)S(1)}, bf16[4,256,1024]{2,1,0:T(8,128)(2,1)}, u32[]{:S(2)}) %copy-start.3) | copy-done | bytes 2097176
  9.8 1.2 %pack_rows.3 = (bf16[2,128,1024]{2,1,0:T(8,128)(2,1)S(1)}, bf16[2,128,1024]{2,1,0:T(8,128)(2,1)S(1)}, bf16[2,128,1024]{2,1,0:T(8,128)(2,1)S(1)}) custom-call(s32[1]{0:T(128)} %bitcast.me_ref, s32[1]{0:T(128)} %bitcast.1.place_ref, s32[4]{0:T(128)S(1)} %copy-done.6, bf16[4,256,1024]{2,1,0:T(8,128)(2,1)S(1)} %copy-done.1, bf16[4,256,1024]{2,1,0:T(8,128)(2,1)S(1)} %copy-done.3), custom_call_target="tpu_custom_call" | custom-call | bytes 3145728 | tf_op jit(solution)/shard_map/pack_rows/pallas_call | solution.py:250
  10.9 1.6 %collective-permute-start = (bf16[2,128,1024]{2,1,0:T(8,128)(2,1)S(1)}, bf16[2,128,1024]{2,1,0:T(8,128)(2,1)S(1)}, u32[]{:S(2)}, u32[]{:S(2)}) collective-permute-start(bf16[2,128,1024]{2,1,0:T(8,128)(2,1)S(1)} %get-tuple-element.44), channel_id=1, source_target_pairs={{0,8},{4,12},{8,0},{12,4},{16,24},{20,28},{24,16},{28,20},{1,9},{5... | collective-permute-start | bytes 1572872 | tf_op jit(solution)/shard_map/ppermute | solution.py:27
  12.5 1.5 %collective-permute-start.1 = (bf16[2,128,1024]{2,1,0:T(8,128)(2,1)S(1)}, bf16[2,128,1024]{2,1,0:T(8,128)(2,1)S(1)}, u32[]{:S(2)}, u32[]{:S(2)}) collective-permute-start(bf16[2,128,1024]{2,1,0:T(8,128)(2,1)S(1)} %get-tuple-element.45), channel_id=1, source_target_pairs={{0,16},{4,20},{8,24},{12,28},{16,0},{20,4},{24,8},{28,12},{1,17},{... | collective-permute-start | bytes 1572872 | tf_op jit(solution)/shard_map/ppermute | solution.py:27
  14.5 2.6 %collective-permute-start.15 = (bf16[2,2,256,256]{3,2,1,0:T(8,128)(2,1)S(1)}, bf16[2,2,256,256]{3,2,1,0:T(8,128)(2,1)S(1)}, u32[]{:S(2)}, u32[]{:S(2)}) collective-permute-start(bf16[2,2,256,256]{3,2,1,0:T(8,128)(2,1)S(1)} %get-tuple-element.70), channel_id=1, source_target_pairs={{0,2},{1,3},{2,0},{3,1},{4,6},{5,7},{6,4},{7,5},{8,10},{9,11},{10,... | collective-permute-start | bytes 1572872 | tf_op jit(solution)/shard_map/ppermute | solution.py:27
  17.1 7.5 %prepare.1 = (f32[1,1024,1024]{2,1,0:T(8,128)S(1)}, bf16[1,1024,1024]{2,1,0:T(8,128)(2,1)S(1)}) custom-call(s32[1]{0:T(128)} %bitcast.me_ref, s32[1,1024]{1,0:T(1,128)S(1)} %copy-done.11, s32[2,1,1024]{2,1,0:T(1,128)S(1)} %copy-done.10, f32[1,1024,1024]{2,1,0:T(8,128)S(1)} %copy-done.7), custom_call_target="tpu_custom_call" | custom-call | flops 6442450944 | bytes 14680064 | tf_op jit(solution)/shard_map/prepare/pallas_call | solution.py:79
  24.6 1.7 %pack_rows.2 = (bf16[2,128,1024]{2,1,0:T(8,128)(2,1)S(1)}, bf16[2,128,1024]{2,1,0:T(8,128)(2,1)S(1)}, bf16[2,128,1024]{2,1,0:T(8,128)(2,1)S(1)}, bf16[2,128,1024...) custom-call(s32[1]{0:T(128)} %bitcast.me_ref, s32[1]{0:T(128)} %bitcast.1.place_ref, s32[4]{0:T(128)S(1)} %copy-done.6, ...), custom_call_target="tpu_custom_call" | custom-call | bytes 5242880 | tf_op jit(solution)/shard_map/pack_rows/pallas_call | solution.py:250
  26.4 9.1 %collective-permute-done.1.rest_2_ = bf16[2,128,1024]{2,1,0:T(8,128)(2,1)S(1)} collective-permute-done((bf16[2,128,1024]{2,1,0:T(8,128)(2,1)S(1)}, bf16[2,128,1024]{2,1,0:T(8,128)(2,1)S(1)}, u32[]{:S(2)}, u32[]{:S(2)}) %collective-permute-start.1) | collective-permute-done | bytes 524320 | tf_op jit(solution)/shard_map/ppermute | solution.py:27
  35.6 2.5 %collective-permute-done.2.rest_3_ = bf16[2,128,1024]{2,1,0:T(8,128)(2,1)S(1)} collective-permute-done((bf16[2,128,1024]{2,1,0:T(8,128)(2,1)S(1)}, bf16[2,128,1024]{2,1,0:T(8,128)(2,1)S(1)}, u32[]{:S(2)}, u32[]{:S(2)}) %collective-permute-start.2) | collective-permute-done | bytes 524320 | tf_op jit(solution)/shard_map/ppermute | solution.py:27
  38.1 1.5 %collective-permute-start.4 = (bf16[2,128,1024]{2,1,0:T(8,128)(2,1)S(1)}, bf16[2,128,1024]{2,1,0:T(8,128)(2,1)S(1)}, u32[]{:S(2)}, u32[]{:S(2)}) collective-permute-start(bf16[2,128,1024]{2,1,0:T(8,128)(2,1)S(1)} %get-tuple-element.51), channel_id=1, source_target_pairs={{0,4},{4,0},{8,12},{12,8},{16,20},{20,16},{24,28},{28,24},{1,5},{5... | collective-permute-start | bytes 1572872 | tf_op jit(solution)/shard_map/ppermute | solution.py:27
  39.6 2.5 %collective-permute-start.16 = (bf16[2,1,256,256]{3,2,1,0:T(8,128)(2,1)S(1)}, bf16[2,1,256,256]{3,2,1,0:T(8,128)(2,1)S(1)}, u32[]{:S(2)}, u32[]{:S(2)}) collective-permute-start(bf16[2,1,256,256]{3,2,1,0:T(8,128)(2,1)S(1)} %copy-done.9), channel_id=1, source_target_pairs={{0,3},{1,2},{2,1},{3,0},{4,7},{5,6},{6,5},{7,4},{8,11},{9,10},{10,... | collective-permute-start | bytes 786440 | tf_op jit(solution)/shard_map/ppermute | solution.py:27
  42.1 2.4 %first_half.1 = (bf16[2,1,512,1024]{3,2,1,0:T(8,128)(2,1)S(1)}, bf16[2,1,512,1024]{3,2,1,0:T(8,128)(2,1)S(1)}) custom-call(s32[1]{0:T(128)} %bitcast.me_ref, f32[1,1024,1024]{2,1,0:T(8,128)S(1)} %get-tuple-element.41.turned_ref, bf16[1,1024,1024]{2,1,0:T(8,128)(2,1)S(1)} %get-tuple-element.42.select_ref, ...), custom_call_target="tpu_custom_call" | custom-call | flops 2147483648 | bytes 14680064 | tf_op jit(solution)/shard_map/first_half/pallas_call | solution.py:148
  44.5 2.8 %collective-permute-done.5.rest_1_ = bf16[2,128,1024]{2,1,0:T(8,128)(2,1)S(1)} collective-permute-done((bf16[2,128,1024]{2,1,0:T(8,128)(2,1)S(1)}, bf16[2,128,1024]{2,1,0:T(8,128)(2,1)S(1)}, u32[]{:S(2)}, u32[]{:S(2)}) %collective-permute-start.5) | collective-permute-done | bytes 524320 | tf_op jit(solution)/shard_map/ppermute | solution.py:27
  47.4 12.5 %collective-permute-done.6.rest_2_ = bf16[2,128,1024]{2,1,0:T(8,128)(2,1)S(1)} collective-permute-done((bf16[2,128,1024]{2,1,0:T(8,128)(2,1)S(1)}, bf16[2,128,1024]{2,1,0:T(8,128)(2,1)S(1)}, u32[]{:S(2)}, u32[]{:S(2)}) %collective-permute-start.6) | collective-permute-done | bytes 524320 | tf_op jit(solution)/shard_map/ppermute | solution.py:27
  59.9 2.8 %cross_first.1 = (bf16[128,1024]{1,0:T(8,128)(2,1)S(1)}, bf16[128,1024]{1,0:T(8,128)(2,1)S(1)}, bf16[128,1024]{1,0:T(8,128)(2,1)S(1)}, bf16[128,1024]{1,0:T(8,128)(2,1)S(1)}, bf16[2,1,512,1024]{3,2,1,0:T(8,128)(2,1)S(1)}) custom-call(s32[1]{0:T(128)} %bitcast.me_ref, f32[1,1024,1024]{2,1,0:T(8,128)S(1)} %get-tuple-element.41.turned_ref, ...), custom_call_target="tpu_custom_call" | custom-call | flops 2147483648 | bytes 14680064 | tf_op jit(solution)/shard_map/cross_first/pallas_call | solution.py:178
  62.7 1.4 %collective-permute-start.13 = (bf16[128,1024]{1,0:T(8,128)(2,1)S(1)}, bf16[128,1024]{1,0:T(8,128)(2,1)S(1)}, u32[]{:S(2)}, u32[]{:S(2)}) collective-permute-start(bf16[128,1024]{1,0:T(8,128)(2,1)S(1)} %get-tuple-element.67), channel_id=1, source_target_pairs={{0,24},{4,28},{8,16},{12,20},{16,8},{20,12},{24,0},{28,4},{1,25},{... | collective-permute-start | bytes 786440 | tf_op jit(solution)/shard_map/ppermute | solution.py:27
  64.1 4.8 %ladder.1 = (bf16[256,768]{1,0:T(8,128)(2,1)S(1)}, bf16[256,768]{1,0:T(8,128)(2,1)S(1)}, bf16[256,768]{1,0:T(8,128)(2,1)S(1)}, bf16[256,768]{1,0:T(8,128)(2,1)S(1)}) custom-call(s32[1]{0:T(128)} %bitcast.1.place_ref, s32[4]{0:T(128)S(1)} %copy-done.6, s32[2,4,1024]{2,1,0:T(4,128)S(1)} %copy-done.5, bf16[4,256,1024]{2,1,0:T(8,128)(2,1)S(1)} %copy-done.1, ...), custom_call_target="tpu_custom_call" | custom-call | flops 4294967296 | bytes 8388608 | tf_op jit(solution)/shard_map/ladder/pallas_call | solution.py:377
  69.4 2.6 %collective-permute-start.18 = (bf16[256,768]{1,0:T(8,128)(2,1)S(1)}, bf16[256,768]{1,0:T(8,128)(2,1)S(1)}, u32[]{:S(2)}, u32[]{:S(2)}) collective-permute-start(bf16[256,768]{1,0:T(8,128)(2,1)S(1)} %get-tuple-element.75), channel_id=1, source_target_pairs={{0,2},{1,3},{2,0},{3,1},{4,6},{5,7},{6,4},{7,5},{8,10},{9,11},{10,... | collective-permute-start | bytes 1179656 | tf_op jit(solution)/shard_map/ppermute | solution.py:27
  72.0 1.4 %collective-permute-start.19 = (bf16[256,768]{1,0:T(8,128)(2,1)S(1)}, bf16[256,768]{1,0:T(8,128)(2,1)S(1)}, u32[]{:S(2)}, u32[]{:S(2)}) collective-permute-start(bf16[256,768]{1,0:T(8,128)(2,1)S(1)} %get-tuple-element.76), channel_id=1, source_target_pairs={{0,3},{1,2},{2,1},{3,0},{4,7},{5,6},{6,5},{7,4},{8,11},{9,10},{10,... | collective-permute-start | bytes 1179656 | tf_op jit(solution)/shard_map/ppermute | solution.py:27
  74.2 1.3 %collective-permute-start.9 = (bf16[128,1024]{1,0:T(8,128)(2,1)S(1)}, bf16[128,1024]{1,0:T(8,128)(2,1)S(1)}, u32[]{:S(2)}, u32[]{:S(2)}) collective-permute-start(bf16[128,1024]{1,0:T(8,128)(2,1)S(1)} %get-tuple-element.61), channel_id=1, source_target_pairs={{0,8},{4,12},{8,0},{12,4},{16,24},{20,28},{24,16},{28,20},{1,9},{5... | collective-permute-start | bytes 786440 | tf_op jit(solution)/shard_map/ppermute | solution.py:27
  75.5 4.7 %cross_second.1 = (bf16[128,1024]{1,0:T(8,128)(2,1)S(1)}, bf16[128,1024]{1,0:T(8,128)(2,1)S(1)}, bf16[128,1024]{1,0:T(8,128)(2,1)S(1)}, bf16[128,1024]{1,0:T(8,128)(2,1)S(1)}) custom-call(s32[1]{0:T(128)} %bitcast.me_ref, f32[1,1024,1024]{2,1,0:T(8,128)S(1)} %get-tuple-element.41.turned_ref, bf16[1,1024,1024]{2,1,0:T(8,128)(2,1)S(1)} %get-tuple-element.42.select_ref, ...), custom_call_target="tpu_custom_call" | custom-call | flops 4294967296 | bytes 14680064 | tf_op jit(solution)/shard_map/cross_second/pallas_call | solution.py:202
  80.4 1.2 %collective-permute-done.9.rest_2_ = bf16[128,1024]{1,0:T(8,128)(2,1)S(1)} collective-permute-done((bf16[128,1024]{1,0:T(8,128)(2,1)S(1)}, bf16[128,1024]{1,0:T(8,128)(2,1)S(1)}, u32[]{:S(2)}, u32[]{:S(2)}) %collective-permute-start.9) | collective-permute-done | bytes 262176 | tf_op jit(solution)/shard_map/ppermute | solution.py:27
  81.5 1.6 %collective-permute-start.14 = (bf16[128,1024]{1,0:T(8,128)(2,1)S(1)}, bf16[128,1024]{1,0:T(8,128)(2,1)S(1)}, u32[]{:S(2)}, u32[]{:S(2)}) collective-permute-start(bf16[128,1024]{1,0:T(8,128)(2,1)S(1)} %get-tuple-element.69), channel_id=1, source_target_pairs={{0,28},{4,24},{8,20},{12,16},{16,12},{20,8},{24,4},{28,0},{1,29},{... | collective-permute-start | bytes 786440 | tf_op jit(solution)/shard_map/ppermute | solution.py:27
  83.1 4.7 %collective-permute-done.17.rest_9_ = bf16[256,768]{1,0:T(8,128)(2,1)S(1)} collective-permute-done((bf16[256,768]{1,0:T(8,128)(2,1)S(1)}, bf16[256,768]{1,0:T(8,128)(2,1)S(1)}, u32[]{:S(2)}, u32[]{:S(2)}) %collective-permute-start.17) | collective-permute-done | bytes 393248 | tf_op jit(solution)/shard_map/ppermute | solution.py:27
  88.3 10.9 %collective-permute-done.18.rest_10_ = bf16[256,768]{1,0:T(8,128)(2,1)S(1)} collective-permute-done((bf16[256,768]{1,0:T(8,128)(2,1)S(1)}, bf16[256,768]{1,0:T(8,128)(2,1)S(1)}, u32[]{:S(2)}, u32[]{:S(2)}) %collective-permute-start.18) | collective-permute-done | bytes 393248 | tf_op jit(solution)/shard_map/ppermute | solution.py:27
  99.2 1.9 %ladder_diagonal.1.diagonal_ref = f32[4,256,256]{2,1,0:T(8,128)S(1)} custom-call(s32[4]{0:T(128)S(1)} %copy-done.6, s32[2,4,1024]{2,1,0:T(4,128)S(1)} %copy-done.5, bf16[4,256,1024]{2,1,0:T(8,128)(2,1)S(1)} %copy-done.1, bf16[4,256,1024]{2,1,0:T(8,128)(2,1)S(1)} %copy-done.4), custom_call_target="tpu_custom_call" | custom-call | flops 1073741824 | bytes 8388608 | tf_op jit(solution)/shard_map/ladder_diagonal/pallas_call | solution.py:319
  101.1 6.0 %collective-permute-done.10.rest_3_ = bf16[128,1024]{1,0:T(8,128)(2,1)S(1)} collective-permute-done((bf16[128,1024]{1,0:T(8,128)(2,1)S(1)}, bf16[128,1024]{1,0:T(8,128)(2,1)S(1)}, u32[]{:S(2)}, u32[]{:S(2)}) %collective-permute-start.10) | collective-permute-done | bytes 262176 | tf_op jit(solution)/shard_map/ppermute | solution.py:27
  107.2 3.2 %finish.1 = bf16[4,256,1024]{2,1,0:T(8,128)(2,1)} custom-call(s32[1]{0:T(128)} %bitcast.me_ref, s32[1]{0:T(128)} %bitcast.1.place_ref, s32[4]{0:T(128)S(1)} %copy-done.6, f32[4,256,256]{2,1,0:T(8,128)S(1)} %ladder_diagonal.1.diagonal_ref, bf16[128,1024]{1,0:T(8,128)(2,1)S(1)} %get-tuple-element.58.rest_0_, ...), custom_call_target="tpu_custom_call" | custom-call | bytes 6291456 | tf_op jit(solution)/shard_map/finish/pallas_call | solution.py:417
  (42 shorter events, 3.4 us)
Async XLA Ops:
  0.0 1.6 %copy-start = (bf16[4,256,1024]{2,1,0:T(8,128)(2,1)S(1)}, bf16[4,256,1024]{2,1,0:T(8,128)(2,1)}, u32[]{:S(2)}) copy-start(bf16[4,256,1024]{2,1,0:T(8,128)(2,1)} %eta_ref.5) | copy-start | bytes 6291460
  1.6 1.6 %copy-start.2 = (bf16[4,256,1024]{2,1,0:T(8,128)(2,1)S(1)}, bf16[4,256,1024]{2,1,0:T(8,128)(2,1)}, u32[]{:S(2)}) copy-start(bf16[4,256,1024]{2,1,0:T(8,128)(2,1)} %gamma_ref.5) | copy-start | bytes 6291460
  3.2 5.0 %copy-start.1 = (bf16[4,256,1024]{2,1,0:T(8,128)(2,1)S(1)}, bf16[4,256,1024]{2,1,0:T(8,128)(2,1)}, u32[]{:S(2)}) copy-start(bf16[4,256,1024]{2,1,0:T(8,128)(2,1)} %eta_ref.5) | copy-start | bytes 6291460
  3.2 5.0 %copy-start.6 = (s32[4]{0:T(128)S(1)}, s32[4]{0:T(128)}, u32[]{:S(2)}) copy-start(s32[4]{0:T(128)} %sizes_ref.9) | copy-start | bytes 52
  3.2 13.9 %copy-start.11 = (s32[1,1024]{1,0:T(1,128)S(1)}, s32[1,1024]{1,0:T(1,128)}, u32[]{:S(2)}) copy-start(s32[1,1024]{1,0:T(1,128)} %map_ref.1) | copy-start | bytes 12292
  4.4 0.7 copy-start.8
  5.1 32.9 %collective-permute-start.3 = (bf16[2,3,256,256]{3,2,1,0:T(8,128)(2,1)}, bf16[2,3,256,256]{3,2,1,0:T(8,128)(2,1)S(1)}, u32[]{:S(2)}, u32[]{:S(2)}) collective-permute-start(bf16[2,3,256,256]{3,2,1,0:T(8,128)(2,1)} %get-tuple-element.50), channel_id=1, source_target_pairs={{0,1},{1,0},{2,3},{3,2},{4,5},{5,4},{6,7},{7,6},{8,9},{9,8},{10,11... | collective-permute-start | bytes 2359304 | tf_op jit(solution)/shard_map/ppermute | solution.py:27
  8.2 1.6 %copy-start.3 = (bf16[4,256,1024]{2,1,0:T(8,128)(2,1)S(1)}, bf16[4,256,1024]{2,1,0:T(8,128)(2,1)}, u32[]{:S(2)}) copy-start(bf16[4,256,1024]{2,1,0:T(8,128)(2,1)} %gamma_ref.5) | copy-start | bytes 6291460
  9.7 7.3 %copy-start.7 = (f32[1,1024,1024]{2,1,0:T(8,128)S(1)}, f32[1,1024,1024]{2,1,0:T(8,128)}, u32[]{:S(2)}) copy-start(f32[1,1024,1024]{2,1,0:T(8,128)} %weights_ref.1) | copy-start | bytes 12582916
  9.8 7.3 %copy-start.10 = (s32[2,1,1024]{2,1,0:T(1,128)S(1)}, s32[2,1,1024]{2,1,0:T(1,128)}, u32[]{:S(2)}) copy-start(s32[2,1,1024]{2,1,0:T(1,128)} %occ_ref.4) | copy-start | bytes 24580
  10.9 15.4 %collective-permute-start = (bf16[2,128,1024]{2,1,0:T(8,128)(2,1)S(1)}, bf16[2,128,1024]{2,1,0:T(8,128)(2,1)S(1)}, u32[]{:S(2)}, u32[]{:S(2)}) collective-permute-start(bf16[2,128,1024]{2,1,0:T(8,128)(2,1)S(1)} %get-tuple-element.44), channel_id=1, source_target_pairs={{0,8},{4,12},{8,0},{12,4},{16,24},{20,28},{24,16},{28,20},{1,9},{5... | collective-permute-start | bytes 1572872 | tf_op jit(solution)/shard_map/ppermute | solution.py:27
  12.5 23.1 %collective-permute-start.1 = (bf16[2,128,1024]{2,1,0:T(8,128)(2,1)S(1)}, bf16[2,128,1024]{2,1,0:T(8,128)(2,1)S(1)}, u32[]{:S(2)}, u32[]{:S(2)}) collective-permute-start(bf16[2,128,1024]{2,1,0:T(8,128)(2,1)S(1)} %get-tuple-element.45), channel_id=1, source_target_pairs={{0,16},{4,20},{8,24},{12,28},{16,0},{20,4},{24,8},{28,12},{1,17},{... | collective-permute-start | bytes 1572872 | tf_op jit(solution)/shard_map/ppermute | solution.py:27
  14.0 24.1 %collective-permute-start.2 = (bf16[2,128,1024]{2,1,0:T(8,128)(2,1)S(1)}, bf16[2,128,1024]{2,1,0:T(8,128)(2,1)S(1)}, u32[]{:S(2)}, u32[]{:S(2)}) collective-permute-start(bf16[2,128,1024]{2,1,0:T(8,128)(2,1)S(1)} %get-tuple-element.46), channel_id=1, source_target_pairs={{0,24},{4,28},{8,16},{12,20},{16,8},{20,12},{24,0},{28,4},{1,25},{... | collective-permute-start | bytes 1572872 | tf_op jit(solution)/shard_map/ppermute | solution.py:27
  14.5 10.1 %copy-start.4 = (bf16[4,256,1024]{2,1,0:T(8,128)(2,1)S(1)}, bf16[4,256,1024]{2,1,0:T(8,128)(2,1)}, u32[]{:S(2)}) copy-start(bf16[4,256,1024]{2,1,0:T(8,128)(2,1)} %gamma_ref.5) | copy-start | bytes 6291460
  14.5 25.2 %collective-permute-start.15 = (bf16[2,2,256,256]{3,2,1,0:T(8,128)(2,1)S(1)}, bf16[2,2,256,256]{3,2,1,0:T(8,128)(2,1)S(1)}, u32[]{:S(2)}, u32[]{:S(2)}) collective-permute-start(bf16[2,2,256,256]{3,2,1,0:T(8,128)(2,1)S(1)} %get-tuple-element.70), channel_id=1, source_target_pairs={{0,2},{1,3},{2,0},{3,1},{4,6},{5,7},{6,4},{7,5},{8,10},{9,11},{10,... | collective-permute-start | bytes 1572872 | tf_op jit(solution)/shard_map/ppermute | solution.py:27
  24.6 15.1 %copy-start.9 = (bf16[2,1,256,256]{3,2,1,0:T(8,128)(2,1)S(1)}, bf16[2,1,256,256]{3,2,1,0:T(8,128)(2,1)}, u32[]{:S(2)}) copy-start(bf16[2,1,256,256]{3,2,1,0:T(8,128)(2,1)} %copy-done.8) | copy-start | bytes 786436
  26.3 21.0 %collective-permute-start.5 = (bf16[2,128,1024]{2,1,0:T(8,128)(2,1)S(1)}, bf16[2,128,1024]{2,1,0:T(8,128)(2,1)S(1)}, u32[]{:S(2)}, u32[]{:S(2)}) collective-permute-start(bf16[2,128,1024]{2,1,0:T(8,128)(2,1)S(1)} %get-tuple-element.53), channel_id=1, source_target_pairs={{0,12},{4,8},{8,4},{12,0},{16,28},{20,24},{24,20},{28,16},{1,13},{... | collective-permute-start | bytes 1572872 | tf_op jit(solution)/shard_map/ppermute | solution.py:27
  35.5 24.4 %collective-permute-start.6 = (bf16[2,128,1024]{2,1,0:T(8,128)(2,1)S(1)}, bf16[2,128,1024]{2,1,0:T(8,128)(2,1)S(1)}, u32[]{:S(2)}, u32[]{:S(2)}) collective-permute-start(bf16[2,128,1024]{2,1,0:T(8,128)(2,1)S(1)} %get-tuple-element.55), channel_id=1, source_target_pairs={{0,20},{4,16},{8,28},{12,24},{16,4},{20,0},{24,12},{28,8},{1,21},{... | collective-permute-start | bytes 1572872 | tf_op jit(solution)/shard_map/ppermute | solution.py:27
  38.1 21.8 %collective-permute-start.7 = (bf16[2,128,1024]{2,1,0:T(8,128)(2,1)S(1)}, bf16[2,128,1024]{2,1,0:T(8,128)(2,1)S(1)}, u32[]{:S(2)}, u32[]{:S(2)}) collective-permute-start(bf16[2,128,1024]{2,1,0:T(8,128)(2,1)S(1)} %get-tuple-element.57), channel_id=1, source_target_pairs={{0,28},{4,24},{8,20},{12,16},{16,12},{20,8},{24,4},{28,0},{1,29},{... | collective-permute-start | bytes 1572872 | tf_op jit(solution)/shard_map/ppermute | solution.py:27
  38.1 21.8 %collective-permute-start.4 = (bf16[2,128,1024]{2,1,0:T(8,128)(2,1)S(1)}, bf16[2,128,1024]{2,1,0:T(8,128)(2,1)S(1)}, u32[]{:S(2)}, u32[]{:S(2)}) collective-permute-start(bf16[2,128,1024]{2,1,0:T(8,128)(2,1)S(1)} %get-tuple-element.51), channel_id=1, source_target_pairs={{0,4},{4,0},{8,12},{12,8},{16,20},{20,16},{24,28},{28,24},{1,5},{5... | collective-permute-start | bytes 1572872 | tf_op jit(solution)/shard_map/ppermute | solution.py:27
  39.6 24.5 %collective-permute-start.16 = (bf16[2,1,256,256]{3,2,1,0:T(8,128)(2,1)S(1)}, bf16[2,1,256,256]{3,2,1,0:T(8,128)(2,1)S(1)}, u32[]{:S(2)}, u32[]{:S(2)}) collective-permute-start(bf16[2,1,256,256]{3,2,1,0:T(8,128)(2,1)S(1)} %copy-done.9), channel_id=1, source_target_pairs={{0,3},{1,2},{2,1},{3,0},{4,7},{5,6},{6,5},{7,4},{8,11},{9,10},{10,... | collective-permute-start | bytes 786440 | tf_op jit(solution)/shard_map/ppermute | solution.py:27
  59.9 4.2 %copy-start.5 = (s32[2,4,1024]{2,1,0:T(4,128)S(1)}, s32[2,4,1024]{2,1,0:T(4,128)}, u32[]{:S(2)}) copy-start(s32[2,4,1024]{2,1,0:T(4,128)} %occ_ref.5) | copy-start | bytes 98308
  62.7 11.5 %collective-permute-start.13 = (bf16[128,1024]{1,0:T(8,128)(2,1)S(1)}, bf16[128,1024]{1,0:T(8,128)(2,1)S(1)}, u32[]{:S(2)}, u32[]{:S(2)}) collective-permute-start(bf16[128,1024]{1,0:T(8,128)(2,1)S(1)} %get-tuple-element.67), channel_id=1, source_target_pairs={{0,24},{4,28},{8,16},{12,20},{16,8},{20,12},{24,0},{28,4},{1,25},{... | collective-permute-start | bytes 786440 | tf_op jit(solution)/shard_map/ppermute | solution.py:27
  68.9 18.8 %collective-permute-start.17 = (bf16[256,768]{1,0:T(8,128)(2,1)S(1)}, bf16[256,768]{1,0:T(8,128)(2,1)S(1)}, u32[]{:S(2)}, u32[]{:S(2)}) collective-permute-start(bf16[256,768]{1,0:T(8,128)(2,1)S(1)} %get-tuple-element.74), channel_id=1, source_target_pairs={{0,1},{1,0},{2,3},{3,2},{4,5},{5,4},{6,7},{7,6},{8,9},{9,8},{10,11... | collective-permute-start | bytes 1179656 | tf_op jit(solution)/shard_map/ppermute | solution.py:27
  69.4 29.8 %collective-permute-start.18 = (bf16[256,768]{1,0:T(8,128)(2,1)S(1)}, bf16[256,768]{1,0:T(8,128)(2,1)S(1)}, u32[]{:S(2)}, u32[]{:S(2)}) collective-permute-start(bf16[256,768]{1,0:T(8,128)(2,1)S(1)} %get-tuple-element.75), channel_id=1, source_target_pairs={{0,2},{1,3},{2,0},{3,1},{4,6},{5,7},{6,4},{7,5},{8,10},{9,11},{10,... | collective-permute-start | bytes 1179656 | tf_op jit(solution)/shard_map/ppermute | solution.py:27
  72.0 29.1 %collective-permute-start.19 = (bf16[256,768]{1,0:T(8,128)(2,1)S(1)}, bf16[256,768]{1,0:T(8,128)(2,1)S(1)}, u32[]{:S(2)}, u32[]{:S(2)}) collective-permute-start(bf16[256,768]{1,0:T(8,128)(2,1)S(1)} %get-tuple-element.76), channel_id=1, source_target_pairs={{0,3},{1,2},{2,1},{3,0},{4,7},{5,6},{6,5},{7,4},{8,11},{9,10},{10,... | collective-permute-start | bytes 1179656 | tf_op jit(solution)/shard_map/ppermute | solution.py:27
  73.4 7.0 %collective-permute-start.11 = (bf16[128,1024]{1,0:T(8,128)(2,1)S(1)}, bf16[128,1024]{1,0:T(8,128)(2,1)S(1)}, u32[]{:S(2)}, u32[]{:S(2)}) collective-permute-start(bf16[128,1024]{1,0:T(8,128)(2,1)S(1)} %get-tuple-element.64), channel_id=1, source_target_pairs={{0,16},{4,20},{8,24},{12,28},{16,0},{20,4},{24,8},{28,12},{1,17},{... | collective-permute-start | bytes 786440 | tf_op jit(solution)/shard_map/ppermute | solution.py:27
  74.2 7.3 %collective-permute-start.9 = (bf16[128,1024]{1,0:T(8,128)(2,1)S(1)}, bf16[128,1024]{1,0:T(8,128)(2,1)S(1)}, u32[]{:S(2)}, u32[]{:S(2)}) collective-permute-start(bf16[128,1024]{1,0:T(8,128)(2,1)S(1)} %get-tuple-element.61), channel_id=1, source_target_pairs={{0,8},{4,12},{8,0},{12,4},{16,24},{20,28},{24,16},{28,20},{1,9},{5... | collective-permute-start | bytes 786440 | tf_op jit(solution)/shard_map/ppermute | solution.py:27
  80.4 20.8 %collective-permute-start.8 = (bf16[128,1024]{1,0:T(8,128)(2,1)S(1)}, bf16[128,1024]{1,0:T(8,128)(2,1)S(1)}, u32[]{:S(2)}, u32[]{:S(2)}) collective-permute-start(bf16[128,1024]{1,0:T(8,128)(2,1)S(1)} %get-tuple-element.60), channel_id=1, source_target_pairs={{0,4},{4,0},{8,12},{12,8},{16,20},{20,16},{24,28},{28,24},{1,5},{5... | collective-permute-start | bytes 786440 | tf_op jit(solution)/shard_map/ppermute | solution.py:27
  81.5 19.6 %collective-permute-start.14 = (bf16[128,1024]{1,0:T(8,128)(2,1)S(1)}, bf16[128,1024]{1,0:T(8,128)(2,1)S(1)}, u32[]{:S(2)}, u32[]{:S(2)}) collective-permute-start(bf16[128,1024]{1,0:T(8,128)(2,1)S(1)} %get-tuple-element.69), channel_id=1, source_target_pairs={{0,28},{4,24},{8,20},{12,16},{16,12},{20,8},{24,4},{28,0},{1,29},{... | collective-permute-start | bytes 786440 | tf_op jit(solution)/shard_map/ppermute | solution.py:27
  87.7 13.4 %collective-permute-start.12 = (bf16[128,1024]{1,0:T(8,128)(2,1)S(1)}, bf16[128,1024]{1,0:T(8,128)(2,1)S(1)}, u32[]{:S(2)}, u32[]{:S(2)}) collective-permute-start(bf16[128,1024]{1,0:T(8,128)(2,1)S(1)} %get-tuple-element.66), channel_id=1, source_target_pairs={{0,20},{4,16},{8,28},{12,24},{16,4},{20,0},{24,12},{28,8},{1,21},{... | collective-permute-start | bytes 786440 | tf_op jit(solution)/shard_map/ppermute | solution.py:27
  99.2 7.9 %collective-permute-start.10 = (bf16[128,1024]{1,0:T(8,128)(2,1)S(1)}, bf16[128,1024]{1,0:T(8,128)(2,1)S(1)}, u32[]{:S(2)}, u32[]{:S(2)}) collective-permute-start(bf16[128,1024]{1,0:T(8,128)(2,1)S(1)} %get-tuple-element.63), channel_id=1, source_target_pairs={{0,12},{4,8},{8,4},{12,0},{16,28},{20,24},{24,20},{28,16},{1,13},{... | collective-permute-start | bytes 786440 | tf_op jit(solution)/shard_map/ppermute | solution.py:27

commit v4 on v3

--- a/solution.py
+++ b/solution.py
@@ -43,6 +43,22 @@
 def block_order(blocks):
     half = list(range(0, blocks, 2))
     return half, [d for d in range(blocks) if d not in half]
+
+
+def free_weight(occ_ref, chan, size):
+    occupied = occ_ref[0] + occ_ref[1]
+    own = lax.broadcasted_iota(jnp.int32, occupied.shape, 0) == chan
+    free = jnp.sum(jnp.where(own, 1 - occupied, 0), axis=0, keepdims=True)
+    live = lax.broadcasted_iota(jnp.int32, free.shape, 1) < size
+    return jnp.where(live, free, 0).astype(F32)
+
+
+def diagonal_blocks(sizes_ref, occ_ref, eta_ref, gamma_ref, out_ref):
+    for c in range(eta_ref.shape[0]):
+        weight = free_weight(occ_ref, c, sizes_ref[c]).astype(BF16)
+        out_ref[c] = lax.dot_general(
+            eta_ref[c] * weight, gamma_ref[c], NT, preferred_element_type=F32
+        ) + lax.dot_general(gamma_ref[c] * weight, eta_ref[c], NT, preferred_element_type=F32)
 
 
 def prepare_kernel(
@@ -74,20 +90,33 @@
                 turned_ref[q, top : top + tall, start : start + height] = total
 
 
-def prepare(me, order, recouple_map, recoupled_occupation, recouple_weights):
+def prepare_whole_kernel(ph_count, states, order, *refs):
+    prepare_kernel(ph_count, states, order, *refs[:4], *refs[-3:-1])
+    diagonal_blocks(*refs[4:-3], refs[-1])
+
+
+def prepare(me, order, recouple_map, recoupled_occupation, recouple_weights, *pair):
     ph_count, states = recouple_map.shape
+    kernel, extra = prepare_kernel, ()
+    flops = 6 * ph_count * states**3
+    if pair:
+        chan_count, rows, columns = pair[-1].shape
+        kernel = prepare_whole_kernel
+        extra = (jax.ShapeDtypeStruct((chan_count, rows, rows), F32),)
+        flops += 4 * chan_count * rows * rows * columns
     return pl.pallas_call(
-        functools.partial(prepare_kernel, ph_count, states, order),
+        functools.partial(kernel, ph_count, states, order),
         out_shape=(
             jax.ShapeDtypeStruct(recouple_weights.shape, F32),
             jax.ShapeDtypeStruct(recouple_weights.shape, BF16),
+            *extra,
         ),
-        in_specs=[SMEM] + [VMEM] * 3,
-        out_specs=(VMEM, VMEM),
+        in_specs=[SMEM] + [VMEM] * 3 + [SMEM] * bool(pair) + [VMEM] * len(pair[1:]),
+        out_specs=(VMEM,) * (2 + len(extra)),
         compiler_params=params(12),
-        cost_estimate=cost(6 * ph_count * states**3, 14 * ph_count * states**2),
+        cost_estimate=cost(flops, 14 * ph_count * states**2),
         name="prepare",
-    )(me, recouple_map, recoupled_occupation, recouple_weights)
+    )(me, recouple_map, recoupled_occupation, recouple_weights, *pair)
 
 
 def weigh_blocks(states, order, me, turned_ref, recv_refs, bar_ref):
@@ -211,120 +240,60 @@
     )(me, turned, select, bar, second_bar)
 
 
-def pack_rows_kernel(shape, blocks, partners, me_ref, place_ref, sizes_ref, *rest):
+def pack_kernel(shape, blocks, tiles, partners, steps, me_ref, place_ref, sizes_ref, *rest):
     chan_count, tile_rows, states = shape
-    source_refs, out_refs = rest[:2], rest[2 : 2 + len(partners)]
-    held, sems = rest[2 + len(partners) :]
+    source_refs, block_refs = rest[:2], rest[2 : 2 + len(partners)]
+    owner_refs, (held, sems) = rest[2 + len(partners) : -2], rest[-2:]
     rows = chan_count * tile_rows // blocks
-    copies = []
+    place = place_ref[0]
+    copies, places = [], []
+
+    def fetch(source, target):
+        copies.append(pltpu.make_async_copy(source, target, sems.at[len(copies)]))
+        copies[-1].start()
+
     for slot, d in enumerate(partners):
         start = (me_ref[0] ^ d) * rows
         chan = start // tile_rows
-        inside = start - chan * tile_rows
+        places.append((chan, start - chan * tile_rows))
         for n, source_ref in enumerate(source_refs):
-            copies.append(
-                pltpu.make_async_copy(
-                    source_ref.at[chan, aligned(inside, rows), :],
-                    held.at[slot, n],
-                    sems.at[len(copies)],
-                )
-            )
-    for copy in copies:
-        copy.start()
-    row = lax.broadcasted_iota(jnp.int32, (rows, states), 0) + place_ref[0] * tile_rows
-    column = lax.broadcasted_iota(jnp.int32, (rows, states), 1)
-    for slot, d in enumerate(partners):
-        start = (me_ref[0] ^ d) * rows
-        chan = start // tile_rows
-        inside = start - chan * tile_rows
-        live = jnp.maximum(row + inside, column) < sizes_ref[chan]
+            fetch(source_ref.at[chan, aligned(places[-1][1], rows), :], held.at[slot, n])
+    for step, owner_ref in zip(steps, owner_refs):
+        owner = place ^ step
+        for n, source_ref in enumerate(source_refs):
+            for m, other in enumerate(range(step, tiles)):
+                column = aligned((owner ^ other) * tile_rows, tile_rows)
+                fetch(source_ref.at[owner, :, column], owner_ref.at[n, m])
+    row = lax.broadcasted_iota(jnp.int32, (rows, states), 0) + place * tile_rows
+    highest = jnp.maximum(row, lax.broadcasted_iota(jnp.int32, (rows, states), 1))
+    for slot, (chan, inside) in enumerate(places):
+        live = jnp.maximum(highest, row + inside) < sizes_ref[chan]
         for n in range(2):
             copies[2 * slot + n].wait()
             values = held[slot, n]
-            out_refs[slot][n] = jnp.where(live, values, jnp.zeros_like(values))
-
-
-def pack_rows(me, place, sizes, eta, gamma, blocks, partners):
-    chan_count, tile_rows, states = eta.shape
-    shape = (2, chan_count * tile_rows // blocks, states)
-    return pl.pallas_call(
-        functools.partial(pack_rows_kernel, eta.shape, blocks, partners),
-        out_shape=[jax.ShapeDtypeStruct(shape, BF16)] * len(partners),
+            block_refs[slot][n] = jnp.where(live, values, jnp.zeros_like(values))
+    for copy in copies[2 * len(partners) :]:
+        copy.wait()
+
+
+def pack(me, place, sizes, eta, gamma, blocks, tiles, partners, steps, mib):
+    chan_count, rows, states = eta.shape
+    shapes = [(2, chan_count * rows // blocks, states)] * len(partners)
+    shapes += [(2, tiles - step, rows, rows) for step in steps]
+    out = pl.pallas_call(
+        functools.partial(pack_kernel, eta.shape, blocks, tiles, partners, steps),
+        out_shape=[jax.ShapeDtypeStruct(shape, BF16) for shape in shapes],
         in_specs=[SMEM] * 3 + [HBM] * 2,
-        out_specs=[VMEM] * len(partners),
+        out_specs=[VMEM] * len(shapes),
         scratch_shapes=[
-            pltpu.VMEM((len(partners), *shape), BF16),
-            pltpu.SemaphoreType.DMA((2 * len(partners),)),
+            pltpu.VMEM((len(partners), *shapes[0]), BF16),
+            pltpu.SemaphoreType.DMA((2 * len(partners) + 2 * sum(tiles - s for s in steps),)),
         ],
-        compiler_params=params(8),
-        cost_estimate=cost(0, 8 * len(partners) * shape[1] * states),
-        name="pack_rows",
+        compiler_params=params(mib),
+        cost_estimate=cost(0, 8 * len(partners) * shapes[0][1] * states),
+        name="pack",
     )(me, place, sizes, eta, gamma)
-
-
-def pack_owners_kernel(tiles, rows, place_ref, eta_ref, gamma_ref, *rest):
-    out_refs, sems = rest[:-1], rest[-1]
-    copies = []
-    for step in range(1, tiles):
-        owner = place_ref[0] ^ step
-        for n, source_ref in enumerate((eta_ref, gamma_ref)):
-            for m, other in enumerate(range(step, tiles)):
-                copies.append(
-                    pltpu.make_async_copy(
-                        source_ref.at[owner, :, aligned((owner ^ other) * rows, rows)],
-                        out_refs[step - 1].at[n, m],
-                        sems.at[len(copies)],
-                    )
-                )
-    for copy in copies:
-        copy.start()
-    for copy in copies:
-        copy.wait()
-
-
-def pack_owners(place, eta, gamma):
-    tiles, rows, _ = eta.shape
-    return pl.pallas_call(
-        functools.partial(pack_owners_kernel, tiles, rows),
-        out_shape=[
-            jax.ShapeDtypeStruct((2, tiles - step, rows, rows), BF16) for step in range(1, tiles)
-        ],
-        in_specs=[SMEM] + [HBM] * 2,
-        out_specs=[VMEM] * (tiles - 1),
-        scratch_shapes=[pltpu.SemaphoreType.DMA((tiles * (tiles - 1),))],
-        compiler_params=params(8),
-        cost_estimate=cost(0, 4 * tiles * (tiles - 1) * rows * rows),
-        name="pack_owners",
-    )(place, eta, gamma)
-
-
-def free_weight(occ_ref, chan, size):
-    occupied = occ_ref[0] + occ_ref[1]
-    own = lax.broadcasted_iota(jnp.int32, occupied.shape, 0) == chan
-    free = jnp.sum(jnp.where(own, 1 - occupied, 0), axis=0, keepdims=True)
-    live = lax.broadcasted_iota(jnp.int32, free.shape, 1) < size
-    return jnp.where(live, free, 0).astype(F32)
-
-
-def diagonal_kernel(sizes_ref, occ_ref, eta_ref, gamma_ref, out_ref):
-    for c in range(eta_ref.shape[0]):
-        weight = free_weight(occ_ref, c, sizes_ref[c]).astype(BF16)
-        out_ref[c] = lax.dot_general(
-            eta_ref[c] * weight, gamma_ref[c], NT, preferred_element_type=F32
-        ) + lax.dot_general(gamma_ref[c] * weight, eta_ref[c], NT, preferred_element_type=F32)
-
-
-def ladder_diagonal(sizes, pair_occupation, eta, gamma):
-    chan_count, rows, states = eta.shape
-    return pl.pallas_call(
-        diagonal_kernel,
-        out_shape=jax.ShapeDtypeStruct((chan_count, rows, rows), F32),
-        in_specs=[SMEM] + [VMEM] * 3,
-        out_specs=VMEM,
-        compiler_params=params(8),
-        cost_estimate=cost(4 * chan_count * rows * rows * states, 8 * chan_count * rows * states),
-        name="ladder_diagonal",
-    )(sizes, pair_occupation, eta, gamma)
+    return dict(zip(partners, out)), dict(zip(steps, out[len(partners) :]))
 
 
 def ladder_kernel(tiles, rows, place_ref, sizes_ref, occ_ref, eta_ref, gamma_ref, *rest):
@@ -362,14 +331,16 @@
         here, there = slice(0, rows), slice(other * rows, (other + 1) * rows)
         eta[there, here] = -eta[here, there].T
         gamma[there, here] = gamma[here, there].T
-    for k in reversed(range(tiles)):
-        here = slice(k * rows, (k + 1) * rows)
-        total = jnp.dot(eta[here, :] * scale, gamma[...], preferred_element_type=F32)
-        total = total - jnp.dot(gamma[here, :] * scale, eta[...], preferred_element_type=F32)
-        for m in range(1, tiles):
-            out_refs[k][:, (m - 1) * rows : m * rows] = total[
-                :, (k ^ m) * rows : ((k ^ m) + 1) * rows
-            ].astype(BF16)
+    for k in reversed(range(tiles - 1)):
+        here, later = slice(k * rows, (k + 1) * rows), slice((k + 1) * rows, tiles * rows)
+        total = jnp.dot(eta[here, :] * scale, gamma[:, later], preferred_element_type=F32)
+        total -= jnp.dot(gamma[here, :] * scale, eta[:, later], preferred_element_type=F32)
+        total = total.astype(BF16)
+        for other in range(k + 1, tiles):
+            block = total[:, (other - k - 1) * rows : (other - k) * rows]
+            column = slice(((k ^ other) - 1) * rows, (k ^ other) * rows)
+            out_refs[k][:, column] = block
+            out_refs[other][:, column] = block.T
 
 
 def ladder_blocks(place, sizes, pair_occupation, eta, gamma, packed):
@@ -386,21 +357,22 @@
             pltpu.SemaphoreType.DMA((2 * tiles,)),
         ],
         compiler_params=params(12),
-        cost_estimate=cost(4 * states**3, 8 * states**2),
+        cost_estimate=cost(2 * states**3, 8 * states**2),
         name="ladder",
     )(place, sizes, pair_occupation, eta, gamma, *packed)
 
 
 def finish_kernel(blocks, me_ref, place_ref, sizes_ref, diagonal_ref, *rest):
-    back_refs, ladder_refs = rest[:blocks], rest[blocks:-2]
-    out_ref, back = rest[-2:]
+    back_refs, ladder_refs = rest[:blocks], rest[blocks:-4]
+    out_ref, back, held, sems = rest[-4:]
     chan_count, tile_rows, states = out_ref.shape
     place = place_ref[0]
     rows = back_refs[0].shape[0]
     for d, back_ref in enumerate(back_refs):
         back[aligned((me_ref[0] ^ d) * rows, rows), :] = back_ref[...]
-    row = lax.broadcasted_iota(jnp.int32, (tile_rows, tile_rows), 0)
+    row = lax.broadcasted_iota(jnp.int32, (tile_rows, tile_rows), 0) + place * tile_rows
     column = lax.broadcasted_iota(jnp.int32, (tile_rows, tile_rows), 1)
+    copies = []
     for k, ladder_ref in enumerate(ladder_refs):
         c = place ^ k
         for m in range(len(ladder_refs)):
@@ -408,8 +380,12 @@
             start = (place ^ m) * tile_rows
             span = aligned(start, tile_rows)
             total = ladder.astype(F32) + back[aligned(c * tile_rows, tile_rows), span].astype(F32)
-            live = jnp.maximum(row + place * tile_rows, column + start) < sizes_ref[c]
-            out_ref[c, :, span] = jnp.where(live, total, 0.0).astype(BF16)
+            live = jnp.maximum(row, column + start) < sizes_ref[c]
+            held[c, :, span] = jnp.where(live, total, 0.0).astype(BF16)
+        copies.append(pltpu.make_async_copy(held.at[c], out_ref.at[c], sems.at[k]))
+        copies[-1].start()
+    for copy in copies:
+        copy.wait()
 
 
 def finish(me, place, sizes, shape, diagonal, back, ladder):
@@ -418,8 +394,12 @@
         functools.partial(finish_kernel, len(back)),
         out_shape=jax.ShapeDtypeStruct(shape, BF16),
         in_specs=[SMEM] * 3 + [VMEM] * (1 + len(back) + len(ladder)),
-        out_specs=VMEM,
-        scratch_shapes=[pltpu.VMEM((chan_count * tile_rows, states), BF16)],
+        out_specs=HBM,
+        scratch_shapes=[
+            pltpu.VMEM((chan_count * tile_rows, states), BF16),
+            pltpu.VMEM(shape, BF16),
+            pltpu.SemaphoreType.DMA((len(ladder),)),
+        ],
         compiler_params=params(12),
         cost_estimate=cost(0, 6 * chan_count * tile_rows * states),
         name="finish",
@@ -475,32 +455,43 @@
         return xor_permute(message, "tile", tiles, k)
 
     first, second = order = block_order(chans)
-    near = [d for d in first if d]
+    near = [1] + [d for d in first if d]
     late = [d for d in range(chans) if d not in near]
-    packed = dict(
-        zip(near, pack_rows(me, place, chan_sizes, generator, hamiltonian, chans, near))
+    pair = (generator, hamiltonian)
+    steps = list(range(1, tiles))
+    packed, lacking = pack(me, place, chan_sizes, *pair, chans, tiles, near, steps[1:2], 50)
+    for kept, rest in zip(
+        (packed, lacking),
+        pack(me, place, chan_sizes, *pair, chans, tiles, late, steps[:1] + steps[2:], 12),
+    ):
+        kept.update(rest)
+    turned, select, diagonal = prepare(
+        me,
+        first + second,
+        recouple_map,
+        recoupled_occupation,
+        recouple_weights,
+        chan_sizes,
+        pair_occupation,
+        generator,
+        hamiltonian,
     )
-    received = {d: to_chan(packed[d], d) for d in near}
-    lacking = list(pack_owners(place, generator, hamiltonian))
-    packed.update(
-        zip(late, pack_rows(me, place, chan_sizes, generator, hamiltonian, chans, late))
-    )
-    turned, select = prepare(
-        me, first + second, recouple_map, recoupled_occupation, recouple_weights
-    )
-    for k in range(1, tiles):
-        if k > 2:
-            lacking[k - 1] = after(lacking[k - 1], lacking[k - 2], select)
-        lacking[k - 1] = to_tile(lacking[k - 1], k)
-    received[0] = packed[0]
-    for d in near:
+
+    received = {0: packed[0], 1: to_chan(packed[1], 1)}
+    for d in first[1:]:
+        received[d] = to_chan(packed[d], d)
         received[d + 1] = to_chan(after(packed[d + 1], received[d], select), d + 1)
-    received[1] = to_chan(after(packed[1], lacking[0], select), 1)
-    diagonal = ladder_diagonal(chan_sizes, pair_occupation, generator, hamiltonian)
+    lacking[1] = after(lacking[1], received[1])
+    for k in steps:
+        lacking[k] = to_tile(after(lacking[k], lacking[k - 1], select) if k > 2 else lacking[k], k)
 
     bar, left = first_half(me, first, turned, select, [received[d] for d in first])
-    ladder = ladder_blocks(place, chan_sizes, pair_occupation, generator, hamiltonian, lacking)
-    ladder = [to_tile(block, k) if k else block for k, block in enumerate(ladder)]
+    ladder = ladder_blocks(place, chan_sizes, pair_occupation, generator, hamiltonian, [lacking[k] for k in steps])
+    left = after(left, ladder[0])
+    ladder = list(ladder)
+    ladder[1] = to_tile(ladder[1], 1)
+    for k in range(2, tiles):
+        ladder[k] = to_tile(after(ladder[k], ladder[1]) if k == 2 else ladder[k], k)
 
     back = {}
     sent, second_bar = cross_first(
@@ -512,7 +503,10 @@
             back[d] = to_chan(block, d)
     sent = cross_second(me, second, turned, select, bar, second_bar, flat, chans)
     for d, block in zip(second, sent):
-        back[d] = to_chan(block if d == 1 else after(block, back[d - 1]), d)
+        waits = [ladder[-1]] if d == 1 else [back[d - 1]]
+        if d == chans - 1:
+            waits.append(back[1])
+        back[d] = to_chan(after(block, *waits), d)
     back = [back[d] for d in range(chans)]
     return finish(me, place, chan_sizes, generator.shape, diagonal, back, ladder)
 

time: 111 us -> 96.5 us (0.87)
  waiting for transfers between devices: 49.9 us -> 35.8 us
  starting transfers between devices: 23.5 us -> 29.6 us
  local copies, waits for them, and re-layouts: 5.49 us -> 1.43 us
  Pallas kernels: 31.4 us -> 29.2 us
    ppermute x20, waiting for transfers between devices: 49.9 us -> 35.8 us  [xor_permute(): return lax.ppermute(block, axis, [(i, i ^ step) for i in range(size)])]
    ppermute x20, starting transfers between devices: 23.5 us -> 29.6 us  [xor_permute(): return lax.ppermute(block, axis, [(i, i ^ step) for i in range(size)])]
    unnamed x24 -> x16, local copies, waits for them, and re-layouts: 5.49 us -> 1.43 us
    pallas_call x1, Pallas kernels: 4.82 us -> 3.25 us  [ladder_blocks(): pl.pallas_call(functools.partial(ladder_kernel, tiles, rows), out_shape=[...]
    pallas_call x5 -> x3, Pallas kernels: 13.5 us -> 13.4 us  [the longest x1 9.21 us: prepare(): pl.pallas_call(functools.partial(kernel, ph_count, states, order), out_sh...]
  transfers between devices with their start and end apart: 20 -> 20, of which waited for: 9 -> 8; matrix products, arithmetic and copies ran while one was open for 0% -> 0% of each run, Pallas kernels for 24% -> 25%
where the time goes in v4:
time: 96.5 us; the launch traced here: 96.3 us
  waiting for transfers between devices  35.8 us (37%)
  starting transfers between devices  29.6 us (31%)
  Pallas kernels  29.2 us (30%)
  local copies, waits for them, and re-layouts  1.43 us (1%)
    ppermute x20, waiting for transfers between devices, xor_permute(): return lax.ppermute(block, axis, [(i, i ^ step) for i in range(size)])  35.8 us
    ppermute x20, starting transfers between devices, xor_permute(): return lax.ppermute(block, axis, [(i, i ^ step) for i in range(size)])  29.6 us
    pallas_call x1, Pallas kernels, prepare(): pl.pallas_call(functools.partial(kernel, ph_count, states, order), out_sh...  9.21 us
    pallas_call x1, Pallas kernels, cross_second(): pl.pallas_call(functools.partial(cross_second_kernel, states, order), out...  4.67 us
    pallas_call x2, Pallas kernels, pack(): pl.pallas_call(functools.partial(pack_kernel, eta.shape, blocks, tiles, p...  4.19 us
    pallas_call x1, Pallas kernels, ladder_blocks(): pl.pallas_call(functools.partial(ladder_kernel, tiles, rows), out_shape=[...  3.25 us
    pallas_call x1, Pallas kernels, cross_first(): pl.pallas_call(functools.partial(cross_first_kernel, states, order), out_...  2.72 us
    pallas_call x1, Pallas kernels, finish(): pl.pallas_call(functools.partial(finish_kernel, len(back)), out_shape=jax...  2.71 us
  transfers between devices with their start and end apart: 20, of which 8 were waited for; matrix products, arithmetic and copies ran while one was open for 0% of the time, Pallas kernels for 25%

profile of v4, /device:TPU:0, one launch (start us, length us, event | category | flops | bytes accessed | tf_op | source)
XLA Modules:
  0.0 96.3 jit_solution(14045142138603075385)
XLA Ops:
  0.0 0.7 copy-done.2
  0.7 2.6 %pack.3 = (bf16[2,128,1024]{2,1,0:T(8,128)(2,1)S(1)}, bf16[2,128,1024]{2,1,0:T(8,128)(2,1)S(1)}, bf16[2,128,1024]{2,1,0:T(8,128)(2,1)S(1)}, bf16[2,128,1024]{2,1...) custom-call(s32[1]{0:T(128)} %bitcast.refs_0_.me_ref, s32[1]{0:T(128)} %bitcast.1.place_ref, s32[4]{0:T(128)S(1)} %copy-done.2, ...), custom_call_target="tpu_custom_call" | custom-call | bytes 4194304 | tf_op jit(solution)/shard_map/pack/pallas_call | solution.py:283
  3.8 2.6 %collective-permute-start = (bf16[2,128,1024]{2,1,0:T(8,128)(2,1)S(1)}, bf16[2,128,1024]{2,1,0:T(8,128)(2,1)S(1)}, u32[]{:S(2)}, u32[]{:S(2)}) collective-permute-start(bf16[2,128,1024]{2,1,0:T(8,128)(2,1)S(1)} %get-tuple-element.49), channel_id=1, source_target_pairs={{0,8},{4,12},{8,0},{12,4},{16,24},{20,28},{24,16},{28,20},{1,9},{5... | collective-permute-start | bytes 1572872 | tf_op jit(solution)/shard_map/ppermute | solution.py:27
  6.3 1.5 %collective-permute-start.1 = (bf16[2,128,1024]{2,1,0:T(8,128)(2,1)S(1)}, bf16[2,128,1024]{2,1,0:T(8,128)(2,1)S(1)}, u32[]{:S(2)}, u32[]{:S(2)}) collective-permute-start(bf16[2,128,1024]{2,1,0:T(8,128)(2,1)S(1)} %get-tuple-element.50), channel_id=1, source_target_pairs={{0,16},{4,20},{8,24},{12,28},{16,0},{20,4},{24,8},{28,12},{1,17},{... | collective-permute-start | bytes 1572872 | tf_op jit(solution)/shard_map/ppermute | solution.py:27
  7.9 3.0 %collective-permute-start.5 = (bf16[2,2,256,256]{3,2,1,0:T(8,128)(2,1)S(1)}, bf16[2,2,256,256]{3,2,1,0:T(8,128)(2,1)S(1)}, u32[]{:S(2)}, u32[]{:S(2)}) collective-permute-start(bf16[2,2,256,256]{3,2,1,0:T(8,128)(2,1)S(1)} %get-tuple-element.57), channel_id=1, source_target_pairs={{0,2},{1,3},{2,0},{3,1},{4,6},{5,7},{6,4},{7,5},{8,10},{9,11},{10,... | collective-permute-start | bytes 1572872 | tf_op jit(solution)/shard_map/ppermute | solution.py:27
  10.9 1.6 %pack.2 = (bf16[2,128,1024]{2,1,0:T(8,128)(2,1)S(1)}, bf16[2,128,1024]{2,1,0:T(8,128)(2,1)S(1)}, bf16[2,128,1024]{2,1,0:T(8,128)(2,1)S(1)}, bf16[2,128,1024]{2,1...) custom-call(s32[1]{0:T(128)} %bitcast.refs_0_.me_ref, ...), custom_call_target="tpu_custom_call" | custom-call | bytes 4194304 | tf_op jit(solution)/shard_map/pack/pallas_call | solution.py:283
  12.6 1.6 %collective-permute-start.4 = (bf16[2,3,256,256]{3,2,1,0:T(8,128)(2,1)S(1)}, bf16[2,3,256,256]{3,2,1,0:T(8,128)(2,1)S(1)}, u32[]{:S(2)}, u32[]{:S(2)}) collective-permute-start(bf16[2,3,256,256]{3,2,1,0:T(8,128)(2,1)S(1)} %get-tuple-element.56), channel_id=1, source_target_pairs={{0,1},{1,0},{2,3},{3,2},{4,5},{5,4},{6,7},{7,6},{8,9},{9,8},{10,11... | collective-permute-start | bytes 2359304 | tf_op jit(solution)/shard_map/ppermute | solution.py:27
  14.2 0.8 copy-done.4
  15.0 9.2 %prepare.1 = (f32[1,1024,1024]{2,1,0:T(8,128)S(1)}, bf16[1,1024,1024]{2,1,0:T(8,128)(2,1)S(1)}, f32[4,256,256]{2,1,0:T(8,128)S(1)}) custom-call(s32[1]{0:T(128)} %bitcast.refs_0_.me_ref, s32[1,1024]{1,0:T(1,128)S(1)} %copy-done.7, s32[2,1,1024]{2,1,0:T(1,128)S(1)} %copy-done.6, f32[1,1024,1024]{2,1,0:T(8,128)S(1)} %copy-done.3, s32[4]{0:T(128)S(1)} %copy-done.2, ...), custom_call_target="tpu_custom_call" | custom-call | flops 7516192768 | bytes 14680064 | tf_op jit(solution)/shard_map/prepare/pallas_call | solution.py:107
  24.2 7.2 %collective-permute-done.2.rest_3_ = bf16[2,128,1024]{2,1,0:T(8,128)(2,1)S(1)} collective-permute-done((bf16[2,128,1024]{2,1,0:T(8,128)(2,1)S(1)}, bf16[2,128,1024]{2,1,0:T(8,128)(2,1)S(1)}, u32[]{:S(2)}, u32[]{:S(2)}) %collective-permute-start.2) | collective-permute-done | bytes 524320 | tf_op jit(solution)/shard_map/ppermute | solution.py:27
  32.1 1.3 %collective-permute-start.8 = (bf16[2,128,1024]{2,1,0:T(8,128)(2,1)S(1)}, bf16[2,128,1024]{2,1,0:T(8,128)(2,1)S(1)}, u32[]{:S(2)}, u32[]{:S(2)}) collective-permute-start(bf16[2,128,1024]{2,1,0:T(8,128)(2,1)S(1)} %get-tuple-element.65), channel_id=1, source_target_pairs={{0,20},{4,16},{8,28},{12,24},{16,4},{20,0},{24,12},{28,8},{1,21},{... | collective-permute-start | bytes 1572872 | tf_op jit(solution)/shard_map/ppermute | solution.py:27
  33.3 0.9 collective-permute-start.9
  34.3 3.6 %collective-permute-start.6 = (bf16[2,1,256,256]{3,2,1,0:T(8,128)(2,1)S(1)}, bf16[2,1,256,256]{3,2,1,0:T(8,128)(2,1)S(1)}, u32[]{:S(2)}, u32[]{:S(2)}) collective-permute-start(bf16[2,1,256,256]{3,2,1,0:T(8,128)(2,1)S(1)} %get-tuple-element.59), channel_id=1, source_target_pairs={{0,3},{1,2},{2,1},{3,0},{4,7},{5,6},{6,5},{7,4},{8,11},{9,10},{10,... | collective-permute-start | bytes 786440 | tf_op jit(solution)/shard_map/ppermute | solution.py:27
  37.9 2.4 %first_half.1 = (bf16[2,1,512,1024]{3,2,1,0:T(8,128)(2,1)S(1)}, bf16[2,1,512,1024]{3,2,1,0:T(8,128)(2,1)S(1)}) custom-call(s32[1]{0:T(128)} %bitcast.refs_0_.me_ref, f32[1,1024,1024]{2,1,0:T(8,128)S(1)} %get-tuple-element.46.turned_ref, bf16[1,1024,1024]{2,1,0:T(8,128)(2,1)S(1)} %get-tuple-element.47.select_ref, ...), custom_call_target="tpu_custom_call" | custom-call | flops 2147483648 | bytes 14680064 | tf_op jit(solution)/shard_map/first_half/pallas_call | solution.py:177
  40.3 6.1 %collective-permute-done.6.rest_2_ = bf16[2,1,256,256]{3,2,1,0:T(8,128)(2,1)S(1)} collective-permute-done((bf16[2,1,256,256]{3,2,1,0:T(8,128)(2,1)S(1)}, bf16[2,1,256,256]{3,2,1,0:T(8,128)(2,1)S(1)}, u32[]{:S(2)}, u32[]{:S(2)}) %collective-permute-start.6) | collective-permute-done | bytes 262176 | tf_op jit(solution)/shard_map/ppermute | solution.py:27
  46.4 0.7 collective-permute-done.4.rest_0_
  47.1 3.2 %ladder.1 = (bf16[256,768]{1,0:T(8,128)(2,1)S(1)}, bf16[256,768]{1,0:T(8,128)(2,1)S(1)}, bf16[256,768]{1,0:T(8,128)(2,1)S(1)}, bf16[256,768]{1,0:T(8,128)(2,1)S(1)}) custom-call(s32[1]{0:T(128)} %bitcast.1.place_ref, s32[4]{0:T(128)S(1)} %copy-done.2, s32[2,4,1024]{2,1,0:T(4,128)S(1)} %copy-done.5, bf16[4,256,1024]{2,1,0:T(8,128)(2,1)S(1)} %copy-done, ...), custom_call_target="tpu_custom_call" | custom-call | flops 2147483648 | bytes 8388608 | tf_op jit(solution)/shard_map/ladder/pallas_call | solution.py:348
  50.3 2.5 %collective-permute-start.10 = (bf16[256,768]{1,0:T(8,128)(2,1)S(1)}, bf16[256,768]{1,0:T(8,128)(2,1)S(1)}, u32[]{:S(2)}, u32[]{:S(2)}) collective-permute-start(bf16[256,768]{1,0:T(8,128)(2,1)S(1)} %get-tuple-element.71), channel_id=1, source_target_pairs={{0,3},{1,2},{2,1},{3,0},{4,7},{5,6},{6,5},{7,4},{8,11},{9,10},{10,... | collective-permute-start | bytes 1179656 | tf_op jit(solution)/shard_map/ppermute | solution.py:27
  52.8 2.4 %collective-permute-start.18 = (bf16[256,768]{1,0:T(8,128)(2,1)S(1)}, bf16[256,768]{1,0:T(8,128)(2,1)S(1)}, u32[]{:S(2)}, u32[]{:S(2)}) collective-permute-start(bf16[256,768]{1,0:T(8,128)(2,1)S(1)} %get-tuple-element.82), channel_id=1, source_target_pairs={{0,1},{1,0},{2,3},{3,2},{4,5},{5,4},{6,7},{7,6},{8,9},{9,8},{10,11... | collective-permute-start | bytes 1179656 | tf_op jit(solution)/shard_map/ppermute | solution.py:27
  55.2 2.3 %collective-permute-done.9.rest_3_ = bf16[2,128,1024]{2,1,0:T(8,128)(2,1)S(1)} collective-permute-done((bf16[2,128,1024]{2,1,0:T(8,128)(2,1)S(1)}, bf16[2,128,1024]{2,1,0:T(8,128)(2,1)S(1)}, u32[]{:S(2)}, u32[]{:S(2)}) %collective-permute-start.9) | collective-permute-done | bytes 524320 | tf_op jit(solution)/shard_map/ppermute | solution.py:27
  57.5 2.7 %cross_first.1 = (bf16[128,1024]{1,0:T(8,128)(2,1)S(1)}, bf16[128,1024]{1,0:T(8,128)(2,1)S(1)}, bf16[128,1024]{1,0:T(8,128)(2,1)S(1)}, bf16[128,1024]{1,0:T(8,128)(2,1)S(1)}, bf16[2,1,512,1024]{3,2,1,0:T(8,128)(2,1)S(1)}) custom-call(s32[1]{0:T(128)} %bitcast.refs_0_.me_ref, f32[1,1024,1024]{2,1,0:T(8,128)S(1)} %get-tuple-element.46.turned_ref, ...), custom_call_target="tpu_custom_call" | custom-call | flops 2147483648 | bytes 14680064 | tf_op jit(solution)/shard_map/cross_first/pallas_call | solution.py:207
  60.3 1.0 %collective-permute-start.12 = (bf16[128,1024]{1,0:T(8,128)(2,1)S(1)}, bf16[128,1024]{1,0:T(8,128)(2,1)S(1)}, u32[]{:S(2)}, u32[]{:S(2)}) collective-permute-start(bf16[128,1024]{1,0:T(8,128)(2,1)S(1)} %get-tuple-element.73), channel_id=1, source_target_pairs={{0,8},{4,12},{8,0},{12,4},{16,24},{20,28},{24,16},{28,20},{1,9},{5... | collective-permute-start | bytes 786440 | tf_op jit(solution)/shard_map/ppermute | solution.py:27
  61.3 4.7 %cross_second.1 = (bf16[128,1024]{1,0:T(8,128)(2,1)S(1)}, bf16[128,1024]{1,0:T(8,128)(2,1)S(1)}, bf16[128,1024]{1,0:T(8,128)(2,1)S(1)}, bf16[128,1024]{1,0:T(8,128)(2,1)S(1)}) custom-call(s32[1]{0:T(128)} %bitcast.refs_0_.me_ref, f32[1,1024,1024]{2,1,0:T(8,128)S(1)} %get-tuple-element.46.turned_ref, bf16[1,1024,1024]{2,1,0:T(8,128)(2,1)S(1)} %get-tuple-element.47.select_ref, ...), custom_call_target="tpu_custom_call" | custom-call | flops 4294967296 | bytes 14680064 | tf_op jit(solution)/shard_map/cross_second/pallas_call | solution.py:231
  66.0 1.1 %collective-permute-start.14 = (bf16[128,1024]{1,0:T(8,128)(2,1)S(1)}, bf16[128,1024]{1,0:T(8,128)(2,1)S(1)}, u32[]{:S(2)}, u32[]{:S(2)}) collective-permute-start(bf16[128,1024]{1,0:T(8,128)(2,1)S(1)} %get-tuple-element.76), channel_id=1, source_target_pairs={{0,16},{4,20},{8,24},{12,28},{16,0},{20,4},{24,8},{28,12},{1,17},{... | collective-permute-start | bytes 786440 | tf_op jit(solution)/shard_map/ppermute | solution.py:27
  67.1 1.4 %collective-permute-start.16 = (bf16[128,1024]{1,0:T(8,128)(2,1)S(1)}, bf16[128,1024]{1,0:T(8,128)(2,1)S(1)}, u32[]{:S(2)}, u32[]{:S(2)}) collective-permute-start(bf16[128,1024]{1,0:T(8,128)(2,1)S(1)} %get-tuple-element.79), channel_id=1, source_target_pairs={{0,24},{4,28},{8,16},{12,20},{16,8},{20,12},{24,0},{28,4},{1,25},{... | collective-permute-start | bytes 786440 | tf_op jit(solution)/shard_map/ppermute | solution.py:27
  68.6 1.2 %collective-permute-done.18.rest_9_ = bf16[256,768]{1,0:T(8,128)(2,1)S(1)} collective-permute-done((bf16[256,768]{1,0:T(8,128)(2,1)S(1)}, bf16[256,768]{1,0:T(8,128)(2,1)S(1)}, u32[]{:S(2)}, u32[]{:S(2)}) %collective-permute-start.18) | collective-permute-done | bytes 393248 | tf_op jit(solution)/shard_map/ppermute | solution.py:27
  69.8 2.6 %collective-permute-start.19 = (bf16[256,768]{1,0:T(8,128)(2,1)S(1)}, bf16[256,768]{1,0:T(8,128)(2,1)S(1)}, u32[]{:S(2)}, u32[]{:S(2)}) collective-permute-start(bf16[256,768]{1,0:T(8,128)(2,1)S(1)} %get-tuple-element.84), channel_id=1, source_target_pairs={{0,2},{1,3},{2,0},{3,1},{4,6},{5,7},{6,4},{7,5},{8,10},{9,11},{10,... | collective-permute-start | bytes 1179656 | tf_op jit(solution)/shard_map/ppermute | solution.py:27
  72.3 1.2 %collective-permute-start.13 = (bf16[128,1024]{1,0:T(8,128)(2,1)S(1)}, bf16[128,1024]{1,0:T(8,128)(2,1)S(1)}, u32[]{:S(2)}, u32[]{:S(2)}) collective-permute-start(bf16[128,1024]{1,0:T(8,128)(2,1)S(1)} %get-tuple-element.75), channel_id=1, source_target_pairs={{0,12},{4,8},{8,4},{12,0},{16,28},{20,24},{24,20},{28,16},{1,13},{... | collective-permute-start | bytes 786440 | tf_op jit(solution)/shard_map/ppermute | solution.py:27
  73.5 6.2 %collective-permute-done.14.rest_4_ = bf16[128,1024]{1,0:T(8,128)(2,1)S(1)} collective-permute-done((bf16[128,1024]{1,0:T(8,128)(2,1)S(1)}, bf16[128,1024]{1,0:T(8,128)(2,1)S(1)}, u32[]{:S(2)}, u32[]{:S(2)}) %collective-permute-start.14) | collective-permute-done | bytes 262176 | tf_op jit(solution)/shard_map/ppermute | solution.py:27
  79.7 1.8 %collective-permute-start.17 = (bf16[128,1024]{1,0:T(8,128)(2,1)S(1)}, bf16[128,1024]{1,0:T(8,128)(2,1)S(1)}, u32[]{:S(2)}, u32[]{:S(2)}) collective-permute-start(bf16[128,1024]{1,0:T(8,128)(2,1)S(1)} %get-tuple-element.81), channel_id=1, source_target_pairs={{0,28},{4,24},{8,20},{12,16},{16,12},{20,8},{24,4},{28,0},{1,29},{... | collective-permute-start | bytes 786440 | tf_op jit(solution)/shard_map/ppermute | solution.py:27
  81.5 11.9 %collective-permute-done.15.rest_5_ = bf16[128,1024]{1,0:T(8,128)(2,1)S(1)} collective-permute-done((bf16[128,1024]{1,0:T(8,128)(2,1)S(1)}, bf16[128,1024]{1,0:T(8,128)(2,1)S(1)}, u32[]{:S(2)}, u32[]{:S(2)}) %collective-permute-start.15) | collective-permute-done | bytes 262176 | tf_op jit(solution)/shard_map/ppermute | solution.py:27
  93.4 2.7 %finish.1 = bf16[4,256,1024]{2,1,0:T(8,128)(2,1)} custom-call(s32[1]{0:T(128)} %bitcast.refs_0_.me_ref, s32[1]{0:T(128)} %bitcast.1.place_ref, s32[4]{0:T(128)S(1)} %copy-done.2, f32[4,256,256]{2,1,0:T(8,128)S(1)} %get-tuple-element.45.diagonal_ref, bf16[128,1024]{1,0:T(8,128)(2,1)S(1)} %get-tuple-element.68.rest_0_, ...), custom_call_target="tpu_custom_call" | custom-call | bytes 6291456 | tf_op jit(solution)/shard_map/finish/pallas_call | solution.py:393
  (32 shorter events, 1.3 us)
Async XLA Ops:
  0.0 0.7 copy-start.2
  0.7 10.3 %copy-start = (bf16[4,256,1024]{2,1,0:T(8,128)(2,1)S(1)}, bf16[4,256,1024]{2,1,0:T(8,128)(2,1)}, u32[]{:S(2)}) copy-start(bf16[4,256,1024]{2,1,0:T(8,128)(2,1)} %eta_ref.1) | copy-start | bytes 6291460
  0.7 10.3 %copy-start.1 = (bf16[4,256,1024]{2,1,0:T(8,128)(2,1)S(1)}, bf16[4,256,1024]{2,1,0:T(8,128)(2,1)}, u32[]{:S(2)}) copy-start(bf16[4,256,1024]{2,1,0:T(8,128)(2,1)} %gamma_ref.1) | copy-start | bytes 6291460
  0.7 13.5 %copy-start.6 = (s32[2,1,1024]{2,1,0:T(1,128)S(1)}, s32[2,1,1024]{2,1,0:T(1,128)}, u32[]{:S(2)}) copy-start(s32[2,1,1024]{2,1,0:T(1,128)} %refs_2_.1) | copy-start | bytes 24580
  3.3 9.3 %collective-permute-start.3 = (bf16[2,128,1024]{2,1,0:T(8,128)(2,1)S(1)}, bf16[2,128,1024]{2,1,0:T(8,128)(2,1)S(1)}, u32[]{:S(2)}, u32[]{:S(2)}) collective-permute-start(bf16[2,128,1024]{2,1,0:T(8,128)(2,1)S(1)} %get-tuple-element.55), channel_id=1, source_target_pairs={{0,4},{4,0},{8,12},{12,8},{16,20},{20,16},{24,28},{28,24},{1,5},{5... | collective-permute-start | bytes 1572872 | tf_op jit(solution)/shard_map/ppermute | solution.py:27
  3.8 27.8 %collective-permute-start = (bf16[2,128,1024]{2,1,0:T(8,128)(2,1)S(1)}, bf16[2,128,1024]{2,1,0:T(8,128)(2,1)S(1)}, u32[]{:S(2)}, u32[]{:S(2)}) collective-permute-start(bf16[2,128,1024]{2,1,0:T(8,128)(2,1)S(1)} %get-tuple-element.49), channel_id=1, source_target_pairs={{0,8},{4,12},{8,0},{12,4},{16,24},{20,28},{24,16},{28,20},{1,9},{5... | collective-permute-start | bytes 1572872 | tf_op jit(solution)/shard_map/ppermute | solution.py:27
  6.3 25.2 %collective-permute-start.1 = (bf16[2,128,1024]{2,1,0:T(8,128)(2,1)S(1)}, bf16[2,128,1024]{2,1,0:T(8,128)(2,1)S(1)}, u32[]{:S(2)}, u32[]{:S(2)}) collective-permute-start(bf16[2,128,1024]{2,1,0:T(8,128)(2,1)S(1)} %get-tuple-element.50), channel_id=1, source_target_pairs={{0,16},{4,20},{8,24},{12,28},{16,0},{20,4},{24,8},{28,12},{1,17},{... | collective-permute-start | bytes 1572872 | tf_op jit(solution)/shard_map/ppermute | solution.py:27
  7.9 23.6 %collective-permute-start.2 = (bf16[2,128,1024]{2,1,0:T(8,128)(2,1)S(1)}, bf16[2,128,1024]{2,1,0:T(8,128)(2,1)S(1)}, u32[]{:S(2)}, u32[]{:S(2)}) collective-permute-start(bf16[2,128,1024]{2,1,0:T(8,128)(2,1)S(1)} %get-tuple-element.51), channel_id=1, source_target_pairs={{0,24},{4,28},{8,16},{12,20},{16,8},{20,12},{24,0},{28,4},{1,25},{... | collective-permute-start | bytes 1572872 | tf_op jit(solution)/shard_map/ppermute | solution.py:27
  7.9 6.3 %copy-start.7 = (s32[1,1024]{1,0:T(1,128)S(1)}, s32[1,1024]{1,0:T(1,128)}, u32[]{:S(2)}) copy-start(s32[1,1024]{1,0:T(1,128)} %refs_1_.1) | copy-start | bytes 12292
  7.9 6.3 %copy-start.3 = (f32[1,1024,1024]{2,1,0:T(8,128)S(1)}, f32[1,1024,1024]{2,1,0:T(8,128)}, u32[]{:S(2)}) copy-start(f32[1,1024,1024]{2,1,0:T(8,128)} %refs_3_.1) | copy-start | bytes 12582916
  7.9 26.4 %collective-permute-start.5 = (bf16[2,2,256,256]{3,2,1,0:T(8,128)(2,1)S(1)}, bf16[2,2,256,256]{3,2,1,0:T(8,128)(2,1)S(1)}, u32[]{:S(2)}, u32[]{:S(2)}) collective-permute-start(bf16[2,2,256,256]{3,2,1,0:T(8,128)(2,1)S(1)} %get-tuple-element.57), channel_id=1, source_target_pairs={{0,2},{1,3},{2,0},{3,1},{4,6},{5,7},{6,4},{7,5},{8,10},{9,11},{10,... | collective-permute-start | bytes 1572872 | tf_op jit(solution)/shard_map/ppermute | solution.py:27
  12.6 34.5 %collective-permute-start.4 = (bf16[2,3,256,256]{3,2,1,0:T(8,128)(2,1)S(1)}, bf16[2,3,256,256]{3,2,1,0:T(8,128)(2,1)S(1)}, u32[]{:S(2)}, u32[]{:S(2)}) collective-permute-start(bf16[2,3,256,256]{3,2,1,0:T(8,128)(2,1)S(1)} %get-tuple-element.56), channel_id=1, source_target_pairs={{0,1},{1,0},{2,3},{3,2},{4,5},{5,4},{6,7},{7,6},{8,9},{9,8},{10,11... | collective-permute-start | bytes 2359304 | tf_op jit(solution)/shard_map/ppermute | solution.py:27
  14.2 0.8 copy-start.4
  31.6 23.6 %collective-permute-start.7 = (bf16[2,128,1024]{2,1,0:T(8,128)(2,1)S(1)}, bf16[2,128,1024]{2,1,0:T(8,128)(2,1)S(1)}, u32[]{:S(2)}, u32[]{:S(2)}) collective-permute-start(bf16[2,128,1024]{2,1,0:T(8,128)(2,1)S(1)} %get-tuple-element.63), channel_id=1, source_target_pairs={{0,12},{4,8},{8,4},{12,0},{16,28},{20,24},{24,20},{28,16},{1,13},{... | collective-permute-start | bytes 1572872 | tf_op jit(solution)/shard_map/ppermute | solution.py:27
  32.1 23.1 %collective-permute-start.8 = (bf16[2,128,1024]{2,1,0:T(8,128)(2,1)S(1)}, bf16[2,128,1024]{2,1,0:T(8,128)(2,1)S(1)}, u32[]{:S(2)}, u32[]{:S(2)}) collective-permute-start(bf16[2,128,1024]{2,1,0:T(8,128)(2,1)S(1)} %get-tuple-element.65), channel_id=1, source_target_pairs={{0,20},{4,16},{8,28},{12,24},{16,4},{20,0},{24,12},{28,8},{1,21},{... | collective-permute-start | bytes 1572872 | tf_op jit(solution)/shard_map/ppermute | solution.py:27
  33.3 24.2 %collective-permute-start.9 = (bf16[2,128,1024]{2,1,0:T(8,128)(2,1)S(1)}, bf16[2,128,1024]{2,1,0:T(8,128)(2,1)S(1)}, u32[]{:S(2)}, u32[]{:S(2)}) collective-permute-start(bf16[2,128,1024]{2,1,0:T(8,128)(2,1)S(1)} %get-tuple-element.67), channel_id=1, source_target_pairs={{0,28},{4,24},{8,20},{12,16},{16,12},{20,8},{24,4},{28,0},{1,29},{... | collective-permute-start | bytes 1572872 | tf_op jit(solution)/shard_map/ppermute | solution.py:27
  34.3 12.1 %collective-permute-start.6 = (bf16[2,1,256,256]{3,2,1,0:T(8,128)(2,1)S(1)}, bf16[2,1,256,256]{3,2,1,0:T(8,128)(2,1)S(1)}, u32[]{:S(2)}, u32[]{:S(2)}) collective-permute-start(bf16[2,1,256,256]{3,2,1,0:T(8,128)(2,1)S(1)} %get-tuple-element.59), channel_id=1, source_target_pairs={{0,3},{1,2},{2,1},{3,0},{4,7},{5,6},{6,5},{7,4},{8,11},{9,10},{10,... | collective-permute-start | bytes 786440 | tf_op jit(solution)/shard_map/ppermute | solution.py:27
  37.9 9.2 %copy-start.5 = (s32[2,4,1024]{2,1,0:T(4,128)S(1)}, s32[2,4,1024]{2,1,0:T(4,128)}, u32[]{:S(2)}) copy-start(s32[2,4,1024]{2,1,0:T(4,128)} %occ_ref.1) | copy-start | bytes 98308
  50.3 18.2 %collective-permute-start.10 = (bf16[256,768]{1,0:T(8,128)(2,1)S(1)}, bf16[256,768]{1,0:T(8,128)(2,1)S(1)}, u32[]{:S(2)}, u32[]{:S(2)}) collective-permute-start(bf16[256,768]{1,0:T(8,128)(2,1)S(1)} %get-tuple-element.71), channel_id=1, source_target_pairs={{0,3},{1,2},{2,1},{3,0},{4,7},{5,6},{6,5},{7,4},{8,11},{9,10},{10,... | collective-permute-start | bytes 1179656 | tf_op jit(solution)/shard_map/ppermute | solution.py:27
  52.8 16.9 %collective-permute-start.18 = (bf16[256,768]{1,0:T(8,128)(2,1)S(1)}, bf16[256,768]{1,0:T(8,128)(2,1)S(1)}, u32[]{:S(2)}, u32[]{:S(2)}) collective-permute-start(bf16[256,768]{1,0:T(8,128)(2,1)S(1)} %get-tuple-element.82), channel_id=1, source_target_pairs={{0,1},{1,0},{2,3},{3,2},{4,5},{5,4},{6,7},{7,6},{8,9},{9,8},{10,11... | collective-permute-start | bytes 1179656 | tf_op jit(solution)/shard_map/ppermute | solution.py:27
  60.3 12.1 %collective-permute-start.12 = (bf16[128,1024]{1,0:T(8,128)(2,1)S(1)}, bf16[128,1024]{1,0:T(8,128)(2,1)S(1)}, u32[]{:S(2)}, u32[]{:S(2)}) collective-permute-start(bf16[128,1024]{1,0:T(8,128)(2,1)S(1)} %get-tuple-element.73), channel_id=1, source_target_pairs={{0,8},{4,12},{8,0},{12,4},{16,24},{20,28},{24,16},{28,20},{1,9},{5... | collective-permute-start | bytes 786440 | tf_op jit(solution)/shard_map/ppermute | solution.py:27
  66.0 13.7 %collective-permute-start.14 = (bf16[128,1024]{1,0:T(8,128)(2,1)S(1)}, bf16[128,1024]{1,0:T(8,128)(2,1)S(1)}, u32[]{:S(2)}, u32[]{:S(2)}) collective-permute-start(bf16[128,1024]{1,0:T(8,128)(2,1)S(1)} %get-tuple-element.76), channel_id=1, source_target_pairs={{0,16},{4,20},{8,24},{12,28},{16,0},{20,4},{24,8},{28,12},{1,17},{... | collective-permute-start | bytes 786440 | tf_op jit(solution)/shard_map/ppermute | solution.py:27
  67.1 12.6 %collective-permute-start.16 = (bf16[128,1024]{1,0:T(8,128)(2,1)S(1)}, bf16[128,1024]{1,0:T(8,128)(2,1)S(1)}, u32[]{:S(2)}, u32[]{:S(2)}) collective-permute-start(bf16[128,1024]{1,0:T(8,128)(2,1)S(1)} %get-tuple-element.79), channel_id=1, source_target_pairs={{0,24},{4,28},{8,16},{12,20},{16,8},{20,12},{24,0},{28,4},{1,25},{... | collective-permute-start | bytes 786440 | tf_op jit(solution)/shard_map/ppermute | solution.py:27
  68.6 11.2 %collective-permute-start.11 = (bf16[128,1024]{1,0:T(8,128)(2,1)S(1)}, bf16[128,1024]{1,0:T(8,128)(2,1)S(1)}, u32[]{:S(2)}, u32[]{:S(2)}) collective-permute-start(bf16[128,1024]{1,0:T(8,128)(2,1)S(1)} %get-tuple-element.72), channel_id=1, source_target_pairs={{0,4},{4,0},{8,12},{12,8},{16,20},{20,16},{24,28},{28,24},{1,5},{5... | collective-permute-start | bytes 786440 | tf_op jit(solution)/shard_map/ppermute | solution.py:27
  69.8 23.6 %collective-permute-start.19 = (bf16[256,768]{1,0:T(8,128)(2,1)S(1)}, bf16[256,768]{1,0:T(8,128)(2,1)S(1)}, u32[]{:S(2)}, u32[]{:S(2)}) collective-permute-start(bf16[256,768]{1,0:T(8,128)(2,1)S(1)} %get-tuple-element.84), channel_id=1, source_target_pairs={{0,2},{1,3},{2,0},{3,1},{4,6},{5,7},{6,4},{7,5},{8,10},{9,11},{10,... | collective-permute-start | bytes 1179656 | tf_op jit(solution)/shard_map/ppermute | solution.py:27
  72.3 9.2 %collective-permute-start.13 = (bf16[128,1024]{1,0:T(8,128)(2,1)S(1)}, bf16[128,1024]{1,0:T(8,128)(2,1)S(1)}, u32[]{:S(2)}, u32[]{:S(2)}) collective-permute-start(bf16[128,1024]{1,0:T(8,128)(2,1)S(1)} %get-tuple-element.75), channel_id=1, source_target_pairs={{0,12},{4,8},{8,4},{12,0},{16,28},{20,24},{24,20},{28,16},{1,13},{... | collective-permute-start | bytes 786440 | tf_op jit(solution)/shard_map/ppermute | solution.py:27
  79.7 13.7 %collective-permute-start.15 = (bf16[128,1024]{1,0:T(8,128)(2,1)S(1)}, bf16[128,1024]{1,0:T(8,128)(2,1)S(1)}, u32[]{:S(2)}, u32[]{:S(2)}) collective-permute-start(bf16[128,1024]{1,0:T(8,128)(2,1)S(1)} %get-tuple-element.78), channel_id=1, source_target_pairs={{0,20},{4,16},{8,28},{12,24},{16,4},{20,0},{24,12},{28,8},{1,21},{... | collective-permute-start | bytes 786440 | tf_op jit(solution)/shard_map/ppermute | solution.py:27
  79.7 13.7 %collective-permute-start.17 = (bf16[128,1024]{1,0:T(8,128)(2,1)S(1)}, bf16[128,1024]{1,0:T(8,128)(2,1)S(1)}, u32[]{:S(2)}, u32[]{:S(2)}) collective-permute-start(bf16[128,1024]{1,0:T(8,128)(2,1)S(1)} %get-tuple-element.81), channel_id=1, source_target_pairs={{0,28},{4,24},{8,20},{12,16},{16,12},{20,8},{24,4},{28,0},{1,29},{... | collective-permute-start | bytes 786440 | tf_op jit(solution)/shard_map/ppermute | solution.py:27

commit v5 on v4

--- a/solution.py
+++ b/solution.py
@@ -27,22 +27,17 @@
     return lax.ppermute(block, axis, [(i, i ^ step) for i in range(size)])
 
 
-def after(message, *arrived):
-    return lax.optimization_barrier((message, *arrived))[0]
-
-
 def aligned(start, size):
     return pl.ds(pl.multiple_of(start, size), size)
 
 
 def row_tiles(states):
-    rows = min(256, states)
-    return [(start, rows) for start in range(0, states, rows)]
+    return [(start, min(256, states - start)) for start in range(0, states, 256)]
 
 
 def block_order(blocks):
-    half = list(range(0, blocks, 2))
-    return half, [d for d in range(blocks) if d not in half]
+    first = [0, 1, *range(2, blocks, 2)]
+    return first, [d for d in range(blocks) if d not in first]
 
 
 def free_weight(occ_ref, chan, size):
@@ -140,69 +135,73 @@
                 ).astype(BF16)
 
 
-def cross_blocks(states, order, me, turned_ref, left_ref, bar_refs, out_refs):
+def cross_rows(q, span, inner, left_ref, bar_ref):
+    return jnp.dot(
+        left_ref[0, q, span, inner], bar_ref[1, q], preferred_element_type=F32
+    ) - jnp.dot(left_ref[1, q, span, inner], bar_ref[0, q], preferred_element_type=F32)
+
+
+def store_blocks(states, order, me, q, top, crossed, turned_ref, out_refs):
     rows = out_refs[0].shape[0]
+    step = min(rows, crossed.shape[0])
+    for base in range(0, crossed.shape[0], step):
+        slot, inside = divmod(top + base, rows)
+        weights = turned_ref[q, aligned((me ^ order[slot]) * rows + inside, step), :]
+        out_refs[slot][inside : inside + step, q * states : (q + 1) * states] = (
+            crossed[base : base + step] * weights
+        ).astype(BF16)
+
+
+def first_kernel(states, order, me_ref, turned_ref, select_ref, *rest):
+    recv_refs, (bar_ref, left_ref, part_ref) = rest[:-3], rest[-3:]
+    weigh_blocks(states, order, me_ref[0], turned_ref, recv_refs, bar_ref)
+    turn_blocks(select_ref, bar_ref, left_ref)
     for q in range(turned_ref.shape[0]):
-        columns = slice(q * states, (q + 1) * states)
+        for top, height in row_tiles(bar_ref.shape[2]):
+            span = slice(top, top + height)
+            part_ref[q, span, :] = cross_rows(
+                q, span, slice(0, bar_ref.shape[2]), left_ref, bar_ref
+            )
+
+
+def first_part(me, order, turned, select, received):
+    ph_count, states, _ = turned.shape
+    rows = received[0].shape[1] * len(order)
+    shape = jax.ShapeDtypeStruct((2, ph_count, rows, states), BF16)
+    return pl.pallas_call(
+        functools.partial(first_kernel, states, order),
+        out_shape=(shape, shape, jax.ShapeDtypeStruct((ph_count, rows, states), F32)),
+        in_specs=[SMEM] + [VMEM] * (2 + len(order)),
+        out_specs=(VMEM,) * 3,
+        compiler_params=params(8),
+        cost_estimate=cost(8 * ph_count * rows * states**2, 14 * ph_count * states**2),
+        name="first_part",
+    )(me, turned, select, *received)
+
+
+def cross_first_kernel(states, order, me_ref, turned_ref, left_ref, part_ref, *rest):
+    first, second = order
+    recv_refs, out_refs = rest[: len(second)], rest[len(second) : len(second) + len(first)]
+    if second:
+        weigh_blocks(states, second, me_ref[0], turned_ref, recv_refs, rest[-1])
+    for q in range(turned_ref.shape[0]):
         for top, height in row_tiles(left_ref.shape[2]):
             span = slice(top, top + height)
-            crossed = jnp.zeros((height, states), F32)
-            start = 0
-            for bar_ref in bar_refs:
-                inner = slice(start, start + bar_ref.shape[2])
-                start = inner.stop
-                for n, sign in ((0, 1), (1, -1)):
-                    crossed += sign * jnp.dot(
-                        left_ref[n, q, span, inner], bar_ref[1 - n, q], preferred_element_type=F32
-                    )
-            step = min(rows, height)
-            for base in range(0, height, step):
-                slot, inside = divmod(top + base, rows)
-                weights = turned_ref[q, aligned((me ^ order[slot]) * rows + inside, step), :]
-                out_refs[slot][inside : inside + step, columns] = (
-                    crossed[base : base + step] * weights
-                ).astype(BF16)
-
-
-def first_kernel(states, order, me_ref, turned_ref, select_ref, *rest):
-    recv_refs, (bar_ref, left_ref) = rest[:-2], rest[-2:]
-    weigh_blocks(states, order, me_ref[0], turned_ref, recv_refs, bar_ref)
-    turn_blocks(select_ref, bar_ref, left_ref)
-
-
-def first_half(me, order, turned, select, received):
-    ph_count, states, _ = turned.shape
-    rows = received[0].shape[1]
-    shape = jax.ShapeDtypeStruct((2, ph_count, rows * len(order), states), BF16)
-    return pl.pallas_call(
-        functools.partial(first_kernel, states, order),
-        out_shape=(shape, shape),
-        in_specs=[SMEM] + [VMEM] * (2 + len(order)),
-        out_specs=(VMEM, VMEM),
-        compiler_params=params(8),
-        cost_estimate=cost(4 * ph_count * shape.shape[2] * states**2, 14 * ph_count * states**2),
-        name="first_half",
-    )(me, turned, select, *received)
-
-
-def cross_first_kernel(states, order, me_ref, turned_ref, bar_ref, left_ref, *rest):
-    first, second = order
-    recv_refs, out_refs = rest[: len(second)], rest[len(second) : len(second) + len(first)]
-    bar_refs = [bar_ref]
-    if second:
-        weigh_blocks(states, second, me_ref[0], turned_ref, recv_refs, rest[-1])
-        bar_refs.append(rest[-1])
-    cross_blocks(states, first, me_ref[0], turned_ref, left_ref, bar_refs, out_refs)
-
-
-def cross_first(me, order, turned, bar, left, received, flat):
+            crossed = part_ref[q, span, :]
+            if second:
+                inner = slice(left_ref.shape[2], states)
+                crossed += cross_rows(q, span, inner, left_ref, rest[-1])
+            store_blocks(states, first, me_ref[0], q, top, crossed, turned_ref, out_refs)
+
+
+def cross_first(me, order, turned, left, part, received, flat):
     ph_count, states, _ = turned.shape
     first, second = order
     blocks = len(first) + len(second)
     out_shape = [jax.ShapeDtypeStruct((flat[0] // blocks, flat[1]), BF16)] * len(first)
     if second:
         out_shape.append(
-            jax.ShapeDtypeStruct((2, ph_count, states - bar.shape[2], states), BF16)
+            jax.ShapeDtypeStruct((2, ph_count, states - left.shape[2], states), BF16)
         )
     out = pl.pallas_call(
         functools.partial(cross_first_kernel, states, order),
@@ -212,7 +211,7 @@
         compiler_params=params(8),
         cost_estimate=cost(2 * ph_count * states**3, 14 * ph_count * states**2),
         name="cross_first",
-    )(me, turned, bar, left, *received)
+    )(me, turned, left, part, *received)
     return out[: len(first)], out[-1]
 
 
@@ -221,9 +220,13 @@
 ):
     out_refs, left_ref = rest[:-1], rest[-1]
     turn_blocks(select_ref, second_bar_ref, left_ref)
-    cross_blocks(
-        states, order, me_ref[0], turned_ref, left_ref, [bar_ref, second_bar_ref], out_refs
-    )
+    middle = bar_ref.shape[2]
+    for q in range(turned_ref.shape[0]):
+        for top, height in row_tiles(left_ref.shape[2]):
+            span = slice(top, top + height)
+            crossed = cross_rows(q, span, slice(0, middle), left_ref, bar_ref)
+            crossed += cross_rows(q, span, slice(middle, states), left_ref, second_bar_ref)
+            store_blocks(states, order, me_ref[0], q, top, crossed, turned_ref, out_refs)
 
 
 def cross_second(me, order, turned, select, bar, second_bar, flat, blocks):
@@ -420,6 +423,52 @@
     return first + jnp.swapaxes(mirrored, 1, 2)
 
 
+WAITS = {
+    "lack1": ("in1",),
+    "lack3": ("in2", "prepare"),
+    "in3": ("in2", "prepare"),
+    "in5": ("in4", "prepare"),
+    "in7": ("in6", "prepare"),
+    "cross_first": ("ladder",),
+    "own2": ("own1",),
+    "back1": ("own3",),
+    "back3": ("back2",),
+    "back5": ("back4",),
+    "back7": ("back6", "back1"),
+}
+
+
+ORDER = (
+    "pack_near",
+    "pack_late",
+    "prepare",
+    "in1",
+    "in2",
+    "in4",
+    "in6",
+    "lack1",
+    "lack2",
+    "lack3",
+    "in3",
+    "in5",
+    "in7",
+    "first",
+    "ladder",
+    "own1",
+    "own2",
+    "own3",
+    "cross_first",
+    "back1",
+    "back2",
+    "back4",
+    "back6",
+    "cross_second",
+    "back3",
+    "back5",
+    "back7",
+)
+
+
 def per_device(
     chans,
     tiles,
@@ -455,60 +504,89 @@
         return xor_permute(message, "tile", tiles, k)
 
     first, second = order = block_order(chans)
-    near = [1] + [d for d in first if d]
+    near = first[1:]
     late = [d for d in range(chans) if d not in near]
     pair = (generator, hamiltonian)
     steps = list(range(1, tiles))
-    packed, lacking = pack(me, place, chan_sizes, *pair, chans, tiles, near, steps[1:2], 50)
-    for kept, rest in zip(
-        (packed, lacking),
-        pack(me, place, chan_sizes, *pair, chans, tiles, late, steps[:1] + steps[2:], 12),
-    ):
-        kept.update(rest)
-    turned, select, diagonal = prepare(
-        me,
-        first + second,
-        recouple_map,
-        recoupled_occupation,
-        recouple_weights,
-        chan_sizes,
-        pair_occupation,
-        generator,
-        hamiltonian,
-    )
-
-    received = {0: packed[0], 1: to_chan(packed[1], 1)}
-    for d in first[1:]:
-        received[d] = to_chan(packed[d], d)
-        received[d + 1] = to_chan(after(packed[d + 1], received[d], select), d + 1)
-    lacking[1] = after(lacking[1], received[1])
-    for k in steps:
-        lacking[k] = to_tile(after(lacking[k], lacking[k - 1], select) if k > 2 else lacking[k], k)
-
-    bar, left = first_half(me, first, turned, select, [received[d] for d in first])
-    ladder = ladder_blocks(place, chan_sizes, pair_occupation, generator, hamiltonian, [lacking[k] for k in steps])
-    left = after(left, ladder[0])
-    ladder = list(ladder)
-    ladder[1] = to_tile(ladder[1], 1)
-    for k in range(2, tiles):
-        ladder[k] = to_tile(after(ladder[k], ladder[1]) if k == 2 else ladder[k], k)
-
-    back = {}
-    sent, second_bar = cross_first(
-        me, order, turned, bar, left, [received[d] for d in second], flat
-    )
-    back[0] = sent[0]
-    for d, block in zip(first, sent):
-        if d:
-            back[d] = to_chan(block, d)
-    sent = cross_second(me, second, turned, select, bar, second_bar, flat, chans)
-    for d, block in zip(second, sent):
-        waits = [ladder[-1]] if d == 1 else [back[d - 1]]
-        if d == chans - 1:
-            waits.append(back[1])
-        back[d] = to_chan(after(block, *waits), d)
-    back = [back[d] for d in range(chans)]
-    return finish(me, place, chan_sizes, generator.shape, diagonal, back, ladder)
+    done = {}
+
+    def value(name):
+        if name not in done:
+            done[name] = make[name]()
+        return done[name]
+
+    def held(name, operand):
+        waits = [value(wait) for wait in WAITS.get(name, ()) if wait in make]
+        waits = [w[1] if isinstance(w, tuple) else w[0] if isinstance(w, list) else w for w in waits]
+        return lax.optimization_barrier((operand, waits))[0] if waits else operand
+
+    def pack_part(partners, chosen, mib):
+        return pack(me, place, chan_sizes, *pair, chans, tiles, partners, chosen, mib)
+
+    def to_chan(name, block, d):
+        return xor_permute(held(name, block), "chan", chans, d) if d else block
+
+    def to_tile(name, block, k):
+        return xor_permute(held(name, block), "tile", tiles, k) if k else block
+
+    def make_first():
+        turned, select, _ = value("prepare")
+        received = held("first", [value(f"in{d}") for d in first])
+        return first_part(me, first, turned, select, received)
+
+    def make_ladder():
+        lacking = held("ladder", [value(f"lack{k}") for k in steps])
+        return ladder_blocks(place, chan_sizes, pair_occupation, *pair, lacking)
+
+    def make_cross_first():
+        _, left, part = value("first")
+        part = held("cross_first", part)
+        received = [value(f"in{d}") for d in second]
+        return cross_first(me, order, value("prepare")[0], left, part, received, flat)
+
+    def make_cross_second():
+        turned, select, _ = value("prepare")
+        bar, second_bar = held("cross_second", (value("first")[0], value("cross_first")[1]))
+        return cross_second(me, second, turned, select, bar, second_bar, flat, chans)
+
+    make = {
+        "pack_near": lambda: pack_part(near, steps[1:2], 50),
+        "pack_late": lambda: pack_part(late, steps[:1] + steps[2:], 12),
+        "prepare": lambda: prepare(
+            me,
+            first + second,
+            recouple_map,
+            recoupled_occupation,
+            recouple_weights,
+            chan_sizes,
+            pair_occupation,
+            *pair,
+        ),
+        "first": make_first,
+        "ladder": make_ladder,
+        "cross_first": make_cross_first,
+        "cross_second": make_cross_second,
+    }
+    for d in range(chans):
+        source = "pack_near" if d in near else "pack_late"
+        make[f"in{d}"] = lambda d=d, s=source: to_chan(f"in{d}", value(s)[0][d], d)
+        group, place_in, blocks = (
+            ("cross_first", first.index(d), 0) if d in first else ("cross_second", second.index(d), 1)
+        )
+        make[f"back{d}"] = lambda d=d, g=group, i=place_in, b=blocks: to_chan(
+            f"back{d}", (value(g) if b else value(g)[0])[i], d
+        )
+    for k in range(tiles):
+        source = "pack_near" if k in steps[1:2] else "pack_late"
+        make[f"lack{k}"] = lambda k=k, s=source: to_tile(f"lack{k}", value(s)[1][k], k)
+        make[f"own{k}"] = lambda k=k: to_tile(f"own{k}", value("ladder")[k], k)
+
+    for name in ORDER:
+        if name in make:
+            value(name)
+    back = [value(f"back{d}") for d in range(chans)]
+    ladder = [value(f"own{k}") for k in range(tiles)]
+    return finish(me, place, chan_sizes, generator.shape, value("prepare")[2], back, ladder)
 
 
 def per_device_whole(
@@ -533,8 +611,8 @@
     turned, select = prepare(
         alone, order[0], recouple_map, recoupled_occupation, recouple_weights
     )
-    bar, left = first_half(alone, order[0], turned, select, [received])
-    sent, _ = cross_first(alone, order, turned, bar, left, [], flat)
+    _, left, part = first_part(alone, order[0], turned, select, [received])
+    sent, _ = cross_first(alone, order, turned, left, part, [], flat)
     back = lax.all_to_all(sent[0], "chan", 0, 0, tiled=True).reshape(generator.shape)
     ladder = ladder_gathered(chan_sizes, pair_occupation, generator, hamiltonian)
     return jnp.where(live, ladder + back.astype(F32), 0.0).astype(BF16)

time: 96.5 us -> 92.9 us (0.963)
  starting transfers between devices: 29.6 us -> 21.4 us
  waiting for transfers between devices: 35.8 us -> 39.1 us
  Pallas kernels: 29.2 us -> 30.4 us
    ppermute x20, starting transfers between devices: 29.6 us -> 21.4 us  [xor_permute(): return lax.ppermute(block, axis, [(i, i ^ step) for i in range(size)])]
    ppermute x20, waiting for transfers between devices: 35.8 us -> 39.1 us  [xor_permute(): return lax.ppermute(block, axis, [(i, i ^ step) for i in range(size)])]
    pallas_call x1, Pallas kernels: 2.41 us -> 5.1 us  [first_part(): pl.pallas_call(functools.partial(first_kernel, states, order), out_shape=...]
  transfers between devices with their start and end apart: 20 -> 20, of which waited for: 8 -> 8; matrix products, arithmetic and copies ran while one was open for 0% -> 0% of each run, Pallas kernels for 25% -> 27%
where the time goes in v5:
time: 92.9 us; the launch traced here: 92.7 us
  waiting for transfers between devices  39.1 us (42%)
  Pallas kernels  30.4 us (33%)
  starting transfers between devices  21.4 us (23%)
  local copies, waits for them, and re-layouts  1.58 us (2%)
    ppermute x20, waiting for transfers between devices, xor_permute(): return lax.ppermute(block, axis, [(i, i ^ step) for i in range(size)])  39.1 us
    ppermute x20, starting transfers between devices, xor_permute(): return lax.ppermute(block, axis, [(i, i ^ step) for i in range(size)])  21.4 us
    pallas_call x1, Pallas kernels, prepare(): pl.pallas_call(functools.partial(kernel, ph_count, states, order), out_sh...  9.23 us
    pallas_call x1, Pallas kernels, first_part(): pl.pallas_call(functools.partial(first_kernel, states, order), out_shape=...  5.1 us
    pallas_call x1, Pallas kernels, cross_second(): pl.pallas_call(functools.partial(cross_second_kernel, states, order), out...  4.08 us
    pallas_call x2, Pallas kernels, pack(): pl.pallas_call(functools.partial(pack_kernel, eta.shape, blocks, tiles, p...  4.02 us
    pallas_call x1, Pallas kernels, ladder_blocks(): pl.pallas_call(functools.partial(ladder_kernel, tiles, rows), out_shape=[...  3.24 us
    pallas_call x1, Pallas kernels, finish(): pl.pallas_call(functools.partial(finish_kernel, len(back)), out_shape=jax...  2.71 us
  transfers between devices with their start and end apart: 20, of which 8 were waited for; matrix products, arithmetic and copies ran while one was open for 0% of the time, Pallas kernels for 27%

profile of v5, /device:TPU:0, one launch (start us, length us, event | category | flops | bytes accessed | tf_op | source)
XLA Modules:
  0.0 92.7 jit_solution(15387796057030408798)
XLA Ops:
  0.0 0.8 copy-done.2
  0.8 2.4 %pack.3 = (bf16[2,128,1024]{2,1,0:T(8,128)(2,1)S(1)}, bf16[2,128,1024]{2,1,0:T(8,128)(2,1)S(1)}, bf16[2,128,1024]{2,1,0:T(8,128)(2,1)S(1)}, bf16[2,128,1024]{2,1...) custom-call(s32[1]{0:T(128)} %bitcast.refs_0_.me_ref, s32[1]{0:T(128)} %bitcast.1.place_ref, s32[4]{0:T(128)S(1)} %copy-done.2, ...), custom_call_target="tpu_custom_call" | custom-call | bytes 4194304 | tf_op jit(solution)/shard_map/pack/pallas_call | solution.py:286
  3.3 0.4 collective-permute-start
  3.7 2.6 %collective-permute-start.1 = (bf16[2,128,1024]{2,1,0:T(8,128)(2,1)S(1)}, bf16[2,128,1024]{2,1,0:T(8,128)(2,1)S(1)}, u32[]{:S(2)}, u32[]{:S(2)}) collective-permute-start(bf16[2,128,1024]{2,1,0:T(8,128)(2,1)S(1)} %get-tuple-element.51), channel_id=1, source_target_pairs={{0,8},{4,12},{8,0},{12,4},{16,24},{20,28},{24,16},{28,20},{1,9},{5... | collective-permute-start | bytes 1572872 | tf_op jit(solution)/shard_map/ppermute | solution.py:27
  6.3 1.6 %collective-permute-start.2 = (bf16[2,128,1024]{2,1,0:T(8,128)(2,1)S(1)}, bf16[2,128,1024]{2,1,0:T(8,128)(2,1)S(1)}, u32[]{:S(2)}, u32[]{:S(2)}) collective-permute-start(bf16[2,128,1024]{2,1,0:T(8,128)(2,1)S(1)} %get-tuple-element.52), channel_id=1, source_target_pairs={{0,16},{4,20},{8,24},{12,28},{16,0},{20,4},{24,8},{28,12},{1,17},{... | collective-permute-start | bytes 1572872 | tf_op jit(solution)/shard_map/ppermute | solution.py:27
  7.9 2.9 %collective-permute-start.5 = (bf16[2,2,256,256]{3,2,1,0:T(8,128)(2,1)S(1)}, bf16[2,2,256,256]{3,2,1,0:T(8,128)(2,1)S(1)}, u32[]{:S(2)}, u32[]{:S(2)}) collective-permute-start(bf16[2,2,256,256]{3,2,1,0:T(8,128)(2,1)S(1)} %get-tuple-element.58), channel_id=1, source_target_pairs={{0,2},{1,3},{2,0},{3,1},{4,6},{5,7},{6,4},{7,5},{8,10},{9,11},{10,... | collective-permute-start | bytes 1572872 | tf_op jit(solution)/shard_map/ppermute | solution.py:27
  10.8 1.6 %pack.2 = (bf16[2,128,1024]{2,1,0:T(8,128)(2,1)S(1)}, bf16[2,128,1024]{2,1,0:T(8,128)(2,1)S(1)}, bf16[2,128,1024]{2,1,0:T(8,128)(2,1)S(1)}, bf16[2,128,1024]{2,1...) custom-call(s32[1]{0:T(128)} %bitcast.refs_0_.me_ref, ...), custom_call_target="tpu_custom_call" | custom-call | bytes 4194304 | tf_op jit(solution)/shard_map/pack/pallas_call | solution.py:286
  12.5 1.6 %collective-permute-start.4 = (bf16[2,3,256,256]{3,2,1,0:T(8,128)(2,1)S(1)}, bf16[2,3,256,256]{3,2,1,0:T(8,128)(2,1)S(1)}, u32[]{:S(2)}, u32[]{:S(2)}) collective-permute-start(bf16[2,3,256,256]{3,2,1,0:T(8,128)(2,1)S(1)} %get-tuple-element.57), channel_id=1, source_target_pairs={{0,1},{1,0},{2,3},{3,2},{4,5},{5,4},{6,7},{7,6},{8,9},{9,8},{10,11... | collective-permute-start | bytes 2359304 | tf_op jit(solution)/shard_map/ppermute | solution.py:27
  14.1 0.8 copy-done.4
  14.9 9.2 %prepare.1 = (f32[1,1024,1024]{2,1,0:T(8,128)S(1)}, bf16[1,1024,1024]{2,1,0:T(8,128)(2,1)S(1)}, f32[4,256,256]{2,1,0:T(8,128)S(1)}) custom-call(s32[1]{0:T(128)} %bitcast.refs_0_.me_ref, s32[1,1024]{1,0:T(1,128)S(1)} %copy-done.6, s32[2,1,1024]{2,1,0:T(1,128)S(1)} %copy-done.5, f32[1,1024,1024]{2,1,0:T(8,128)S(1)} %copy-done.3, s32[4]{0:T(128)S(1)} %copy-done.2, ...), custom_call_target="tpu_custom_call" | custom-call | flops 7516192768 | bytes 14680064 | tf_op jit(solution)/shard_map/prepare/pallas_call | solution.py:102
  24.2 7.1 %collective-permute-done.3.rest_4_ = bf16[2,128,1024]{2,1,0:T(8,128)(2,1)S(1)} collective-permute-done((bf16[2,128,1024]{2,1,0:T(8,128)(2,1)S(1)}, bf16[2,128,1024]{2,1,0:T(8,128)(2,1)S(1)}, u32[]{:S(2)}, u32[]{:S(2)}) %collective-permute-start.3) | collective-permute-done | bytes 524320 | tf_op jit(solution)/shard_map/ppermute | solution.py:27
  31.5 0.6 collective-permute-start.7
  32.1 1.2 %collective-permute-start.8 = (bf16[2,128,1024]{2,1,0:T(8,128)(2,1)S(1)}, bf16[2,128,1024]{2,1,0:T(8,128)(2,1)S(1)}, u32[]{:S(2)}, u32[]{:S(2)}) collective-permute-start(bf16[2,128,1024]{2,1,0:T(8,128)(2,1)S(1)} %get-tuple-element.66), channel_id=1, source_target_pairs={{0,20},{4,16},{8,28},{12,24},{16,4},{20,0},{24,12},{28,8},{1,21},{... | collective-permute-start | bytes 1572872 | tf_op jit(solution)/shard_map/ppermute | solution.py:27
  33.3 1.6 %collective-permute-done.5.rest_1_ = bf16[2,2,256,256]{3,2,1,0:T(8,128)(2,1)S(1)} collective-permute-done((bf16[2,2,256,256]{3,2,1,0:T(8,128)(2,1)S(1)}, bf16[2,2,256,256]{3,2,1,0:T(8,128)(2,1)S(1)}, u32[]{:S(2)}, u32[]{:S(2)}) %collective-permute-start.5) | collective-permute-done | bytes 524320 | tf_op jit(solution)/shard_map/ppermute | solution.py:27
  35.1 11.2 %collective-permute-done.6.rest_2_ = bf16[2,1,256,256]{3,2,1,0:T(8,128)(2,1)S(1)} collective-permute-done((bf16[2,1,256,256]{3,2,1,0:T(8,128)(2,1)S(1)}, bf16[2,1,256,256]{3,2,1,0:T(8,128)(2,1)S(1)}, u32[]{:S(2)}, u32[]{:S(2)}) %collective-permute-start.6) | collective-permute-done | bytes 262176 | tf_op jit(solution)/shard_map/ppermute | solution.py:27
  46.3 0.7 collective-permute-done.4.rest_0_
  46.9 3.2 %ladder.1 = (bf16[256,768]{1,0:T(8,128)(2,1)S(1)}, bf16[256,768]{1,0:T(8,128)(2,1)S(1)}, bf16[256,768]{1,0:T(8,128)(2,1)S(1)}, bf16[256,768]{1,0:T(8,128)(2,1)S(1)}) custom-call(s32[1]{0:T(128)} %bitcast.1.place_ref, s32[4]{0:T(128)S(1)} %copy-done.2, s32[2,4,1024]{2,1,0:T(4,128)S(1)} %copy-done.4, bf16[4,256,1024]{2,1,0:T(8,128)(2,1)S(1)} %copy-done, ...), custom_call_target="tpu_custom_call" | custom-call | flops 2147483648 | bytes 8388608 | tf_op jit(solution)/shard_map/ladder/pallas_call | solution.py:351
  50.2 2.6 %collective-permute-start.10 = (bf16[256,768]{1,0:T(8,128)(2,1)S(1)}, bf16[256,768]{1,0:T(8,128)(2,1)S(1)}, u32[]{:S(2)}, u32[]{:S(2)}) collective-permute-start(bf16[256,768]{1,0:T(8,128)(2,1)S(1)} %get-tuple-element.71), channel_id=1, source_target_pairs={{0,3},{1,2},{2,1},{3,0},{4,7},{5,6},{6,5},{7,4},{8,11},{9,10},{10,... | collective-permute-start | bytes 1179656 | tf_op jit(solution)/shard_map/ppermute | solution.py:27
  52.8 5.1 %first_part.1 = (bf16[2,1,640,1024]{3,2,1,0:T(8,128)(2,1)S(1)}, bf16[2,1,640,1024]{3,2,1,0:T(8,128)(2,1)S(1)}, f32[1,640,1024]{2,1,0:T(8,128)S(1)}) custom-call(s32[1]{0:T(128)} %bitcast.refs_0_.me_ref, f32[1,1024,1024]{2,1,0:T(8,128)S(1)} %get-tuple-element.47.turned_ref, bf16[1,1024,1024]{2,1,0:T(8,128)(2,1)S(1)} %get-tuple-element.48.select_ref, ...), custom_call_target="tpu_custom_call" | custom-call | flops 5368709120 | bytes 14680064 | tf_op jit(solution)/shard_map/first_part/pallas_call | solution.py:171
  57.9 2.0 %cross_first.1 = (bf16[128,1024]{1,0:T(8,128)(2,1)S(1)}, bf16[128,1024]{1,0:T(8,128)(2,1)S(1)}, bf16[128,1024]{1,0:T(8,128)(2,1)S(1)}, bf16[128,1024]{1,0:T(8,12...) custom-call(s32[1]{0:T(128)} %bitcast.refs_0_.me_ref, ...), custom_call_target="tpu_custom_call" | custom-call | flops 2147483648 | bytes 14680064 | tf_op jit(solution)/shard_map/cross_first/pallas_call | solution.py:206
  59.9 1.5 %collective-permute-start.12 = (bf16[128,1024]{1,0:T(8,128)(2,1)S(1)}, bf16[128,1024]{1,0:T(8,128)(2,1)S(1)}, u32[]{:S(2)}, u32[]{:S(2)}) collective-permute-start(bf16[128,1024]{1,0:T(8,128)(2,1)S(1)} %get-tuple-element.73), channel_id=1, source_target_pairs={{0,8},{4,12},{8,0},{12,4},{16,24},{20,28},{24,16},{28,20},{1,9},{5... | collective-permute-start | bytes 786440 | tf_op jit(solution)/shard_map/ppermute | solution.py:27
  61.4 1.5 %collective-permute-start.14 = (bf16[128,1024]{1,0:T(8,128)(2,1)S(1)}, bf16[128,1024]{1,0:T(8,128)(2,1)S(1)}, u32[]{:S(2)}, u32[]{:S(2)}) collective-permute-start(bf16[128,1024]{1,0:T(8,128)(2,1)S(1)} %get-tuple-element.78), channel_id=1, source_target_pairs={{0,16},{4,20},{8,24},{12,28},{16,0},{20,4},{24,8},{28,12},{1,17},{... | collective-permute-start | bytes 786440 | tf_op jit(solution)/shard_map/ppermute | solution.py:27
  62.9 0.5 collective-permute-start.16
  63.5 6.0 %collective-permute-done.18.rest_9_ = bf16[256,768]{1,0:T(8,128)(2,1)S(1)} collective-permute-done((bf16[256,768]{1,0:T(8,128)(2,1)S(1)}, bf16[256,768]{1,0:T(8,128)(2,1)S(1)}, u32[]{:S(2)}, u32[]{:S(2)}) %collective-permute-start.18) | collective-permute-done | bytes 393248 | tf_op jit(solution)/shard_map/ppermute | solution.py:27
  69.5 0.6 collective-permute-start.19
  70.1 4.1 %cross_second.1 = (bf16[128,1024]{1,0:T(8,128)(2,1)S(1)}, bf16[128,1024]{1,0:T(8,128)(2,1)S(1)}, bf16[128,1024]{1,0:T(8,128)(2,1)S(1)}) custom-call(s32[1]{0:T(128)} %bitcast.refs_0_.me_ref, f32[1,1024,1024]{2,1,0:T(8,128)S(1)} %get-tuple-element.47.turned_ref, bf16[1,1024,1024]{2,1,0:T(8,128)(2,1)S(1)} %get-tuple-element.48.select_ref, ...), custom_call_target="tpu_custom_call" | custom-call | flops 4294967296 | bytes 14680064 | tf_op jit(solution)/shard_map/cross_second/pallas_call | solution.py:234
  74.2 1.6 %collective-permute-start.13 = (bf16[128,1024]{1,0:T(8,128)(2,1)S(1)}, bf16[128,1024]{1,0:T(8,128)(2,1)S(1)}, u32[]{:S(2)}, u32[]{:S(2)}) collective-permute-start(bf16[128,1024]{1,0:T(8,128)(2,1)S(1)} %get-tuple-element.77), channel_id=1, source_target_pairs={{0,12},{4,8},{8,4},{12,0},{16,28},{20,24},{24,20},{28,16},{1,13},{... | collective-permute-start | bytes 786440 | tf_op jit(solution)/shard_map/ppermute | solution.py:27
  75.8 1.1 %collective-permute-start.15 = (bf16[128,1024]{1,0:T(8,128)(2,1)S(1)}, bf16[128,1024]{1,0:T(8,128)(2,1)S(1)}, u32[]{:S(2)}, u32[]{:S(2)}) collective-permute-start(bf16[128,1024]{1,0:T(8,128)(2,1)S(1)} %get-tuple-element.80), channel_id=1, source_target_pairs={{0,20},{4,16},{8,28},{12,24},{16,4},{20,0},{24,12},{28,8},{1,21},{... | collective-permute-start | bytes 786440 | tf_op jit(solution)/shard_map/ppermute | solution.py:27
  77.0 0.6 collective-permute-start.17
  77.6 4.9 %collective-permute-done.13.rest_3_ = bf16[128,1024]{1,0:T(8,128)(2,1)S(1)} collective-permute-done((bf16[128,1024]{1,0:T(8,128)(2,1)S(1)}, bf16[128,1024]{1,0:T(8,128)(2,1)S(1)}, u32[]{:S(2)}, u32[]{:S(2)}) %collective-permute-start.13) | collective-permute-done | bytes 262176 | tf_op jit(solution)/shard_map/ppermute | solution.py:27
  82.5 7.4 %collective-permute-done.15.rest_5_ = bf16[128,1024]{1,0:T(8,128)(2,1)S(1)} collective-permute-done((bf16[128,1024]{1,0:T(8,128)(2,1)S(1)}, bf16[128,1024]{1,0:T(8,128)(2,1)S(1)}, u32[]{:S(2)}, u32[]{:S(2)}) %collective-permute-start.15) | collective-permute-done | bytes 262176 | tf_op jit(solution)/shard_map/ppermute | solution.py:27
  89.9 2.7 %finish.1 = bf16[4,256,1024]{2,1,0:T(8,128)(2,1)} custom-call(s32[1]{0:T(128)} %bitcast.refs_0_.me_ref, s32[1]{0:T(128)} %bitcast.1.place_ref, s32[4]{0:T(128)S(1)} %copy-done.2, f32[4,256,256]{2,1,0:T(8,128)S(1)} %get-tuple-element.46.diagonal_ref, bf16[128,1024]{1,0:T(8,128)(2,1)S(1)} %get-tuple-element.69.rest_0_, ...), custom_call_target="tpu_custom_call" | custom-call | bytes 6291456 | tf_op jit(solution)/shard_map/finish/pallas_call | solution.py:396
  (30 shorter events, 0.5 us)
Async XLA Ops:
  0.0 10.8 %copy-start = (bf16[4,256,1024]{2,1,0:T(8,128)(2,1)S(1)}, bf16[4,256,1024]{2,1,0:T(8,128)(2,1)}, u32[]{:S(2)}) copy-start(bf16[4,256,1024]{2,1,0:T(8,128)(2,1)} %eta_ref.1) | copy-start | bytes 6291460
  0.0 10.8 %copy-start.1 = (bf16[4,256,1024]{2,1,0:T(8,128)(2,1)S(1)}, bf16[4,256,1024]{2,1,0:T(8,128)(2,1)}, u32[]{:S(2)}) copy-start(bf16[4,256,1024]{2,1,0:T(8,128)(2,1)} %gamma_ref.1) | copy-start | bytes 6291460
  0.0 0.8 copy-start.2
  3.2 10.9 %copy-start.3 = (f32[1,1024,1024]{2,1,0:T(8,128)S(1)}, f32[1,1024,1024]{2,1,0:T(8,128)}, u32[]{:S(2)}) copy-start(f32[1,1024,1024]{2,1,0:T(8,128)} %refs_3_.1) | copy-start | bytes 12582916
  3.2 10.9 %copy-start.5 = (s32[2,1,1024]{2,1,0:T(1,128)S(1)}, s32[2,1,1024]{2,1,0:T(1,128)}, u32[]{:S(2)}) copy-start(s32[2,1,1024]{2,1,0:T(1,128)} %refs_2_.1) | copy-start | bytes 24580
  3.3 10.9 %copy-start.6 = (s32[1,1024]{1,0:T(1,128)S(1)}, s32[1,1024]{1,0:T(1,128)}, u32[]{:S(2)}) copy-start(s32[1,1024]{1,0:T(1,128)} %refs_1_.1) | copy-start | bytes 12292
  3.3 9.2 %collective-permute-start = (bf16[2,128,1024]{2,1,0:T(8,128)(2,1)S(1)}, bf16[2,128,1024]{2,1,0:T(8,128)(2,1)S(1)}, u32[]{:S(2)}, u32[]{:S(2)}) collective-permute-start(bf16[2,128,1024]{2,1,0:T(8,128)(2,1)S(1)} %get-tuple-element.50), channel_id=1, source_target_pairs={{0,4},{4,0},{8,12},{12,8},{16,20},{20,16},{24,28},{28,24},{1,5},{5... | collective-permute-start | bytes 1572872 | tf_op jit(solution)/shard_map/ppermute | solution.py:27
  3.7 20.4 %collective-permute-start.1 = (bf16[2,128,1024]{2,1,0:T(8,128)(2,1)S(1)}, bf16[2,128,1024]{2,1,0:T(8,128)(2,1)S(1)}, u32[]{:S(2)}, u32[]{:S(2)}) collective-permute-start(bf16[2,128,1024]{2,1,0:T(8,128)(2,1)S(1)} %get-tuple-element.51), channel_id=1, source_target_pairs={{0,8},{4,12},{8,0},{12,4},{16,24},{20,28},{24,16},{28,20},{1,9},{5... | collective-permute-start | bytes 1572872 | tf_op jit(solution)/shard_map/ppermute | solution.py:27
  6.3 25.2 %collective-permute-start.2 = (bf16[2,128,1024]{2,1,0:T(8,128)(2,1)S(1)}, bf16[2,128,1024]{2,1,0:T(8,128)(2,1)S(1)}, u32[]{:S(2)}, u32[]{:S(2)}) collective-permute-start(bf16[2,128,1024]{2,1,0:T(8,128)(2,1)S(1)} %get-tuple-element.52), channel_id=1, source_target_pairs={{0,16},{4,20},{8,24},{12,28},{16,0},{20,4},{24,8},{28,12},{1,17},{... | collective-permute-start | bytes 1572872 | tf_op jit(solution)/shard_map/ppermute | solution.py:27
  7.9 23.4 %collective-permute-start.3 = (bf16[2,128,1024]{2,1,0:T(8,128)(2,1)S(1)}, bf16[2,128,1024]{2,1,0:T(8,128)(2,1)S(1)}, u32[]{:S(2)}, u32[]{:S(2)}) collective-permute-start(bf16[2,128,1024]{2,1,0:T(8,128)(2,1)S(1)} %get-tuple-element.53), channel_id=1, source_target_pairs={{0,24},{4,28},{8,16},{12,20},{16,8},{20,12},{24,0},{28,4},{1,25},{... | collective-permute-start | bytes 1572872 | tf_op jit(solution)/shard_map/ppermute | solution.py:27
  7.9 27.0 %collective-permute-start.5 = (bf16[2,2,256,256]{3,2,1,0:T(8,128)(2,1)S(1)}, bf16[2,2,256,256]{3,2,1,0:T(8,128)(2,1)S(1)}, u32[]{:S(2)}, u32[]{:S(2)}) collective-permute-start(bf16[2,2,256,256]{3,2,1,0:T(8,128)(2,1)S(1)} %get-tuple-element.58), channel_id=1, source_target_pairs={{0,2},{1,3},{2,0},{3,1},{4,6},{5,7},{6,4},{7,5},{8,10},{9,11},{10,... | collective-permute-start | bytes 1572872 | tf_op jit(solution)/shard_map/ppermute | solution.py:27
  12.5 34.5 %collective-permute-start.4 = (bf16[2,3,256,256]{3,2,1,0:T(8,128)(2,1)S(1)}, bf16[2,3,256,256]{3,2,1,0:T(8,128)(2,1)S(1)}, u32[]{:S(2)}, u32[]{:S(2)}) collective-permute-start(bf16[2,3,256,256]{3,2,1,0:T(8,128)(2,1)S(1)} %get-tuple-element.57), channel_id=1, source_target_pairs={{0,1},{1,0},{2,3},{3,2},{4,5},{5,4},{6,7},{7,6},{8,9},{9,8},{10,11... | collective-permute-start | bytes 2359304 | tf_op jit(solution)/shard_map/ppermute | solution.py:27
  14.1 0.8 copy-start.4
  24.1 22.1 %collective-permute-start.6 = (bf16[2,1,256,256]{3,2,1,0:T(8,128)(2,1)S(1)}, bf16[2,1,256,256]{3,2,1,0:T(8,128)(2,1)S(1)}, u32[]{:S(2)}, u32[]{:S(2)}) collective-permute-start(bf16[2,1,256,256]{3,2,1,0:T(8,128)(2,1)S(1)} %get-tuple-element.60), channel_id=1, source_target_pairs={{0,3},{1,2},{2,1},{3,0},{4,7},{5,6},{6,5},{7,4},{8,11},{9,10},{10,... | collective-permute-start | bytes 786440 | tf_op jit(solution)/shard_map/ppermute | solution.py:27
  31.5 26.4 %collective-permute-start.7 = (bf16[2,128,1024]{2,1,0:T(8,128)(2,1)S(1)}, bf16[2,128,1024]{2,1,0:T(8,128)(2,1)S(1)}, u32[]{:S(2)}, u32[]{:S(2)}) collective-permute-start(bf16[2,128,1024]{2,1,0:T(8,128)(2,1)S(1)} %get-tuple-element.64), channel_id=1, source_target_pairs={{0,12},{4,8},{8,4},{12,0},{16,28},{20,24},{24,20},{28,16},{1,13},{... | collective-permute-start | bytes 1572872 | tf_op jit(solution)/shard_map/ppermute | solution.py:27
  32.1 25.8 %collective-permute-start.8 = (bf16[2,128,1024]{2,1,0:T(8,128)(2,1)S(1)}, bf16[2,128,1024]{2,1,0:T(8,128)(2,1)S(1)}, u32[]{:S(2)}, u32[]{:S(2)}) collective-permute-start(bf16[2,128,1024]{2,1,0:T(8,128)(2,1)S(1)} %get-tuple-element.66), channel_id=1, source_target_pairs={{0,20},{4,16},{8,28},{12,24},{16,4},{20,0},{24,12},{28,8},{1,21},{... | collective-permute-start | bytes 1572872 | tf_op jit(solution)/shard_map/ppermute | solution.py:27
  34.9 23.0 %collective-permute-start.9 = (bf16[2,128,1024]{2,1,0:T(8,128)(2,1)S(1)}, bf16[2,128,1024]{2,1,0:T(8,128)(2,1)S(1)}, u32[]{:S(2)}, u32[]{:S(2)}) collective-permute-start(bf16[2,128,1024]{2,1,0:T(8,128)(2,1)S(1)} %get-tuple-element.68), channel_id=1, source_target_pairs={{0,28},{4,24},{8,20},{12,16},{16,12},{20,8},{24,4},{28,0},{1,29},{... | collective-permute-start | bytes 1572872 | tf_op jit(solution)/shard_map/ppermute | solution.py:27
  50.2 19.9 %collective-permute-start.10 = (bf16[256,768]{1,0:T(8,128)(2,1)S(1)}, bf16[256,768]{1,0:T(8,128)(2,1)S(1)}, u32[]{:S(2)}, u32[]{:S(2)}) collective-permute-start(bf16[256,768]{1,0:T(8,128)(2,1)S(1)} %get-tuple-element.71), channel_id=1, source_target_pairs={{0,3},{1,2},{2,1},{3,0},{4,7},{5,6},{6,5},{7,4},{8,11},{9,10},{10,... | collective-permute-start | bytes 1179656 | tf_op jit(solution)/shard_map/ppermute | solution.py:27
  52.8 16.7 %collective-permute-start.18 = (bf16[256,768]{1,0:T(8,128)(2,1)S(1)}, bf16[256,768]{1,0:T(8,128)(2,1)S(1)}, u32[]{:S(2)}, u32[]{:S(2)}) collective-permute-start(bf16[256,768]{1,0:T(8,128)(2,1)S(1)} %get-tuple-element.61), channel_id=1, source_target_pairs={{0,1},{1,0},{2,3},{3,2},{4,5},{5,4},{6,7},{7,6},{8,9},{9,8},{10,11... | collective-permute-start | bytes 1179656 | tf_op jit(solution)/shard_map/ppermute | solution.py:27
  59.9 14.3 %collective-permute-start.12 = (bf16[128,1024]{1,0:T(8,128)(2,1)S(1)}, bf16[128,1024]{1,0:T(8,128)(2,1)S(1)}, u32[]{:S(2)}, u32[]{:S(2)}) collective-permute-start(bf16[128,1024]{1,0:T(8,128)(2,1)S(1)} %get-tuple-element.73), channel_id=1, source_target_pairs={{0,8},{4,12},{8,0},{12,4},{16,24},{20,28},{24,16},{28,20},{1,9},{5... | collective-permute-start | bytes 786440 | tf_op jit(solution)/shard_map/ppermute | solution.py:27
  61.4 14.4 %collective-permute-start.14 = (bf16[128,1024]{1,0:T(8,128)(2,1)S(1)}, bf16[128,1024]{1,0:T(8,128)(2,1)S(1)}, u32[]{:S(2)}, u32[]{:S(2)}) collective-permute-start(bf16[128,1024]{1,0:T(8,128)(2,1)S(1)} %get-tuple-element.78), channel_id=1, source_target_pairs={{0,16},{4,20},{8,24},{12,28},{16,0},{20,4},{24,8},{28,12},{1,17},{... | collective-permute-start | bytes 786440 | tf_op jit(solution)/shard_map/ppermute | solution.py:27
  62.9 14.0 %collective-permute-start.16 = (bf16[128,1024]{1,0:T(8,128)(2,1)S(1)}, bf16[128,1024]{1,0:T(8,128)(2,1)S(1)}, u32[]{:S(2)}, u32[]{:S(2)}) collective-permute-start(bf16[128,1024]{1,0:T(8,128)(2,1)S(1)} %get-tuple-element.81), channel_id=1, source_target_pairs={{0,24},{4,28},{8,16},{12,20},{16,8},{20,12},{24,0},{28,4},{1,25},{... | collective-permute-start | bytes 786440 | tf_op jit(solution)/shard_map/ppermute | solution.py:27
  69.5 20.4 %collective-permute-start.19 = (bf16[256,768]{1,0:T(8,128)(2,1)S(1)}, bf16[256,768]{1,0:T(8,128)(2,1)S(1)}, u32[]{:S(2)}, u32[]{:S(2)}) collective-permute-start(bf16[256,768]{1,0:T(8,128)(2,1)S(1)} %get-tuple-element.86), channel_id=1, source_target_pairs={{0,2},{1,3},{2,0},{3,1},{4,6},{5,7},{6,4},{7,5},{8,10},{9,11},{10,... | collective-permute-start | bytes 1179656 | tf_op jit(solution)/shard_map/ppermute | solution.py:27
  70.1 6.9 %collective-permute-start.11 = (bf16[128,1024]{1,0:T(8,128)(2,1)S(1)}, bf16[128,1024]{1,0:T(8,128)(2,1)S(1)}, u32[]{:S(2)}, u32[]{:S(2)}) collective-permute-start(bf16[128,1024]{1,0:T(8,128)(2,1)S(1)} %get-tuple-element.72), channel_id=1, source_target_pairs={{0,4},{4,0},{8,12},{12,8},{16,20},{20,16},{24,28},{28,24},{1,5},{5... | collective-permute-start | bytes 786440 | tf_op jit(solution)/shard_map/ppermute | solution.py:27
  74.2 8.3 %collective-permute-start.13 = (bf16[128,1024]{1,0:T(8,128)(2,1)S(1)}, bf16[128,1024]{1,0:T(8,128)(2,1)S(1)}, u32[]{:S(2)}, u32[]{:S(2)}) collective-permute-start(bf16[128,1024]{1,0:T(8,128)(2,1)S(1)} %get-tuple-element.77), channel_id=1, source_target_pairs={{0,12},{4,8},{8,4},{12,0},{16,28},{20,24},{24,20},{28,16},{1,13},{... | collective-permute-start | bytes 786440 | tf_op jit(solution)/shard_map/ppermute | solution.py:27
  75.8 14.0 %collective-permute-start.15 = (bf16[128,1024]{1,0:T(8,128)(2,1)S(1)}, bf16[128,1024]{1,0:T(8,128)(2,1)S(1)}, u32[]{:S(2)}, u32[]{:S(2)}) collective-permute-start(bf16[128,1024]{1,0:T(8,128)(2,1)S(1)} %get-tuple-element.80), channel_id=1, source_target_pairs={{0,20},{4,16},{8,28},{12,24},{16,4},{20,0},{24,12},{28,8},{1,21},{... | collective-permute-start | bytes 786440 | tf_op jit(solution)/shard_map/ppermute | solution.py:27
  77.0 12.9 %collective-permute-start.17 = (bf16[128,1024]{1,0:T(8,128)(2,1)S(1)}, bf16[128,1024]{1,0:T(8,128)(2,1)S(1)}, u32[]{:S(2)}, u32[]{:S(2)}) collective-permute-start(bf16[128,1024]{1,0:T(8,128)(2,1)S(1)} %get-tuple-element.83), channel_id=1, source_target_pairs={{0,28},{4,24},{8,20},{12,16},{16,12},{20,8},{24,4},{28,0},{1,29},{... | collective-permute-start | bytes 786440 | tf_op jit(solution)/shard_map/ppermute | solution.py:27

commit v6 on v5

--- a/solution.py
+++ b/solution.py
@@ -85,19 +85,37 @@
                 turned_ref[q, top : top + tall, start : start + height] = total
 
 
+def own_rows(place, sizes_ref, occ_ref, eta_ref, gamma_ref, full_refs, scale_ref):
+    tiles, rows, _ = eta_ref.shape
+    weight = free_weight(occ_ref, place, sizes_ref[place])
+    scale_ref[1:2, :] = weight
+    for k in range(tiles):
+        column, later = aligned((place ^ k) * rows, rows), slice(k * rows, (k + 1) * rows)
+        scale_ref[0:1, later] = scale_ref[1:2, column]
+        for n, source_ref in enumerate((eta_ref, gamma_ref)):
+            block = source_ref[place, :, column]
+            full_refs[n][0:rows, later] = block
+            if k:
+                full_refs[n][later, 0:rows] = block.T if n else -block.T
+
+
 def prepare_whole_kernel(ph_count, states, order, *refs):
-    prepare_kernel(ph_count, states, order, *refs[:4], *refs[-3:-1])
-    diagonal_blocks(*refs[4:-3], refs[-1])
-
-
-def prepare(me, order, recouple_map, recoupled_occupation, recouple_weights, *pair):
+    place_ref, refs = refs[0], refs[1:]
+    prepare_kernel(ph_count, states, order, *refs[:4], *refs[8:10])
+    diagonal_blocks(*refs[4:8], refs[10])
+    own_rows(place_ref[0], *refs[4:8], refs[11:13], refs[13])
+
+
+def prepare(me, order, recouple_map, recoupled_occupation, recouple_weights, place=None, *pair):
     ph_count, states = recouple_map.shape
-    kernel, extra = prepare_kernel, ()
+    kernel, extra, lead = prepare_kernel, [], []
     flops = 6 * ph_count * states**3
     if pair:
         chan_count, rows, columns = pair[-1].shape
-        kernel = prepare_whole_kernel
-        extra = (jax.ShapeDtypeStruct((chan_count, rows, rows), F32),)
+        kernel, lead = prepare_whole_kernel, [place]
+        extra = [jax.ShapeDtypeStruct((chan_count, rows, rows), F32)]
+        extra += [jax.ShapeDtypeStruct((columns, columns), BF16)] * 2
+        extra += [jax.ShapeDtypeStruct((8, columns), F32)]
         flops += 4 * chan_count * rows * rows * columns
     return pl.pallas_call(
         functools.partial(kernel, ph_count, states, order),
@@ -106,12 +124,15 @@
             jax.ShapeDtypeStruct(recouple_weights.shape, BF16),
             *extra,
         ),
-        in_specs=[SMEM] + [VMEM] * 3 + [SMEM] * bool(pair) + [VMEM] * len(pair[1:]),
+        in_specs=[SMEM] * (len(lead) + 1)
+        + [VMEM] * 3
+        + [SMEM] * bool(pair)
+        + [VMEM] * len(pair[1:]),
         out_specs=(VMEM,) * (2 + len(extra)),
         compiler_params=params(12),
         cost_estimate=cost(flops, 14 * ph_count * states**2),
         name="prepare",
-    )(me, recouple_map, recoupled_occupation, recouple_weights, *pair)
+    )(*lead, me, recouple_map, recoupled_occupation, recouple_weights, *pair)
 
 
 def weigh_blocks(states, order, me, turned_ref, recv_refs, bar_ref):
@@ -142,7 +163,7 @@
 
 
 def store_blocks(states, order, me, q, top, crossed, turned_ref, out_refs):
-    rows = out_refs[0].shape[0]
+    rows = next(iter(out_refs.values())).shape[0]
     step = min(rows, crossed.shape[0])
     for base in range(0, crossed.shape[0], step):
         slot, inside = divmod(top + base, rows)
@@ -179,46 +200,62 @@
     )(me, turned, select, *received)
 
 
-def cross_first_kernel(states, order, me_ref, turned_ref, left_ref, part_ref, *rest):
+def cross_first_kernel(states, order, slots, fresh, me_ref, turned_ref, left_ref, part_ref, *rest):
     first, second = order
-    recv_refs, out_refs = rest[: len(second)], rest[len(second) : len(second) + len(first)]
-    if second:
-        weigh_blocks(states, second, me_ref[0], turned_ref, recv_refs, rest[-1])
+    recv_refs, rest = (rest[: len(second)], rest[len(second) :]) if fresh else ((), rest)
+    bar_ref, outs = (rest[-1], rest[: len(slots)]) if fresh else (rest[0], rest[1:])
+    if not second:
+        outs = rest
+    out_refs = dict(zip(slots, outs))
+    if second and fresh:
+        weigh_blocks(states, second, me_ref[0], turned_ref, recv_refs, bar_ref)
+    rows = outs[0].shape[0]
+    runs = []
+    for slot in slots:
+        if runs and runs[-1][1] == slot * rows and runs[-1][1] - runs[-1][0] < 256:
+            runs[-1][1] += rows
+        else:
+            runs.append([slot * rows, (slot + 1) * rows])
     for q in range(turned_ref.shape[0]):
-        for top, height in row_tiles(left_ref.shape[2]):
-            span = slice(top, top + height)
-            crossed = part_ref[q, span, :]
-            if second:
-                inner = slice(left_ref.shape[2], states)
-                crossed += cross_rows(q, span, inner, left_ref, rest[-1])
-            store_blocks(states, first, me_ref[0], q, top, crossed, turned_ref, out_refs)
-
-
-def cross_first(me, order, turned, left, part, received, flat):
+        for start, stop in runs:
+            for top, height in row_tiles(stop - start):
+                span = slice(start + top, start + top + height)
+                crossed = part_ref[q, span, :]
+                if second:
+                    inner = slice(left_ref.shape[2], states)
+                    crossed += cross_rows(q, span, inner, left_ref, bar_ref)
+                store_blocks(
+                    states, first, me_ref[0], q, start + top, crossed, turned_ref, out_refs
+                )
+
+
+def cross_first(me, order, slots, turned, left, part, received, second_bar, flat):
     ph_count, states, _ = turned.shape
     first, second = order
+    fresh = second_bar is None
     blocks = len(first) + len(second)
-    out_shape = [jax.ShapeDtypeStruct((flat[0] // blocks, flat[1]), BF16)] * len(first)
-    if second:
+    out_shape = [jax.ShapeDtypeStruct((flat[0] // blocks, flat[1]), BF16)] * len(slots)
+    if second and fresh:
         out_shape.append(
             jax.ShapeDtypeStruct((2, ph_count, states - left.shape[2], states), BF16)
         )
+    operands = received if fresh else [second_bar]
     out = pl.pallas_call(
-        functools.partial(cross_first_kernel, states, order),
+        functools.partial(cross_first_kernel, states, order, slots, fresh),
         out_shape=out_shape,
-        in_specs=[SMEM] + [VMEM] * (3 + len(second)),
+        in_specs=[SMEM] + [VMEM] * (3 + len(operands)),
         out_specs=[VMEM] * len(out_shape),
         compiler_params=params(8),
-        cost_estimate=cost(2 * ph_count * states**3, 14 * ph_count * states**2),
+        cost_estimate=cost(ph_count * states**3, 7 * ph_count * states**2),
         name="cross_first",
-    )(me, turned, left, part, *received)
-    return out[: len(first)], out[-1]
+    )(me, turned, left, part, *operands)
+    return out[: len(slots)], out[-1]
 
 
 def cross_second_kernel(
     states, order, me_ref, turned_ref, select_ref, bar_ref, second_bar_ref, *rest
 ):
-    out_refs, left_ref = rest[:-1], rest[-1]
+    out_refs, left_ref = dict(enumerate(rest[:-1])), rest[-1]
     turn_blocks(select_ref, second_bar_ref, left_ref)
     middle = bar_ref.shape[2]
     for q in range(turned_ref.shape[0]):
@@ -299,27 +336,11 @@
     return dict(zip(partners, out)), dict(zip(steps, out[len(partners) :]))
 
 
-def ladder_kernel(tiles, rows, place_ref, sizes_ref, occ_ref, eta_ref, gamma_ref, *rest):
+def ladder_kernel(tiles, rows, eta_ref, gamma_ref, scale_ref, *rest):
     packed_refs = rest[: tiles - 1]
-    out_refs = rest[tiles - 1 : 2 * tiles - 1]
-    eta, gamma, weight, sems = rest[2 * tiles - 1 :]
-    place = place_ref[0]
-    copies = []
-    for source, full in ((eta_ref, eta), (gamma_ref, gamma)):
-        for k in range(tiles):
-            copies.append(
-                pltpu.make_async_copy(
-                    source.at[place, :, aligned((place ^ k) * rows, rows)],
-                    full.at[0:rows, k * rows : (k + 1) * rows],
-                    sems.at[len(copies)],
-                )
-            )
-    for copy in copies:
-        copy.start()
-    weight[...] = free_weight(occ_ref, place, sizes_ref[place])
-    scale = jnp.concatenate(
-        [weight[:, aligned((place ^ k) * rows, rows)] for k in range(tiles)], axis=1
-    ).astype(BF16)
+    out_refs, (eta, gamma) = rest[tiles - 1 : -2], rest[-2:]
+    del eta_ref, gamma_ref
+    scale = scale_ref[0:1, :].astype(BF16)
     for k in range(1, tiles):
         for n, full in enumerate((eta, gamma)):
             for m, other in enumerate(range(k, tiles)):
@@ -328,12 +349,6 @@
                 full[here, there] = block
                 if other > k:
                     full[there, here] = block.T if n else -block.T
-    for copy in copies:
-        copy.wait()
-    for other in range(1, tiles):
-        here, there = slice(0, rows), slice(other * rows, (other + 1) * rows)
-        eta[there, here] = -eta[here, there].T
-        gamma[there, here] = gamma[here, there].T
     for k in reversed(range(tiles - 1)):
         here, later = slice(k * rows, (k + 1) * rows), slice((k + 1) * rows, tiles * rows)
         total = jnp.dot(eta[here, :] * scale, gamma[:, later], preferred_element_type=F32)
@@ -346,23 +361,22 @@
             out_refs[other][:, column] = block.T
 
 
-def ladder_blocks(place, sizes, pair_occupation, eta, gamma, packed):
-    tiles, rows, states = eta.shape
-    return pl.pallas_call(
+def ladder_blocks(eta, gamma, scale, packed):
+    states = eta.shape[0]
+    tiles = len(packed) + 1
+    rows = states // tiles
+    full = jax.ShapeDtypeStruct(eta.shape, BF16)
+    out = pl.pallas_call(
         functools.partial(ladder_kernel, tiles, rows),
-        out_shape=[jax.ShapeDtypeStruct((rows, states - rows), BF16)] * tiles,
-        in_specs=[SMEM, SMEM, VMEM, HBM, HBM] + [VMEM] * (tiles - 1),
-        out_specs=[VMEM] * tiles,
-        scratch_shapes=[
-            pltpu.VMEM((states, states), BF16),
-            pltpu.VMEM((states, states), BF16),
-            pltpu.VMEM((1, states), F32),
-            pltpu.SemaphoreType.DMA((2 * tiles,)),
-        ],
-        compiler_params=params(12),
+        out_shape=[jax.ShapeDtypeStruct((rows, states - rows), BF16)] * tiles + [full] * 2,
+        in_specs=[VMEM] * (2 + tiles),
+        out_specs=[VMEM] * (tiles + 2),
+        input_output_aliases={0: tiles, 1: tiles + 1},
+        compiler_params=params(8),
         cost_estimate=cost(2 * states**3, 8 * states**2),
         name="ladder",
-    )(place, sizes, pair_occupation, eta, gamma, *packed)
+    )(eta, gamma, scale, *packed)
+    return out[:tiles]
 
 
 def finish_kernel(blocks, me_ref, place_ref, sizes_ref, diagonal_ref, *rest):
@@ -375,16 +389,20 @@
         back[aligned((me_ref[0] ^ d) * rows, rows), :] = back_ref[...]
     row = lax.broadcasted_iota(jnp.int32, (tile_rows, tile_rows), 0) + place * tile_rows
     column = lax.broadcasted_iota(jnp.int32, (tile_rows, tile_rows), 1)
+    starts = [(place ^ m) * tile_rows for m in range(len(ladder_refs))]
+    highest = [jnp.maximum(row, column + start) for start in starts]
     copies = []
     for k, ladder_ref in enumerate(ladder_refs):
         c = place ^ k
-        for m in range(len(ladder_refs)):
-            ladder = ladder_ref[:, (m - 1) * tile_rows : m * tile_rows] if m else diagonal_ref[c]
-            start = (place ^ m) * tile_rows
+        size = sizes_ref[c]
+        for m, start in enumerate(starts):
             span = aligned(start, tile_rows)
-            total = ladder.astype(F32) + back[aligned(c * tile_rows, tile_rows), span].astype(F32)
-            live = jnp.maximum(row, column + start) < sizes_ref[c]
-            held[c, :, span] = jnp.where(live, total, 0.0).astype(BF16)
+            part = back[aligned(c * tile_rows, tile_rows), span]
+            if m:
+                total = ladder_ref[:, (m - 1) * tile_rows : m * tile_rows] + part
+            else:
+                total = (diagonal_ref[c] + part.astype(F32)).astype(BF16)
+            held[c, :, span] = jnp.where(highest[m] < size, total, jnp.zeros_like(total))
         copies.append(pltpu.make_async_copy(held.at[c], out_ref.at[c], sems.at[k]))
         copies[-1].start()
     for copy in copies:
@@ -425,16 +443,16 @@
 
 WAITS = {
     "lack1": ("in1",),
-    "lack3": ("in2", "prepare"),
-    "in3": ("in2", "prepare"),
-    "in5": ("in4", "prepare"),
-    "in7": ("in6", "prepare"),
+    "lack3": ("in2", "prepare",),
+    "in3": ("in2", "prepare",),
+    "in5": ("in4", "prepare",),
+    "in7": ("in6", "prepare",),
     "cross_first": ("ladder",),
-    "own2": ("own1",),
+    "own2": ("own1", "cross_second",),
     "back1": ("own3",),
     "back3": ("back2",),
     "back5": ("back4",),
-    "back7": ("back6", "back1"),
+    "back7": ("back6", "back1",),
 }
 
 
@@ -458,9 +476,10 @@
     "own2",
     "own3",
     "cross_first",
-    "back1",
     "back2",
     "back4",
+    "cross_next",
+    "back1",
     "back6",
     "cross_second",
     "back3",
@@ -504,6 +523,8 @@
         return xor_permute(message, "tile", tiles, k)
 
     first, second = order = block_order(chans)
+    sooner = [slot for slot, d in enumerate(first) if d in (2, 4)]
+    later = [slot for slot in range(len(first)) if slot not in sooner]
     near = first[1:]
     late = [d for d in range(chans) if d not in near]
     pair = (generator, hamiltonian)
@@ -530,22 +551,31 @@
         return xor_permute(held(name, block), "tile", tiles, k) if k else block
 
     def make_first():
-        turned, select, _ = value("prepare")
+        turned, select, *_ = value("prepare")
         received = held("first", [value(f"in{d}") for d in first])
         return first_part(me, first, turned, select, received)
 
     def make_ladder():
         lacking = held("ladder", [value(f"lack{k}") for k in steps])
-        return ladder_blocks(place, chan_sizes, pair_occupation, *pair, lacking)
+        return ladder_blocks(*value("prepare")[3:], lacking)
+
+    def make_cross_next():
+        _, left, part = value("first")
+        second_bar = held("cross_next", value("cross_first")[1])
+        return cross_first(
+            me, order, later, value("prepare")[0], left, part, [], second_bar, flat
+        )
 
     def make_cross_first():
         _, left, part = value("first")
         part = held("cross_first", part)
         received = [value(f"in{d}") for d in second]
-        return cross_first(me, order, value("prepare")[0], left, part, received, flat)
+        return cross_first(
+            me, order, sooner, value("prepare")[0], left, part, received, None, flat
+        )
 
     def make_cross_second():
-        turned, select, _ = value("prepare")
+        turned, select, *_ = value("prepare")
         bar, second_bar = held("cross_second", (value("first")[0], value("cross_first")[1]))
         return cross_second(me, second, turned, select, bar, second_bar, flat, chans)
 
@@ -558,6 +588,7 @@
             recouple_map,
             recoupled_occupation,
             recouple_weights,
+            place,
             chan_sizes,
             pair_occupation,
             *pair,
@@ -565,16 +596,21 @@
         "first": make_first,
         "ladder": make_ladder,
         "cross_first": make_cross_first,
+        "cross_next": make_cross_next,
         "cross_second": make_cross_second,
     }
     for d in range(chans):
         source = "pack_near" if d in near else "pack_late"
         make[f"in{d}"] = lambda d=d, s=source: to_chan(f"in{d}", value(s)[0][d], d)
-        group, place_in, blocks = (
-            ("cross_first", first.index(d), 0) if d in first else ("cross_second", second.index(d), 1)
-        )
-        make[f"back{d}"] = lambda d=d, g=group, i=place_in, b=blocks: to_chan(
-            f"back{d}", (value(g) if b else value(g)[0])[i], d
+        if d in second:
+            make[f"back{d}"] = lambda d=d: to_chan(
+                f"back{d}", value("cross_second")[second.index(d)], d
+            )
+            continue
+        slot = first.index(d)
+        group, slots = ("cross_first", sooner) if slot in sooner else ("cross_next", later)
+        make[f"back{d}"] = lambda d=d, g=group, i=slots.index(slot): to_chan(
+            f"back{d}", value(g)[0][i], d
         )
     for k in range(tiles):
         source = "pack_near" if k in steps[1:2] else "pack_late"
@@ -612,7 +648,7 @@
         alone, order[0], recouple_map, recoupled_occupation, recouple_weights
     )
     _, left, part = first_part(alone, order[0], turned, select, [received])
-    sent, _ = cross_first(alone, order, turned, left, part, [], flat)
+    sent, _ = cross_first(alone, order, [0], turned, left, part, [], None, flat)
     back = lax.all_to_all(sent[0], "chan", 0, 0, tiled=True).reshape(generator.shape)
     ladder = ladder_gathered(chan_sizes, pair_occupation, generator, hamiltonian)
     return jnp.where(live, ladder + back.astype(F32), 0.0).astype(BF16)

time: 92.9 us -> 91 us (0.980)
  Pallas kernels: 30.4 us -> 29.2 us
    pallas_call x1, Pallas kernels: 3.24 us -> 1.99 us  [ladder_blocks(): pl.pallas_call(functools.partial(ladder_kernel, tiles, rows), out_shape=[...]
    pallas_call x1 -> x2, Pallas kernels: 1.96 us -> 2.07 us  [cross_first(): pl.pallas_call(functools.partial(cross_first_kernel, states, order, slots...]
  transfers between devices with their start and end apart: 20 -> 20, of which waited for: 8 -> 11; matrix products, arithmetic and copies ran while one was open for 0% -> 0% of each run, Pallas kernels for 27% -> 27%
where the time goes in v6:
time: 91 us; the launch traced here: 90.8 us
  waiting for transfers between devices  39 us (43%)
  Pallas kernels  29.2 us (32%)
  starting transfers between devices  20.8 us (23%)
  local copies, waits for them, and re-layouts  1.43 us (2%)
    ppermute x20, waiting for transfers between devices, xor_permute(): return lax.ppermute(block, axis, [(i, i ^ step) for i in range(size)])  39 us
    ppermute x20, starting transfers between devices, xor_permute(): return lax.ppermute(block, axis, [(i, i ^ step) for i in range(size)])  20.8 us
    pallas_call x1, Pallas kernels, prepare(): pl.pallas_call(functools.partial(kernel, ph_count, states, order), out_sh...  9.28 us
    pallas_call x1, Pallas kernels, first_part(): pl.pallas_call(functools.partial(first_kernel, states, order), out_shape=...  5.26 us
    pallas_call x2, Pallas kernels, pack(): pl.pallas_call(functools.partial(pack_kernel, eta.shape, blocks, tiles, p...  4.19 us
    pallas_call x1, Pallas kernels, cross_second(): pl.pallas_call(functools.partial(cross_second_kernel, states, order), out...  4.13 us
    pallas_call x1, Pallas kernels, finish(): pl.pallas_call(functools.partial(finish_kernel, len(back)), out_shape=jax...  2.34 us
    pallas_call x2, Pallas kernels, cross_first(): pl.pallas_call(functools.partial(cross_first_kernel, states, order, slots...  2.07 us
  transfers between devices with their start and end apart: 20, of which 11 were waited for; matrix products, arithmetic and copies ran while one was open for 0% of the time, Pallas kernels for 27%

profile of v6, /device:TPU:0, one launch (start us, length us, event | category | flops | bytes accessed | tf_op | source)
XLA Modules:
  0.0 90.8 jit_solution(14875716409957950015)
XLA Ops:
  0.0 0.7 copy-done.2
  0.7 2.6 %pack.3 = (bf16[2,128,1024]{2,1,0:T(8,128)(2,1)S(1)}, bf16[2,128,1024]{2,1,0:T(8,128)(2,1)S(1)}, bf16[2,128,1024]{2,1,0:T(8,128)(2,1)S(1)}, bf16[2,128,1024]{2,1...) custom-call(s32[1]{0:T(128)} %bitcast.refs_1_.me_ref, s32[1]{0:T(128)} %bitcast.1.refs_0_.place_ref, s32[4]{0:T(128)S(1)} %copy-done.2, ...), custom_call_target="tpu_custom_call" | custom-call | bytes 4194304 | tf_op jit(solution)/shard_map/pack/pallas_call | solution.py:323
  3.8 2.6 %collective-permute-start.1 = (bf16[2,128,1024]{2,1,0:T(8,128)(2,1)S(1)}, bf16[2,128,1024]{2,1,0:T(8,128)(2,1)S(1)}, u32[]{:S(2)}, u32[]{:S(2)}) collective-permute-start(bf16[2,128,1024]{2,1,0:T(8,128)(2,1)S(1)} %get-tuple-element.54), channel_id=1, source_target_pairs={{0,8},{4,12},{8,0},{12,4},{16,24},{20,28},{24,16},{28,20},{1,9},{5... | collective-permute-start | bytes 1572872 | tf_op jit(solution)/shard_map/ppermute | solution.py:27
  6.3 1.5 %collective-permute-start.2 = (bf16[2,128,1024]{2,1,0:T(8,128)(2,1)S(1)}, bf16[2,128,1024]{2,1,0:T(8,128)(2,1)S(1)}, u32[]{:S(2)}, u32[]{:S(2)}) collective-permute-start(bf16[2,128,1024]{2,1,0:T(8,128)(2,1)S(1)} %get-tuple-element.55), channel_id=1, source_target_pairs={{0,16},{4,20},{8,24},{12,28},{16,0},{20,4},{24,8},{28,12},{1,17},{... | collective-permute-start | bytes 1572872 | tf_op jit(solution)/shard_map/ppermute | solution.py:27
  7.9 3.0 %collective-permute-start.5 = (bf16[2,2,256,256]{3,2,1,0:T(8,128)(2,1)S(1)}, bf16[2,2,256,256]{3,2,1,0:T(8,128)(2,1)S(1)}, u32[]{:S(2)}, u32[]{:S(2)}) collective-permute-start(bf16[2,2,256,256]{3,2,1,0:T(8,128)(2,1)S(1)} %get-tuple-element.64), channel_id=1, source_target_pairs={{0,2},{1,3},{2,0},{3,1},{4,6},{5,7},{6,4},{7,5},{8,10},{9,11},{10,... | collective-permute-start | bytes 1572872 | tf_op jit(solution)/shard_map/ppermute | solution.py:27
  10.9 1.6 %pack.2 = (bf16[2,128,1024]{2,1,0:T(8,128)(2,1)S(1)}, bf16[2,128,1024]{2,1,0:T(8,128)(2,1)S(1)}, bf16[2,128,1024]{2,1,0:T(8,128)(2,1)S(1)}, bf16[2,128,1024]{2,1...) custom-call(s32[1]{0:T(128)} %bitcast.refs_1_.me_ref, ...), custom_call_target="tpu_custom_call" | custom-call | bytes 4194304 | tf_op jit(solution)/shard_map/pack/pallas_call | solution.py:323
  12.6 1.6 %collective-permute-start.4 = (bf16[2,3,256,256]{3,2,1,0:T(8,128)(2,1)S(1)}, bf16[2,3,256,256]{3,2,1,0:T(8,128)(2,1)S(1)}, u32[]{:S(2)}, u32[]{:S(2)}) collective-permute-start(bf16[2,3,256,256]{3,2,1,0:T(8,128)(2,1)S(1)} %get-tuple-element.63), channel_id=1, source_target_pairs={{0,1},{1,0},{2,3},{3,2},{4,5},{5,4},{6,7},{7,6},{8,9},{9,8},{10,11... | collective-permute-start | bytes 2359304 | tf_op jit(solution)/shard_map/ppermute | solution.py:27
  14.2 0.8 copy-done.4
  15.0 9.3 %prepare.1 = (f32[1,1024,1024]{2,1,0:T(8,128)S(1)}, bf16[1,1024,1024]{2,1,0:T(8,128)(2,1)S(1)}, f32[4,256,256]{2,1,0:T(8,128)S(1)}, bf16[1024,1024]{1,0:T(8,128)...) custom-call(s32[1]{0:T(128)} %bitcast.1.refs_0_.place_ref, s32[1]{0:T(128)} %bitcast.refs_1_.me_ref, ...), custom_call_target="tpu_custom_call" | custom-call | flops 7516192768 | bytes 14680064 | tf_op jit(solution)/shard_map/prepare/pallas_call | solution.py:120
  24.3 7.1 %collective-permute-done.3.rest_4_ = bf16[2,128,1024]{2,1,0:T(8,128)(2,1)S(1)} collective-permute-done((bf16[2,128,1024]{2,1,0:T(8,128)(2,1)S(1)}, bf16[2,128,1024]{2,1,0:T(8,128)(2,1)S(1)}, u32[]{:S(2)}, u32[]{:S(2)}) %collective-permute-start.3) | collective-permute-done | bytes 524320 | tf_op jit(solution)/shard_map/ppermute | solution.py:27
  32.1 1.3 %collective-permute-start.8 = (bf16[2,128,1024]{2,1,0:T(8,128)(2,1)S(1)}, bf16[2,128,1024]{2,1,0:T(8,128)(2,1)S(1)}, u32[]{:S(2)}, u32[]{:S(2)}) collective-permute-start(bf16[2,128,1024]{2,1,0:T(8,128)(2,1)S(1)} %get-tuple-element.72), channel_id=1, source_target_pairs={{0,20},{4,16},{8,28},{12,24},{16,4},{20,0},{24,12},{28,8},{1,21},{... | collective-permute-start | bytes 1572872 | tf_op jit(solution)/shard_map/ppermute | solution.py:27
  33.3 1.6 %collective-permute-done.5.rest_1_ = bf16[2,2,256,256]{3,2,1,0:T(8,128)(2,1)S(1)} collective-permute-done((bf16[2,2,256,256]{3,2,1,0:T(8,128)(2,1)S(1)}, bf16[2,2,256,256]{3,2,1,0:T(8,128)(2,1)S(1)}, u32[]{:S(2)}, u32[]{:S(2)}) %collective-permute-start.5) | collective-permute-done | bytes 524320 | tf_op jit(solution)/shard_map/ppermute | solution.py:27
  35.0 11.3 %collective-permute-done.6.rest_2_ = bf16[2,1,256,256]{3,2,1,0:T(8,128)(2,1)S(1)} collective-permute-done((bf16[2,1,256,256]{3,2,1,0:T(8,128)(2,1)S(1)}, bf16[2,1,256,256]{3,2,1,0:T(8,128)(2,1)S(1)}, u32[]{:S(2)}, u32[]{:S(2)}) %collective-permute-start.6) | collective-permute-done | bytes 262176 | tf_op jit(solution)/shard_map/ppermute | solution.py:27
  46.3 0.8 collective-permute-done.4.rest_0_
  47.1 2.0 %ladder.1 = (bf16[256,768]{1,0:T(8,128)(2,1)S(1)}, bf16[256,768]{1,0:T(8,128)(2,1)S(1)}, bf16[256,768]{1,0:T(8,128)(2,1)S(1)}, bf16[256,768]{1,0:T(8,128)(2,1)S(...) custom-call(bf16[1024,1024]{1,0:T(8,128)(2,1)S(1)} %get-tuple-elemen, ...), custom_call_target="tpu_custom_call", output_to_operand_aliasing={{4}: (0, {}), {5}: (1, {})} | custom-call | flops 2147483648 | bytes 8388608 | tf_op jit(solution)/shard_map/ladder/pallas_call | solution.py:369
  49.1 2.5 %collective-permute-start.10 = (bf16[256,768]{1,0:T(8,128)(2,1)S(1)}, bf16[256,768]{1,0:T(8,128)(2,1)S(1)}, u32[]{:S(2)}, u32[]{:S(2)}) collective-permute-start(bf16[256,768]{1,0:T(8,128)(2,1)S(1)} %get-tuple-element.78), channel_id=1, source_target_pairs={{0,3},{1,2},{2,1},{3,0},{4,7},{5,6},{6,5},{7,4},{8,11},{9,10},{10,... | collective-permute-start | bytes 1179656 | tf_op jit(solution)/shard_map/ppermute | solution.py:27
  51.6 5.3 %first_part.1 = (bf16[2,1,640,1024]{3,2,1,0:T(8,128)(2,1)S(1)}, bf16[2,1,640,1024]{3,2,1,0:T(8,128)(2,1)S(1)}, f32[1,640,1024]{2,1,0:T(8,128)S(1)}) custom-call(s32[1]{0:T(128)} %bitcast.refs_1_.me_ref, f32[1,1024,1024]{2,1,0:T(8,128)S(1)} %get-tuple-element.50.turned_ref, bf16[1,1024,1024]{2,1,0:T(8,128)(2,1)S(1)} %get-tuple-element.51.select_ref, ...), custom_call_target="tpu_custom_call" | custom-call | flops 5368709120 | bytes 14680064 | tf_op jit(solution)/shard_map/first_part/pallas_call | solution.py:192
  57.5 0.9 cross_first.2
  58.4 1.0 %collective-permute-start.12 = (bf16[128,1024]{1,0:T(8,128)(2,1)S(1)}, bf16[128,1024]{1,0:T(8,128)(2,1)S(1)}, u32[]{:S(2)}, u32[]{:S(2)}) collective-permute-start(bf16[128,1024]{1,0:T(8,128)(2,1)S(1)} %get-tuple-element.80), channel_id=1, source_target_pairs={{0,8},{4,12},{8,0},{12,4},{16,24},{20,28},{24,16},{28,20},{1,9},{5... | collective-permute-start | bytes 786440 | tf_op jit(solution)/shard_map/ppermute | solution.py:27
  59.5 1.5 %collective-permute-start.14 = (bf16[128,1024]{1,0:T(8,128)(2,1)S(1)}, bf16[128,1024]{1,0:T(8,128)(2,1)S(1)}, u32[]{:S(2)}, u32[]{:S(2)}) collective-permute-start(bf16[128,1024]{1,0:T(8,128)(2,1)S(1)} %get-tuple-element.84), channel_id=1, source_target_pairs={{0,16},{4,20},{8,24},{12,28},{16,0},{20,4},{24,8},{28,12},{1,17},{... | collective-permute-start | bytes 786440 | tf_op jit(solution)/shard_map/ppermute | solution.py:27
  60.9 1.2 %cross_first.3 = (bf16[128,1024]{1,0:T(8,128)(2,1)S(1)}, bf16[128,1024]{1,0:T(8,128)(2,1)S(1)}, bf16[128,1024]{1,0:T(8,128)(2,1)S(1)}) custom-call(s32[1]{0:T(128)} %bitcast.refs_1_.me_ref, f32[1,1024,1024]{2,1,0:T(8,128)S(1)} %get-tuple-element.50.turned_ref, bf16[2,1,640,1024]{3,2,1,0:T(8,128)(2,1)S(1)} %get-tuple-element.57.left_ref, ...), custom_call_target="tpu_custom_call" | custom-call | flops 1073741824 | bytes 7340032 | tf_op jit(solution)/shard_map/cross_first/pallas_call | solution.py:243
  62.1 1.1 %collective-permute-start.16 = (bf16[128,1024]{1,0:T(8,128)(2,1)S(1)}, bf16[128,1024]{1,0:T(8,128)(2,1)S(1)}, u32[]{:S(2)}, u32[]{:S(2)}) collective-permute-start(bf16[128,1024]{1,0:T(8,128)(2,1)S(1)} %get-tuple-element.87), channel_id=1, source_target_pairs={{0,24},{4,28},{8,16},{12,20},{16,8},{20,12},{24,0},{28,4},{1,25},{... | collective-permute-start | bytes 786440 | tf_op jit(solution)/shard_map/ppermute | solution.py:27
  63.2 4.1 %cross_second.1 = (bf16[128,1024]{1,0:T(8,128)(2,1)S(1)}, bf16[128,1024]{1,0:T(8,128)(2,1)S(1)}, bf16[128,1024]{1,0:T(8,128)(2,1)S(1)}) custom-call(s32[1]{0:T(128)} %bitcast.refs_1_.me_ref, f32[1,1024,1024]{2,1,0:T(8,128)S(1)} %get-tuple-element.50.turned_ref, bf16[1,1024,1024]{2,1,0:T(8,128)(2,1)S(1)} %get-tuple-element.51.select_ref, ...), custom_call_target="tpu_custom_call" | custom-call | flops 4294967296 | bytes 14680064 | tf_op jit(solution)/shard_map/cross_second/pallas_call | solution.py:271
  67.4 1.1 %collective-permute-done.18.rest_9_ = bf16[256,768]{1,0:T(8,128)(2,1)S(1)} collective-permute-done((bf16[256,768]{1,0:T(8,128)(2,1)S(1)}, bf16[256,768]{1,0:T(8,128)(2,1)S(1)}, u32[]{:S(2)}, u32[]{:S(2)}) %collective-permute-start.18) | collective-permute-done | bytes 393248 | tf_op jit(solution)/shard_map/ppermute | solution.py:27
  68.4 1.6 %collective-permute-start.19 = (bf16[256,768]{1,0:T(8,128)(2,1)S(1)}, bf16[256,768]{1,0:T(8,128)(2,1)S(1)}, u32[]{:S(2)}, u32[]{:S(2)}) collective-permute-start(bf16[256,768]{1,0:T(8,128)(2,1)S(1)} %get-tuple-element.92), channel_id=1, source_target_pairs={{0,2},{1,3},{2,0},{3,1},{4,6},{5,7},{6,4},{7,5},{8,10},{9,11},{10,... | collective-permute-start | bytes 1179656 | tf_op jit(solution)/shard_map/ppermute | solution.py:27
  70.0 1.1 %collective-permute-start.13 = (bf16[128,1024]{1,0:T(8,128)(2,1)S(1)}, bf16[128,1024]{1,0:T(8,128)(2,1)S(1)}, u32[]{:S(2)}, u32[]{:S(2)}) collective-permute-start(bf16[128,1024]{1,0:T(8,128)(2,1)S(1)} %get-tuple-element.83), channel_id=1, source_target_pairs={{0,12},{4,8},{8,4},{12,0},{16,28},{20,24},{24,20},{28,16},{1,13},{... | collective-permute-start | bytes 786440 | tf_op jit(solution)/shard_map/ppermute | solution.py:27
  71.1 2.1 %collective-permute-done.14.rest_4_ = bf16[128,1024]{1,0:T(8,128)(2,1)S(1)} collective-permute-done((bf16[128,1024]{1,0:T(8,128)(2,1)S(1)}, bf16[128,1024]{1,0:T(8,128)(2,1)S(1)}, u32[]{:S(2)}, u32[]{:S(2)}) %collective-permute-start.14) | collective-permute-done | bytes 262176 | tf_op jit(solution)/shard_map/ppermute | solution.py:27
  73.2 0.8 collective-permute-start.17
  74.0 4.4 %collective-permute-done.13.rest_3_ = bf16[128,1024]{1,0:T(8,128)(2,1)S(1)} collective-permute-done((bf16[128,1024]{1,0:T(8,128)(2,1)S(1)}, bf16[128,1024]{1,0:T(8,128)(2,1)S(1)}, u32[]{:S(2)}, u32[]{:S(2)}) %collective-permute-start.13) | collective-permute-done | bytes 262176 | tf_op jit(solution)/shard_map/ppermute | solution.py:27
  78.3 8.5 %collective-permute-done.15.rest_5_ = bf16[128,1024]{1,0:T(8,128)(2,1)S(1)} collective-permute-done((bf16[128,1024]{1,0:T(8,128)(2,1)S(1)}, bf16[128,1024]{1,0:T(8,128)(2,1)S(1)}, u32[]{:S(2)}, u32[]{:S(2)}) %collective-permute-start.15) | collective-permute-done | bytes 262176 | tf_op jit(solution)/shard_map/ppermute | solution.py:27
  86.8 1.5 %collective-permute-done.19.rest_10_ = bf16[256,768]{1,0:T(8,128)(2,1)S(1)} collective-permute-done((bf16[256,768]{1,0:T(8,128)(2,1)S(1)}, bf16[256,768]{1,0:T(8,128)(2,1)S(1)}, u32[]{:S(2)}, u32[]{:S(2)}) %collective-permute-start.19) | collective-permute-done | bytes 393248 | tf_op jit(solution)/shard_map/ppermute | solution.py:27
  88.3 2.3 %finish.1 = bf16[4,256,1024]{2,1,0:T(8,128)(2,1)} custom-call(s32[1]{0:T(128)} %bitcast.refs_1_.me_ref, s32[1]{0:T(128)} %bitcast.1.refs_0_.place_ref, s32[4]{0:T(128)S(1)} %copy-done.2, f32[4,256,256]{2,1,0:T(8,128)S(1)} %get-tuple-element.49.diagonal_ref, bf16[128,1024]{1,0:T(8,128)(2,1)S(1)} %get-tuple-element.76.rest_0_, ...), custom_call_target="tpu_custom_call" | custom-call | bytes 6291456 | tf_op jit(solution)/shard_map/finish/pallas_call | solution.py:414
  (31 shorter events, 2.0 us)
Async XLA Ops:
  0.0 0.7 copy-start.2
  0.7 10.3 %copy-start = (bf16[4,256,1024]{2,1,0:T(8,128)(2,1)S(1)}, bf16[4,256,1024]{2,1,0:T(8,128)(2,1)}, u32[]{:S(2)}) copy-start(bf16[4,256,1024]{2,1,0:T(8,128)(2,1)} %rest_0_.3) | copy-start | bytes 6291460
  0.7 10.3 %copy-start.1 = (bf16[4,256,1024]{2,1,0:T(8,128)(2,1)S(1)}, bf16[4,256,1024]{2,1,0:T(8,128)(2,1)}, u32[]{:S(2)}) copy-start(bf16[4,256,1024]{2,1,0:T(8,128)(2,1)} %rest_1_.3) | copy-start | bytes 6291460
  0.7 13.5 %copy-start.5 = (s32[2,1,1024]{2,1,0:T(1,128)S(1)}, s32[2,1,1024]{2,1,0:T(1,128)}, u32[]{:S(2)}) copy-start(s32[2,1,1024]{2,1,0:T(1,128)} %refs_3_.1) | copy-start | bytes 24580
  3.3 9.3 %collective-permute-start = (bf16[2,128,1024]{2,1,0:T(8,128)(2,1)S(1)}, bf16[2,128,1024]{2,1,0:T(8,128)(2,1)S(1)}, u32[]{:S(2)}, u32[]{:S(2)}) collective-permute-start(bf16[2,128,1024]{2,1,0:T(8,128)(2,1)S(1)} %get-tuple-element.53), channel_id=1, source_target_pairs={{0,4},{4,0},{8,12},{12,8},{16,20},{20,16},{24,28},{28,24},{1,5},{5... | collective-permute-start | bytes 1572872 | tf_op jit(solution)/shard_map/ppermute | solution.py:27
  3.8 20.5 %collective-permute-start.1 = (bf16[2,128,1024]{2,1,0:T(8,128)(2,1)S(1)}, bf16[2,128,1024]{2,1,0:T(8,128)(2,1)S(1)}, u32[]{:S(2)}, u32[]{:S(2)}) collective-permute-start(bf16[2,128,1024]{2,1,0:T(8,128)(2,1)S(1)} %get-tuple-element.54), channel_id=1, source_target_pairs={{0,8},{4,12},{8,0},{12,4},{16,24},{20,28},{24,16},{28,20},{1,9},{5... | collective-permute-start | bytes 1572872 | tf_op jit(solution)/shard_map/ppermute | solution.py:27
  6.3 25.2 %collective-permute-start.2 = (bf16[2,128,1024]{2,1,0:T(8,128)(2,1)S(1)}, bf16[2,128,1024]{2,1,0:T(8,128)(2,1)S(1)}, u32[]{:S(2)}, u32[]{:S(2)}) collective-permute-start(bf16[2,128,1024]{2,1,0:T(8,128)(2,1)S(1)} %get-tuple-element.55), channel_id=1, source_target_pairs={{0,16},{4,20},{8,24},{12,28},{16,0},{20,4},{24,8},{28,12},{1,17},{... | collective-permute-start | bytes 1572872 | tf_op jit(solution)/shard_map/ppermute | solution.py:27
  7.9 23.6 %collective-permute-start.3 = (bf16[2,128,1024]{2,1,0:T(8,128)(2,1)S(1)}, bf16[2,128,1024]{2,1,0:T(8,128)(2,1)S(1)}, u32[]{:S(2)}, u32[]{:S(2)}) collective-permute-start(bf16[2,128,1024]{2,1,0:T(8,128)(2,1)S(1)} %get-tuple-element.56), channel_id=1, source_target_pairs={{0,24},{4,28},{8,16},{12,20},{16,8},{20,12},{24,0},{28,4},{1,25},{... | collective-permute-start | bytes 1572872 | tf_op jit(solution)/shard_map/ppermute | solution.py:27
  7.9 6.3 %copy-start.6 = (s32[1,1024]{1,0:T(1,128)S(1)}, s32[1,1024]{1,0:T(1,128)}, u32[]{:S(2)}) copy-start(s32[1,1024]{1,0:T(1,128)} %refs_2_.1) | copy-start | bytes 12292
  7.9 6.3 %copy-start.3 = (f32[1,1024,1024]{2,1,0:T(8,128)S(1)}, f32[1,1024,1024]{2,1,0:T(8,128)}, u32[]{:S(2)}) copy-start(f32[1,1024,1024]{2,1,0:T(8,128)} %refs_4_.1) | copy-start | bytes 12582916
  7.9 27.1 %collective-permute-start.5 = (bf16[2,2,256,256]{3,2,1,0:T(8,128)(2,1)S(1)}, bf16[2,2,256,256]{3,2,1,0:T(8,128)(2,1)S(1)}, u32[]{:S(2)}, u32[]{:S(2)}) collective-permute-start(bf16[2,2,256,256]{3,2,1,0:T(8,128)(2,1)S(1)} %get-tuple-element.64), channel_id=1, source_target_pairs={{0,2},{1,3},{2,0},{3,1},{4,6},{5,7},{6,4},{7,5},{8,10},{9,11},{10,... | collective-permute-start | bytes 1572872 | tf_op jit(solution)/shard_map/ppermute | solution.py:27
  12.6 34.5 %collective-permute-start.4 = (bf16[2,3,256,256]{3,2,1,0:T(8,128)(2,1)S(1)}, bf16[2,3,256,256]{3,2,1,0:T(8,128)(2,1)S(1)}, u32[]{:S(2)}, u32[]{:S(2)}) collective-permute-start(bf16[2,3,256,256]{3,2,1,0:T(8,128)(2,1)S(1)} %get-tuple-element.63), channel_id=1, source_target_pairs={{0,1},{1,0},{2,3},{3,2},{4,5},{5,4},{6,7},{7,6},{8,9},{9,8},{10,11... | collective-permute-start | bytes 2359304 | tf_op jit(solution)/shard_map/ppermute | solution.py:27
  14.2 0.8 copy-start.4
  24.3 22.0 %collective-permute-start.6 = (bf16[2,1,256,256]{3,2,1,0:T(8,128)(2,1)S(1)}, bf16[2,1,256,256]{3,2,1,0:T(8,128)(2,1)S(1)}, u32[]{:S(2)}, u32[]{:S(2)}) collective-permute-start(bf16[2,1,256,256]{3,2,1,0:T(8,128)(2,1)S(1)} %get-tuple-element.66), channel_id=1, source_target_pairs={{0,3},{1,2},{2,1},{3,0},{4,7},{5,6},{6,5},{7,4},{8,11},{9,10},{10,... | collective-permute-start | bytes 786440 | tf_op jit(solution)/shard_map/ppermute | solution.py:27
  31.6 25.4 %collective-permute-start.7 = (bf16[2,128,1024]{2,1,0:T(8,128)(2,1)S(1)}, bf16[2,128,1024]{2,1,0:T(8,128)(2,1)S(1)}, u32[]{:S(2)}, u32[]{:S(2)}) collective-permute-start(bf16[2,128,1024]{2,1,0:T(8,128)(2,1)S(1)} %get-tuple-element.70), channel_id=1, source_target_pairs={{0,12},{4,8},{8,4},{12,0},{16,28},{20,24},{24,20},{28,16},{1,13},{... | collective-permute-start | bytes 1572872 | tf_op jit(solution)/shard_map/ppermute | solution.py:27
  32.1 24.9 %collective-permute-start.8 = (bf16[2,128,1024]{2,1,0:T(8,128)(2,1)S(1)}, bf16[2,128,1024]{2,1,0:T(8,128)(2,1)S(1)}, u32[]{:S(2)}, u32[]{:S(2)}) collective-permute-start(bf16[2,128,1024]{2,1,0:T(8,128)(2,1)S(1)} %get-tuple-element.72), channel_id=1, source_target_pairs={{0,20},{4,16},{8,28},{12,24},{16,4},{20,0},{24,12},{28,8},{1,21},{... | collective-permute-start | bytes 1572872 | tf_op jit(solution)/shard_map/ppermute | solution.py:27
  35.0 22.6 %collective-permute-start.9 = (bf16[2,128,1024]{2,1,0:T(8,128)(2,1)S(1)}, bf16[2,128,1024]{2,1,0:T(8,128)(2,1)S(1)}, u32[]{:S(2)}, u32[]{:S(2)}) collective-permute-start(bf16[2,128,1024]{2,1,0:T(8,128)(2,1)S(1)} %get-tuple-element.74), channel_id=1, source_target_pairs={{0,28},{4,24},{8,20},{12,16},{16,12},{20,8},{24,4},{28,0},{1,29},{... | collective-permute-start | bytes 1572872 | tf_op jit(solution)/shard_map/ppermute | solution.py:27
  49.1 14.2 %collective-permute-start.10 = (bf16[256,768]{1,0:T(8,128)(2,1)S(1)}, bf16[256,768]{1,0:T(8,128)(2,1)S(1)}, u32[]{:S(2)}, u32[]{:S(2)}) collective-permute-start(bf16[256,768]{1,0:T(8,128)(2,1)S(1)} %get-tuple-element.78), channel_id=1, source_target_pairs={{0,3},{1,2},{2,1},{3,0},{4,7},{5,6},{6,5},{7,4},{8,11},{9,10},{10,... | collective-permute-start | bytes 1179656 | tf_op jit(solution)/shard_map/ppermute | solution.py:27
  56.8 11.6 %collective-permute-start.18 = (bf16[256,768]{1,0:T(8,128)(2,1)S(1)}, bf16[256,768]{1,0:T(8,128)(2,1)S(1)}, u32[]{:S(2)}, u32[]{:S(2)}) collective-permute-start(bf16[256,768]{1,0:T(8,128)(2,1)S(1)} %get-tuple-element.67), channel_id=1, source_target_pairs={{0,1},{1,0},{2,3},{3,2},{4,5},{5,4},{6,7},{7,6},{8,9},{9,8},{10,11... | collective-permute-start | bytes 1179656 | tf_op jit(solution)/shard_map/ppermute | solution.py:27
  58.4 11.6 %collective-permute-start.12 = (bf16[128,1024]{1,0:T(8,128)(2,1)S(1)}, bf16[128,1024]{1,0:T(8,128)(2,1)S(1)}, u32[]{:S(2)}, u32[]{:S(2)}) collective-permute-start(bf16[128,1024]{1,0:T(8,128)(2,1)S(1)} %get-tuple-element.80), channel_id=1, source_target_pairs={{0,8},{4,12},{8,0},{12,4},{16,24},{20,28},{24,16},{28,20},{1,9},{5... | collective-permute-start | bytes 786440 | tf_op jit(solution)/shard_map/ppermute | solution.py:27
  59.5 13.7 %collective-permute-start.14 = (bf16[128,1024]{1,0:T(8,128)(2,1)S(1)}, bf16[128,1024]{1,0:T(8,128)(2,1)S(1)}, u32[]{:S(2)}, u32[]{:S(2)}) collective-permute-start(bf16[128,1024]{1,0:T(8,128)(2,1)S(1)} %get-tuple-element.84), channel_id=1, source_target_pairs={{0,16},{4,20},{8,24},{12,28},{16,0},{20,4},{24,8},{28,12},{1,17},{... | collective-permute-start | bytes 786440 | tf_op jit(solution)/shard_map/ppermute | solution.py:27
  62.1 11.1 %collective-permute-start.16 = (bf16[128,1024]{1,0:T(8,128)(2,1)S(1)}, bf16[128,1024]{1,0:T(8,128)(2,1)S(1)}, u32[]{:S(2)}, u32[]{:S(2)}) collective-permute-start(bf16[128,1024]{1,0:T(8,128)(2,1)S(1)} %get-tuple-element.87), channel_id=1, source_target_pairs={{0,24},{4,28},{8,16},{12,20},{16,8},{20,12},{24,0},{28,4},{1,25},{... | collective-permute-start | bytes 786440 | tf_op jit(solution)/shard_map/ppermute | solution.py:27
  63.2 9.9 %collective-permute-start.11 = (bf16[128,1024]{1,0:T(8,128)(2,1)S(1)}, bf16[128,1024]{1,0:T(8,128)(2,1)S(1)}, u32[]{:S(2)}, u32[]{:S(2)}) collective-permute-start(bf16[128,1024]{1,0:T(8,128)(2,1)S(1)} %get-tuple-element.79), channel_id=1, source_target_pairs={{0,4},{4,0},{8,12},{12,8},{16,20},{20,16},{24,28},{28,24},{1,5},{5... | collective-permute-start | bytes 786440 | tf_op jit(solution)/shard_map/ppermute | solution.py:27
  68.4 19.9 %collective-permute-start.19 = (bf16[256,768]{1,0:T(8,128)(2,1)S(1)}, bf16[256,768]{1,0:T(8,128)(2,1)S(1)}, u32[]{:S(2)}, u32[]{:S(2)}) collective-permute-start(bf16[256,768]{1,0:T(8,128)(2,1)S(1)} %get-tuple-element.92), channel_id=1, source_target_pairs={{0,2},{1,3},{2,0},{3,1},{4,6},{5,7},{6,4},{7,5},{8,10},{9,11},{10,... | collective-permute-start | bytes 1179656 | tf_op jit(solution)/shard_map/ppermute | solution.py:27
  70.0 8.3 %collective-permute-start.13 = (bf16[128,1024]{1,0:T(8,128)(2,1)S(1)}, bf16[128,1024]{1,0:T(8,128)(2,1)S(1)}, u32[]{:S(2)}, u32[]{:S(2)}) collective-permute-start(bf16[128,1024]{1,0:T(8,128)(2,1)S(1)} %get-tuple-element.83), channel_id=1, source_target_pairs={{0,12},{4,8},{8,4},{12,0},{16,28},{20,24},{24,20},{28,16},{1,13},{... | collective-permute-start | bytes 786440 | tf_op jit(solution)/shard_map/ppermute | solution.py:27
  73.2 13.7 %collective-permute-start.15 = (bf16[128,1024]{1,0:T(8,128)(2,1)S(1)}, bf16[128,1024]{1,0:T(8,128)(2,1)S(1)}, u32[]{:S(2)}, u32[]{:S(2)}) collective-permute-start(bf16[128,1024]{1,0:T(8,128)(2,1)S(1)} %get-tuple-element.86), channel_id=1, source_target_pairs={{0,20},{4,16},{8,28},{12,24},{16,4},{20,0},{24,12},{28,8},{1,21},{... | collective-permute-start | bytes 786440 | tf_op jit(solution)/shard_map/ppermute | solution.py:27
  73.2 15.1 %collective-permute-start.17 = (bf16[128,1024]{1,0:T(8,128)(2,1)S(1)}, bf16[128,1024]{1,0:T(8,128)(2,1)S(1)}, u32[]{:S(2)}, u32[]{:S(2)}) collective-permute-start(bf16[128,1024]{1,0:T(8,128)(2,1)S(1)} %get-tuple-element.89), channel_id=1, source_target_pairs={{0,28},{4,24},{8,20},{12,16},{16,12},{20,8},{24,4},{28,0},{1,29},{... | collective-permute-start | bytes 786440 | tf_op jit(solution)/shard_map/ppermute | solution.py:27

commit v7 on v6

--- a/solution.py
+++ b/solution.py
@@ -380,13 +380,14 @@
 
 
 def finish_kernel(blocks, me_ref, place_ref, sizes_ref, diagonal_ref, *rest):
-    back_refs, ladder_refs = rest[:blocks], rest[blocks:-4]
+    back_refs, ladder_refs = rest[: blocks - 1], rest[blocks - 1 : -4]
     out_ref, back, held, sems = rest[-4:]
     chan_count, tile_rows, states = out_ref.shape
     place = place_ref[0]
     rows = back_refs[0].shape[0]
     for d, back_ref in enumerate(back_refs):
         back[aligned((me_ref[0] ^ d) * rows, rows), :] = back_ref[...]
+    back[aligned((me_ref[0] ^ (blocks - 1)) * rows, rows), :] = jnp.zeros((rows, states), BF16)
     row = lax.broadcasted_iota(jnp.int32, (tile_rows, tile_rows), 0) + place * tile_rows
     column = lax.broadcasted_iota(jnp.int32, (tile_rows, tile_rows), 1)
     starts = [(place ^ m) * tile_rows for m in range(len(ladder_refs))]
@@ -394,7 +395,6 @@
     copies = []
     for k, ladder_ref in enumerate(ladder_refs):
         c = place ^ k
-        size = sizes_ref[c]
         for m, start in enumerate(starts):
             span = aligned(start, tile_rows)
             part = back[aligned(c * tile_rows, tile_rows), span]
@@ -402,7 +402,7 @@
                 total = ladder_ref[:, (m - 1) * tile_rows : m * tile_rows] + part
             else:
                 total = (diagonal_ref[c] + part.astype(F32)).astype(BF16)
-            held[c, :, span] = jnp.where(highest[m] < size, total, jnp.zeros_like(total))
+            held[c, :, span] = jnp.where(highest[m] < sizes_ref[c], total, jnp.zeros_like(total))
         copies.append(pltpu.make_async_copy(held.at[c], out_ref.at[c], sems.at[k]))
         copies[-1].start()
     for copy in copies:
@@ -412,7 +412,7 @@
 def finish(me, place, sizes, shape, diagonal, back, ladder):
     chan_count, tile_rows, states = shape
     return pl.pallas_call(
-        functools.partial(finish_kernel, len(back)),
+        functools.partial(finish_kernel, len(back) + 1),
         out_shape=jax.ShapeDtypeStruct(shape, BF16),
         in_specs=[SMEM] * 3 + [VMEM] * (1 + len(back) + len(ladder)),
         out_specs=HBM,
@@ -427,6 +427,60 @@
     )(me, place, sizes, diagonal, *back, *ladder)
 
 
+def finish_last_kernel(
+    blocks, me_ref, place_ref, sizes_ref, started_ref, diagonal_ref, back_ref, *rest
+):
+    del started_ref
+    ladder_refs, (out_ref, ladder, held, sem) = rest[:-4], rest[-4:]
+    tile_rows = out_ref.shape[1]
+    place = place_ref[0]
+    rows = back_ref.shape[0]
+    first_row = (me_ref[0] ^ (blocks - 1)) * rows
+    c = first_row // tile_rows
+    inside = pl.multiple_of(first_row - c * tile_rows, rows)
+    span = pl.ds(inside, rows)
+    for k, ladder_ref in enumerate(ladder_refs):
+
+        @pl.when((c ^ place) == k)
+        def _(ladder_ref=ladder_ref):
+            ladder[...] = ladder_ref[span, :]
+
+    row = lax.broadcasted_iota(jnp.int32, (rows, tile_rows), 0) + (place * tile_rows + inside)
+    column = lax.broadcasted_iota(jnp.int32, (rows, tile_rows), 1)
+    for m in range(len(ladder_refs)):
+        start = (place ^ m) * tile_rows
+        columns = aligned(start, tile_rows)
+        part = back_ref[:, columns]
+        if m:
+            total = ladder[:, (m - 1) * tile_rows : m * tile_rows] + part
+        else:
+            total = (diagonal_ref[c, span, :] + part.astype(F32)).astype(BF16)
+        live = jnp.maximum(row, column + start) < sizes_ref[c]
+        held[:, columns] = jnp.where(live, total, jnp.zeros_like(total))
+    copy = pltpu.make_async_copy(held, out_ref.at[c, span, :], sem)
+    copy.start()
+    copy.wait()
+
+
+def finish_last(me, place, sizes, started, diagonal, back, blocks, ladder):
+    rows, states = back.shape
+    return pl.pallas_call(
+        functools.partial(finish_last_kernel, blocks),
+        out_shape=jax.ShapeDtypeStruct(started.shape, BF16),
+        in_specs=[SMEM] * 3 + [HBM] + [VMEM] * (2 + len(ladder)),
+        out_specs=HBM,
+        scratch_shapes=[
+            pltpu.VMEM((rows, ladder[0].shape[1]), BF16),
+            pltpu.VMEM((rows, states), BF16),
+            pltpu.SemaphoreType.DMA,
+        ],
+        input_output_aliases={3: 0},
+        compiler_params=params(4),
+        cost_estimate=cost(0, 6 * rows * states),
+        name="finish_last",
+    )(me, place, sizes, started, diagonal, back, *ladder)
+
+
 def ladder_gathered(sizes, pair_occupation, eta, gamma):
     _, rows, states = eta.shape
     columns = lax.broadcasted_iota(jnp.int32, (eta.shape[0], states), 1)
@@ -448,11 +502,12 @@
     "in5": ("in4", "prepare",),
     "in7": ("in6", "prepare",),
     "cross_first": ("ladder",),
-    "own2": ("own1", "cross_second",),
-    "back1": ("own3",),
-    "back3": ("back2",),
+    "own2": ("own3",),
+    "back1": ("own3", "back2",),
+    "back3": ("back2", "back1",),
     "back5": ("back4",),
     "back7": ("back6", "back1",),
+    "own1": ("own3",),
 }
 
 
@@ -622,7 +677,9 @@
             value(name)
     back = [value(f"back{d}") for d in range(chans)]
     ladder = [value(f"own{k}") for k in range(tiles)]
-    return finish(me, place, chan_sizes, generator.shape, value("prepare")[2], back, ladder)
+    diagonal = value("prepare")[2]
+    started = finish(me, place, chan_sizes, generator.shape, diagonal, back[:-1], ladder)
+    return finish_last(me, place, chan_sizes, started, diagonal, back[-1], chans, ladder)
 
 
 def per_device_whole(

time: 91 us -> 88.9 us (0.977)
  waiting for transfers between devices: 39 us -> 31.9 us
  starting transfers between devices: 20.8 us -> 23.5 us
  Pallas kernels: 29.2 us -> 30.7 us
    ppermute x20, waiting for transfers between devices: 39 us -> 31.9 us  [xor_permute(): return lax.ppermute(block, axis, [(i, i ^ step) for i in range(size)])]
    ppermute x20, starting transfers between devices: 20.8 us -> 23.5 us  [xor_permute(): return lax.ppermute(block, axis, [(i, i ^ step) for i in range(size)])]
    pallas_call x1 -> x2, Pallas kernels: 2.34 us -> 3.75 us  [the longest x1 2.35 us: finish(): pl.pallas_call(functools.partial(finish_kernel, len(back) + 1), out_shape...]
  transfers between devices with their start and end apart: 20 -> 20, of which waited for: 11 -> 11; matrix products, arithmetic and copies ran while one was open for 0% -> 0% of each run, Pallas kernels for 27% -> 30%
where the time goes in v7:
time: 88.9 us; the launch traced here: 87.8 us
  waiting for transfers between devices  31.9 us (36%)
  Pallas kernels  30.7 us (35%)
  starting transfers between devices  23.5 us (26%)
  local copies, waits for them, and re-layouts  1.43 us (2%)
    ppermute x20, waiting for transfers between devices, xor_permute(): return lax.ppermute(block, axis, [(i, i ^ step) for i in range(size)])  31.9 us
    ppermute x20, starting transfers between devices, xor_permute(): return lax.ppermute(block, axis, [(i, i ^ step) for i in range(size)])  23.5 us
    pallas_call x1, Pallas kernels, prepare(): pl.pallas_call(functools.partial(kernel, ph_count, states, order), out_sh...  9.28 us
    pallas_call x1, Pallas kernels, first_part(): pl.pallas_call(functools.partial(first_kernel, states, order), out_shape=...  5.28 us
    pallas_call x2, Pallas kernels, pack(): pl.pallas_call(functools.partial(pack_kernel, eta.shape, blocks, tiles, p...  4.19 us
    pallas_call x1, Pallas kernels, cross_second(): pl.pallas_call(functools.partial(cross_second_kernel, states, order), out...  4.13 us
    pallas_call x1, Pallas kernels, finish(): pl.pallas_call(functools.partial(finish_kernel, len(back) + 1), out_shape...  2.35 us
    pallas_call x2, Pallas kernels, cross_first(): pl.pallas_call(functools.partial(cross_first_kernel, states, order, slots...  2.06 us
  transfers between devices with their start and end apart: 20, of which 11 were waited for; matrix products, arithmetic and copies ran while one was open for 0% of the time, Pallas kernels for 30%

profile of v7, /device:TPU:0, one launch (start us, length us, event | category | flops | bytes accessed | tf_op | source)
XLA Modules:
  0.0 87.8 jit_solution(10588926416645757486)
XLA Ops:
  0.0 0.7 copy-done.2
  0.7 2.6 %pack.3 = (bf16[2,128,1024]{2,1,0:T(8,128)(2,1)S(1)}, bf16[2,128,1024]{2,1,0:T(8,128)(2,1)S(1)}, bf16[2,128,1024]{2,1,0:T(8,128)(2,1)S(1)}, bf16[2,128,1024]{2,1...) custom-call(s32[1]{0:T(128)} %bitcast.refs_1_.me_ref, s32[1]{0:T(128)} %bitcast.1.refs_0_.place_ref, s32[4]{0:T(128)S(1)} %copy-done.2, ...), custom_call_target="tpu_custom_call" | custom-call | bytes 4194304 | tf_op jit(solution)/shard_map/pack/pallas_call | solution.py:323
  3.8 2.6 %collective-permute-start.1 = (bf16[2,128,1024]{2,1,0:T(8,128)(2,1)S(1)}, bf16[2,128,1024]{2,1,0:T(8,128)(2,1)S(1)}, u32[]{:S(2)}, u32[]{:S(2)}) collective-permute-start(bf16[2,128,1024]{2,1,0:T(8,128)(2,1)S(1)} %get-tuple-element.55), channel_id=1, source_target_pairs={{0,8},{4,12},{8,0},{12,4},{16,24},{20,28},{24,16},{28,20},{1,9},{5... | collective-permute-start | bytes 1572872 | tf_op jit(solution)/shard_map/ppermute | solution.py:27
  6.3 1.5 %collective-permute-start.2 = (bf16[2,128,1024]{2,1,0:T(8,128)(2,1)S(1)}, bf16[2,128,1024]{2,1,0:T(8,128)(2,1)S(1)}, u32[]{:S(2)}, u32[]{:S(2)}) collective-permute-start(bf16[2,128,1024]{2,1,0:T(8,128)(2,1)S(1)} %get-tuple-element.56), channel_id=1, source_target_pairs={{0,16},{4,20},{8,24},{12,28},{16,0},{20,4},{24,8},{28,12},{1,17},{... | collective-permute-start | bytes 1572872 | tf_op jit(solution)/shard_map/ppermute | solution.py:27
  7.9 3.0 %collective-permute-start.5 = (bf16[2,2,256,256]{3,2,1,0:T(8,128)(2,1)S(1)}, bf16[2,2,256,256]{3,2,1,0:T(8,128)(2,1)S(1)}, u32[]{:S(2)}, u32[]{:S(2)}) collective-permute-start(bf16[2,2,256,256]{3,2,1,0:T(8,128)(2,1)S(1)} %get-tuple-element.65), channel_id=1, source_target_pairs={{0,2},{1,3},{2,0},{3,1},{4,6},{5,7},{6,4},{7,5},{8,10},{9,11},{10,... | collective-permute-start | bytes 1572872 | tf_op jit(solution)/shard_map/ppermute | solution.py:27
  10.9 1.6 %pack.2 = (bf16[2,128,1024]{2,1,0:T(8,128)(2,1)S(1)}, bf16[2,128,1024]{2,1,0:T(8,128)(2,1)S(1)}, bf16[2,128,1024]{2,1,0:T(8,128)(2,1)S(1)}, bf16[2,128,1024]{2,1...) custom-call(s32[1]{0:T(128)} %bitcast.refs_1_.me_ref, ...), custom_call_target="tpu_custom_call" | custom-call | bytes 4194304 | tf_op jit(solution)/shard_map/pack/pallas_call | solution.py:323
  12.6 1.6 %collective-permute-start.4 = (bf16[2,3,256,256]{3,2,1,0:T(8,128)(2,1)S(1)}, bf16[2,3,256,256]{3,2,1,0:T(8,128)(2,1)S(1)}, u32[]{:S(2)}, u32[]{:S(2)}) collective-permute-start(bf16[2,3,256,256]{3,2,1,0:T(8,128)(2,1)S(1)} %get-tuple-element.64), channel_id=1, source_target_pairs={{0,1},{1,0},{2,3},{3,2},{4,5},{5,4},{6,7},{7,6},{8,9},{9,8},{10,11... | collective-permute-start | bytes 2359304 | tf_op jit(solution)/shard_map/ppermute | solution.py:27
  14.2 0.8 copy-done.4
  15.0 9.3 %prepare.1 = (f32[1,1024,1024]{2,1,0:T(8,128)S(1)}, bf16[1,1024,1024]{2,1,0:T(8,128)(2,1)S(1)}, f32[4,256,256]{2,1,0:T(8,128)S(1)}, bf16[1024,1024]{1,0:T(8,128)...) custom-call(s32[1]{0:T(128)} %bitcast.1.refs_0_.place_ref, s32[1]{0:T(128)} %bitcast.refs_1_.me_ref, ...), custom_call_target="tpu_custom_call" | custom-call | flops 7516192768 | bytes 14680064 | tf_op jit(solution)/shard_map/prepare/pallas_call | solution.py:120
  24.3 7.1 %collective-permute-done.3.rest_4_ = bf16[2,128,1024]{2,1,0:T(8,128)(2,1)S(1)} collective-permute-done((bf16[2,128,1024]{2,1,0:T(8,128)(2,1)S(1)}, bf16[2,128,1024]{2,1,0:T(8,128)(2,1)S(1)}, u32[]{:S(2)}, u32[]{:S(2)}) %collective-permute-start.3) | collective-permute-done | bytes 524320 | tf_op jit(solution)/shard_map/ppermute | solution.py:27
  32.1 1.3 %collective-permute-start.8 = (bf16[2,128,1024]{2,1,0:T(8,128)(2,1)S(1)}, bf16[2,128,1024]{2,1,0:T(8,128)(2,1)S(1)}, u32[]{:S(2)}, u32[]{:S(2)}) collective-permute-start(bf16[2,128,1024]{2,1,0:T(8,128)(2,1)S(1)} %get-tuple-element.73), channel_id=1, source_target_pairs={{0,20},{4,16},{8,28},{12,24},{16,4},{20,0},{24,12},{28,8},{1,21},{... | collective-permute-start | bytes 1572872 | tf_op jit(solution)/shard_map/ppermute | solution.py:27
  33.3 1.6 %collective-permute-done.5.rest_1_ = bf16[2,2,256,256]{3,2,1,0:T(8,128)(2,1)S(1)} collective-permute-done((bf16[2,2,256,256]{3,2,1,0:T(8,128)(2,1)S(1)}, bf16[2,2,256,256]{3,2,1,0:T(8,128)(2,1)S(1)}, u32[]{:S(2)}, u32[]{:S(2)}) %collective-permute-start.5) | collective-permute-done | bytes 524320 | tf_op jit(solution)/shard_map/ppermute | solution.py:27
  35.0 11.3 %collective-permute-done.6.rest_2_ = bf16[2,1,256,256]{3,2,1,0:T(8,128)(2,1)S(1)} collective-permute-done((bf16[2,1,256,256]{3,2,1,0:T(8,128)(2,1)S(1)}, bf16[2,1,256,256]{3,2,1,0:T(8,128)(2,1)S(1)}, u32[]{:S(2)}, u32[]{:S(2)}) %collective-permute-start.6) | collective-permute-done | bytes 262176 | tf_op jit(solution)/shard_map/ppermute | solution.py:27
  46.3 0.8 collective-permute-done.4.rest_0_
  47.1 2.0 %ladder.1 = (bf16[256,768]{1,0:T(8,128)(2,1)S(1)}, bf16[256,768]{1,0:T(8,128)(2,1)S(1)}, bf16[256,768]{1,0:T(8,128)(2,1)S(1)}, bf16[256,768]{1,0:T(8,128)(2,1)S(...) custom-call(bf16[1024,1024]{1,0:T(8,128)(2,1)S(1)} %get-tuple-elemen, ...), custom_call_target="tpu_custom_call", output_to_operand_aliasing={{4}: (0, {}), {5}: (1, {})} | custom-call | flops 2147483648 | bytes 8388608 | tf_op jit(solution)/shard_map/ladder/pallas_call | solution.py:369
  49.1 2.5 %collective-permute-start.10 = (bf16[256,768]{1,0:T(8,128)(2,1)S(1)}, bf16[256,768]{1,0:T(8,128)(2,1)S(1)}, u32[]{:S(2)}, u32[]{:S(2)}) collective-permute-start(bf16[256,768]{1,0:T(8,128)(2,1)S(1)} %get-tuple-element.79), channel_id=1, source_target_pairs={{0,3},{1,2},{2,1},{3,0},{4,7},{5,6},{6,5},{7,4},{8,11},{9,10},{10,... | collective-permute-start | bytes 1179656 | tf_op jit(solution)/shard_map/ppermute | solution.py:27
  51.6 5.3 %first_part.1 = (bf16[2,1,640,1024]{3,2,1,0:T(8,128)(2,1)S(1)}, bf16[2,1,640,1024]{3,2,1,0:T(8,128)(2,1)S(1)}, f32[1,640,1024]{2,1,0:T(8,128)S(1)}) custom-call(s32[1]{0:T(128)} %bitcast.refs_1_.me_ref, f32[1,1024,1024]{2,1,0:T(8,128)S(1)} %get-tuple-element.51.turned_ref, bf16[1,1024,1024]{2,1,0:T(8,128)(2,1)S(1)} %get-tuple-element.52.select_ref, ...), custom_call_target="tpu_custom_call" | custom-call | flops 5368709120 | bytes 14680064 | tf_op jit(solution)/shard_map/first_part/pallas_call | solution.py:192
  56.9 0.6 collective-permute-done.9.rest_2_
  57.5 0.9 %cross_first.2 = (bf16[128,1024]{1,0:T(8,128)(2,1)S(1)}, bf16[128,1024]{1,0:T(8,128)(2,1)S(1)}, bf16[2,1,384,1024]{3,2,1,0:T(8,128)(2,1)S(1)}) custom-call(s32[1]{0:T(128)} %bitcast.refs_1_.me_ref, f32[1,1024,1024]{2,1,0:T(8,128)S(1)} %get-tuple-element.51.turned_ref, bf16[2,1,640,1024]{3,2,1,0:T(8,128)(2,1)S(1)} %get-tuple-element.58.left_ref, ...), custom_call_target="tpu_custom_call" | custom-call | flops 1073741824 | bytes 7340032 | tf_op jit(solution)/shard_map/cross_first/pallas_call | solution.py:243
  58.4 1.0 %collective-permute-start.11 = (bf16[128,1024]{1,0:T(8,128)(2,1)S(1)}, bf16[128,1024]{1,0:T(8,128)(2,1)S(1)}, u32[]{:S(2)}, u32[]{:S(2)}) collective-permute-start(bf16[128,1024]{1,0:T(8,128)(2,1)S(1)} %get-tuple-element.80), channel_id=1, source_target_pairs={{0,8},{4,12},{8,0},{12,4},{16,24},{20,28},{24,16},{28,20},{1,9},{5... | collective-permute-start | bytes 786440 | tf_op jit(solution)/shard_map/ppermute | solution.py:27
  59.5 1.4 %collective-permute-start.14 = (bf16[128,1024]{1,0:T(8,128)(2,1)S(1)}, bf16[128,1024]{1,0:T(8,128)(2,1)S(1)}, u32[]{:S(2)}, u32[]{:S(2)}) collective-permute-start(bf16[128,1024]{1,0:T(8,128)(2,1)S(1)} %get-tuple-element.85), channel_id=1, source_target_pairs={{0,16},{4,20},{8,24},{12,28},{16,0},{20,4},{24,8},{28,12},{1,17},{... | collective-permute-start | bytes 786440 | tf_op jit(solution)/shard_map/ppermute | solution.py:27
  60.9 1.2 %cross_first.3 = (bf16[128,1024]{1,0:T(8,128)(2,1)S(1)}, bf16[128,1024]{1,0:T(8,128)(2,1)S(1)}, bf16[128,1024]{1,0:T(8,128)(2,1)S(1)}) custom-call(s32[1]{0:T(128)} %bitcast.refs_1_.me_ref, f32[1,1024,1024]{2,1,0:T(8,128)S(1)} %get-tuple-element.51.turned_ref, bf16[2,1,640,1024]{3,2,1,0:T(8,128)(2,1)S(1)} %get-tuple-element.58.left_ref, ...), custom_call_target="tpu_custom_call" | custom-call | flops 1073741824 | bytes 7340032 | tf_op jit(solution)/shard_map/cross_first/pallas_call | solution.py:243
  62.1 1.2 %collective-permute-start.16 = (bf16[128,1024]{1,0:T(8,128)(2,1)S(1)}, bf16[128,1024]{1,0:T(8,128)(2,1)S(1)}, u32[]{:S(2)}, u32[]{:S(2)}) collective-permute-start(bf16[128,1024]{1,0:T(8,128)(2,1)S(1)} %get-tuple-element.88), channel_id=1, source_target_pairs={{0,24},{4,28},{8,16},{12,20},{16,8},{20,12},{24,0},{28,4},{1,25},{... | collective-permute-start | bytes 786440 | tf_op jit(solution)/shard_map/ppermute | solution.py:27
  63.2 1.6 %collective-permute-start.17 = (bf16[256,768]{1,0:T(8,128)(2,1)S(1)}, bf16[256,768]{1,0:T(8,128)(2,1)S(1)}, u32[]{:S(2)}, u32[]{:S(2)}) collective-permute-start(bf16[256,768]{1,0:T(8,128)(2,1)S(1)} %get-tuple-element.90), channel_id=1, source_target_pairs={{0,1},{1,0},{2,3},{3,2},{4,5},{5,4},{6,7},{7,6},{8,9},{9,8},{10,11... | collective-permute-start | bytes 1179656 | tf_op jit(solution)/shard_map/ppermute | solution.py:27
  64.8 2.6 %collective-permute-start.18 = (bf16[256,768]{1,0:T(8,128)(2,1)S(1)}, bf16[256,768]{1,0:T(8,128)(2,1)S(1)}, u32[]{:S(2)}, u32[]{:S(2)}) collective-permute-start(bf16[256,768]{1,0:T(8,128)(2,1)S(1)} %get-tuple-element.92), channel_id=1, source_target_pairs={{0,2},{1,3},{2,0},{3,1},{4,6},{5,7},{6,4},{7,5},{8,10},{9,11},{10,... | collective-permute-start | bytes 1179656 | tf_op jit(solution)/shard_map/ppermute | solution.py:27
  67.7 4.1 %cross_second.1 = (bf16[128,1024]{1,0:T(8,128)(2,1)S(1)}, bf16[128,1024]{1,0:T(8,128)(2,1)S(1)}, bf16[128,1024]{1,0:T(8,128)(2,1)S(1)}) custom-call(s32[1]{0:T(128)} %bitcast.refs_1_.me_ref, f32[1,1024,1024]{2,1,0:T(8,128)S(1)} %get-tuple-element.51.turned_ref, bf16[1,1024,1024]{2,1,0:T(8,128)(2,1)S(1)} %get-tuple-element.52.select_ref, ...), custom_call_target="tpu_custom_call" | custom-call | flops 4294967296 | bytes 14680064 | tf_op jit(solution)/shard_map/cross_second/pallas_call | solution.py:271
  71.9 1.3 %collective-permute-done.14.rest_4_ = bf16[128,1024]{1,0:T(8,128)(2,1)S(1)} collective-permute-done((bf16[128,1024]{1,0:T(8,128)(2,1)S(1)}, bf16[128,1024]{1,0:T(8,128)(2,1)S(1)}, u32[]{:S(2)}, u32[]{:S(2)}) %collective-permute-start.14) | collective-permute-done | bytes 262176 | tf_op jit(solution)/shard_map/ppermute | solution.py:27
  73.2 1.8 %collective-permute-start.13 = (bf16[128,1024]{1,0:T(8,128)(2,1)S(1)}, bf16[128,1024]{1,0:T(8,128)(2,1)S(1)}, u32[]{:S(2)}, u32[]{:S(2)}) collective-permute-start(bf16[128,1024]{1,0:T(8,128)(2,1)S(1)} %get-tuple-element.84), channel_id=1, source_target_pairs={{0,12},{4,8},{8,4},{12,0},{16,28},{20,24},{24,20},{28,16},{1,13},{... | collective-permute-start | bytes 786440 | tf_op jit(solution)/shard_map/ppermute | solution.py:27
  75.3 6.5 %collective-permute-done.15.rest_5_ = bf16[128,1024]{1,0:T(8,128)(2,1)S(1)} collective-permute-done((bf16[128,1024]{1,0:T(8,128)(2,1)S(1)}, bf16[128,1024]{1,0:T(8,128)(2,1)S(1)}, u32[]{:S(2)}, u32[]{:S(2)}) %collective-permute-start.15) | collective-permute-done | bytes 262176 | tf_op jit(solution)/shard_map/ppermute | solution.py:27
  81.8 2.0 %collective-permute-done.18.rest_9_.rest_2_ = bf16[256,768]{1,0:T(8,128)(2,1)S(1)} collective-permute-done((bf16[256,768]{1,0:T(8,128)(2,1)S(1)}, bf16[256,768]{1,0:T(8,128)(2,1)S(1)}, u32[]{:S(2)}, u32[]{:S(2)}) %collective-permute-start.18) | collective-permute-done | bytes 393248 | tf_op jit(solution)/shard_map/ppermute | solution.py:27
  83.8 2.4 %finish.1.started_ref = bf16[4,256,1024]{2,1,0:T(8,128)(2,1)} custom-call(s32[1]{0:T(128)} %bitcast.refs_1_.me_ref, s32[1]{0:T(128)} %bitcast.1.refs_0_.place_ref, s32[4]{0:T(128)S(1)} %copy-done.2, f32[4,256,256]{2,1,0:T(8,128)S(1)} %get-tuple-element.50.diagonal_ref, bf16[128,1024]{1,0:T(8,128)(2,1)S(1)} %get-tuple-element.77.rest_0_, ...), custom_call_target="tpu_custom_call" | custom-call | bytes 6291456 | tf_op jit(solution)/shard_map/finish/pallas_call | solution.py:414
  86.3 1.4 %finish_last.1 = bf16[4,256,1024]{2,1,0:T(8,128)(2,1)} custom-call(s32[1]{0:T(128)} %bitcast.refs_1_.me_ref, s32[1]{0:T(128)} %bitcast.1.refs_0_.place_ref, s32[4]{0:T(128)S(1)} %copy-done.2, bf16[4,256,1024]{2,1,0:T(8,128)(2,1)} %finish.1.started_ref, f32[4,256,256]{2,1,0:T(8,128)S(1)} %get-tuple-element.50.diagonal_ref, ...), custom_call_target="tpu_custom_call", output_to_operand_aliasing={{}: (3, {})} | custom-call | bytes 786432 | tf_op jit(solution)/shard_map/finish_last/pallas_call | solution.py:467
  (32 shorter events, 2.1 us)
Async XLA Ops:
  0.0 0.7 copy-start.2
  0.7 10.3 %copy-start = (bf16[4,256,1024]{2,1,0:T(8,128)(2,1)S(1)}, bf16[4,256,1024]{2,1,0:T(8,128)(2,1)}, u32[]{:S(2)}) copy-start(bf16[4,256,1024]{2,1,0:T(8,128)(2,1)} %rest_0_.3) | copy-start | bytes 6291460
  0.7 10.3 %copy-start.1 = (bf16[4,256,1024]{2,1,0:T(8,128)(2,1)S(1)}, bf16[4,256,1024]{2,1,0:T(8,128)(2,1)}, u32[]{:S(2)}) copy-start(bf16[4,256,1024]{2,1,0:T(8,128)(2,1)} %rest_1_.3) | copy-start | bytes 6291460
  0.7 13.5 %copy-start.5 = (s32[2,1,1024]{2,1,0:T(1,128)S(1)}, s32[2,1,1024]{2,1,0:T(1,128)}, u32[]{:S(2)}) copy-start(s32[2,1,1024]{2,1,0:T(1,128)} %refs_3_.1) | copy-start | bytes 24580
  3.3 9.3 %collective-permute-start = (bf16[2,128,1024]{2,1,0:T(8,128)(2,1)S(1)}, bf16[2,128,1024]{2,1,0:T(8,128)(2,1)S(1)}, u32[]{:S(2)}, u32[]{:S(2)}) collective-permute-start(bf16[2,128,1024]{2,1,0:T(8,128)(2,1)S(1)} %get-tuple-element.54), channel_id=1, source_target_pairs={{0,4},{4,0},{8,12},{12,8},{16,20},{20,16},{24,28},{28,24},{1,5},{5... | collective-permute-start | bytes 1572872 | tf_op jit(solution)/shard_map/ppermute | solution.py:27
  3.8 20.5 %collective-permute-start.1 = (bf16[2,128,1024]{2,1,0:T(8,128)(2,1)S(1)}, bf16[2,128,1024]{2,1,0:T(8,128)(2,1)S(1)}, u32[]{:S(2)}, u32[]{:S(2)}) collective-permute-start(bf16[2,128,1024]{2,1,0:T(8,128)(2,1)S(1)} %get-tuple-element.55), channel_id=1, source_target_pairs={{0,8},{4,12},{8,0},{12,4},{16,24},{20,28},{24,16},{28,20},{1,9},{5... | collective-permute-start | bytes 1572872 | tf_op jit(solution)/shard_map/ppermute | solution.py:27
  6.3 25.2 %collective-permute-start.2 = (bf16[2,128,1024]{2,1,0:T(8,128)(2,1)S(1)}, bf16[2,128,1024]{2,1,0:T(8,128)(2,1)S(1)}, u32[]{:S(2)}, u32[]{:S(2)}) collective-permute-start(bf16[2,128,1024]{2,1,0:T(8,128)(2,1)S(1)} %get-tuple-element.56), channel_id=1, source_target_pairs={{0,16},{4,20},{8,24},{12,28},{16,0},{20,4},{24,8},{28,12},{1,17},{... | collective-permute-start | bytes 1572872 | tf_op jit(solution)/shard_map/ppermute | solution.py:27
  7.9 23.6 %collective-permute-start.3 = (bf16[2,128,1024]{2,1,0:T(8,128)(2,1)S(1)}, bf16[2,128,1024]{2,1,0:T(8,128)(2,1)S(1)}, u32[]{:S(2)}, u32[]{:S(2)}) collective-permute-start(bf16[2,128,1024]{2,1,0:T(8,128)(2,1)S(1)} %get-tuple-element.57), channel_id=1, source_target_pairs={{0,24},{4,28},{8,16},{12,20},{16,8},{20,12},{24,0},{28,4},{1,25},{... | collective-permute-start | bytes 1572872 | tf_op jit(solution)/shard_map/ppermute | solution.py:27
  7.9 6.3 %copy-start.6 = (s32[1,1024]{1,0:T(1,128)S(1)}, s32[1,1024]{1,0:T(1,128)}, u32[]{:S(2)}) copy-start(s32[1,1024]{1,0:T(1,128)} %refs_2_.1) | copy-start | bytes 12292
  7.9 6.3 %copy-start.3 = (f32[1,1024,1024]{2,1,0:T(8,128)S(1)}, f32[1,1024,1024]{2,1,0:T(8,128)}, u32[]{:S(2)}) copy-start(f32[1,1024,1024]{2,1,0:T(8,128)} %refs_4_.1) | copy-start | bytes 12582916
  7.9 27.1 %collective-permute-start.5 = (bf16[2,2,256,256]{3,2,1,0:T(8,128)(2,1)S(1)}, bf16[2,2,256,256]{3,2,1,0:T(8,128)(2,1)S(1)}, u32[]{:S(2)}, u32[]{:S(2)}) collective-permute-start(bf16[2,2,256,256]{3,2,1,0:T(8,128)(2,1)S(1)} %get-tuple-element.65), channel_id=1, source_target_pairs={{0,2},{1,3},{2,0},{3,1},{4,6},{5,7},{6,4},{7,5},{8,10},{9,11},{10,... | collective-permute-start | bytes 1572872 | tf_op jit(solution)/shard_map/ppermute | solution.py:27
  12.6 34.5 %collective-permute-start.4 = (bf16[2,3,256,256]{3,2,1,0:T(8,128)(2,1)S(1)}, bf16[2,3,256,256]{3,2,1,0:T(8,128)(2,1)S(1)}, u32[]{:S(2)}, u32[]{:S(2)}) collective-permute-start(bf16[2,3,256,256]{3,2,1,0:T(8,128)(2,1)S(1)} %get-tuple-element.64), channel_id=1, source_target_pairs={{0,1},{1,0},{2,3},{3,2},{4,5},{5,4},{6,7},{7,6},{8,9},{9,8},{10,11... | collective-permute-start | bytes 2359304 | tf_op jit(solution)/shard_map/ppermute | solution.py:27
  14.2 0.8 copy-start.4
  24.3 22.0 %collective-permute-start.6 = (bf16[2,1,256,256]{3,2,1,0:T(8,128)(2,1)S(1)}, bf16[2,1,256,256]{3,2,1,0:T(8,128)(2,1)S(1)}, u32[]{:S(2)}, u32[]{:S(2)}) collective-permute-start(bf16[2,1,256,256]{3,2,1,0:T(8,128)(2,1)S(1)} %get-tuple-element.67), channel_id=1, source_target_pairs={{0,3},{1,2},{2,1},{3,0},{4,7},{5,6},{6,5},{7,4},{8,11},{9,10},{10,... | collective-permute-start | bytes 786440 | tf_op jit(solution)/shard_map/ppermute | solution.py:27
  31.6 25.3 %collective-permute-start.7 = (bf16[2,128,1024]{2,1,0:T(8,128)(2,1)S(1)}, bf16[2,128,1024]{2,1,0:T(8,128)(2,1)S(1)}, u32[]{:S(2)}, u32[]{:S(2)}) collective-permute-start(bf16[2,128,1024]{2,1,0:T(8,128)(2,1)S(1)} %get-tuple-element.71), channel_id=1, source_target_pairs={{0,12},{4,8},{8,4},{12,0},{16,28},{20,24},{24,20},{28,16},{1,13},{... | collective-permute-start | bytes 1572872 | tf_op jit(solution)/shard_map/ppermute | solution.py:27
  32.1 24.8 %collective-permute-start.8 = (bf16[2,128,1024]{2,1,0:T(8,128)(2,1)S(1)}, bf16[2,128,1024]{2,1,0:T(8,128)(2,1)S(1)}, u32[]{:S(2)}, u32[]{:S(2)}) collective-permute-start(bf16[2,128,1024]{2,1,0:T(8,128)(2,1)S(1)} %get-tuple-element.73), channel_id=1, source_target_pairs={{0,20},{4,16},{8,28},{12,24},{16,4},{20,0},{24,12},{28,8},{1,21},{... | collective-permute-start | bytes 1572872 | tf_op jit(solution)/shard_map/ppermute | solution.py:27
  35.0 22.6 %collective-permute-start.9 = (bf16[2,128,1024]{2,1,0:T(8,128)(2,1)S(1)}, bf16[2,128,1024]{2,1,0:T(8,128)(2,1)S(1)}, u32[]{:S(2)}, u32[]{:S(2)}) collective-permute-start(bf16[2,128,1024]{2,1,0:T(8,128)(2,1)S(1)} %get-tuple-element.75), channel_id=1, source_target_pairs={{0,28},{4,24},{8,20},{12,16},{16,12},{20,8},{24,4},{28,0},{1,29},{... | collective-permute-start | bytes 1572872 | tf_op jit(solution)/shard_map/ppermute | solution.py:27
  49.1 14.1 %collective-permute-start.10 = (bf16[256,768]{1,0:T(8,128)(2,1)S(1)}, bf16[256,768]{1,0:T(8,128)(2,1)S(1)}, u32[]{:S(2)}, u32[]{:S(2)}) collective-permute-start(bf16[256,768]{1,0:T(8,128)(2,1)S(1)} %get-tuple-element.79), channel_id=1, source_target_pairs={{0,3},{1,2},{2,1},{3,0},{4,7},{5,6},{6,5},{7,4},{8,11},{9,10},{10,... | collective-permute-start | bytes 1179656 | tf_op jit(solution)/shard_map/ppermute | solution.py:27
  58.4 9.3 %collective-permute-start.11 = (bf16[128,1024]{1,0:T(8,128)(2,1)S(1)}, bf16[128,1024]{1,0:T(8,128)(2,1)S(1)}, u32[]{:S(2)}, u32[]{:S(2)}) collective-permute-start(bf16[128,1024]{1,0:T(8,128)(2,1)S(1)} %get-tuple-element.80), channel_id=1, source_target_pairs={{0,8},{4,12},{8,0},{12,4},{16,24},{20,28},{24,16},{28,20},{1,9},{5... | collective-permute-start | bytes 786440 | tf_op jit(solution)/shard_map/ppermute | solution.py:27
  59.5 13.7 %collective-permute-start.14 = (bf16[128,1024]{1,0:T(8,128)(2,1)S(1)}, bf16[128,1024]{1,0:T(8,128)(2,1)S(1)}, u32[]{:S(2)}, u32[]{:S(2)}) collective-permute-start(bf16[128,1024]{1,0:T(8,128)(2,1)S(1)} %get-tuple-element.85), channel_id=1, source_target_pairs={{0,16},{4,20},{8,24},{12,28},{16,0},{20,4},{24,8},{28,12},{1,17},{... | collective-permute-start | bytes 786440 | tf_op jit(solution)/shard_map/ppermute | solution.py:27
  62.1 12.9 %collective-permute-start.16 = (bf16[128,1024]{1,0:T(8,128)(2,1)S(1)}, bf16[128,1024]{1,0:T(8,128)(2,1)S(1)}, u32[]{:S(2)}, u32[]{:S(2)}) collective-permute-start(bf16[128,1024]{1,0:T(8,128)(2,1)S(1)} %get-tuple-element.88), channel_id=1, source_target_pairs={{0,24},{4,28},{8,16},{12,20},{16,8},{20,12},{24,0},{28,4},{1,25},{... | collective-permute-start | bytes 786440 | tf_op jit(solution)/shard_map/ppermute | solution.py:27
  63.2 18.6 %collective-permute-start.17 = (bf16[256,768]{1,0:T(8,128)(2,1)S(1)}, bf16[256,768]{1,0:T(8,128)(2,1)S(1)}, u32[]{:S(2)}, u32[]{:S(2)}) collective-permute-start(bf16[256,768]{1,0:T(8,128)(2,1)S(1)} %get-tuple-element.90), channel_id=1, source_target_pairs={{0,1},{1,0},{2,3},{3,2},{4,5},{5,4},{6,7},{7,6},{8,9},{9,8},{10,11... | collective-permute-start | bytes 1179656 | tf_op jit(solution)/shard_map/ppermute | solution.py:27
  64.8 18.9 %collective-permute-start.18 = (bf16[256,768]{1,0:T(8,128)(2,1)S(1)}, bf16[256,768]{1,0:T(8,128)(2,1)S(1)}, u32[]{:S(2)}, u32[]{:S(2)}) collective-permute-start(bf16[256,768]{1,0:T(8,128)(2,1)S(1)} %get-tuple-element.92), channel_id=1, source_target_pairs={{0,2},{1,3},{2,0},{3,1},{4,6},{5,7},{6,4},{7,5},{8,10},{9,11},{10,... | collective-permute-start | bytes 1179656 | tf_op jit(solution)/shard_map/ppermute | solution.py:27
  67.7 5.4 %collective-permute-start.12 = (bf16[128,1024]{1,0:T(8,128)(2,1)S(1)}, bf16[128,1024]{1,0:T(8,128)(2,1)S(1)}, u32[]{:S(2)}, u32[]{:S(2)}) collective-permute-start(bf16[128,1024]{1,0:T(8,128)(2,1)S(1)} %get-tuple-element.81), channel_id=1, source_target_pairs={{0,4},{4,0},{8,12},{12,8},{16,20},{20,16},{24,28},{28,24},{1,5},{5... | collective-permute-start | bytes 786440 | tf_op jit(solution)/shard_map/ppermute | solution.py:27
  73.2 8.6 %collective-permute-start.15 = (bf16[128,1024]{1,0:T(8,128)(2,1)S(1)}, bf16[128,1024]{1,0:T(8,128)(2,1)S(1)}, u32[]{:S(2)}, u32[]{:S(2)}) collective-permute-start(bf16[128,1024]{1,0:T(8,128)(2,1)S(1)} %get-tuple-element.87), channel_id=1, source_target_pairs={{0,20},{4,16},{8,28},{12,24},{16,4},{20,0},{24,12},{28,8},{1,21},{... | collective-permute-start | bytes 786440 | tf_op jit(solution)/shard_map/ppermute | solution.py:27
  73.2 10.6 %collective-permute-start.13 = (bf16[128,1024]{1,0:T(8,128)(2,1)S(1)}, bf16[128,1024]{1,0:T(8,128)(2,1)S(1)}, u32[]{:S(2)}, u32[]{:S(2)}) collective-permute-start(bf16[128,1024]{1,0:T(8,128)(2,1)S(1)} %get-tuple-element.84), channel_id=1, source_target_pairs={{0,12},{4,8},{8,4},{12,0},{16,28},{20,24},{24,20},{28,16},{1,13},{... | collective-permute-start | bytes 786440 | tf_op jit(solution)/shard_map/ppermute | solution.py:27
  75.0 11.3 %collective-permute-start.19 = (bf16[128,1024]{1,0:T(8,128)(2,1)S(1)}, bf16[128,1024]{1,0:T(8,128)(2,1)S(1)}, u32[]{:S(2)}, u32[]{:S(2)}) collective-permute-start(bf16[128,1024]{1,0:T(8,128)(2,1)S(1)} %get-tuple-element.94), channel_id=1, source_target_pairs={{0,28},{4,24},{8,20},{12,16},{16,12},{20,8},{24,4},{28,0},{1,29},{... | collective-permute-start | bytes 786440 | tf_op jit(solution)/shard_map/ppermute | solution.py:27

commit v8 on v7

--- a/solution.py
+++ b/solution.py
@@ -506,7 +506,7 @@
     "back1": ("own3", "back2",),
     "back3": ("back2", "back1",),
     "back5": ("back4",),
-    "back7": ("back6", "back1",),
+    "back7": ("back6",),
     "own1": ("own3",),
 }
 
@@ -522,8 +522,8 @@
     "lack1",
     "lack2",
     "lack3",
+    "in5",
     "in3",
-    "in5",
     "in7",
     "first",
     "ladder",

time: 88.9 us -> 88.9 us (level)
  no operation moved by 1% of the time
where the time goes in v8:
time: 88.9 us; the launch traced here: 87.8 us
  waiting for transfers between devices  31.9 us (36%)
  Pallas kernels  30.7 us (35%)
  starting transfers between devices  23.5 us (26%)
  local copies, waits for them, and re-layouts  1.43 us (2%)
    ppermute x20, waiting for transfers between devices, xor_permute(): return lax.ppermute(block, axis, [(i, i ^ step) for i in range(size)])  31.9 us
    ppermute x20, starting transfers between devices, xor_permute(): return lax.ppermute(block, axis, [(i, i ^ step) for i in range(size)])  23.5 us
    pallas_call x1, Pallas kernels, prepare(): pl.pallas_call(functools.partial(kernel, ph_count, states, order), out_sh...  9.28 us
    pallas_call x1, Pallas kernels, first_part(): pl.pallas_call(functools.partial(first_kernel, states, order), out_shape=...  5.28 us
    pallas_call x2, Pallas kernels, pack(): pl.pallas_call(functools.partial(pack_kernel, eta.shape, blocks, tiles, p...  4.19 us
    pallas_call x1, Pallas kernels, cross_second(): pl.pallas_call(functools.partial(cross_second_kernel, states, order), out...  4.13 us
    pallas_call x1, Pallas kernels, finish(): pl.pallas_call(functools.partial(finish_kernel, len(back) + 1), out_shape...  2.35 us
    pallas_call x2, Pallas kernels, cross_first(): pl.pallas_call(functools.partial(cross_first_kernel, states, order, slots...  2.06 us
  transfers between devices with their start and end apart: 20, of which 11 were waited for; matrix products, arithmetic and copies ran while one was open for 0% of the time, Pallas kernels for 30%

profile of v8, /device:TPU:0, one launch (start us, length us, event | category | flops | bytes accessed | tf_op | source)
XLA Modules:
  0.0 87.8 jit_solution(10588926416645757486)
XLA Ops:
  0.0 0.7 copy-done.2
  0.7 2.6 %pack.3 = (bf16[2,128,1024]{2,1,0:T(8,128)(2,1)S(1)}, bf16[2,128,1024]{2,1,0:T(8,128)(2,1)S(1)}, bf16[2,128,1024]{2,1,0:T(8,128)(2,1)S(1)}, bf16[2,128,1024]{2,1...) custom-call(s32[1]{0:T(128)} %bitcast.refs_1_.me_ref, s32[1]{0:T(128)} %bitcast.1.refs_0_.place_ref, s32[4]{0:T(128)S(1)} %copy-done.2, ...), custom_call_target="tpu_custom_call" | custom-call | bytes 4194304 | tf_op jit(solution)/shard_map/pack/pallas_call | solution.py:323
  3.8 2.6 %collective-permute-start.1 = (bf16[2,128,1024]{2,1,0:T(8,128)(2,1)S(1)}, bf16[2,128,1024]{2,1,0:T(8,128)(2,1)S(1)}, u32[]{:S(2)}, u32[]{:S(2)}) collective-permute-start(bf16[2,128,1024]{2,1,0:T(8,128)(2,1)S(1)} %get-tuple-element.55), channel_id=1, source_target_pairs={{0,8},{4,12},{8,0},{12,4},{16,24},{20,28},{24,16},{28,20},{1,9},{5... | collective-permute-start | bytes 1572872 | tf_op jit(solution)/shard_map/ppermute | solution.py:27
  6.3 1.5 %collective-permute-start.2 = (bf16[2,128,1024]{2,1,0:T(8,128)(2,1)S(1)}, bf16[2,128,1024]{2,1,0:T(8,128)(2,1)S(1)}, u32[]{:S(2)}, u32[]{:S(2)}) collective-permute-start(bf16[2,128,1024]{2,1,0:T(8,128)(2,1)S(1)} %get-tuple-element.56), channel_id=1, source_target_pairs={{0,16},{4,20},{8,24},{12,28},{16,0},{20,4},{24,8},{28,12},{1,17},{... | collective-permute-start | bytes 1572872 | tf_op jit(solution)/shard_map/ppermute | solution.py:27
  7.9 3.0 %collective-permute-start.5 = (bf16[2,2,256,256]{3,2,1,0:T(8,128)(2,1)S(1)}, bf16[2,2,256,256]{3,2,1,0:T(8,128)(2,1)S(1)}, u32[]{:S(2)}, u32[]{:S(2)}) collective-permute-start(bf16[2,2,256,256]{3,2,1,0:T(8,128)(2,1)S(1)} %get-tuple-element.65), channel_id=1, source_target_pairs={{0,2},{1,3},{2,0},{3,1},{4,6},{5,7},{6,4},{7,5},{8,10},{9,11},{10,... | collective-permute-start | bytes 1572872 | tf_op jit(solution)/shard_map/ppermute | solution.py:27
  10.9 1.6 %pack.2 = (bf16[2,128,1024]{2,1,0:T(8,128)(2,1)S(1)}, bf16[2,128,1024]{2,1,0:T(8,128)(2,1)S(1)}, bf16[2,128,1024]{2,1,0:T(8,128)(2,1)S(1)}, bf16[2,128,1024]{2,1...) custom-call(s32[1]{0:T(128)} %bitcast.refs_1_.me_ref, ...), custom_call_target="tpu_custom_call" | custom-call | bytes 4194304 | tf_op jit(solution)/shard_map/pack/pallas_call | solution.py:323
  12.6 1.6 %collective-permute-start.4 = (bf16[2,3,256,256]{3,2,1,0:T(8,128)(2,1)S(1)}, bf16[2,3,256,256]{3,2,1,0:T(8,128)(2,1)S(1)}, u32[]{:S(2)}, u32[]{:S(2)}) collective-permute-start(bf16[2,3,256,256]{3,2,1,0:T(8,128)(2,1)S(1)} %get-tuple-element.64), channel_id=1, source_target_pairs={{0,1},{1,0},{2,3},{3,2},{4,5},{5,4},{6,7},{7,6},{8,9},{9,8},{10,11... | collective-permute-start | bytes 2359304 | tf_op jit(solution)/shard_map/ppermute | solution.py:27
  14.2 0.8 copy-done.4
  15.0 9.3 %prepare.1 = (f32[1,1024,1024]{2,1,0:T(8,128)S(1)}, bf16[1,1024,1024]{2,1,0:T(8,128)(2,1)S(1)}, f32[4,256,256]{2,1,0:T(8,128)S(1)}, bf16[1024,1024]{1,0:T(8,128)...) custom-call(s32[1]{0:T(128)} %bitcast.1.refs_0_.place_ref, s32[1]{0:T(128)} %bitcast.refs_1_.me_ref, ...), custom_call_target="tpu_custom_call" | custom-call | flops 7516192768 | bytes 14680064 | tf_op jit(solution)/shard_map/prepare/pallas_call | solution.py:120
  24.3 7.1 %collective-permute-done.3.rest_4_ = bf16[2,128,1024]{2,1,0:T(8,128)(2,1)S(1)} collective-permute-done((bf16[2,128,1024]{2,1,0:T(8,128)(2,1)S(1)}, bf16[2,128,1024]{2,1,0:T(8,128)(2,1)S(1)}, u32[]{:S(2)}, u32[]{:S(2)}) %collective-permute-start.3) | collective-permute-done | bytes 524320 | tf_op jit(solution)/shard_map/ppermute | solution.py:27
  32.1 1.3 %collective-permute-start.8 = (bf16[2,128,1024]{2,1,0:T(8,128)(2,1)S(1)}, bf16[2,128,1024]{2,1,0:T(8,128)(2,1)S(1)}, u32[]{:S(2)}, u32[]{:S(2)}) collective-permute-start(bf16[2,128,1024]{2,1,0:T(8,128)(2,1)S(1)} %get-tuple-element.73), channel_id=1, source_target_pairs={{0,20},{4,16},{8,28},{12,24},{16,4},{20,0},{24,12},{28,8},{1,21},{... | collective-permute-start | bytes 1572872 | tf_op jit(solution)/shard_map/ppermute | solution.py:27
  33.3 1.6 %collective-permute-done.5.rest_1_ = bf16[2,2,256,256]{3,2,1,0:T(8,128)(2,1)S(1)} collective-permute-done((bf16[2,2,256,256]{3,2,1,0:T(8,128)(2,1)S(1)}, bf16[2,2,256,256]{3,2,1,0:T(8,128)(2,1)S(1)}, u32[]{:S(2)}, u32[]{:S(2)}) %collective-permute-start.5) | collective-permute-done | bytes 524320 | tf_op jit(solution)/shard_map/ppermute | solution.py:27
  35.0 11.3 %collective-permute-done.6.rest_2_ = bf16[2,1,256,256]{3,2,1,0:T(8,128)(2,1)S(1)} collective-permute-done((bf16[2,1,256,256]{3,2,1,0:T(8,128)(2,1)S(1)}, bf16[2,1,256,256]{3,2,1,0:T(8,128)(2,1)S(1)}, u32[]{:S(2)}, u32[]{:S(2)}) %collective-permute-start.6) | collective-permute-done | bytes 262176 | tf_op jit(solution)/shard_map/ppermute | solution.py:27
  46.3 0.8 collective-permute-done.4.rest_0_
  47.1 2.0 %ladder.1 = (bf16[256,768]{1,0:T(8,128)(2,1)S(1)}, bf16[256,768]{1,0:T(8,128)(2,1)S(1)}, bf16[256,768]{1,0:T(8,128)(2,1)S(1)}, bf16[256,768]{1,0:T(8,128)(2,1)S(...) custom-call(bf16[1024,1024]{1,0:T(8,128)(2,1)S(1)} %get-tuple-elemen, ...), custom_call_target="tpu_custom_call", output_to_operand_aliasing={{4}: (0, {}), {5}: (1, {})} | custom-call | flops 2147483648 | bytes 8388608 | tf_op jit(solution)/shard_map/ladder/pallas_call | solution.py:369
  49.1 2.5 %collective-permute-start.10 = (bf16[256,768]{1,0:T(8,128)(2,1)S(1)}, bf16[256,768]{1,0:T(8,128)(2,1)S(1)}, u32[]{:S(2)}, u32[]{:S(2)}) collective-permute-start(bf16[256,768]{1,0:T(8,128)(2,1)S(1)} %get-tuple-element.79), channel_id=1, source_target_pairs={{0,3},{1,2},{2,1},{3,0},{4,7},{5,6},{6,5},{7,4},{8,11},{9,10},{10,... | collective-permute-start | bytes 1179656 | tf_op jit(solution)/shard_map/ppermute | solution.py:27
  51.6 5.3 %first_part.1 = (bf16[2,1,640,1024]{3,2,1,0:T(8,128)(2,1)S(1)}, bf16[2,1,640,1024]{3,2,1,0:T(8,128)(2,1)S(1)}, f32[1,640,1024]{2,1,0:T(8,128)S(1)}) custom-call(s32[1]{0:T(128)} %bitcast.refs_1_.me_ref, f32[1,1024,1024]{2,1,0:T(8,128)S(1)} %get-tuple-element.51.turned_ref, bf16[1,1024,1024]{2,1,0:T(8,128)(2,1)S(1)} %get-tuple-element.52.select_ref, ...), custom_call_target="tpu_custom_call" | custom-call | flops 5368709120 | bytes 14680064 | tf_op jit(solution)/shard_map/first_part/pallas_call | solution.py:192
  56.9 0.6 collective-permute-done.9.rest_2_
  57.5 0.9 %cross_first.2 = (bf16[128,1024]{1,0:T(8,128)(2,1)S(1)}, bf16[128,1024]{1,0:T(8,128)(2,1)S(1)}, bf16[2,1,384,1024]{3,2,1,0:T(8,128)(2,1)S(1)}) custom-call(s32[1]{0:T(128)} %bitcast.refs_1_.me_ref, f32[1,1024,1024]{2,1,0:T(8,128)S(1)} %get-tuple-element.51.turned_ref, bf16[2,1,640,1024]{3,2,1,0:T(8,128)(2,1)S(1)} %get-tuple-element.58.left_ref, ...), custom_call_target="tpu_custom_call" | custom-call | flops 1073741824 | bytes 7340032 | tf_op jit(solution)/shard_map/cross_first/pallas_call | solution.py:243
  58.4 1.0 %collective-permute-start.11 = (bf16[128,1024]{1,0:T(8,128)(2,1)S(1)}, bf16[128,1024]{1,0:T(8,128)(2,1)S(1)}, u32[]{:S(2)}, u32[]{:S(2)}) collective-permute-start(bf16[128,1024]{1,0:T(8,128)(2,1)S(1)} %get-tuple-element.80), channel_id=1, source_target_pairs={{0,8},{4,12},{8,0},{12,4},{16,24},{20,28},{24,16},{28,20},{1,9},{5... | collective-permute-start | bytes 786440 | tf_op jit(solution)/shard_map/ppermute | solution.py:27
  59.5 1.4 %collective-permute-start.14 = (bf16[128,1024]{1,0:T(8,128)(2,1)S(1)}, bf16[128,1024]{1,0:T(8,128)(2,1)S(1)}, u32[]{:S(2)}, u32[]{:S(2)}) collective-permute-start(bf16[128,1024]{1,0:T(8,128)(2,1)S(1)} %get-tuple-element.85), channel_id=1, source_target_pairs={{0,16},{4,20},{8,24},{12,28},{16,0},{20,4},{24,8},{28,12},{1,17},{... | collective-permute-start | bytes 786440 | tf_op jit(solution)/shard_map/ppermute | solution.py:27
  60.9 1.2 %cross_first.3 = (bf16[128,1024]{1,0:T(8,128)(2,1)S(1)}, bf16[128,1024]{1,0:T(8,128)(2,1)S(1)}, bf16[128,1024]{1,0:T(8,128)(2,1)S(1)}) custom-call(s32[1]{0:T(128)} %bitcast.refs_1_.me_ref, f32[1,1024,1024]{2,1,0:T(8,128)S(1)} %get-tuple-element.51.turned_ref, bf16[2,1,640,1024]{3,2,1,0:T(8,128)(2,1)S(1)} %get-tuple-element.58.left_ref, ...), custom_call_target="tpu_custom_call" | custom-call | flops 1073741824 | bytes 7340032 | tf_op jit(solution)/shard_map/cross_first/pallas_call | solution.py:243
  62.1 1.2 %collective-permute-start.16 = (bf16[128,1024]{1,0:T(8,128)(2,1)S(1)}, bf16[128,1024]{1,0:T(8,128)(2,1)S(1)}, u32[]{:S(2)}, u32[]{:S(2)}) collective-permute-start(bf16[128,1024]{1,0:T(8,128)(2,1)S(1)} %get-tuple-element.88), channel_id=1, source_target_pairs={{0,24},{4,28},{8,16},{12,20},{16,8},{20,12},{24,0},{28,4},{1,25},{... | collective-permute-start | bytes 786440 | tf_op jit(solution)/shard_map/ppermute | solution.py:27
  63.2 1.6 %collective-permute-start.17 = (bf16[256,768]{1,0:T(8,128)(2,1)S(1)}, bf16[256,768]{1,0:T(8,128)(2,1)S(1)}, u32[]{:S(2)}, u32[]{:S(2)}) collective-permute-start(bf16[256,768]{1,0:T(8,128)(2,1)S(1)} %get-tuple-element.90), channel_id=1, source_target_pairs={{0,1},{1,0},{2,3},{3,2},{4,5},{5,4},{6,7},{7,6},{8,9},{9,8},{10,11... | collective-permute-start | bytes 1179656 | tf_op jit(solution)/shard_map/ppermute | solution.py:27
  64.8 2.6 %collective-permute-start.18 = (bf16[256,768]{1,0:T(8,128)(2,1)S(1)}, bf16[256,768]{1,0:T(8,128)(2,1)S(1)}, u32[]{:S(2)}, u32[]{:S(2)}) collective-permute-start(bf16[256,768]{1,0:T(8,128)(2,1)S(1)} %get-tuple-element.92), channel_id=1, source_target_pairs={{0,2},{1,3},{2,0},{3,1},{4,6},{5,7},{6,4},{7,5},{8,10},{9,11},{10,... | collective-permute-start | bytes 1179656 | tf_op jit(solution)/shard_map/ppermute | solution.py:27
  67.7 4.1 %cross_second.1 = (bf16[128,1024]{1,0:T(8,128)(2,1)S(1)}, bf16[128,1024]{1,0:T(8,128)(2,1)S(1)}, bf16[128,1024]{1,0:T(8,128)(2,1)S(1)}) custom-call(s32[1]{0:T(128)} %bitcast.refs_1_.me_ref, f32[1,1024,1024]{2,1,0:T(8,128)S(1)} %get-tuple-element.51.turned_ref, bf16[1,1024,1024]{2,1,0:T(8,128)(2,1)S(1)} %get-tuple-element.52.select_ref, ...), custom_call_target="tpu_custom_call" | custom-call | flops 4294967296 | bytes 14680064 | tf_op jit(solution)/shard_map/cross_second/pallas_call | solution.py:271
  71.9 1.3 %collective-permute-done.14.rest_4_ = bf16[128,1024]{1,0:T(8,128)(2,1)S(1)} collective-permute-done((bf16[128,1024]{1,0:T(8,128)(2,1)S(1)}, bf16[128,1024]{1,0:T(8,128)(2,1)S(1)}, u32[]{:S(2)}, u32[]{:S(2)}) %collective-permute-start.14) | collective-permute-done | bytes 262176 | tf_op jit(solution)/shard_map/ppermute | solution.py:27
  73.2 1.8 %collective-permute-start.13 = (bf16[128,1024]{1,0:T(8,128)(2,1)S(1)}, bf16[128,1024]{1,0:T(8,128)(2,1)S(1)}, u32[]{:S(2)}, u32[]{:S(2)}) collective-permute-start(bf16[128,1024]{1,0:T(8,128)(2,1)S(1)} %get-tuple-element.84), channel_id=1, source_target_pairs={{0,12},{4,8},{8,4},{12,0},{16,28},{20,24},{24,20},{28,16},{1,13},{... | collective-permute-start | bytes 786440 | tf_op jit(solution)/shard_map/ppermute | solution.py:27
  75.3 6.5 %collective-permute-done.15.rest_5_ = bf16[128,1024]{1,0:T(8,128)(2,1)S(1)} collective-permute-done((bf16[128,1024]{1,0:T(8,128)(2,1)S(1)}, bf16[128,1024]{1,0:T(8,128)(2,1)S(1)}, u32[]{:S(2)}, u32[]{:S(2)}) %collective-permute-start.15) | collective-permute-done | bytes 262176 | tf_op jit(solution)/shard_map/ppermute | solution.py:27
  81.8 2.0 %collective-permute-done.18.rest_9_.rest_2_ = bf16[256,768]{1,0:T(8,128)(2,1)S(1)} collective-permute-done((bf16[256,768]{1,0:T(8,128)(2,1)S(1)}, bf16[256,768]{1,0:T(8,128)(2,1)S(1)}, u32[]{:S(2)}, u32[]{:S(2)}) %collective-permute-start.18) | collective-permute-done | bytes 393248 | tf_op jit(solution)/shard_map/ppermute | solution.py:27
  83.8 2.4 %finish.1.started_ref = bf16[4,256,1024]{2,1,0:T(8,128)(2,1)} custom-call(s32[1]{0:T(128)} %bitcast.refs_1_.me_ref, s32[1]{0:T(128)} %bitcast.1.refs_0_.place_ref, s32[4]{0:T(128)S(1)} %copy-done.2, f32[4,256,256]{2,1,0:T(8,128)S(1)} %get-tuple-element.50.diagonal_ref, bf16[128,1024]{1,0:T(8,128)(2,1)S(1)} %get-tuple-element.77.rest_0_, ...), custom_call_target="tpu_custom_call" | custom-call | bytes 6291456 | tf_op jit(solution)/shard_map/finish/pallas_call | solution.py:414
  86.3 1.4 %finish_last.1 = bf16[4,256,1024]{2,1,0:T(8,128)(2,1)} custom-call(s32[1]{0:T(128)} %bitcast.refs_1_.me_ref, s32[1]{0:T(128)} %bitcast.1.refs_0_.place_ref, s32[4]{0:T(128)S(1)} %copy-done.2, bf16[4,256,1024]{2,1,0:T(8,128)(2,1)} %finish.1.started_ref, f32[4,256,256]{2,1,0:T(8,128)S(1)} %get-tuple-element.50.diagonal_ref, ...), custom_call_target="tpu_custom_call", output_to_operand_aliasing={{}: (3, {})} | custom-call | bytes 786432 | tf_op jit(solution)/shard_map/finish_last/pallas_call | solution.py:467
  (32 shorter events, 2.1 us)
Async XLA Ops:
  0.0 0.7 copy-start.2
  0.7 10.3 %copy-start = (bf16[4,256,1024]{2,1,0:T(8,128)(2,1)S(1)}, bf16[4,256,1024]{2,1,0:T(8,128)(2,1)}, u32[]{:S(2)}) copy-start(bf16[4,256,1024]{2,1,0:T(8,128)(2,1)} %rest_0_.3) | copy-start | bytes 6291460
  0.7 10.3 %copy-start.1 = (bf16[4,256,1024]{2,1,0:T(8,128)(2,1)S(1)}, bf16[4,256,1024]{2,1,0:T(8,128)(2,1)}, u32[]{:S(2)}) copy-start(bf16[4,256,1024]{2,1,0:T(8,128)(2,1)} %rest_1_.3) | copy-start | bytes 6291460
  0.7 13.5 %copy-start.5 = (s32[2,1,1024]{2,1,0:T(1,128)S(1)}, s32[2,1,1024]{2,1,0:T(1,128)}, u32[]{:S(2)}) copy-start(s32[2,1,1024]{2,1,0:T(1,128)} %refs_3_.1) | copy-start | bytes 24580
  3.3 9.3 %collective-permute-start = (bf16[2,128,1024]{2,1,0:T(8,128)(2,1)S(1)}, bf16[2,128,1024]{2,1,0:T(8,128)(2,1)S(1)}, u32[]{:S(2)}, u32[]{:S(2)}) collective-permute-start(bf16[2,128,1024]{2,1,0:T(8,128)(2,1)S(1)} %get-tuple-element.54), channel_id=1, source_target_pairs={{0,4},{4,0},{8,12},{12,8},{16,20},{20,16},{24,28},{28,24},{1,5},{5... | collective-permute-start | bytes 1572872 | tf_op jit(solution)/shard_map/ppermute | solution.py:27
  3.8 20.5 %collective-permute-start.1 = (bf16[2,128,1024]{2,1,0:T(8,128)(2,1)S(1)}, bf16[2,128,1024]{2,1,0:T(8,128)(2,1)S(1)}, u32[]{:S(2)}, u32[]{:S(2)}) collective-permute-start(bf16[2,128,1024]{2,1,0:T(8,128)(2,1)S(1)} %get-tuple-element.55), channel_id=1, source_target_pairs={{0,8},{4,12},{8,0},{12,4},{16,24},{20,28},{24,16},{28,20},{1,9},{5... | collective-permute-start | bytes 1572872 | tf_op jit(solution)/shard_map/ppermute | solution.py:27
  6.3 25.2 %collective-permute-start.2 = (bf16[2,128,1024]{2,1,0:T(8,128)(2,1)S(1)}, bf16[2,128,1024]{2,1,0:T(8,128)(2,1)S(1)}, u32[]{:S(2)}, u32[]{:S(2)}) collective-permute-start(bf16[2,128,1024]{2,1,0:T(8,128)(2,1)S(1)} %get-tuple-element.56), channel_id=1, source_target_pairs={{0,16},{4,20},{8,24},{12,28},{16,0},{20,4},{24,8},{28,12},{1,17},{... | collective-permute-start | bytes 1572872 | tf_op jit(solution)/shard_map/ppermute | solution.py:27
  7.9 23.6 %collective-permute-start.3 = (bf16[2,128,1024]{2,1,0:T(8,128)(2,1)S(1)}, bf16[2,128,1024]{2,1,0:T(8,128)(2,1)S(1)}, u32[]{:S(2)}, u32[]{:S(2)}) collective-permute-start(bf16[2,128,1024]{2,1,0:T(8,128)(2,1)S(1)} %get-tuple-element.57), channel_id=1, source_target_pairs={{0,24},{4,28},{8,16},{12,20},{16,8},{20,12},{24,0},{28,4},{1,25},{... | collective-permute-start | bytes 1572872 | tf_op jit(solution)/shard_map/ppermute | solution.py:27
  7.9 6.3 %copy-start.6 = (s32[1,1024]{1,0:T(1,128)S(1)}, s32[1,1024]{1,0:T(1,128)}, u32[]{:S(2)}) copy-start(s32[1,1024]{1,0:T(1,128)} %refs_2_.1) | copy-start | bytes 12292
  7.9 6.3 %copy-start.3 = (f32[1,1024,1024]{2,1,0:T(8,128)S(1)}, f32[1,1024,1024]{2,1,0:T(8,128)}, u32[]{:S(2)}) copy-start(f32[1,1024,1024]{2,1,0:T(8,128)} %refs_4_.1) | copy-start | bytes 12582916
  7.9 27.1 %collective-permute-start.5 = (bf16[2,2,256,256]{3,2,1,0:T(8,128)(2,1)S(1)}, bf16[2,2,256,256]{3,2,1,0:T(8,128)(2,1)S(1)}, u32[]{:S(2)}, u32[]{:S(2)}) collective-permute-start(bf16[2,2,256,256]{3,2,1,0:T(8,128)(2,1)S(1)} %get-tuple-element.65), channel_id=1, source_target_pairs={{0,2},{1,3},{2,0},{3,1},{4,6},{5,7},{6,4},{7,5},{8,10},{9,11},{10,... | collective-permute-start | bytes 1572872 | tf_op jit(solution)/shard_map/ppermute | solution.py:27
  12.6 34.5 %collective-permute-start.4 = (bf16[2,3,256,256]{3,2,1,0:T(8,128)(2,1)S(1)}, bf16[2,3,256,256]{3,2,1,0:T(8,128)(2,1)S(1)}, u32[]{:S(2)}, u32[]{:S(2)}) collective-permute-start(bf16[2,3,256,256]{3,2,1,0:T(8,128)(2,1)S(1)} %get-tuple-element.64), channel_id=1, source_target_pairs={{0,1},{1,0},{2,3},{3,2},{4,5},{5,4},{6,7},{7,6},{8,9},{9,8},{10,11... | collective-permute-start | bytes 2359304 | tf_op jit(solution)/shard_map/ppermute | solution.py:27
  14.2 0.8 copy-start.4
  24.3 22.0 %collective-permute-start.6 = (bf16[2,1,256,256]{3,2,1,0:T(8,128)(2,1)S(1)}, bf16[2,1,256,256]{3,2,1,0:T(8,128)(2,1)S(1)}, u32[]{:S(2)}, u32[]{:S(2)}) collective-permute-start(bf16[2,1,256,256]{3,2,1,0:T(8,128)(2,1)S(1)} %get-tuple-element.67), channel_id=1, source_target_pairs={{0,3},{1,2},{2,1},{3,0},{4,7},{5,6},{6,5},{7,4},{8,11},{9,10},{10,... | collective-permute-start | bytes 786440 | tf_op jit(solution)/shard_map/ppermute | solution.py:27
  31.6 25.3 %collective-permute-start.7 = (bf16[2,128,1024]{2,1,0:T(8,128)(2,1)S(1)}, bf16[2,128,1024]{2,1,0:T(8,128)(2,1)S(1)}, u32[]{:S(2)}, u32[]{:S(2)}) collective-permute-start(bf16[2,128,1024]{2,1,0:T(8,128)(2,1)S(1)} %get-tuple-element.71), channel_id=1, source_target_pairs={{0,12},{4,8},{8,4},{12,0},{16,28},{20,24},{24,20},{28,16},{1,13},{... | collective-permute-start | bytes 1572872 | tf_op jit(solution)/shard_map/ppermute | solution.py:27
  32.1 24.8 %collective-permute-start.8 = (bf16[2,128,1024]{2,1,0:T(8,128)(2,1)S(1)}, bf16[2,128,1024]{2,1,0:T(8,128)(2,1)S(1)}, u32[]{:S(2)}, u32[]{:S(2)}) collective-permute-start(bf16[2,128,1024]{2,1,0:T(8,128)(2,1)S(1)} %get-tuple-element.73), channel_id=1, source_target_pairs={{0,20},{4,16},{8,28},{12,24},{16,4},{20,0},{24,12},{28,8},{1,21},{... | collective-permute-start | bytes 1572872 | tf_op jit(solution)/shard_map/ppermute | solution.py:27
  35.0 22.6 %collective-permute-start.9 = (bf16[2,128,1024]{2,1,0:T(8,128)(2,1)S(1)}, bf16[2,128,1024]{2,1,0:T(8,128)(2,1)S(1)}, u32[]{:S(2)}, u32[]{:S(2)}) collective-permute-start(bf16[2,128,1024]{2,1,0:T(8,128)(2,1)S(1)} %get-tuple-element.75), channel_id=1, source_target_pairs={{0,28},{4,24},{8,20},{12,16},{16,12},{20,8},{24,4},{28,0},{1,29},{... | collective-permute-start | bytes 1572872 | tf_op jit(solution)/shard_map/ppermute | solution.py:27
  49.1 14.1 %collective-permute-start.10 = (bf16[256,768]{1,0:T(8,128)(2,1)S(1)}, bf16[256,768]{1,0:T(8,128)(2,1)S(1)}, u32[]{:S(2)}, u32[]{:S(2)}) collective-permute-start(bf16[256,768]{1,0:T(8,128)(2,1)S(1)} %get-tuple-element.79), channel_id=1, source_target_pairs={{0,3},{1,2},{2,1},{3,0},{4,7},{5,6},{6,5},{7,4},{8,11},{9,10},{10,... | collective-permute-start | bytes 1179656 | tf_op jit(solution)/shard_map/ppermute | solution.py:27
  58.4 9.3 %collective-permute-start.11 = (bf16[128,1024]{1,0:T(8,128)(2,1)S(1)}, bf16[128,1024]{1,0:T(8,128)(2,1)S(1)}, u32[]{:S(2)}, u32[]{:S(2)}) collective-permute-start(bf16[128,1024]{1,0:T(8,128)(2,1)S(1)} %get-tuple-element.80), channel_id=1, source_target_pairs={{0,8},{4,12},{8,0},{12,4},{16,24},{20,28},{24,16},{28,20},{1,9},{5... | collective-permute-start | bytes 786440 | tf_op jit(solution)/shard_map/ppermute | solution.py:27
  59.5 13.7 %collective-permute-start.14 = (bf16[128,1024]{1,0:T(8,128)(2,1)S(1)}, bf16[128,1024]{1,0:T(8,128)(2,1)S(1)}, u32[]{:S(2)}, u32[]{:S(2)}) collective-permute-start(bf16[128,1024]{1,0:T(8,128)(2,1)S(1)} %get-tuple-element.85), channel_id=1, source_target_pairs={{0,16},{4,20},{8,24},{12,28},{16,0},{20,4},{24,8},{28,12},{1,17},{... | collective-permute-start | bytes 786440 | tf_op jit(solution)/shard_map/ppermute | solution.py:27
  62.1 12.9 %collective-permute-start.16 = (bf16[128,1024]{1,0:T(8,128)(2,1)S(1)}, bf16[128,1024]{1,0:T(8,128)(2,1)S(1)}, u32[]{:S(2)}, u32[]{:S(2)}) collective-permute-start(bf16[128,1024]{1,0:T(8,128)(2,1)S(1)} %get-tuple-element.88), channel_id=1, source_target_pairs={{0,24},{4,28},{8,16},{12,20},{16,8},{20,12},{24,0},{28,4},{1,25},{... | collective-permute-start | bytes 786440 | tf_op jit(solution)/shard_map/ppermute | solution.py:27
  63.2 18.6 %collective-permute-start.17 = (bf16[256,768]{1,0:T(8,128)(2,1)S(1)}, bf16[256,768]{1,0:T(8,128)(2,1)S(1)}, u32[]{:S(2)}, u32[]{:S(2)}) collective-permute-start(bf16[256,768]{1,0:T(8,128)(2,1)S(1)} %get-tuple-element.90), channel_id=1, source_target_pairs={{0,1},{1,0},{2,3},{3,2},{4,5},{5,4},{6,7},{7,6},{8,9},{9,8},{10,11... | collective-permute-start | bytes 1179656 | tf_op jit(solution)/shard_map/ppermute | solution.py:27
  64.8 18.9 %collective-permute-start.18 = (bf16[256,768]{1,0:T(8,128)(2,1)S(1)}, bf16[256,768]{1,0:T(8,128)(2,1)S(1)}, u32[]{:S(2)}, u32[]{:S(2)}) collective-permute-start(bf16[256,768]{1,0:T(8,128)(2,1)S(1)} %get-tuple-element.92), channel_id=1, source_target_pairs={{0,2},{1,3},{2,0},{3,1},{4,6},{5,7},{6,4},{7,5},{8,10},{9,11},{10,... | collective-permute-start | bytes 1179656 | tf_op jit(solution)/shard_map/ppermute | solution.py:27
  67.7 5.4 %collective-permute-start.12 = (bf16[128,1024]{1,0:T(8,128)(2,1)S(1)}, bf16[128,1024]{1,0:T(8,128)(2,1)S(1)}, u32[]{:S(2)}, u32[]{:S(2)}) collective-permute-start(bf16[128,1024]{1,0:T(8,128)(2,1)S(1)} %get-tuple-element.81), channel_id=1, source_target_pairs={{0,4},{4,0},{8,12},{12,8},{16,20},{20,16},{24,28},{28,24},{1,5},{5... | collective-permute-start | bytes 786440 | tf_op jit(solution)/shard_map/ppermute | solution.py:27
  73.2 8.6 %collective-permute-start.15 = (bf16[128,1024]{1,0:T(8,128)(2,1)S(1)}, bf16[128,1024]{1,0:T(8,128)(2,1)S(1)}, u32[]{:S(2)}, u32[]{:S(2)}) collective-permute-start(bf16[128,1024]{1,0:T(8,128)(2,1)S(1)} %get-tuple-element.87), channel_id=1, source_target_pairs={{0,20},{4,16},{8,28},{12,24},{16,4},{20,0},{24,12},{28,8},{1,21},{... | collective-permute-start | bytes 786440 | tf_op jit(solution)/shard_map/ppermute | solution.py:27
  73.2 10.6 %collective-permute-start.13 = (bf16[128,1024]{1,0:T(8,128)(2,1)S(1)}, bf16[128,1024]{1,0:T(8,128)(2,1)S(1)}, u32[]{:S(2)}, u32[]{:S(2)}) collective-permute-start(bf16[128,1024]{1,0:T(8,128)(2,1)S(1)} %get-tuple-element.84), channel_id=1, source_target_pairs={{0,12},{4,8},{8,4},{12,0},{16,28},{20,24},{24,20},{28,16},{1,13},{... | collective-permute-start | bytes 786440 | tf_op jit(solution)/shard_map/ppermute | solution.py:27
  75.0 11.3 %collective-permute-start.19 = (bf16[128,1024]{1,0:T(8,128)(2,1)S(1)}, bf16[128,1024]{1,0:T(8,128)(2,1)S(1)}, u32[]{:S(2)}, u32[]{:S(2)}) collective-permute-start(bf16[128,1024]{1,0:T(8,128)(2,1)S(1)} %get-tuple-element.94), channel_id=1, source_target_pairs={{0,28},{4,24},{8,20},{12,16},{16,12},{20,8},{24,4},{28,0},{1,29},{... | collective-permute-start | bytes 786440 | tf_op jit(solution)/shard_map/ppermute | solution.py:27
